TPU v7x, 128 devices: a whole 4x4x4 slice. The times are simulated.
128 devices in a mesh: group: 8 (over z, core), mp: 16 (over x, y).
Axes of the slice: x: 4, y: 4, z: 4, core: 2. Of those that a mesh axis runs over, the one named last changes fastest.
Arguments:
- tokens: bfloat16 [1024, 16384], P('group', 'mp'), may hold values from -6 to 6
- gate_weight: bfloat16 [16384, 26624], P('mp', 'group'), may hold values from -0.046875 to 0.046875
- up_weight: bfloat16 [16384, 26624], P('mp', 'group'), may hold values from -0.046875 to 0.046875
- down_weight: bfloat16 [26624, 16384], P('group', 'mp'), may hold values from -0.0390625 to 0.0390625
Outputs:
- mixed: bfloat16 [1024, 16384], P('group', 'mp')
All inputs are finite; a program needn't handle non-finite values.
Results may differ from a plain program's by a relative error of at most 0.034.
Values may be sent and summed in bfloat16 or wider, within the bound.
No kernel may reach another device: no remote copies, remote signals or barrier semaphores. Data moves between devices by JAX's collectives and lax.ppermute only.
A program may use at most 128 MiB of HBM per device.

v0:
```python
import jax
import jax.numpy as jnp
from jax import lax
from jax.sharding import PartitionSpec as P


def local(tokens, gate_weight, up_weight, down_weight):
    shard_piece = lax.all_gather(tokens, "group", axis=0, tiled=True)
    gate_part = jnp.dot(shard_piece, gate_weight, preferred_element_type=jnp.float32)
    up_part = jnp.dot(shard_piece, up_weight, preferred_element_type=jnp.float32)
    partial_value = jnp.stack((gate_part, up_part), axis=1)
    summed = lax.psum_scatter(
        partial_value.astype(jnp.bfloat16), "mp", scatter_dimension=2, tiled=True
    ).astype(jnp.float32)
    hidden = (jax.nn.silu(summed[:, 0]) * summed[:, 1]).astype(jnp.bfloat16)
    down_terms = jnp.dot(
        lax.all_gather(hidden, "mp", axis=1, tiled=True),
        down_weight,
        preferred_element_type=jnp.float32,
    )
    own_rows = tokens.shape[0]
    overall = lax.psum(down_terms, "group")
    result = lax.dynamic_slice_in_dim(overall, lax.axis_index("group") * own_rows, own_rows, 0)
    return result.astype(jnp.bfloat16)


def solution(mesh):
    placed = (P("group", "mp"), P("mp", "group"), P("mp", "group"), P("group", "mp"))
    return jax.shard_map(
        local, mesh=mesh, in_specs=placed, out_specs=P("group", "mp"), check_vma=False
    )
```

profile of v0, /device:TPU:1, one launch (start us, length us, event | category | flops | bytes accessed | tf_op | source)
XLA Modules:
  0.0 431.9 jit_solution(8712380223336989760)
XLA Ops:
  6.5 0.0 all-gather.3.cloned.1.call-start
  6.5 0.7 all-gather.3.cloned.1.call-update
  7.3 0.0 all-reduce.4.cloned.1.call-start
  7.3 30.8 %all-gather.3.cloned.1.call-done = bf16[1024,1024]{1,0:T(8,128)(2,1)} async-done(((bf16[128,1024]{1,0:T(8,128)(2,1)}), bf16[1024,1024]{1,0:T(8,128)(2,1)}) %all-gather.3.cloned.1.call-update) | async-done | bytes 2097168 | tf_op jit(solution)/shard_map/all_gather | solution.py:8
  38.1 0.0 copy-start
  38.1 10.8 %fusion = bf16[1024,1,3328]{2,0,1:T(8,128)(2,1)S(1)} fusion(bf16[1024,1024]{1,0:T(8,128)(2,1)} %all-gather.3.cloned.1.call-done, bf16[1024,3328]{1,0:T(8,128)(2,1)} %param.5), kind=kOutput, calls=%fused_computation.3 | convolution fusion | flops 6982729728 | bytes 15728640 | tf_op jit(solution)/shard_map/dot_general | solution.py:9
  48.9 0.0 copy-done
  49.0 10.6 %fusion.1 = bf16[1024,1,3328]{2,0,1:T(8,128)(2,1)S(1)} fusion(bf16[1024,1024]{1,0:T(8,128)(2,1)S(1)} %copy-done, bf16[1024,3328]{1,0:T(8,128)(2,1)} %param.6), kind=kOutput, calls=%fused_computation.4 | convolution fusion | flops 6982729728 | bytes 15728640 | tf_op jit(solution)/shard_map/dot_general | solution.py:10
  59.6 6.1 %pad_maximum_fusion = bf16[1024,2,3328]{2,0,1:T(8,128)(2,1)} fusion(bf16[1024,1,3328]{2,0,1:T(8,128)(2,1)S(1)} %fusion.1, bf16[1024,1,3328]{2,0,1:T(8,128)(2,1)S(1)} %fusion), kind=kLoop, calls=%fused_computation | loop fusion | flops 6815744 | bytes 27262976 | tf_op jit(solution)/shard_map/stack | solution.py:11
  65.7 34.0 %copy.5 = bf16[1024,2,3328]{0,1,2:T(2,128)(2,1)} copy(bf16[1024,2,3328]{2,0,1:T(8,128)(2,1)} %pad_maximum_fusion) | data formatting | bytes 27262976 | tf_op jit(solution)/shard_map/stack | solution.py:11
  99.6 0.0 copy-start.1
  99.6 0.0 all-reduce.4.cloned.1.call-update
  99.6 0.0 all-gather.5.cloned.1.call-start
  99.7 0.6 copy-done.1
  100.3 0.6 dynamic-slice
  101.5 186.5 %all-reduce.4.cloned.1.call-done = bf16[1024,2,3328]{0,1,2:T(2,128)(2,1)} async-done(((bf16[1024,2,3328]{0,1,2:T(2,128)(2,1)}), bf16[1024,2,3328]{0,1,2:T(2,128)(2,1)}) %all-reduce.4.cloned.1.call-update) | async-done | bytes 13631504
  288.1 1.7 dynamic-slice_convert_fusion
  289.8 1.3 fusion.3
  291.1 1.1 fusion.2
  292.3 0.0 all-gather.5.cloned.1.call-update
  292.3 63.5 %all-gather.5.cloned.1.call-done = bf16[1024,3328]{0,1:T(8,128)(2,1)} async-done(((bf16[1024,208]{0,1:T(8,128)(2,1)}), bf16[1024,3328]{0,1:T(8,128)(2,1)}) %all-gather.5.cloned.1.call-update) | async-done | bytes 6815760 | tf_op jit(solution)/shard_map/all_gather | solution.py:17
  355.8 12.8 %fusion.4 = f32[1024,1024]{1,0:T(8,128)} fusion(bf16[1024,3328]{0,1:T(8,128)(2,1)} %all-gather.5.cloned.1.call-done, bf16[3328,1024]{1,0:T(8,128)(2,1)} %param.7), kind=kOutput, calls=%fused_computation.11 | convolution fusion | flops 6979321856 | bytes 17825792 | tf_op jit(solution)/shard_map/dot_general | solution.py:16
  368.6 56.1 %all-reduce.5 = bf16[1024,1024]{1,0:T(8,128)(2,1)S(1)} all-reduce(f32[1024,1024]{1,0:T(8,128)} %fusion.4), channel_id=1, replica_groups=mesh['group'=8,'mp'=16] {'group'}, use_global_device_ids=true, to_apply=%region_1.2 | all-reduce | flops 1048576 | bytes 6291456 | tf_op jit(solution)/shard_map/psum | solution.py:22
  424.7 0.7 dynamic-slice_convert_fusion.1
Async XLA Ops:
  6.5 31.6 %all-gather.3.cloned.1.call-start = ((), (), s32[]{:S(2)}) async-start(), calls=%async_computation | async-start | bytes 2359296 | tf_op jit(solution)/shard_map/all_gather | solution.py:8
  7.3 280.8 %all-reduce.4.cloned.1.call-start = ((), (), s32[]{:S(2)}) async-start(), calls=%async_computation.2 | async-start | bytes 27262976
  38.1 10.8 %copy-start = (bf16[1024,1024]{1,0:T(8,128)(2,1)S(1)}, bf16[1024,1024]{1,0:T(8,128)(2,1)}, u32[]{:S(2)}) copy-start(bf16[1024,1024]{1,0:T(8,128)(2,1)} %all-gather.3.cloned.1.call-done) | copy-start | bytes 6291460
  99.6 0.7 copy-start.1
  99.6 256.2 %all-gather.5.cloned.1.call-start = ((), (), s32[]{:S(2)}) async-start(), calls=%async_computation.1 | async-start | bytes 7241728 | tf_op jit(solution)/shard_map/all_gather | solution.py:17
Sparse Core Ops, SparseCore 0:
  9.1 28.9 all-gather.2
  99.8 188.2 all-reduce.3
  292.4 63.3 all-gather.4
where the time goes:
time: 435 us; the launch traced here: 432 us
  waiting for transfers between devices  282 us (65%)
  blocking collectives  56.1 us (13%)
  local copies, waits for them, and re-layouts  37.2 us (9%)
  matrix products  34.2 us (8%)
  between operations  13.8 us (3%)
  other arithmetic  8.94 us (2%)
    unnamed x4, waiting for transfers between devices  187 us
    all_gather x1, waiting for transfers between devices, local(): lax.all_gather(hidden, 'mp', axis=1, tiled=True)  63.5 us
    psum x1, blocking collectives, local(): overall = lax.psum(down_terms, 'group')  56.1 us
    another operation x1, local copies, waits for them, and re-layouts, local(): partial_value = jnp.stack((gate_part, up_part), axis=1)  34 us
    all_gather x1, waiting for transfers between devices, local(): shard_piece = lax.all_gather(tokens, 'group', axis=0, tiled=True)  30.8 us
    dot_general x1, matrix products, local(): jnp.dot(lax.all_gather(hidden, 'mp', axis=1, tiled=True), down_weight, pr...  12.8 us
    dot_general x1, matrix products, local(): jnp.dot(shard_piece, gate_weight, preferred_element_type=jnp.float32)  10.8 us
    dot_general x1, matrix products, local(): jnp.dot(shard_piece, up_weight, preferred_element_type=jnp.float32)  10.6 us
  transfers between devices with their start and end apart: 3, of which 3 were waited for; matrix products, arithmetic and copies ran while one was open for 0% of the time, Pallas kernels for 0%

commit v1 on v0

v1 whole, which is shorter than its diff:
```python
import jax
import jax.numpy as jnp
from jax import lax
from jax.sharding import PartitionSpec as P


def local(tokens, gate_weight, up_weight, down_weight):
    rows = lax.all_gather(tokens, "group", axis=0, tiled=True)
    gate_part = jnp.dot(rows, gate_weight, preferred_element_type=jnp.float32).astype(jnp.bfloat16)
    up_part = jnp.dot(rows, up_weight, preferred_element_type=jnp.float32).astype(jnp.bfloat16)
    gate = lax.psum_scatter(gate_part, "mp", scatter_dimension=0, tiled=True).astype(jnp.float32)
    up = lax.psum_scatter(up_part, "mp", scatter_dimension=0, tiled=True).astype(jnp.float32)
    hidden = (jax.nn.silu(gate) * up).astype(jnp.bfloat16)
    hidden = lax.all_gather(hidden, "mp", axis=0, tiled=True)
    down = jnp.dot(hidden, down_weight, preferred_element_type=jnp.float32).astype(jnp.bfloat16)
    return lax.psum_scatter(down, "group", scatter_dimension=0, tiled=True)


def solution(mesh):
    placed = (P("group", "mp"), P("mp", "group"), P("mp", "group"), P("group", "mp"))
    return jax.shard_map(
        local, mesh=mesh, in_specs=placed, out_specs=P("group", "mp"), check_vma=False
    )
```

time: 435 us -> 336 us (0.77)
  blocking collectives: 56.1 us -> 0 us
  local copies, waits for them, and re-layouts: 37.2 us -> 1.52 us
  other arithmetic: 8.94 us -> 2.16 us
    unnamed x4 -> x5, waiting for transfers between devices: 187 us -> 0.78 us
    reduce_scatter x0 -> x3, waiting for transfers between devices: none -> 183 us  [the longest x1 85.5 us: local(): lax.psum_scatter(gate_part, 'mp', scatter_dimension=0, tiled=True)]
    psum x1 -> x0, blocking collectives: 56.1 us -> none  [local(): overall = lax.psum(down_terms, 'group')]
    another operation x1 -> x0, local copies, waits for them, and re-layouts: 34 us -> none  [local(): partial_value = jnp.stack((gate_part, up_part), axis=1)]
    another operation x1 -> x0, other arithmetic: 6.06 us -> none  [local(): partial_value = jnp.stack((gate_part, up_part), axis=1)]
  transfers between devices with their start and end apart: 3 -> 5, of which waited for: 3 -> 5; matrix products, arithmetic and copies ran while one was open for 0% -> 4% of each run, Pallas kernels for 0% -> 0%
where the time goes in v1:
time: 336 us; the launch traced here: 333 us
  waiting for transfers between devices  279 us (83%)
  matrix products  37 us (11%)
  between operations  13.1 us (4%)
    reduce_scatter x1, waiting for transfers between devices, local(): lax.psum_scatter(gate_part, 'mp', scatter_dimension=0, tiled=True)  85.5 us
    reduce_scatter x1, waiting for transfers between devices, local(): lax.psum_scatter(up_part, 'mp', scatter_dimension=0, tiled=True)  67.4 us
    all_gather x1, waiting for transfers between devices, local(): hidden = lax.all_gather(hidden, 'mp', axis=0, tiled=True)  64.1 us
    all_gather x1, waiting for transfers between devices, local(): rows = lax.all_gather(tokens, 'group', axis=0, tiled=True)  30.8 us
    reduce_scatter x1, waiting for transfers between devices, local(): return lax.psum_scatter(down, 'group', scatter_dimension=0, tiled=True)  30.6 us
    dot_general x1, matrix products, local(): jnp.dot(rows, up_weight, preferred_element_type=jnp.float32)  12.4 us
    dot_general x1, matrix products, local(): jnp.dot(hidden, down_weight, preferred_element_type=jnp.float32)  12.4 us
    dot_general x1, matrix products, local(): jnp.dot(rows, gate_weight, preferred_element_type=jnp.float32)  12.1 us
  transfers between devices with their start and end apart: 5, of which 5 were waited for; matrix products, arithmetic and copies ran while one was open for 4% of the time, Pallas kernels for 0%

profile of v1, /device:TPU:1, one launch (start us, length us, event | category | flops | bytes accessed | tf_op | source)
XLA Modules:
  0.0 333.1 jit_solution(11986623517666503571)
XLA Ops:
  6.5 0.0 all-gather.3.cloned.1.call-start
  6.5 0.7 all-gather.3.cloned.1.call-update
  7.3 0.0 reduce-scatter.6.cloned.1.call-start
  7.3 30.8 %all-gather.3.cloned.1.call-done = bf16[1024,1024]{1,0:T(8,128)(2,1)} async-done(((bf16[128,1024]{1,0:T(8,128)(2,1)}), bf16[1024,1024]{1,0:T(8,128)(2,1)}) %all-gather.3.cloned.1.call-update) | async-done | bytes 2097168 | tf_op jit(solution)/shard_map/all_gather | solution.py:8
  38.1 12.4 %convolution_convert_fusion = bf16[1024,3328]{1,0:T(8,128)(2,1)} fusion(bf16[1024,1024]{1,0:T(8,128)(2,1)} %all-gather.3.cloned.1.call-done, bf16[1024,3328]{1,0:T(8,128)(2,1)} %param.6), kind=kOutput, calls=%fused_computation | convolution fusion | flops 6982729728 | bytes 15728640 | tf_op jit(solution)/shard_map/dot_general | solution.py:10
  50.6 0.0 copy-start
  50.6 0.0 reduce-scatter.6.cloned.1.call-update
  50.6 0.0 reduce-scatter.4.cloned.1.call-start
  50.6 1.5 copy-done
  52.2 12.1 %convolution_convert_fusion.1 = bf16[1024,3328]{1,0:T(8,128)(2,1)} fusion(bf16[1024,1024]{1,0:T(8,128)(2,1)S(1)} %copy-done, bf16[1024,3328]{1,0:T(8,128)(2,1)} %param.5), kind=kOutput, calls=%fused_computation.1 | convolution fusion | flops 6982729728 | bytes 15728640 | tf_op jit(solution)/shard_map/dot_general | solution.py:9
  64.3 0.0 reduce-scatter.4.cloned.1.call-update
  64.3 0.0 all-gather.5.cloned.1.call-start
  64.4 67.4 %reduce-scatter.6.cloned.1.call-done = bf16[64,3328]{1,0:T(8,128)(2,1)} async-done(((bf16[1024,3328]{1,0:T(8,128)(2,1)}), bf16[64,3328]{1,0:T(8,128)(2,1)}) %reduce-scatter.6.cloned.1.call-update) | async-done | bytes 426000 | tf_op jit(solution)/shard_map/reduce_scatter | solution.py:12
  131.7 85.5 %reduce-scatter.4.cloned.1.call-done = bf16[64,3328]{1,0:T(8,128)(2,1)} async-done(((bf16[1024,3328]{1,0:T(8,128)(2,1)}), bf16[64,3328]{1,0:T(8,128)(2,1)}) %reduce-scatter.4.cloned.1.call-update) | async-done | bytes 426000 | tf_op jit(solution)/shard_map/reduce_scatter | solution.py:11
  217.2 2.2 fusion.4
  219.4 0.0 all-gather.5.cloned.1.call-update
  219.4 0.0 reduce-scatter.8.cloned.1.call-start
  219.5 64.1 %all-gather.5.cloned.1.call-done = bf16[1024,3328]{1,0:T(8,128)(2,1)} async-done(((bf16[64,3328]{1,0:T(8,128)(2,1)}), bf16[1024,3328]{1,0:T(8,128)(2,1)}) %all-gather.5.cloned.1.call-update) | async-done | bytes 6815760 | tf_op jit(solution)/shard_map/all_gather | solution.py:14
  283.6 12.4 %convolution_convert_fusion.2 = bf16[1024,1024]{1,0:T(8,128)(2,1)} fusion(bf16[1024,3328]{1,0:T(8,128)(2,1)} %all-gather.5.cloned.1.call-done, bf16[3328,1024]{1,0:T(8,128)(2,1)} %param.7), kind=kOutput, calls=%fused_computation.2 | convolution fusion | flops 6980370432 | bytes 15728640 | tf_op jit(solution)/shard_map/dot_general | solution.py:15
  296.0 0.0 reduce-scatter.8.cloned.1.call-update
  296.0 30.6 %reduce-scatter.8.cloned.1.call-done = bf16[128,1024]{1,0:T(8,128)(2,1)} async-done(((bf16[1024,1024]{1,0:T(8,128)(2,1)}), bf16[128,1024]{1,0:T(8,128)(2,1)}) %reduce-scatter.8.cloned.1.call-update) | async-done | bytes 262160 | tf_op jit(solution)/shard_map/reduce_scatter | solution.py:16
Async XLA Ops:
  6.5 31.6 %all-gather.3.cloned.1.call-start = ((), (), s32[]{:S(2)}) async-start(), calls=%async_computation.3 | async-start | bytes 2359296 | tf_op jit(solution)/shard_map/all_gather | solution.py:8
  7.3 124.5 %reduce-scatter.6.cloned.1.call-start = ((), (), s32[]{:S(2)}) async-start(), calls=%async_computation.5 | async-start | bytes 7241728 | tf_op jit(solution)/shard_map/reduce_scatter | solution.py:12
  50.6 1.6 copy-start
  50.6 166.6 %reduce-scatter.4.cloned.1.call-start = ((), (), s32[]{:S(2)}) async-start(), calls=%async_computation.4 | async-start | bytes 7241728 | tf_op jit(solution)/shard_map/reduce_scatter | solution.py:11
  64.3 219.2 %all-gather.5.cloned.1.call-start = ((), (), s32[]{:S(2)}) async-start(), calls=%async_computation.6 | async-start | bytes 7241728 | tf_op jit(solution)/shard_map/all_gather | solution.py:14
  219.4 107.1 %reduce-scatter.8.cloned.1.call-start = ((), (), s32[]{:S(2)}) async-start(), calls=%async_computation.7 | async-start | bytes 2359296 | tf_op jit(solution)/shard_map/reduce_scatter | solution.py:16
Sparse Core Ops, SparseCore 0:
  9.1 28.9 all-gather.2
  50.7 80.9 reduce-scatter.5
  135.6 81.5 reduce-scatter.3
  219.5 63.9 all-gather.4
  296.1 30.3 reduce-scatter.7

commit v2 on v1

v2 whole, which is shorter than its diff:
```python
import functools

import jax
import jax.numpy as jnp
import numpy as np
from jax import lax
from jax.experimental import pallas as pl
from jax.experimental.pallas import tpu as pltpu
from jax.sharding import PartitionSpec as P

BF = jnp.bfloat16
F32 = jnp.float32

PAIR = {"e": (1, 0, 3, 2), "o": (3, 2, 1, 0)}
BIT = {"e": (0, 1, 1, 0), "o": (0, 0, 1, 1)}
ORDERS = (
    (("x", "e"), ("x", "o"), ("y", "e"), ("y", "o")),
    (("x", "o"), ("x", "e"), ("y", "o"), ("y", "e")),
), (
    (("y", "e"), ("y", "o"), ("x", "e"), ("x", "o")),
    (("y", "o"), ("y", "e"), ("x", "o"), ("x", "e")),
)


def partner(m, link):
    axis, kind = link
    x, y = divmod(m, 4)
    return 4 * PAIR[kind][x] + y if axis == "x" else 4 * x + PAIR[kind][y]


def bit_of(m, link):
    axis, kind = link
    x, y = divmod(m, 4)
    return BIT[kind][x if axis == "x" else y]


def pairs_of(flow, step):
    return [
        (g * 16 + m, g * 16 + partner(m, ORDERS[g % 2][flow][step]))
        for g in range(8)
        for m in range(16)
    ]


def mask_table():
    table = np.zeros((2, 2, 16), np.int32)
    for core in range(2):
        for flow in range(2):
            for m in range(16):
                own = 0
                for link in ORDERS[core][flow]:
                    own = 2 * own + bit_of(m, link)
                table[core, flow, m] = 15 ^ own
    return table


def group_pairs(shift):
    return [(g, (g + 2 * shift) % 8) for g in range(8)]


SWAP = [(g, g ^ 1) for g in range(8)]


def swap(a):
    return lax.ppermute(a, "group", SWAP)


def exchange(a, flow, step):
    return lax.ppermute(a, ("group", "mp"), pairs_of(flow, step))


def project_body(info, t0, s0, t1, s1, gate, up, send, keep, plain, turned):
    @pl.when(pl.program_id(0) == 0)
    def _():
        half = t0.shape[0]
        for t, (mine, other) in enumerate(((t0, s0), (t1, s1))):
            plain[pl.ds(2 * t * half, half)] = mine[...]
            plain[pl.ds((2 * t + 1) * half, half)] = other[...]
        for t in range(2):
            for r in range(16):
                source = pl.multiple_of(t * 256 + (r ^ info[0]) * 16, 16)
                turned[pl.ds(t * 256 + r * 16, 16)] = plain[pl.ds(source, 16)]

    both = jnp.concatenate((gate[...], up[...]), axis=1)
    res = jnp.dot(turned[...], both, preferred_element_type=F32).astype(BF)
    for t in range(2):
        for k in range(2):
            part = res[t * 256 : (t + 1) * 256, k * 128 : (k + 1) * 128]
            send[k, t] = part[:128]
            keep[k, t] = part[128:]


def project(info, tokens, gate, up, columns):
    tiles = columns // 128
    whole = pl.BlockSpec((128, 1024), lambda j, info: (0, 0))
    weight = pl.BlockSpec((1024, 128), lambda j, info: (0, info[1] + j))
    out = pl.BlockSpec((2, 2, 128, 128), lambda j, info: (0, 0, 0, j))
    shape = jax.ShapeDtypeStruct((2, 2, 128, columns), BF)
    return pl.pallas_call(
        project_body,
        grid_spec=pltpu.PrefetchScalarGridSpec(
            num_scalar_prefetch=1,
            grid=(tiles,),
            in_specs=[whole] * 4 + [weight] * 2,
            out_specs=[out] * 2,
            scratch_shapes=[pltpu.VMEM((512, 1024), BF)] * 2,
        ),
        out_shape=[shape] * 2,
        compiler_params=pltpu.CompilerParams(vmem_limit_bytes=24 << 20),
        cost_estimate=pl.CostEstimate(
            flops=2 * 512 * 1024 * 2 * columns, bytes_accessed=12 << 20, transcendentals=0
        ),
        name="project",
    )(info, *tokens, gate, up)


def down_tile(theirs, mine, weight):
    rows = jnp.concatenate((theirs[0], mine[0], theirs[1], mine[1]), axis=0)
    return jnp.dot(rows, weight[...], preferred_element_type=F32)


def down_first_body(info, theirs, mine, weight, out):
    res = down_tile(theirs, mine, weight)
    for t in range(2):
        for r in range(16):
            target = pl.multiple_of((r ^ info[0]) * 16, 16)
            out[t, pl.ds(target, 16)] = res[t * 256 + r * 16 : t * 256 + (r + 1) * 16]


def down_last_body(info, theirs, mine, weight, before, send, keep, turned):
    res = down_tile(theirs, mine, weight)
    for t in range(2):
        for r in range(16):
            target = pl.multiple_of((r ^ info[0]) * 16, 16)
            turned[t, pl.ds(target, 16)] = res[t * 256 + r * 16 : t * 256 + (r + 1) * 16]
    total = turned[...] + before[...]
    keep[...] = total[:, :128]
    send[...] = total[:, 128:].astype(BF)


def down(info, theirs, mine, weight, before=None):
    depth = theirs.shape[2]
    wide = 256
    hidden = pl.BlockSpec((2, 128, depth), lambda j, info: (0, 0, 0))
    weights = pl.BlockSpec((depth, wide), lambda j, info: (info[1], j))
    total = pl.BlockSpec((2, 256, wide), lambda j, info: (0, 0, j))
    half = pl.BlockSpec((2, 128, wide), lambda j, info: (0, 0, j))
    first = before is None
    return pl.pallas_call(
        down_first_body if first else down_last_body,
        grid_spec=pltpu.PrefetchScalarGridSpec(
            num_scalar_prefetch=1,
            grid=(1024 // wide,),
            in_specs=[hidden, hidden, weights] + ([] if first else [total]),
            out_specs=total if first else [half, half],
            scratch_shapes=[] if first else [pltpu.VMEM((2, 256, wide), F32)],
        ),
        out_shape=jax.ShapeDtypeStruct((2, 256, 1024), F32)
        if first
        else [
            jax.ShapeDtypeStruct((2, 128, 1024), BF),
            jax.ShapeDtypeStruct((2, 128, 1024), F32),
        ],
        compiler_params=pltpu.CompilerParams(vmem_limit_bytes=24 << 20),
        cost_estimate=pl.CostEstimate(
            flops=2 * 512 * 1024 * depth, bytes_accessed=7 << 20, transcendentals=0
        ),
        name="down",
    )(info, theirs, mine, weight, *(() if first else (before,)))


def add(a, b):
    return (a.astype(F32) + b.astype(F32)).astype(BF)


def reduce_and_gather(send, keep, flow):
    for step in range(3):
        came = exchange(send, flow, step)
        half = keep.shape[2] // 2
        send = add(keep[:, :, :half], came[:, :, :half])
        keep = add(keep[:, :, half:], came[:, :, half:])
    came = exchange(send, flow, 3)
    total = keep.astype(F32) + came.astype(F32)
    mine = (jax.nn.silu(total[0]) * total[1]).astype(BF)
    for step in (3, 2, 1):
        theirs = exchange(mine, flow, step)
        mine = jnp.concatenate((theirs, mine), axis=1)
    return exchange(mine, flow, 0), mine


def local(tokens, gate_weight, up_weight, down_weight):
    core = lax.axis_index("group") % 2
    masks = jnp.asarray(mask_table())[core, :, lax.axis_index("mp")]
    columns = gate_weight.shape[1] // 2

    def info(flow, offset):
        return jnp.stack((masks[flow], jnp.asarray(offset, jnp.int32)))

    def fetch(shift):
        return lax.ppermute(tokens, "group", group_pairs(-shift))

    opposite, after, before = fetch(2), fetch(1), fetch(-1)
    pair_a = (tokens, swap(tokens), opposite, swap(opposite))
    pair_b = (after, swap(after), before, swap(before))

    given = (1 - core) * columns
    gate_other = swap(lax.dynamic_slice_in_dim(gate_weight, given, columns, 1))
    up_other = swap(lax.dynamic_slice_in_dim(up_weight, given, columns, 1))
    down_other = swap(lax.dynamic_slice_in_dim(down_weight, given, columns, 0))

    def unit(pair, flow, own):
        if own:
            send, keep = project(
                info(flow, core * (columns // 128)), pair, gate_weight, up_weight, columns
            )
        else:
            send, keep = project(info(flow, 0), pair, gate_other, up_other, columns)
        return reduce_and_gather(send, keep, flow)

    a_own = unit(pair_a, 0, True)
    b_own = unit(pair_b, 1, True)
    a_other = unit(pair_a, 0, False)
    b_other = unit(pair_b, 1, False)

    a_half = down(info(0, core), *a_own, down_weight)
    b_half = down(info(1, core), *b_own, down_weight)
    a_send, a_keep = down(info(0, 0), *a_other, down_other, a_half)
    b_send, b_keep = down(info(1, 0), *b_other, down_other, b_half)

    a_total = a_keep + swap(a_send).astype(F32)
    b_total = b_keep + swap(b_send).astype(F32)
    from_opposite = lax.ppermute(a_total[1].astype(BF), "group", group_pairs(2))
    from_before = lax.ppermute(b_total[0].astype(BF), "group", group_pairs(1))
    from_after = lax.ppermute(b_total[1].astype(BF), "group", group_pairs(-1))
    total = a_total[0] + from_opposite.astype(F32)
    total = total + from_before.astype(F32) + from_after.astype(F32)
    return total.astype(BF)


def solution(mesh):
    placed = (P("group", "mp"), P("mp", "group"), P("mp", "group"), P("group", "mp"))
    return jax.shard_map(
        local, mesh=mesh, in_specs=placed, out_specs=P("group", "mp"), check_vma=False
    )
```

time: 336 us -> 237 us (0.71)
  waiting for transfers between devices: 279 us -> 108 us
  starting transfers between devices: 0.17 us -> 56.4 us
  Pallas kernels: 0 us -> 49.8 us
  matrix products: 37 us -> 0 us
  between operations: 13.1 us -> 0.47 us
  local copies, waits for them, and re-layouts: 1.52 us -> 12.5 us
  other arithmetic: 2.16 us -> 9.45 us
    reduce_scatter x3 -> x0, waiting for transfers between devices: 183 us -> none  [the longest x1 85.5 us: local(): lax.psum_scatter(gate_part, 'mp', scatter_dimension=0, tiled=True)]
    ppermute x0 -> x47, waiting for transfers between devices: none -> 108 us  [the longest x32 90.2 us: exchange(): return lax.ppermute(a, ('group', 'mp'), pairs_of(flow, step))]
    all_gather x2 -> x0, waiting for transfers between devices: 94.9 us -> none  [the longest x1 64.1 us: local(): hidden = lax.all_gather(hidden, 'mp', axis=0, tiled=True)]
    ppermute x0 -> x47, starting transfers between devices: none -> 56.4 us  [the longest x32 29 us: exchange(): return lax.ppermute(a, ('group', 'mp'), pairs_of(flow, step))]
    pallas_call x0 -> x8, Pallas kernels: none -> 49.8 us  [the longest x4 33.8 us: project(): pl.pallas_call(project_body, grid_spec=pltpu.PrefetchScalarGridSpec(num_s...]
    dot_general x3 -> x0, matrix products: 37 us -> none  [the longest x1 12.4 us: local(): jnp.dot(rows, up_weight, preferred_element_type=jnp.float32)]
    unnamed x2 -> x16, local copies, waits for them, and re-layouts: 1.52 us -> 6.84 us
    dynamic_slice x0 -> x4, local copies, waits for them, and re-layouts: none -> 5.04 us  [the longest x1 1.98 us: local(): up_other = swap(lax.dynamic_slice_in_dim(up_weight, given, columns, 1))]
  transfers between devices with their start and end apart: 5 -> 47, of which waited for: 5 -> 25; matrix products, arithmetic and copies ran while one was open for 4% -> 6% of each run, Pallas kernels for 0% -> 21%
where the time goes in v2:
time: 237 us; the launch traced here: 236 us
  waiting for transfers between devices  108 us (46%)
  starting transfers between devices  56.4 us (24%)
  Pallas kernels  49.8 us (21%)
  local copies, waits for them, and re-layouts  12.5 us (5%)
  other arithmetic  9.45 us (4%)
    ppermute x32, waiting for transfers between devices, exchange(): return lax.ppermute(a, ('group', 'mp'), pairs_of(flow, step))  90.2 us
    pallas_call x4, Pallas kernels, project(): pl.pallas_call(project_body, grid_spec=pltpu.PrefetchScalarGridSpec(num_s...  33.8 us
    ppermute x32, starting transfers between devices, exchange(): return lax.ppermute(a, ('group', 'mp'), pairs_of(flow, step))  29 us
    ppermute x9, starting transfers between devices, swap(): return lax.ppermute(a, 'group', SWAP)  17.9 us
    pallas_call x4, Pallas kernels, down(): pl.pallas_call(down_first_body if first else down_last_body, grid_spec=pl...  16 us
    ppermute x1, waiting for transfers between devices, local(): from_before = lax.ppermute(b_total[0].astype(BF), 'group', group_pairs(1))  8.11 us
    unnamed x16, local copies, waits for them, and re-layouts  6.84 us
    ppermute x3, starting transfers between devices, fetch(): return lax.ppermute(tokens, 'group', group_pairs(-shift))  5.89 us
  transfers between devices with their start and end apart: 47, of which 25 were waited for; matrix products, arithmetic and copies ran while one was open for 6% of the time, Pallas kernels for 21%

profile of v2, /device:TPU:1, one launch (start us, length us, event | category | flops | bytes accessed | tf_op | source)
XLA Modules:
  0.0 236.4 jit_solution(9703275107264436402)
XLA Ops:
  0.0 4.4 %collective-permute-start.1 = (bf16[128,1024]{1,0:T(8,128)(2,1)}, bf16[128,1024]{1,0:T(8,128)(2,1)S(1)}, u32[]{:S(2)}, u32[]{:S(2)}) collective-permute-start(bf16[128,1024]{1,0:T(8,128)(2,1)} %t0.3), channel_id=1, source_target_pairs={{0,64},{16,80},{32,96},{48,112},{64,0},{80,16},{96,32},{112,48},{1... | collective-permute-start | bytes 786440 | tf_op jit(solution)/shard_map/ppermute | solution.py:200
  7.6 3.1 %collective-permute-done.1.t1 = bf16[128,1024]{1,0:T(8,128)(2,1)S(1)} collective-permute-done((bf16[128,1024]{1,0:T(8,128)(2,1)}, bf16[128,1024]{1,0:T(8,128)(2,1)S(1)}, u32[]{:S(2)}, u32[]{:S(2)}) %collective-permute-start.1) | collective-permute-done | bytes 262176 | tf_op jit(solution)/shard_map/ppermute | solution.py:200
  10.7 2.1 collective-permute-start.2
  14.8 2.1 collective-permute-done.24.t0
  16.9 1.4 collective-permute-start.25
  18.3 2.9 %copy-done = bf16[1024,3328]{1,0:T(8,128)(2,1)S(1)} copy-done((bf16[1024,3328]{1,0:T(8,128)(2,1)S(1)}, bf16[1024,3328]{1,0:T(8,128)(2,1)}, u32[]{:S(2)}) %copy-start) | copy-done | bytes 6815768
  21.3 2.9 %copy-done.2 = bf16[1024,3328]{1,0:T(8,128)(2,1)S(1)} copy-done((bf16[1024,3328]{1,0:T(8,128)(2,1)S(1)}, bf16[1024,3328]{1,0:T(8,128)(2,1)}, u32[]{:S(2)}) %copy-start.2) | copy-done | bytes 6815768
  25.2 8.4 %project.5 = (bf16[2,2,128,1664]{3,2,1,0:T(8,128)(2,1)S(1)}, bf16[2,2,128,1664]{3,2,1,0:T(8,128)(2,1)S(1)}) custom-call(s32[2]{0:T(128)S(1)} %pad_add_fusion.5.info, bf16[128,1024]{1,0:T(8,128)(2,1)S(1)} %copy-done.4, bf16[128,1024]{1,0:T(8,128)(2,1)S(1)} %collective-permute-done.s0, bf16[128,1024]{1,0:T(8,128)(2,1)S(1)} %collective-permute-done.1.t1, ...), custom_call_target="tpu_custom_call" | custom-call | flops 3489660928 | bytes 12582912 | tf_op jit(solution)/shard_map/project/pallas_call | solution.py:99
  33.6 1.4 collective-permute-start.14
  35.0 8.5 %project.7 = (bf16[2,2,128,1664]{3,2,1,0:T(8,128)(2,1)S(1)}, bf16[2,2,128,1664]{3,2,1,0:T(8,128)(2,1)S(1)}) custom-call(s32[2]{0:T(128)S(1)} %pad_add_fusion.4.info, bf16[128,1024]{1,0:T(8,128)(2,1)S(1)} %collective-permute-done.24.t0, bf16[128,1024]{1,0:T(8,128)(2,1)S(1)} %collective-permute-done.25.s0, bf16[128,1024]{1,0:T(8,128)(2,1)S(1)} %collective-permute-done.26.t1, ...), custom_call_target="tpu_custom_call" | custom-call | flops 3489660928 | bytes 12582912 | tf_op jit(solution)/shard_map/project/pallas_call | solution.py:99
  43.5 2.0 collective-permute-start.36
  45.5 2.0 constant_dynamic-slice_fusion.2
  48.3 2.0 constant_dynamic-slice_fusion.1
  50.3 4.4 %collective-permute-done.14 = bf16[2,2,128,1664]{3,2,1,0:T(8,128)(2,1)S(1)} collective-permute-done((bf16[2,2,128,1664]{3,2,1,0:T(8,128)(2,1)S(1)}, bf16[2,2,128,1664]{3,2,1,0:T(8,128)(2,1)S(1)}, u32[]{:S(2)}, u32[]{:S(2)}) %collective-permute-start.14) | collective-permute-done | bytes 1703968 | tf_op jit(solution)/shard_map/ppermute | solution.py:69
  55.1 2.8 %collective-permute-start.15 = (bf16[2,2,64,1664]{3,2,1,0:T(8,128)(2,1)S(1)}, bf16[2,2,64,1664]{3,2,1,0:T(8,128)(2,1)S(1)}, u32[]{:S(2)}, u32[]{:S(2)}) collective-permute-start(bf16[2,2,64,1664]{3,2,1,0:T(8,128)(2,1)S(1)} %get-tuple-element.34), channel_id=1, source_target_pairs={{0,12},{1,13},{2,14},{3,15},{4,8},{5,9},{6,10},{7,11},{8,4},{9,5},... | collective-permute-start | bytes 2555912 | tf_op jit(solution)/shard_map/ppermute | solution.py:69
  57.9 7.8 %collective-permute-done.36 = bf16[2,2,128,1664]{3,2,1,0:T(8,128)(2,1)S(1)} collective-permute-done((bf16[2,2,128,1664]{3,2,1,0:T(8,128)(2,1)S(1)}, bf16[2,2,128,1664]{3,2,1,0:T(8,128)(2,1)S(1)}, u32[]{:S(2)}, u32[]{:S(2)}) %collective-permute-start.36) | collective-permute-done | bytes 1703968 | tf_op jit(solution)/shard_map/ppermute | solution.py:69
  66.6 1.6 collective-permute-start.13
  69.7 5.1 %collective-permute-done.15 = bf16[2,2,64,1664]{3,2,1,0:T(8,128)(2,1)S(1)} collective-permute-done((bf16[2,2,64,1664]{3,2,1,0:T(8,128)(2,1)S(1)}, bf16[2,2,64,1664]{3,2,1,0:T(8,128)(2,1)S(1)}, u32[]{:S(2)}, u32[]{:S(2)}) %collective-permute-start.15) | collective-permute-done | bytes 852000 | tf_op jit(solution)/shard_map/ppermute | solution.py:69
  76.1 2.0 collective-permute-done.37
  78.3 2.6 %collective-permute-start.38 = (bf16[2,2,32,1664]{3,2,1,0:T(8,128)(2,1)S(1)}, bf16[2,2,32,1664]{3,2,1,0:T(8,128)(2,1)S(1)}, u32[]{:S(2)}, u32[]{:S(2)}) collective-permute-start(bf16[2,2,32,1664]{3,2,1,0:T(8,128)(2,1)S(1)} %get-tuple-element.38), channel_id=1, source_target_pairs={{0,3},{1,2},{2,1},{3,0},{4,7},{5,6},{6,5},{7,4},{8,11},{9,10},{10,... | collective-permute-start | bytes 1277960 | tf_op jit(solution)/shard_map/ppermute | solution.py:69
  80.9 8.5 %project.4 = (bf16[2,2,128,1664]{3,2,1,0:T(8,128)(2,1)S(1)}, bf16[2,2,128,1664]{3,2,1,0:T(8,128)(2,1)S(1)}) custom-call(s32[2]{0:T(128)S(1)} %pad_add_fusion.1.info, bf16[128,1024]{1,0:T(8,128)(2,1)S(1)} %copy-done.5, bf16[128,1024]{1,0:T(8,128)(2,1)S(1)} %collective-permute-done.s0, bf16[128,1024]{1,0:T(8,128)(2,1)S(1)} %collective-permute-done.1.t1, ...), custom_call_target="tpu_custom_call" | custom-call | flops 3489660928 | bytes 12582912 | tf_op jit(solution)/shard_map/project/pallas_call | solution.py:99
  89.4 8.5 %project.6 = (bf16[2,2,128,1664]{3,2,1,0:T(8,128)(2,1)S(1)}, bf16[2,2,128,1664]{3,2,1,0:T(8,128)(2,1)S(1)}) custom-call(s32[2]{0:T(128)S(1)} %pad_add_fusion.info, bf16[128,1024]{1,0:T(8,128)(2,1)S(1)} %collective-permute-done.24.t0, bf16[128,1024]{1,0:T(8,128)(2,1)S(1)} %collective-permute-done.25.s0, bf16[128,1024]{1,0:T(8,128)(2,1)S(1)} %collective-permute-done.26.t1, ...), custom_call_target="tpu_custom_call" | custom-call | flops 3489660928 | bytes 12582912 | tf_op jit(solution)/shard_map/project/pallas_call | solution.py:99
  97.9 2.0 collective-permute-start.28
  100.4 5.6 %collective-permute-done.17 = bf16[2,2,16,1664]{3,2,1,0:T(8,128)(2,1)S(1)} collective-permute-done((bf16[2,2,16,1664]{3,2,1,0:T(8,128)(2,1)S(1)}, bf16[2,2,16,1664]{3,2,1,0:T(8,128)(2,1)S(1)}, u32[]{:S(2)}, u32[]{:S(2)}) %collective-permute-start.17) | collective-permute-done | bytes 213024 | tf_op jit(solution)/shard_map/ppermute | solution.py:69
  107.9 4.5 %collective-permute-done.18 = bf16[2,16,1664]{2,1,0:T(8,128)(2,1)S(1)} collective-permute-done((bf16[2,16,1664]{2,1,0:T(8,128)(2,1)S(1)}, bf16[2,16,1664]{2,1,0:T(8,128)(2,1)S(1)}, u32[]{:S(2)}, u32[]{:S(2)}) %collective-permute-start.18) | collective-permute-done | bytes 106528 | tf_op jit(solution)/shard_map/ppermute | solution.py:69
  113.0 2.6 %collective-permute-start.41 = (bf16[2,32,1664]{2,1,0:T(8,128)(2,1)S(1)}, bf16[2,32,1664]{2,1,0:T(8,128)(2,1)S(1)}, u32[]{:S(2)}, u32[]{:S(2)}) collective-permute-start(bf16[2,32,1664]{2,1,0:T(8,128)(2,1)S(1)} %pad_maximum_fusion.11), channel_id=1, source_target_pairs={{0,3},{1,2},{2,1},{3,0},{4,7},{5,6},{6,5},{7,4},{8,11},{9,10},{10,... | collective-permute-start | bytes 638984 | tf_op jit(solution)/shard_map/ppermute | solution.py:69
  115.5 8.0 %collective-permute-done.28 = bf16[2,2,128,1664]{3,2,1,0:T(8,128)(2,1)S(1)} collective-permute-done((bf16[2,2,128,1664]{3,2,1,0:T(8,128)(2,1)S(1)}, bf16[2,2,128,1664]{3,2,1,0:T(8,128)(2,1)S(1)}, u32[]{:S(2)}, u32[]{:S(2)}) %collective-permute-start.28) | collective-permute-done | bytes 1703968 | tf_op jit(solution)/shard_map/ppermute | solution.py:69
  124.7 2.0 collective-permute-start.6
  127.8 9.3 %collective-permute-done.29 = bf16[2,2,64,1664]{3,2,1,0:T(8,128)(2,1)S(1)} collective-permute-done((bf16[2,2,64,1664]{3,2,1,0:T(8,128)(2,1)S(1)}, bf16[2,2,64,1664]{3,2,1,0:T(8,128)(2,1)S(1)}, u32[]{:S(2)}, u32[]{:S(2)}) %collective-permute-start.29) | collective-permute-done | bytes 852000 | tf_op jit(solution)/shard_map/ppermute | solution.py:69
  137.3 1.4 collective-permute-start.30
  139.5 10.9 %collective-permute-done.30 = bf16[2,2,32,1664]{3,2,1,0:T(8,128)(2,1)S(1)} collective-permute-done((bf16[2,2,32,1664]{3,2,1,0:T(8,128)(2,1)S(1)}, bf16[2,2,32,1664]{3,2,1,0:T(8,128)(2,1)S(1)}, u32[]{:S(2)}, u32[]{:S(2)}) %collective-permute-start.30) | collective-permute-done | bytes 426016 | tf_op jit(solution)/shard_map/ppermute | solution.py:69
  151.0 1.4 collective-permute-start.8
  152.3 3.2 %collective-permute-done.31 = bf16[2,2,16,1664]{3,2,1,0:T(8,128)(2,1)S(1)} collective-permute-done((bf16[2,2,16,1664]{3,2,1,0:T(8,128)(2,1)S(1)}, bf16[2,2,16,1664]{3,2,1,0:T(8,128)(2,1)S(1)}, u32[]{:S(2)}, u32[]{:S(2)}) %collective-permute-start.31) | collective-permute-done | bytes 213024 | tf_op jit(solution)/shard_map/ppermute | solution.py:69
  157.1 1.4 collective-permute-start.9
  159.7 1.4 collective-permute-start.33
  162.3 3.3 %collective-permute-done.33 = bf16[2,32,1664]{2,1,0:T(8,128)(2,1)S(1)} collective-permute-done((bf16[2,32,1664]{2,1,0:T(8,128)(2,1)S(1)}, bf16[2,32,1664]{2,1,0:T(8,128)(2,1)S(1)}, u32[]{:S(2)}, u32[]{:S(2)}) %collective-permute-start.33) | collective-permute-done | bytes 213024 | tf_op jit(solution)/shard_map/ppermute | solution.py:69
  167.1 1.7 collective-permute-start.11
  168.8 4.3 %collective-permute-done.34 = bf16[2,64,1664]{2,1,0:T(8,128)(2,1)S(1)} collective-permute-done((bf16[2,64,1664]{2,1,0:T(8,128)(2,1)S(1)}, bf16[2,64,1664]{2,1,0:T(8,128)(2,1)S(1)}, u32[]{:S(2)}, u32[]{:S(2)}) %collective-permute-start.34) | collective-permute-done | bytes 426016 | tf_op jit(solution)/shard_map/ppermute | solution.py:69
  174.1 12.0 %collective-permute-done.11 = bf16[2,64,1664]{2,1,0:T(8,128)(2,1)S(1)} collective-permute-done((bf16[2,64,1664]{2,1,0:T(8,128)(2,1)S(1)}, bf16[2,64,1664]{2,1,0:T(8,128)(2,1)S(1)}, u32[]{:S(2)}, u32[]{:S(2)}) %collective-permute-start.11) | collective-permute-done | bytes 426016 | tf_op jit(solution)/shard_map/ppermute | solution.py:69
  187.0 3.8 %down.6.before = f32[2,256,1024]{2,1,0:T(8,128)S(1)} custom-call(s32[2]{0:T(128)S(1)} %pad_add_fusion.2.info, bf16[2,128,1664]{2,1,0:T(8,128)(2,1)S(1)} %collective-permute-done.43.theirs, bf16[2,128,1664]{2,1,0:T(8,128)(2,1)S(1)} %pad_maximum_fusion.3.mine, bf16[3328,1024]{1,0:T(8,128)(2,1)S(1)} %bitcast.61), custom_call_target="tpu_custom_call" | custom-call | flops 1744830464 | bytes 7340032 | tf_op jit(solution)/shard_map/down/pallas_call | solution.py:149
  190.9 4.3 %collective-permute-done.35.theirs = bf16[2,128,1664]{2,1,0:T(8,128)(2,1)S(1)} collective-permute-done((bf16[2,128,1664]{2,1,0:T(8,128)(2,1)S(1)}, bf16[2,128,1664]{2,1,0:T(8,128)(2,1)S(1)}, u32[]{:S(2)}, u32[]{:S(2)}) %collective-permute-start.35) | collective-permute-done | bytes 852000 | tf_op jit(solution)/shard_map/ppermute | solution.py:69
  195.2 4.1 %down.7 = (bf16[2,128,1024]{2,1,0:T(8,128)(2,1)S(1)}, f32[2,128,1024]{2,1,0:T(8,128)S(1)}) custom-call(s32[2]{0:T(128)S(1)} %pad_add_fusion.info, bf16[2,128,1664]{2,1,0:T(8,128)(2,1)S(1)} %collective-permute-done.35.theirs, bf16[2,128,1664]{2,1,0:T(8,128)(2,1)S(1)} %pad_maximum_fusion.2.mine, bf16[1664,1024]{1,0:T(8,128)(2,1)S(1)} %collective-permute-done.13.weight, ...), custom_call_target="tpu_custom_call" | custom-call | flops 1744830464 | bytes 7340032 | tf_op jit(solution)/shard_map/down/pallas_call | solution.py:149
  199.4 10.8 %collective-permute-start.44 = (bf16[2,128,1024]{2,1,0:T(8,128)(2,1)S(1)}, bf16[2,128,1024]{2,1,0:T(8,128)(2,1)S(1)}, u32[]{:S(2)}, u32[]{:S(2)}) collective-permute-start(bf16[2,128,1024]{2,1,0:T(8,128)(2,1)S(1)} %get-tuple-element.28), channel_id=1, source_target_pairs={{0,16},{16,0},{32,48},{48,32},{64,80},{80,64},{96,112},{112,96},{1... | collective-permute-start | bytes 1572872 | tf_op jit(solution)/shard_map/ppermute | solution.py:65
  210.9 3.8 %down.4.before = f32[2,256,1024]{2,1,0:T(8,128)S(1)} custom-call(s32[2]{0:T(128)S(1)} %pad_add_fusion.3.info, bf16[2,128,1664]{2,1,0:T(8,128)(2,1)S(1)} %collective-permute-done.21.theirs, bf16[2,128,1664]{2,1,0:T(8,128)(2,1)S(1)} %pad_maximum_fusion.1.mine, bf16[3328,1024]{1,0:T(8,128)(2,1)S(1)} %bitcast.61), custom_call_target="tpu_custom_call" | custom-call | flops 1744830464 | bytes 7340032 | tf_op jit(solution)/shard_map/down/pallas_call | solution.py:149
  214.8 4.1 %down.5 = (bf16[2,128,1024]{2,1,0:T(8,128)(2,1)S(1)}, f32[2,128,1024]{2,1,0:T(8,128)S(1)}) custom-call(s32[2]{0:T(128)S(1)} %pad_add_fusion.1.info, bf16[2,128,1664]{2,1,0:T(8,128)(2,1)S(1)} %collective-permute-done.12.theirs, bf16[2,128,1664]{2,1,0:T(8,128)(2,1)S(1)} %pad_maximum_fusion.mine, bf16[1664,1024]{1,0:T(8,128)(2,1)S(1)} %collective-permute-done.13.weight, ...), custom_call_target="tpu_custom_call" | custom-call | flops 1744830464 | bytes 7340032 | tf_op jit(solution)/shard_map/down/pallas_call | solution.py:149
  219.3 2.4 collective-permute-start.46
  223.2 4.3 %collective-permute-done.46 = bf16[128,1024]{1,0:T(8,128)(2,1)S(1)} collective-permute-done((bf16[128,1024]{1,0:T(8,128)(2,1)S(1)}, bf16[128,1024]{1,0:T(8,128)(2,1)S(1)}, u32[]{:S(2)}, u32[]{:S(2)}) %collective-permute-start.46) | collective-permute-done | bytes 262176 | tf_op jit(solution)/shard_map/ppermute | solution.py:234
  227.4 8.1 %collective-permute-done.45 = bf16[128,1024]{1,0:T(8,128)(2,1)S(1)} collective-permute-done((bf16[128,1024]{1,0:T(8,128)(2,1)S(1)}, bf16[128,1024]{1,0:T(8,128)(2,1)S(1)}, u32[]{:S(2)}, u32[]{:S(2)}) %collective-permute-start.45) | collective-permute-done | bytes 262176 | tf_op jit(solution)/shard_map/ppermute | solution.py:233
  (119 shorter events, 28.7 us)
Async XLA Ops:
  0.0 10.7 %collective-permute-start.1 = (bf16[128,1024]{1,0:T(8,128)(2,1)}, bf16[128,1024]{1,0:T(8,128)(2,1)S(1)}, u32[]{:S(2)}, u32[]{:S(2)}) collective-permute-start(bf16[128,1024]{1,0:T(8,128)(2,1)} %t0.3), channel_id=1, source_target_pairs={{0,64},{16,80},{32,96},{48,112},{64,0},{80,16},{96,32},{112,48},{1... | collective-permute-start | bytes 786440 | tf_op jit(solution)/shard_map/ppermute | solution.py:200
  4.4 13.9 %collective-permute-start = (bf16[128,1024]{1,0:T(8,128)(2,1)}, bf16[128,1024]{1,0:T(8,128)(2,1)S(1)}, u32[]{:S(2)}, u32[]{:S(2)}) collective-permute-start(bf16[128,1024]{1,0:T(8,128)(2,1)} %t0.3), channel_id=1, source_target_pairs={{0,16},{16,0},{32,48},{48,32},{64,80},{80,64},{96,112},{112,96},{1... | collective-permute-start | bytes 786440 | tf_op jit(solution)/shard_map/ppermute | solution.py:65
  5.4 11.5 %collective-permute-start.24 = (bf16[128,1024]{1,0:T(8,128)(2,1)}, bf16[128,1024]{1,0:T(8,128)(2,1)S(1)}, u32[]{:S(2)}, u32[]{:S(2)}) collective-permute-start(bf16[128,1024]{1,0:T(8,128)(2,1)} %t0.3), channel_id=1, source_target_pairs={{0,96},{16,112},{32,0},{48,16},{64,32},{80,48},{96,64},{112,80},{1... | collective-permute-start | bytes 786440 | tf_op jit(solution)/shard_map/ppermute | solution.py:200
  5.8 12.5 %collective-permute-start.26 = (bf16[128,1024]{1,0:T(8,128)(2,1)}, bf16[128,1024]{1,0:T(8,128)(2,1)S(1)}, u32[]{:S(2)}, u32[]{:S(2)}) collective-permute-start(bf16[128,1024]{1,0:T(8,128)(2,1)} %t0.3), channel_id=1, source_target_pairs={{0,32},{16,48},{32,64},{48,80},{64,96},{80,112},{96,0},{112,16},{1... | collective-permute-start | bytes 786440 | tf_op jit(solution)/shard_map/ppermute | solution.py:200
  10.7 7.6 %collective-permute-start.2 = (bf16[128,1024]{1,0:T(8,128)(2,1)S(1)}, bf16[128,1024]{1,0:T(8,128)(2,1)S(1)}, u32[]{:S(2)}, u32[]{:S(2)}) collective-permute-start(bf16[128,1024]{1,0:T(8,128)(2,1)S(1)} %collective-permute-done.1.t1), channel_id=1, source_target_pairs={{0,16},{16,0},{32,48},{48,32},{64,80},{80,64},{96,112},{112,96},{1... | collective-permute-start | bytes 786440 | tf_op jit(solution)/shard_map/ppermute | solution.py:65
  16.9 18.1 %collective-permute-start.25 = (bf16[128,1024]{1,0:T(8,128)(2,1)S(1)}, bf16[128,1024]{1,0:T(8,128)(2,1)S(1)}, u32[]{:S(2)}, u32[]{:S(2)}) collective-permute-start(bf16[128,1024]{1,0:T(8,128)(2,1)S(1)} %collective-permute-done.24.t0), channel_id=1, source_target_pairs={{0,16},{16,0},{32,48},{48,32},{64,80},{80,64},{96,112},{112,96},{1... | collective-permute-start | bytes 786440 | tf_op jit(solution)/shard_map/ppermute | solution.py:65
  18.3 16.7 %collective-permute-start.27 = (bf16[128,1024]{1,0:T(8,128)(2,1)S(1)}, bf16[128,1024]{1,0:T(8,128)(2,1)S(1)}, u32[]{:S(2)}, u32[]{:S(2)}) collective-permute-start(bf16[128,1024]{1,0:T(8,128)(2,1)S(1)} %collective-permute-done.26.t1), channel_id=1, source_target_pairs={{0,16},{16,0},{32,48},{48,32},{64,80},{80,64},{96,112},{112,96},{1... | collective-permute-start | bytes 786440 | tf_op jit(solution)/shard_map/ppermute | solution.py:65
  33.6 21.0 %collective-permute-start.14 = (bf16[2,2,128,1664]{3,2,1,0:T(8,128)(2,1)S(1)}, bf16[2,2,128,1664]{3,2,1,0:T(8,128)(2,1)S(1)}, u32[]{:S(2)}, u32[]{:S(2)}) collective-permute-start(bf16[2,2,128,1664]{3,2,1,0:T(8,128)(2,1)S(1)} %get-tuple-element.20), channel_id=1, source_target_pairs={{0,4},{1,5},{2,6},{3,7},{4,0},{5,1},{6,2},{7,3},{8,12},{9,13},{10,... | collective-permute-start | bytes 5111816 | tf_op jit(solution)/shard_map/ppermute | solution.py:69
  43.5 22.3 %collective-permute-start.36 = (bf16[2,2,128,1664]{3,2,1,0:T(8,128)(2,1)S(1)}, bf16[2,2,128,1664]{3,2,1,0:T(8,128)(2,1)S(1)}, u32[]{:S(2)}, u32[]{:S(2)}) collective-permute-start(bf16[2,2,128,1664]{3,2,1,0:T(8,128)(2,1)S(1)} %get-tuple-element.26), channel_id=1, source_target_pairs={{0,12},{1,13},{2,14},{3,15},{4,8},{5,9},{6,10},{7,11},{8,4},{9,5},... | collective-permute-start | bytes 5111816 | tf_op jit(solution)/shard_map/ppermute | solution.py:69
  47.4 33.5 %collective-permute-start.3 = (bf16[1024,1664]{1,0:T(8,128)(2,1)}, bf16[1024,1664]{1,0:T(8,128)(2,1)S(1)}, u32[]{:S(2)}, u32[]{:S(2)}) collective-permute-start(bf16[1024,1664]{1,0:T(8,128)(2,1)} %constant_dynamic-slice_fusion.2), channel_id=1, source_target_pairs={{0,16},{16,0},{32,48},{48,32},{64,80},{80,64},{96,112},{112,96},{1... | collective-permute-start | bytes 10223624 | tf_op jit(solution)/shard_map/ppermute | solution.py:65
  48.3 18.0 %slice-start = ((s8[6815744]{0:T(1024)(128)(4,1)}), s8[4194304]{0:T(1024)(128)(4,1)S(1)}, s32[]{:S(2)}) async-start(s8[6815744]{0:T(1024)(128)(4,1)} %bitcast.60), calls=%async_computation | async-start | bytes 8388608
  50.3 30.6 %collective-permute-start.4 = (bf16[1024,1664]{1,0:T(8,128)(2,1)}, bf16[1024,1664]{1,0:T(8,128)(2,1)S(1)}, u32[]{:S(2)}, u32[]{:S(2)}) collective-permute-start(bf16[1024,1664]{1,0:T(8,128)(2,1)} %constant_dynamic-slice_fusion.1), channel_id=1, source_target_pairs={{0,16},{16,0},{32,48},{48,32},{64,80},{80,64},{96,112},{112,96},{1... | collective-permute-start | bytes 10223624 | tf_op jit(solution)/shard_map/ppermute | solution.py:65
  55.1 19.8 %collective-permute-start.15 = (bf16[2,2,64,1664]{3,2,1,0:T(8,128)(2,1)S(1)}, bf16[2,2,64,1664]{3,2,1,0:T(8,128)(2,1)S(1)}, u32[]{:S(2)}, u32[]{:S(2)}) collective-permute-start(bf16[2,2,64,1664]{3,2,1,0:T(8,128)(2,1)S(1)} %get-tuple-element.34), channel_id=1, source_target_pairs={{0,12},{1,13},{2,14},{3,15},{4,8},{5,9},{6,10},{7,11},{8,4},{9,5},... | collective-permute-start | bytes 2555912 | tf_op jit(solution)/shard_map/ppermute | solution.py:69
  66.2 11.9 %collective-permute-start.37 = (bf16[2,2,64,1664]{3,2,1,0:T(8,128)(2,1)S(1)}, bf16[2,2,64,1664]{3,2,1,0:T(8,128)(2,1)S(1)}, u32[]{:S(2)}, u32[]{:S(2)}) collective-permute-start(bf16[2,2,64,1664]{3,2,1,0:T(8,128)(2,1)S(1)} %get-tuple-element.30), channel_id=1, source_target_pairs={{0,4},{1,5},{2,6},{3,7},{4,0},{5,1},{6,2},{7,3},{8,12},{9,13},{10,... | collective-permute-start | bytes 2555912 | tf_op jit(solution)/shard_map/ppermute | solution.py:69
  66.6 124.2 %collective-permute-start.13 = (bf16[1664,1024]{1,0:T(8,128)(2,1)S(1)}, bf16[1664,1024]{1,0:T(8,128)(2,1)S(1)}, u32[]{:S(2)}, u32[]{:S(2)}) collective-permute-start(bf16[1664,1024]{1,0:T(8,128)(2,1)S(1)} %constant_dynamic-slice_fusion), channel_id=1, source_target_pairs={{0,16},{16,0},{32,48},{48,32},{64,80},{80,64},{96,112},{112,96},{1... | collective-permute-start | bytes 10223624 | tf_op jit(solution)/shard_map/ppermute | solution.py:65
  75.1 24.7 %collective-permute-start.16 = (bf16[2,2,32,1664]{3,2,1,0:T(8,128)(2,1)S(1)}, bf16[2,2,32,1664]{3,2,1,0:T(8,128)(2,1)S(1)}, u32[]{:S(2)}, u32[]{:S(2)}) collective-permute-start(bf16[2,2,32,1664]{3,2,1,0:T(8,128)(2,1)S(1)} %get-tuple-element.42), channel_id=1, source_target_pairs={{0,1},{1,0},{2,3},{3,2},{4,5},{5,4},{6,7},{7,6},{8,9},{9,8},{10,11... | collective-permute-start | bytes 1277960 | tf_op jit(solution)/shard_map/ppermute | solution.py:69
  78.3 21.9 %collective-permute-start.38 = (bf16[2,2,32,1664]{3,2,1,0:T(8,128)(2,1)S(1)}, bf16[2,2,32,1664]{3,2,1,0:T(8,128)(2,1)S(1)}, u32[]{:S(2)}, u32[]{:S(2)}) collective-permute-start(bf16[2,2,32,1664]{3,2,1,0:T(8,128)(2,1)S(1)} %get-tuple-element.38), channel_id=1, source_target_pairs={{0,3},{1,2},{2,1},{3,0},{4,7},{5,6},{6,5},{7,4},{8,11},{9,10},{10,... | collective-permute-start | bytes 1277960 | tf_op jit(solution)/shard_map/ppermute | solution.py:69
  89.3 35.0 %collective-permute-start.5 = (bf16[2,2,128,1664]{3,2,1,0:T(8,128)(2,1)S(1)}, bf16[2,2,128,1664]{3,2,1,0:T(8,128)(2,1)S(1)}, u32[]{:S(2)}, u32[]{:S(2)}) collective-permute-start(bf16[2,2,128,1664]{3,2,1,0:T(8,128)(2,1)S(1)} %get-tuple-element.18), channel_id=1, source_target_pairs={{0,4},{1,5},{2,6},{3,7},{4,0},{5,1},{6,2},{7,3},{8,12},{9,13},{10,... | collective-permute-start | bytes 5111816 | tf_op jit(solution)/shard_map/ppermute | solution.py:69
  97.9 25.7 %collective-permute-start.28 = (bf16[2,2,128,1664]{3,2,1,0:T(8,128)(2,1)S(1)}, bf16[2,2,128,1664]{3,2,1,0:T(8,128)(2,1)S(1)}, u32[]{:S(2)}, u32[]{:S(2)}) collective-permute-start(bf16[2,2,128,1664]{3,2,1,0:T(8,128)(2,1)S(1)} %get-tuple-element.24), channel_id=1, source_target_pairs={{0,12},{1,13},{2,14},{3,15},{4,8},{5,9},{6,10},{7,11},{8,4},{9,5},... | collective-permute-start | bytes 5111816 | tf_op jit(solution)/shard_map/ppermute | solution.py:69
  99.9 6.0 %collective-permute-start.17 = (bf16[2,2,16,1664]{3,2,1,0:T(8,128)(2,1)S(1)}, bf16[2,2,16,1664]{3,2,1,0:T(8,128)(2,1)S(1)}, u32[]{:S(2)}, u32[]{:S(2)}) collective-permute-start(bf16[2,2,16,1664]{3,2,1,0:T(8,128)(2,1)S(1)} %add_convert_fusion.21), channel_id=1, source_target_pairs={{0,3},{1,2},{2,1},{3,0},{4,7},{5,6},{6,5},{7,4},{8,11},{9,10},{10,... | collective-permute-start | bytes 638984 | tf_op jit(solution)/shard_map/ppermute | solution.py:69
  100.3 7.4 %collective-permute-start.39 = (bf16[2,2,16,1664]{3,2,1,0:T(8,128)(2,1)S(1)}, bf16[2,2,16,1664]{3,2,1,0:T(8,128)(2,1)S(1)}, u32[]{:S(2)}, u32[]{:S(2)}) collective-permute-start(bf16[2,2,16,1664]{3,2,1,0:T(8,128)(2,1)S(1)} %add_convert_fusion.17), channel_id=1, source_target_pairs={{0,1},{1,0},{2,3},{3,2},{4,5},{5,4},{6,7},{7,6},{8,9},{9,8},{10,11... | collective-permute-start | bytes 638984 | tf_op jit(solution)/shard_map/ppermute | solution.py:69
  106.1 6.3 %collective-permute-start.18 = (bf16[2,16,1664]{2,1,0:T(8,128)(2,1)S(1)}, bf16[2,16,1664]{2,1,0:T(8,128)(2,1)S(1)}, u32[]{:S(2)}, u32[]{:S(2)}) collective-permute-start(bf16[2,16,1664]{2,1,0:T(8,128)(2,1)S(1)} %fusion.10), channel_id=1, source_target_pairs={{0,3},{1,2},{2,1},{3,0},{4,7},{5,6},{6,5},{7,4},{8,11},{9,10},{10,... | collective-permute-start | bytes 319496 | tf_op jit(solution)/shard_map/ppermute | solution.py:69
  107.8 5.1 %collective-permute-start.40 = (bf16[2,16,1664]{2,1,0:T(8,128)(2,1)S(1)}, bf16[2,16,1664]{2,1,0:T(8,128)(2,1)S(1)}, u32[]{:S(2)}, u32[]{:S(2)}) collective-permute-start(bf16[2,16,1664]{2,1,0:T(8,128)(2,1)S(1)} %fusion.6), channel_id=1, source_target_pairs={{0,1},{1,0},{2,3},{3,2},{4,5},{5,4},{6,7},{7,6},{8,9},{9,8},{10,11... | collective-permute-start | bytes 319496 | tf_op jit(solution)/shard_map/ppermute | solution.py:69
  112.4 14.3 %collective-permute-start.19 = (bf16[2,32,1664]{2,1,0:T(8,128)(2,1)S(1)}, bf16[2,32,1664]{2,1,0:T(8,128)(2,1)S(1)}, u32[]{:S(2)}, u32[]{:S(2)}) collective-permute-start(bf16[2,32,1664]{2,1,0:T(8,128)(2,1)S(1)} %pad_maximum_fusion.9), channel_id=1, source_target_pairs={{0,1},{1,0},{2,3},{3,2},{4,5},{5,4},{6,7},{7,6},{8,9},{9,8},{10,11... | collective-permute-start | bytes 638984 | tf_op jit(solution)/shard_map/ppermute | solution.py:69
  113.0 14.6 %collective-permute-start.41 = (bf16[2,32,1664]{2,1,0:T(8,128)(2,1)S(1)}, bf16[2,32,1664]{2,1,0:T(8,128)(2,1)S(1)}, u32[]{:S(2)}, u32[]{:S(2)}) collective-permute-start(bf16[2,32,1664]{2,1,0:T(8,128)(2,1)S(1)} %pad_maximum_fusion.11), channel_id=1, source_target_pairs={{0,3},{1,2},{2,1},{3,0},{4,7},{5,6},{6,5},{7,4},{8,11},{9,10},{10,... | collective-permute-start | bytes 638984 | tf_op jit(solution)/shard_map/ppermute | solution.py:69
  124.0 13.0 %collective-permute-start.29 = (bf16[2,2,64,1664]{3,2,1,0:T(8,128)(2,1)S(1)}, bf16[2,2,64,1664]{3,2,1,0:T(8,128)(2,1)S(1)}, u32[]{:S(2)}, u32[]{:S(2)}) collective-permute-start(bf16[2,2,64,1664]{3,2,1,0:T(8,128)(2,1)S(1)} %get-tuple-element.32), channel_id=1, source_target_pairs={{0,4},{1,5},{2,6},{3,7},{4,0},{5,1},{6,2},{7,3},{8,12},{9,13},{10,... | collective-permute-start | bytes 2555912 | tf_op jit(solution)/shard_map/ppermute | solution.py:69
  124.7 14.0 %collective-permute-start.6 = (bf16[2,2,64,1664]{3,2,1,0:T(8,128)(2,1)S(1)}, bf16[2,2,64,1664]{3,2,1,0:T(8,128)(2,1)S(1)}, u32[]{:S(2)}, u32[]{:S(2)}) collective-permute-start(bf16[2,2,64,1664]{3,2,1,0:T(8,128)(2,1)S(1)} %get-tuple-element.36), channel_id=1, source_target_pairs={{0,12},{1,13},{2,14},{3,15},{4,8},{5,9},{6,10},{7,11},{8,4},{9,5},... | collective-permute-start | bytes 2555912 | tf_op jit(solution)/shard_map/ppermute | solution.py:69
  126.8 46.9 %collective-permute-start.20 = (bf16[2,64,1664]{2,1,0:T(8,128)(2,1)S(1)}, bf16[2,64,1664]{2,1,0:T(8,128)(2,1)S(1)}, u32[]{:S(2)}, u32[]{:S(2)}) collective-permute-start(bf16[2,64,1664]{2,1,0:T(8,128)(2,1)S(1)} %pad_maximum_fusion.5), channel_id=1, source_target_pairs={{0,12},{1,13},{2,14},{3,15},{4,8},{5,9},{6,10},{7,11},{8,4},{9,5},... | collective-permute-start | bytes 1277960 | tf_op jit(solution)/shard_map/ppermute | solution.py:69
  127.7 38.1 %collective-permute-start.42 = (bf16[2,64,1664]{2,1,0:T(8,128)(2,1)S(1)}, bf16[2,64,1664]{2,1,0:T(8,128)(2,1)S(1)}, u32[]{:S(2)}, u32[]{:S(2)}) collective-permute-start(bf16[2,64,1664]{2,1,0:T(8,128)(2,1)S(1)} %pad_maximum_fusion.7), channel_id=1, source_target_pairs={{0,4},{1,5},{2,6},{3,7},{4,0},{5,1},{6,2},{7,3},{8,12},{9,13},{10,... | collective-permute-start | bytes 1277960 | tf_op jit(solution)/shard_map/ppermute | solution.py:69
  137.3 13.2 %collective-permute-start.30 = (bf16[2,2,32,1664]{3,2,1,0:T(8,128)(2,1)S(1)}, bf16[2,2,32,1664]{3,2,1,0:T(8,128)(2,1)S(1)}, u32[]{:S(2)}, u32[]{:S(2)}) collective-permute-start(bf16[2,2,32,1664]{3,2,1,0:T(8,128)(2,1)S(1)} %get-tuple-element.40), channel_id=1, source_target_pairs={{0,3},{1,2},{2,1},{3,0},{4,7},{5,6},{6,5},{7,4},{8,11},{9,10},{10,... | collective-permute-start | bytes 1277960 | tf_op jit(solution)/shard_map/ppermute | solution.py:69
  138.9 12.0 %collective-permute-start.7 = (bf16[2,2,32,1664]{3,2,1,0:T(8,128)(2,1)S(1)}, bf16[2,2,32,1664]{3,2,1,0:T(8,128)(2,1)S(1)}, u32[]{:S(2)}, u32[]{:S(2)}) collective-permute-start(bf16[2,2,32,1664]{3,2,1,0:T(8,128)(2,1)S(1)} %get-tuple-element.44), channel_id=1, source_target_pairs={{0,1},{1,0},{2,3},{3,2},{4,5},{5,4},{6,7},{7,6},{8,9},{9,8},{10,11... | collective-permute-start | bytes 1277960 | tf_op jit(solution)/shard_map/ppermute | solution.py:69
  150.5 5.1 %collective-permute-start.31 = (bf16[2,2,16,1664]{3,2,1,0:T(8,128)(2,1)S(1)}, bf16[2,2,16,1664]{3,2,1,0:T(8,128)(2,1)S(1)}, u32[]{:S(2)}, u32[]{:S(2)}) collective-permute-start(bf16[2,2,16,1664]{3,2,1,0:T(8,128)(2,1)S(1)} %add_convert_fusion.19), channel_id=1, source_target_pairs={{0,1},{1,0},{2,3},{3,2},{4,5},{5,4},{6,7},{7,6},{8,9},{9,8},{10,11... | collective-permute-start | bytes 638984 | tf_op jit(solution)/shard_map/ppermute | solution.py:69
  151.0 6.0 %collective-permute-start.8 = (bf16[2,2,16,1664]{3,2,1,0:T(8,128)(2,1)S(1)}, bf16[2,2,16,1664]{3,2,1,0:T(8,128)(2,1)S(1)}, u32[]{:S(2)}, u32[]{:S(2)}) collective-permute-start(bf16[2,2,16,1664]{3,2,1,0:T(8,128)(2,1)S(1)} %add_convert_fusion.23), channel_id=1, source_target_pairs={{0,3},{1,2},{2,1},{3,0},{4,7},{5,6},{6,5},{7,4},{8,11},{9,10},{10,... | collective-permute-start | bytes 638984 | tf_op jit(solution)/shard_map/ppermute | solution.py:69
  155.7 3.9 %collective-permute-start.32 = (bf16[2,16,1664]{2,1,0:T(8,128)(2,1)S(1)}, bf16[2,16,1664]{2,1,0:T(8,128)(2,1)S(1)}, u32[]{:S(2)}, u32[]{:S(2)}) collective-permute-start(bf16[2,16,1664]{2,1,0:T(8,128)(2,1)S(1)} %fusion.8), channel_id=1, source_target_pairs={{0,1},{1,0},{2,3},{3,2},{4,5},{5,4},{6,7},{7,6},{8,9},{9,8},{10,11... | collective-permute-start | bytes 319496 | tf_op jit(solution)/shard_map/ppermute | solution.py:69
  157.1 5.1 %collective-permute-start.9 = (bf16[2,16,1664]{2,1,0:T(8,128)(2,1)S(1)}, bf16[2,16,1664]{2,1,0:T(8,128)(2,1)S(1)}, u32[]{:S(2)}, u32[]{:S(2)}) collective-permute-start(bf16[2,16,1664]{2,1,0:T(8,128)(2,1)S(1)} %fusion.12), channel_id=1, source_target_pairs={{0,3},{1,2},{2,1},{3,0},{4,7},{5,6},{6,5},{7,4},{8,11},{9,10},{10,... | collective-permute-start | bytes 319496 | tf_op jit(solution)/shard_map/ppermute | solution.py:69
  159.7 6.0 %collective-permute-start.33 = (bf16[2,32,1664]{2,1,0:T(8,128)(2,1)S(1)}, bf16[2,32,1664]{2,1,0:T(8,128)(2,1)S(1)}, u32[]{:S(2)}, u32[]{:S(2)}) collective-permute-start(bf16[2,32,1664]{2,1,0:T(8,128)(2,1)S(1)} %pad_maximum_fusion.10), channel_id=1, source_target_pairs={{0,3},{1,2},{2,1},{3,0},{4,7},{5,6},{6,5},{7,4},{8,11},{9,10},{10,... | collective-permute-start | bytes 638984 | tf_op jit(solution)/shard_map/ppermute | solution.py:69
  162.3 4.8 %collective-permute-start.10 = (bf16[2,32,1664]{2,1,0:T(8,128)(2,1)S(1)}, bf16[2,32,1664]{2,1,0:T(8,128)(2,1)S(1)}, u32[]{:S(2)}, u32[]{:S(2)}) collective-permute-start(bf16[2,32,1664]{2,1,0:T(8,128)(2,1)S(1)} %pad_maximum_fusion.8), channel_id=1, source_target_pairs={{0,1},{1,0},{2,3},{3,2},{4,5},{5,4},{6,7},{7,6},{8,9},{9,8},{10,11... | collective-permute-start | bytes 638984 | tf_op jit(solution)/shard_map/ppermute | solution.py:69
  165.7 7.4 %collective-permute-start.34 = (bf16[2,64,1664]{2,1,0:T(8,128)(2,1)S(1)}, bf16[2,64,1664]{2,1,0:T(8,128)(2,1)S(1)}, u32[]{:S(2)}, u32[]{:S(2)}) collective-permute-start(bf16[2,64,1664]{2,1,0:T(8,128)(2,1)S(1)} %pad_maximum_fusion.6), channel_id=1, source_target_pairs={{0,4},{1,5},{2,6},{3,7},{4,0},{5,1},{6,2},{7,3},{8,12},{9,13},{10,... | collective-permute-start | bytes 1277960 | tf_op jit(solution)/shard_map/ppermute | solution.py:69
  165.9 21.2 %collective-permute-start.43 = (bf16[2,128,1664]{2,1,0:T(8,128)(2,1)S(1)}, bf16[2,128,1664]{2,1,0:T(8,128)(2,1)S(1)}, u32[]{:S(2)}, u32[]{:S(2)}) collective-permute-start(bf16[2,128,1664]{2,1,0:T(8,128)(2,1)S(1)} %pad_maximum_fusion.3.mine), channel_id=1, source_target_pairs={{0,12},{1,13},{2,14},{3,15},{4,8},{5,9},{6,10},{7,11},{8,4},{9,5},... | collective-permute-start | bytes 2555912 | tf_op jit(solution)/shard_map/ppermute | solution.py:69
  167.1 19.0 %collective-permute-start.11 = (bf16[2,64,1664]{2,1,0:T(8,128)(2,1)S(1)}, bf16[2,64,1664]{2,1,0:T(8,128)(2,1)S(1)}, u32[]{:S(2)}, u32[]{:S(2)}) collective-permute-start(bf16[2,64,1664]{2,1,0:T(8,128)(2,1)S(1)} %pad_maximum_fusion.4), channel_id=1, source_target_pairs={{0,12},{1,13},{2,14},{3,15},{4,8},{5,9},{6,10},{7,11},{8,4},{9,5},... | collective-permute-start | bytes 1277960 | tf_op jit(solution)/shard_map/ppermute | solution.py:69
  173.1 22.1 %collective-permute-start.35 = (bf16[2,128,1664]{2,1,0:T(8,128)(2,1)S(1)}, bf16[2,128,1664]{2,1,0:T(8,128)(2,1)S(1)}, u32[]{:S(2)}, u32[]{:S(2)}) collective-permute-start(bf16[2,128,1664]{2,1,0:T(8,128)(2,1)S(1)} %pad_maximum_fusion.2.mine), channel_id=1, source_target_pairs={{0,12},{1,13},{2,14},{3,15},{4,8},{5,9},{6,10},{7,11},{8,4},{9,5},... | collective-permute-start | bytes 2555912 | tf_op jit(solution)/shard_map/ppermute | solution.py:69
  173.8 37.2 %collective-permute-start.21 = (bf16[2,128,1664]{2,1,0:T(8,128)(2,1)S(1)}, bf16[2,128,1664]{2,1,0:T(8,128)(2,1)S(1)}, u32[]{:S(2)}, u32[]{:S(2)}) collective-permute-start(bf16[2,128,1664]{2,1,0:T(8,128)(2,1)S(1)} %pad_maximum_fusion.1.mine), channel_id=1, source_target_pairs={{0,4},{1,5},{2,6},{3,7},{4,0},{5,1},{6,2},{7,3},{8,12},{9,13},{10,... | collective-permute-start | bytes 2555912 | tf_op jit(solution)/shard_map/ppermute | solution.py:69
  186.2 28.6 %collective-permute-start.12 = (bf16[2,128,1664]{2,1,0:T(8,128)(2,1)S(1)}, bf16[2,128,1664]{2,1,0:T(8,128)(2,1)S(1)}, u32[]{:S(2)}, u32[]{:S(2)}) collective-permute-start(bf16[2,128,1664]{2,1,0:T(8,128)(2,1)S(1)} %pad_maximum_fusion.mine), channel_id=1, source_target_pairs={{0,4},{1,5},{2,6},{3,7},{4,0},{5,1},{6,2},{7,3},{8,12},{9,13},{10,... | collective-permute-start | bytes 2555912 | tf_op jit(solution)/shard_map/ppermute | solution.py:69
  199.4 19.7 %collective-permute-start.44 = (bf16[2,128,1024]{2,1,0:T(8,128)(2,1)S(1)}, bf16[2,128,1024]{2,1,0:T(8,128)(2,1)S(1)}, u32[]{:S(2)}, u32[]{:S(2)}) collective-permute-start(bf16[2,128,1024]{2,1,0:T(8,128)(2,1)S(1)} %get-tuple-element.28), channel_id=1, source_target_pairs={{0,16},{16,0},{32,48},{48,32},{64,80},{80,64},{96,112},{112,96},{1... | collective-permute-start | bytes 1572872 | tf_op jit(solution)/shard_map/ppermute | solution.py:65
  219.0 2.7 %collective-permute-start.22 = (bf16[2,128,1024]{2,1,0:T(8,128)(2,1)S(1)}, bf16[2,128,1024]{2,1,0:T(8,128)(2,1)S(1)}, u32[]{:S(2)}, u32[]{:S(2)}) collective-permute-start(bf16[2,128,1024]{2,1,0:T(8,128)(2,1)S(1)} %get-tuple-element.22), channel_id=1, source_target_pairs={{0,16},{16,0},{32,48},{48,32},{64,80},{80,64},{96,112},{112,96},{1... | collective-permute-start | bytes 1572872 | tf_op jit(solution)/shard_map/ppermute | solution.py:65
  219.3 8.1 %collective-permute-start.46 = (bf16[128,1024]{1,0:T(8,128)(2,1)S(1)}, bf16[128,1024]{1,0:T(8,128)(2,1)S(1)}, u32[]{:S(2)}, u32[]{:S(2)}) collective-permute-start(bf16[128,1024]{1,0:T(8,128)(2,1)S(1)} %get-tuple-element.46), channel_id=1, source_target_pairs={{0,96},{16,112},{32,0},{48,16},{64,32},{80,48},{96,64},{112,80},{1... | collective-permute-start | bytes 786440 | tf_op jit(solution)/shard_map/ppermute | solution.py:234
  221.6 13.9 %collective-permute-start.45 = (bf16[128,1024]{1,0:T(8,128)(2,1)S(1)}, bf16[128,1024]{1,0:T(8,128)(2,1)S(1)}, u32[]{:S(2)}, u32[]{:S(2)}) collective-permute-start(bf16[128,1024]{1,0:T(8,128)(2,1)S(1)} %get-tuple-element.45), channel_id=1, source_target_pairs={{0,32},{16,48},{32,64},{48,80},{64,96},{80,112},{96,0},{112,16},{1... | collective-permute-start | bytes 786440 | tf_op jit(solution)/shard_map/ppermute | solution.py:233
  221.8 13.7 %collective-permute-start.23 = (bf16[128,1024]{1,0:T(8,128)(2,1)S(1)}, bf16[128,1024]{1,0:T(8,128)(2,1)S(1)}, u32[]{:S(2)}, u32[]{:S(2)}) collective-permute-start(bf16[128,1024]{1,0:T(8,128)(2,1)S(1)} %fusion.4), channel_id=1, source_target_pairs={{0,64},{16,80},{32,96},{48,112},{64,0},{80,16},{96,32},{112,48},{1... | collective-permute-start | bytes 786440 | tf_op jit(solution)/shard_map/ppermute | solution.py:232
  (7 other events, 43.9 us)

commit v3 on v1

v3 whole, which is shorter than its diff:
```python
import functools

import jax
import jax.numpy as jnp
from jax import lax
from jax.experimental import pallas as pl
from jax.experimental.pallas import tpu as pltpu
from jax.sharding import PartitionSpec as P

BF = jnp.bfloat16
F32 = jnp.float32

TIMES = {
    "project": 5.0,
    "cut": 3.0,
    "down": 2.5,
    "halves": 2.0,
    "hidden": 2.0,
    "join": 2.0,
    "stack": 1.0,
}

PAIR = {"e": (1, 0, 3, 2), "o": (3, 2, 1, 0)}
ORDERS = (
    (("x", "e"), ("x", "o"), ("y", "e"), ("y", "o")),
    (("x", "o"), ("x", "e"), ("y", "o"), ("y", "e")),
), (
    (("y", "e"), ("y", "o"), ("x", "e"), ("x", "o")),
    (("y", "o"), ("y", "e"), ("x", "o"), ("x", "e")),
)
SWAP = [(g, g ^ 1) for g in range(8)]

HALF = 1664
WIDE = (896, 768)
DOWN = (512, 512)

VMEM = pl.BlockSpec(memory_space=pltpu.VMEM)
ANY = pl.BlockSpec(memory_space=pl.ANY)


def partner(m, link):
    axis, kind = link
    x, y = divmod(m, 4)
    return 4 * PAIR[kind][x] + y if axis == "x" else 4 * x + PAIR[kind][y]


def exchange(a, flow, step):
    pairs = [
        (g * 16 + m, g * 16 + partner(m, ORDERS[g % 2][flow][step]))
        for g in range(8)
        for m in range(16)
    ]
    return lax.ppermute(a, ("group", "mp"), pairs)


def swap(a):
    return lax.ppermute(a, "group", SWAP)


def shift(a, chips):
    return lax.ppermute(a, "group", [(g, (g + 2 * chips) % 8) for g in range(8)])


def core_index():
    return lax.axis_index("group") & 1


def mask_of(flow):
    place = lax.axis_index("mp")
    x, y = place >> 2, place & 3
    lead = x + core_index() * (y - x)
    rest = x + y - lead
    own = 0
    for at in (lead, rest):
        even, odd = ((at + 1) >> 1) & 1, at >> 1
        own = own * 4 + (2 * even + odd if flow == 0 else 2 * odd + even)
    return 15 ^ own


def kernel(body, name, args, shapes, after, scratch=(), limit=2, specs=None):
    specs = specs or [VMEM] * len(args)
    return pl.pallas_call(
        body,
        in_specs=specs + [ANY] * len(after),
        out_specs=[VMEM] * len(shapes),
        out_shape=shapes,
        scratch_shapes=list(scratch),
        compiler_params=pltpu.CompilerParams(vmem_limit_bytes=limit << 20),
        cost_estimate=pl.CostEstimate(
            flops=int(TIMES[name] * 1.15e9), bytes_accessed=0, transcendentals=0
        ),
        name=name,
    )(*args, *after)


def cut_body(axis, pieces, source, *refs):
    outs, sem = refs[-1 - 2 * len(pieces) : -1], refs[-1]
    copies = []
    for which in range(2):
        core = core_index()
        begin = (core if which else 1 - core) * HALF
        at = 0
        for i, size in enumerate(pieces):
            if axis == 1:
                place = source.at[:, pl.ds(pl.multiple_of(begin + at, 128), size)]
            else:
                place = source.at[pl.ds(pl.multiple_of(begin, 128), HALF), pl.ds(at, size)]
            at += size
            n = which * len(pieces) + i
            copies.append(pltpu.make_async_copy(place, outs[n], sem.at[n]))
    for copy in copies:
        copy.start()
    for copy in copies:
        copy.wait()


def cut(axis, pieces, weight, after=()):
    weight = pltpu.with_memory_space_constraint(weight, pltpu.HBM)
    rows = weight.shape[0] if axis == 1 else HALF
    shapes = [pltpu.VMEM((rows, size), BF) for size in pieces] * 2
    out = kernel(
        functools.partial(cut_body, axis, pieces),
        "cut",
        (weight,),
        shapes,
        after,
        [pltpu.SemaphoreType.DMA((2 * len(pieces),))],
        specs=[pl.BlockSpec(memory_space=pltpu.HBM)],
    )
    return out[: len(pieces)], out[len(pieces) :]


def project_body(flow, sizes, *refs):
    count = 2 * len(sizes)
    blocks = refs[:count]
    weights = (refs[count : count + 2], refs[count + 2 : count + 4])
    send, keep, plain, turned = refs[-4:]
    pairs = sum(sizes)
    mask = mask_of(flow)
    at = 0
    for i, size in enumerate(sizes):
        for t in range(size):
            plain[pl.ds(at, 128)] = blocks[2 * i][t]
            plain[pl.ds(at + 128, 128)] = blocks[2 * i + 1][t]
            at += 256
    for t in range(pairs):
        for r in range(16):
            source = pl.multiple_of(t * 256 + (r ^ mask) * 16, 16)
            turned[pl.ds(t * 256 + r * 16, 16)] = plain[pl.ds(source, 16)]

    def store(k, columns, part):
        for t in range(pairs):
            send[k, t, :, columns] = part[t * 256 : t * 256 + 128]
            keep[k, t, :, columns] = part[t * 256 + 128 : t * 256 + 256]

    def multiply(weight):
        return jnp.dot(turned[...], weight, preferred_element_type=F32).astype(BF)

    for piece, base in ((0, 0), (1, WIDE[0])):
        for k in range(2):
            for at in range(0, 768, 256):
                part = multiply(weights[k][piece][:, at : at + 256])
                store(k, pl.ds(base + at, 256), part)
    both = jnp.concatenate((weights[0][0][:, 768:], weights[1][0][:, 768:]), axis=1)
    res = multiply(both)
    for k in range(2):
        store(k, pl.ds(768, 128), res[:, k * 128 : (k + 1) * 128])


def project(flow, tokens, gate, up, after=()):
    sizes = [mine.shape[0] for mine, _ in tokens]
    blocks = [block for both in tokens for block in both]
    rows = 256 * sum(sizes)
    shape = jax.ShapeDtypeStruct((2, sum(sizes), 128, HALF), BF)
    return kernel(
        functools.partial(project_body, flow, sizes),
        "project",
        (*blocks, *gate, *up),
        [shape] * 2,
        after,
        [pltpu.VMEM((rows, 1024), BF)] * 2,
        8,
    )


def down_body(flow, first, last, *refs):
    rows, pieces, refs = refs[0], refs[1:3], refs[3:]
    outs = refs[-1:]
    mask = mask_of(flow)
    left = jnp.concatenate((rows[0], rows[1]), axis=0)
    for j in range(4):
        columns = pl.ds(j * 256, 256)
        weight = pieces[j // 2][:, j % 2 * 256 : (j % 2 + 1) * 256]
        res = jnp.dot(left, weight, preferred_element_type=F32)
        if first:
            outs[0][:, columns] = res
            continue
        for t in range(2):
            for r in range(16):
                place = r ^ mask
                if r < 8:
                    value = res[t * 128 + r * 16 : t * 128 + (r + 1) * 16]
                else:
                    value = refs[0][pl.ds(t * 128 + (r - 8) * 16, 16), columns]
                spot = pl.ds(pl.multiple_of(place * 16, 16), 16)
                outs[0][t, spot, columns] = value
    if last:
        send, keep, total = refs[-3:]
        keep[...] = total[:, :128] + refs[1][:, :128]
        send[...] = (total[:, 128:] + refs[1][:, 128:]).astype(BF)


def down(flow, rows, weights, half=None, before=None, after=()):
    first, last = half is None, before is not None
    if first:
        shapes = [jax.ShapeDtypeStruct((256, 1024), F32)]
    elif last:
        shapes = [
            jax.ShapeDtypeStruct((2, 128, 1024), BF),
            jax.ShapeDtypeStruct((2, 128, 1024), F32),
        ]
    else:
        shapes = [jax.ShapeDtypeStruct((2, 256, 1024), F32)]
    extra = [a for a in (half, before) if a is not None]
    out = kernel(
        functools.partial(down_body, flow, first, last),
        "down",
        (rows, *weights, *extra),
        shapes,
        after,
        [pltpu.VMEM((2, 256, 1024), F32)] if last else (),
        limit=4,
    )
    return out if last else out[0]


def halves_body(keep, came, *refs):
    send, kept = refs[-2:]
    half = kept.shape[2]
    for k in range(2):
        for t in range(2):
            total = keep[k, t].astype(F32) + came[k, t].astype(F32)
            send[k, t] = total[:half].astype(BF)
            kept[k, t] = total[half:].astype(BF)


def halves(keep, came, after):
    shape = jax.ShapeDtypeStruct((2, 2, keep.shape[2] // 2, HALF), BF)
    return kernel(halves_body, "halves", (keep, came), [shape] * 2, after)


def hidden_body(keep, came, *refs):
    gate = keep[0].astype(F32) + came[0].astype(F32)
    up = keep[1].astype(F32) + came[1].astype(F32)
    refs[-1][...] = (gate / (1.0 + jnp.exp(-gate)) * up).astype(BF)


def hidden(keep, came, after):
    shape = jax.ShapeDtypeStruct(keep.shape[1:], BF)
    return kernel(hidden_body, "hidden", (keep, came), [shape], after)[0]


def join_body(theirs, mine, *refs):
    rows = mine.shape[1]
    refs[-1][:, :rows] = theirs[...]
    refs[-1][:, rows:] = mine[...]


def join(theirs, mine, after):
    shape = jax.ShapeDtypeStruct((2, 2 * mine.shape[1], HALF), BF)
    return kernel(join_body, "join", (theirs, mine), [shape], after)[0]


def stack_body(first, second, *refs):
    refs[-1][0] = first[...]
    refs[-1][1] = second[...]


def stack(first, second, after):
    shape = jax.ShapeDtypeStruct((2, *first.shape), BF)
    return kernel(stack_body, "stack", (first, second), [shape], after)[0]


class Line:
    def __init__(self):
        self.last = ()

    def __call__(self, call, *args):
        out = call(*args, after=self.last)
        first = out
        while isinstance(first, (list, tuple)):
            first = first[0]
        self.last = (first,)
        return out


TURNS = "guj0123013120130123123103210230w230221301302"


def local(tokens, gate_weight, up_weight, down_weight):
    line = Line()
    after, before = shift(tokens, -1), shift(tokens, 1)
    near, beside = tokens[None], swap(tokens)[None]
    far = shift(beside, 2)
    pair_a = [(near, beside), (swap(far), far)]
    weights = {"g": (1, WIDE, gate_weight), "u": (1, WIDE, up_weight), "w": (0, DOWN, down_weight)}
    own, other = {}, {}
    sides = []
    finished = {}

    def unit(u):
        flow = u % 2
        held = own if u < 2 else other
        send, keep = line(project, flow, pair_a if flow == 0 else sides, held["g"], held["u"])
        for step in range(3):
            came = exchange(send, flow, step)
            yield
            send, keep = line(halves, keep, came)
        came = exchange(send, flow, 3)
        yield
        rows = line(hidden, keep, came)
        for step in (3, 2, 1):
            theirs = exchange(rows, flow, step)
            yield
            rows = line(join, theirs, rows)
        theirs = exchange(rows, flow, 0)
        yield
        half = line(down, flow, rows, held["w"])
        yield
        finished[u] = line(down, flow, theirs, held["w"], half, finished.get(u - 2))
        yield

    units = [unit(u) for u in range(4)]
    for turn in TURNS:
        if turn in weights:
            given, own[turn] = line(cut, *weights[turn])
            other[turn] = [swap(piece) for piece in given]
        elif turn == "j":
            both = line(stack, after, before)
            sides.append((both, swap(both)))
        else:
            next(units[int(turn)])

    (a_send, a_keep), (b_send, b_keep) = finished[2], finished[3]
    a_total = a_keep + swap(a_send).astype(F32)
    b_total = b_keep + swap(b_send).astype(F32)
    from_opposite = shift(a_total[1].astype(BF), 2)
    from_before = shift(b_total[0].astype(BF), 1)
    from_after = shift(b_total[1].astype(BF), -1)
    total = a_total[0] + from_opposite.astype(F32)
    total = total + from_before.astype(F32) + from_after.astype(F32)
    return total.astype(BF)


def solution(mesh):
    placed = (P("group", "mp"), P("mp", "group"), P("mp", "group"), P("group", "mp"))
    return jax.shard_map(
        local, mesh=mesh, in_specs=placed, out_specs=P("group", "mp"), check_vma=False
    )
```

time: 336 us -> 199 us (0.59)
  waiting for transfers between devices: 279 us -> 100 us
  starting transfers between devices: 0.17 us -> 59.6 us
  Pallas kernels: 0 us -> 37.3 us
  matrix products: 37 us -> 0 us
  between operations: 13.1 us -> 0.41 us
    reduce_scatter x3 -> x0, waiting for transfers between devices: 183 us -> none  [the longest x1 85.5 us: local(): lax.psum_scatter(gate_part, 'mp', scatter_dimension=0, tiled=True)]
    ppermute x0 -> x49, waiting for transfers between devices: none -> 100 us  [the longest x32 80.1 us: exchange(): return lax.ppermute(a, ('group', 'mp'), pairs)]
    all_gather x2 -> x0, waiting for transfers between devices: 94.9 us -> none  [the longest x1 64.1 us: local(): hidden = lax.all_gather(hidden, 'mp', axis=0, tiled=True)]
    ppermute x0 -> x49, starting transfers between devices: none -> 59.6 us  [the longest x32 35.9 us: exchange(): return lax.ppermute(a, ('group', 'mp'), pairs)]
    pallas_call x0 -> x44, Pallas kernels: none -> 37.3 us  [kernel(): pl.pallas_call(body, in_specs=specs + [ANY] * len(after), out_specs=[VMEM...]
    dot_general x3 -> x0, matrix products: 37 us -> none  [the longest x1 12.4 us: local(): jnp.dot(rows, up_weight, preferred_element_type=jnp.float32)]
  transfers between devices with their start and end apart: 5 -> 49, of which waited for: 5 -> 26; matrix products, arithmetic and copies ran while one was open for 4% -> 0% of each run, Pallas kernels for 0% -> 16%
where the time goes in v3:
time: 199 us
  waiting for transfers between devices  100 us (50%)
  starting transfers between devices  59.6 us (30%)
  Pallas kernels  37.3 us (19%)
    ppermute x32, waiting for transfers between devices, exchange(): return lax.ppermute(a, ('group', 'mp'), pairs)  80.1 us
    pallas_call x44, Pallas kernels, kernel(): pl.pallas_call(body, in_specs=specs + [ANY] * len(after), out_specs=[VMEM...  37.3 us
    ppermute x32, starting transfers between devices, exchange(): return lax.ppermute(a, ('group', 'mp'), pairs)  35.9 us
    ppermute x6, waiting for transfers between devices, shift(): lax.ppermute(a, 'group', [(g, (g + 2 * chips) % 8) for g in range(8)])  17.8 us
    ppermute x11, starting transfers between devices, swap(): return lax.ppermute(a, 'group', SWAP)  14.2 us
    ppermute x6, starting transfers between devices, shift(): lax.ppermute(a, 'group', [(g, (g + 2 * chips) % 8) for g in range(8)])  9.57 us
  transfers between devices with their start and end apart: 49, of which 26 were waited for; matrix products, arithmetic and copies ran while one was open for 0% of the time, Pallas kernels for 16%

profile of v3, /device:TPU:1, one launch (start us, length us, event | category | flops | bytes accessed | tf_op | source)
XLA Modules:
  0.0 199.1 jit_solution(16928212347303566934)
XLA Ops:
  0.0 1.4 collective-permute-start
  1.4 1.7 collective-permute-start.8
  3.1 2.1 %collective-permute-start.7 = (bf16[128,1024]{1,0:T(8,128)(2,1)}, bf16[128,1024]{1,0:T(8,128)(2,1)S(1)}, u32[]{:S(2)}, u32[]{:S(2)}) collective-permute-start(bf16[128,1024]{1,0:T(8,128)(2,1)} %param.4), channel_id=1, source_target_pairs={{0,96},{16,112},{32,0},{48,16},{64,32},{80,48},{96,64},{112,80},{1... | collective-permute-start | bytes 786440 | tf_op jit(solution)/shard_map/ppermute | solution.py:61
  5.3 3.0 %cut.3 = (bf16[1024,896]{1,0:T(8,128)(2,1)S(1)}, bf16[1024,768]{1,0:T(8,128)(2,1)S(1)}, bf16[1024,896]{1,0:T(8,128)(2,1)S(1)}, bf16[1024,768]{1,0:T(8,128)(2,1)S(1)}) custom-call(bf16[1024,3328]{1,0:T(8,128)(2,1)} %source.3), custom_call_target="tpu_custom_call" | custom-call | flops 3449999872 | tf_op jit(solution)/shard_map/cut/pallas_call | solution.py:82
  8.7 3.0 %cut.4 = (bf16[1024,896]{1,0:T(8,128)(2,1)S(1)}, bf16[1024,768]{1,0:T(8,128)(2,1)S(1)}, bf16[1024,896]{1,0:T(8,128)(2,1)S(1)}, bf16[1024,768]{1,0:T(8,128)(2,1)S(1)}) custom-call(bf16[1024,3328]{1,0:T(8,128)(2,1)} %source.4, bf16[1024,896]{1,0:T(8,128)(2,1)S(1)} %get-tuple-element.53.refs_0_), custom_call_target="tpu_custom_call" | custom-call | flops 3449999872 | tf_op jit(solution)/shard_map/cut/pallas_call | solution.py:82
  12.0 1.5 collective-permute-start.1
  14.3 6.8 %collective-permute-done.1.refs_3_ = bf16[1,128,1024]{2,1,0:T(8,128)(2,1)S(1)} collective-permute-done((bf16[1,128,1024]{2,1,0:T(8,128)(2,1)S(1)}, bf16[1,128,1024]{2,1,0:T(8,128)(2,1)S(1)}, u32[]{:S(2)}, u32[]{:S(2)}) %collective-permute-start.1) | collective-permute-done | bytes 262176 | tf_op jit(solution)/shard_map/ppermute | solution.py:61
  23.8 3.7 %project.4 = (bf16[2,2,128,1664]{3,2,1,0:T(8,128)(2,1)S(1)}, bf16[2,2,128,1664]{3,2,1,0:T(8,128)(2,1)S(1)}) custom-call(bf16[1,128,1024]{2,1,0:T(8,128)(2,1)S(1)} %bitcast.18, bf16[1,128,1024]{2,1,0:T(8,128)(2,1)S(1)} %bitcast.21, bf16[1,128,1024]{2,1,0:T(8,128)(2,1)S(1)} %collective-permute-done.2.refs_2_, ...), custom_call_target="tpu_custom_call" | custom-call | flops 5750000128 | tf_op jit(solution)/shard_map/project/pallas_call | solution.py:82
  28.9 3.7 %project.5 = (bf16[2,2,128,1664]{3,2,1,0:T(8,128)(2,1)S(1)}, bf16[2,2,128,1664]{3,2,1,0:T(8,128)(2,1)S(1)}) custom-call(bf16[2,128,1024]{2,1,0:T(8,128)(2,1)S(1)} %stack.1.refs_8_.refs_0_, bf16[2,128,1024]{2,1,0:T(8,128)(2,1)S(1)} %collective-permute-done.9.refs_1_, bf16[1024,896]{1,0:T(8,128)(2,1)S(1)} %get-tuple-element.57.refs_4_.refs_2_, ...), custom_call_target="tpu_custom_call" | custom-call | flops 5750000128 | tf_op jit(solution)/shard_map/project/pallas_call | solution.py:82
  32.7 2.2 %collective-permute-start.11 = (bf16[2,2,128,1664]{3,2,1,0:T(8,128)(2,1)S(1)}, bf16[2,2,128,1664]{3,2,1,0:T(8,128)(2,1)S(1)}, u32[]{:S(2)}, u32[]{:S(2)}) collective-permute-start(bf16[2,2,128,1664]{3,2,1,0:T(8,128)(2,1)S(1)} %get-tuple-element.62.refs_8_), channel_id=1, source_target_pairs={{0,12},{1,13},{2,14},{3,15},{4,8},{5,9},{6,10},{7,11},{8,4},{9,5},... | collective-permute-start | bytes 5111816 | tf_op jit(solution)/shard_map/ppermute | solution.py:53
  34.8 3.7 %project.6 = (bf16[2,2,128,1664]{3,2,1,0:T(8,128)(2,1)S(1)}, bf16[2,2,128,1664]{3,2,1,0:T(8,128)(2,1)S(1)}) custom-call(bf16[1,128,1024]{2,1,0:T(8,128)(2,1)S(1)} %bitcast.19, bf16[1,128,1024]{2,1,0:T(8,128)(2,1)S(1)} %bitcast.22, bf16[1,128,1024]{2,1,0:T(8,128)(2,1)S(1)} %collective-permute-done.2.refs_2_, ...), custom_call_target="tpu_custom_call" | custom-call | flops 5750000128 | tf_op jit(solution)/shard_map/project/pallas_call | solution.py:82
  38.6 3.7 %project.7 = (bf16[2,2,128,1664]{3,2,1,0:T(8,128)(2,1)S(1)}, bf16[2,2,128,1664]{3,2,1,0:T(8,128)(2,1)S(1)}) custom-call(bf16[2,128,1024]{2,1,0:T(8,128)(2,1)S(1)} %stack.1.refs_8_.refs_0_, bf16[2,128,1024]{2,1,0:T(8,128)(2,1)S(1)} %collective-permute-done.9.refs_1_, bf16[1024,896]{1,0:T(8,128)(2,1)S(1)} %collective-permute-done.3.refs_4_.refs_2_, ...), custom_call_target="tpu_custom_call" | custom-call | flops 5750000128 | tf_op jit(solution)/shard_map/project/pallas_call | solution.py:82
  43.2 5.4 %collective-permute-done.12.came = bf16[2,2,128,1664]{3,2,1,0:T(8,128)(2,1)S(1)} collective-permute-done((bf16[2,2,128,1664]{3,2,1,0:T(8,128)(2,1)S(1)}, bf16[2,2,128,1664]{3,2,1,0:T(8,128)(2,1)S(1)}, u32[]{:S(2)}, u32[]{:S(2)}) %collective-permute-start.12) | collective-permute-done | bytes 1703968 | tf_op jit(solution)/shard_map/ppermute | solution.py:53
  49.0 6.1 %collective-permute-done.11.came = bf16[2,2,128,1664]{3,2,1,0:T(8,128)(2,1)S(1)} collective-permute-done((bf16[2,2,128,1664]{3,2,1,0:T(8,128)(2,1)S(1)}, bf16[2,2,128,1664]{3,2,1,0:T(8,128)(2,1)S(1)}, u32[]{:S(2)}, u32[]{:S(2)}) %collective-permute-start.11) | collective-permute-done | bytes 1703968 | tf_op jit(solution)/shard_map/ppermute | solution.py:53
  55.6 2.0 collective-permute-start.17
  57.6 15.8 %collective-permute-done.14.came = bf16[2,2,128,1664]{3,2,1,0:T(8,128)(2,1)S(1)} collective-permute-done((bf16[2,2,128,1664]{3,2,1,0:T(8,128)(2,1)S(1)}, bf16[2,2,128,1664]{3,2,1,0:T(8,128)(2,1)S(1)}, u32[]{:S(2)}, u32[]{:S(2)}) %collective-permute-start.14) | collective-permute-done | bytes 1703968 | tf_op jit(solution)/shard_map/ppermute | solution.py:53
  73.9 2.1 %collective-permute-done.13.came = bf16[2,2,64,1664]{3,2,1,0:T(8,128)(2,1)S(1)} collective-permute-done((bf16[2,2,64,1664]{3,2,1,0:T(8,128)(2,1)S(1)}, bf16[2,2,64,1664]{3,2,1,0:T(8,128)(2,1)S(1)}, u32[]{:S(2)}, u32[]{:S(2)}) %collective-permute-start.13) | collective-permute-done | bytes 852000 | tf_op jit(solution)/shard_map/ppermute | solution.py:53
  76.2 2.6 %collective-permute-start.16 = (bf16[2,2,32,1664]{3,2,1,0:T(8,128)(2,1)S(1)}, bf16[2,2,32,1664]{3,2,1,0:T(8,128)(2,1)S(1)}, u32[]{:S(2)}, u32[]{:S(2)}) collective-permute-start(bf16[2,2,32,1664]{3,2,1,0:T(8,128)(2,1)S(1)} %get-tuple-element.73.refs_0_), channel_id=1, source_target_pairs={{0,3},{1,2},{2,1},{3,0},{4,7},{5,6},{6,5},{7,4},{8,11},{9,10},{10,... | collective-permute-start | bytes 1277960 | tf_op jit(solution)/shard_map/ppermute | solution.py:53
  79.1 2.8 %collective-permute-start.15 = (bf16[2,2,64,1664]{3,2,1,0:T(8,128)(2,1)S(1)}, bf16[2,2,64,1664]{3,2,1,0:T(8,128)(2,1)S(1)}, u32[]{:S(2)}, u32[]{:S(2)}) collective-permute-start(bf16[2,2,64,1664]{3,2,1,0:T(8,128)(2,1)S(1)} %get-tuple-element.75.refs_0_), channel_id=1, source_target_pairs={{0,12},{1,13},{2,14},{3,15},{4,8},{5,9},{6,10},{7,11},{8,4},{9,5},... | collective-permute-start | bytes 2555912 | tf_op jit(solution)/shard_map/ppermute | solution.py:53
  84.8 4.6 %collective-permute-done.16.came = bf16[2,2,32,1664]{3,2,1,0:T(8,128)(2,1)S(1)} collective-permute-done((bf16[2,2,32,1664]{3,2,1,0:T(8,128)(2,1)S(1)}, bf16[2,2,32,1664]{3,2,1,0:T(8,128)(2,1)S(1)}, u32[]{:S(2)}, u32[]{:S(2)}) %collective-permute-start.16) | collective-permute-done | bytes 426016 | tf_op jit(solution)/shard_map/ppermute | solution.py:53
  89.8 2.4 %collective-permute-start.23 = (bf16[2,2,32,1664]{3,2,1,0:T(8,128)(2,1)S(1)}, bf16[2,2,32,1664]{3,2,1,0:T(8,128)(2,1)S(1)}, u32[]{:S(2)}, u32[]{:S(2)}) collective-permute-start(bf16[2,2,32,1664]{3,2,1,0:T(8,128)(2,1)S(1)} %get-tuple-element.83.refs_0_), channel_id=1, source_target_pairs={{0,3},{1,2},{2,1},{3,0},{4,7},{5,6},{6,5},{7,4},{8,11},{9,10},{10,... | collective-permute-start | bytes 1277960 | tf_op jit(solution)/shard_map/ppermute | solution.py:53
  92.3 1.6 collective-permute-start.27
  94.8 1.5 collective-permute-done.15.came
  97.4 4.2 %collective-permute-done.23.came = bf16[2,2,32,1664]{3,2,1,0:T(8,128)(2,1)S(1)} collective-permute-done((bf16[2,2,32,1664]{3,2,1,0:T(8,128)(2,1)S(1)}, bf16[2,2,32,1664]{3,2,1,0:T(8,128)(2,1)S(1)}, u32[]{:S(2)}, u32[]{:S(2)}) %collective-permute-start.23) | collective-permute-done | bytes 426016 | tf_op jit(solution)/shard_map/ppermute | solution.py:53
  101.8 1.9 collective-permute-start.28
  103.8 2.8 %collective-permute-start.24 = (bf16[2,2,16,1664]{3,2,1,0:T(8,128)(2,1)S(1)}, bf16[2,2,16,1664]{3,2,1,0:T(8,128)(2,1)S(1)}, u32[]{:S(2)}, u32[]{:S(2)}) collective-permute-start(bf16[2,2,16,1664]{3,2,1,0:T(8,128)(2,1)S(1)} %get-tuple-element.90.refs_0_), channel_id=1, source_target_pairs={{0,3},{1,2},{2,1},{3,0},{4,7},{5,6},{6,5},{7,4},{8,11},{9,10},{10,... | collective-permute-start | bytes 638984 | tf_op jit(solution)/shard_map/ppermute | solution.py:53
  109.0 1.9 collective-permute-start.30
  110.9 1.5 collective-permute-start.34
  113.9 1.6 collective-permute-done.31.theirs
  115.6 1.5 collective-permute-start.33
  118.4 4.6 %collective-permute-done.33.theirs = bf16[2,32,1664]{2,1,0:T(8,128)(2,1)S(1)} collective-permute-done((bf16[2,32,1664]{2,1,0:T(8,128)(2,1)S(1)}, bf16[2,32,1664]{2,1,0:T(8,128)(2,1)S(1)}, u32[]{:S(2)}, u32[]{:S(2)}) %collective-permute-start.33) | collective-permute-done | bytes 213024 | tf_op jit(solution)/shard_map/ppermute | solution.py:53
  123.0 3.0 %cut.5 = (bf16[1664,512]{1,0:T(8,128)(2,1)S(1)}, bf16[1664,512]{1,0:T(8,128)(2,1)S(1)}, bf16[1664,512]{1,0:T(8,128)(2,1)S(1)}, bf16[1664,512]{1,0:T(8,128)(2,1)S(1)}) custom-call(bf16[3328,1024]{1,0:T(8,128)(2,1)} %source.5, bf16[2,64,1664]{2,1,0:T(8,128)(2,1)S(1)} %join.19.refs_0_.mine), custom_call_target="tpu_custom_call" | custom-call | flops 3449999872 | tf_op jit(solution)/shard_map/cut/pallas_call | solution.py:82
  126.1 7.1 %collective-permute-start.40 = (bf16[1664,512]{1,0:T(8,128)(2,1)S(1)}, bf16[1664,512]{1,0:T(8,128)(2,1)S(1)}, u32[]{:S(2)}, u32[]{:S(2)}) collective-permute-start(bf16[1664,512]{1,0:T(8,128)(2,1)S(1)} %get-tuple-element.94), channel_id=1, source_target_pairs={{0,16},{16,0},{32,48},{48,32},{64,80},{80,64},{96,112},{112,96},{1... | collective-permute-start | bytes 5111816 | tf_op jit(solution)/shard_map/ppermute | solution.py:57
  135.2 3.4 %collective-permute-done.32.theirs = bf16[2,32,1664]{2,1,0:T(8,128)(2,1)S(1)} collective-permute-done((bf16[2,32,1664]{2,1,0:T(8,128)(2,1)S(1)}, bf16[2,32,1664]{2,1,0:T(8,128)(2,1)S(1)}, u32[]{:S(2)}, u32[]{:S(2)}) %collective-permute-start.32) | collective-permute-done | bytes 213024 | tf_op jit(solution)/shard_map/ppermute | solution.py:53
  138.8 4.0 %collective-permute-done.37.theirs = bf16[2,64,1664]{2,1,0:T(8,128)(2,1)S(1)} collective-permute-done((bf16[2,64,1664]{2,1,0:T(8,128)(2,1)S(1)}, bf16[2,64,1664]{2,1,0:T(8,128)(2,1)S(1)}, u32[]{:S(2)}, u32[]{:S(2)}) %collective-permute-start.37) | collective-permute-done | bytes 426016 | tf_op jit(solution)/shard_map/ppermute | solution.py:53
  143.4 8.2 %collective-permute-done.36.theirs = bf16[2,64,1664]{2,1,0:T(8,128)(2,1)S(1)} collective-permute-done((bf16[2,64,1664]{2,1,0:T(8,128)(2,1)S(1)}, bf16[2,64,1664]{2,1,0:T(8,128)(2,1)S(1)}, u32[]{:S(2)}, u32[]{:S(2)}) %collective-permute-start.36) | collective-permute-done | bytes 426016 | tf_op jit(solution)/shard_map/ppermute | solution.py:53
  152.8 3.3 %collective-permute-done.35.theirs = bf16[2,64,1664]{2,1,0:T(8,128)(2,1)S(1)} collective-permute-done((bf16[2,64,1664]{2,1,0:T(8,128)(2,1)S(1)}, bf16[2,64,1664]{2,1,0:T(8,128)(2,1)S(1)}, u32[]{:S(2)}, u32[]{:S(2)}) %collective-permute-start.35) | collective-permute-done | bytes 426016 | tf_op jit(solution)/shard_map/ppermute | solution.py:53
  156.3 1.5 collective-permute-start.38
  163.5 1.8 collective-permute-done.42.refs_0_
  165.3 1.4 down.13
  169.2 7.9 %collective-permute-done.38.refs_0_ = bf16[2,128,1664]{2,1,0:T(8,128)(2,1)S(1)} collective-permute-done((bf16[2,128,1664]{2,1,0:T(8,128)(2,1)S(1)}, bf16[2,128,1664]{2,1,0:T(8,128)(2,1)S(1)}, u32[]{:S(2)}, u32[]{:S(2)}) %collective-permute-start.38) | collective-permute-done | bytes 852000 | tf_op jit(solution)/shard_map/ppermute | solution.py:53
  177.1 1.4 down.15
  178.5 2.5 %collective-permute-start.44 = (bf16[2,128,1024]{2,1,0:T(8,128)(2,1)S(1)}, bf16[2,128,1024]{2,1,0:T(8,128)(2,1)S(1)}, u32[]{:S(2)}, u32[]{:S(2)}) collective-permute-start(bf16[2,128,1024]{2,1,0:T(8,128)(2,1)S(1)} %get-tuple-element.99), channel_id=1, source_target_pairs={{0,16},{16,0},{32,48},{48,32},{64,80},{80,64},{96,112},{112,96},{1... | collective-permute-start | bytes 1572872 | tf_op jit(solution)/shard_map/ppermute | solution.py:57
  181.1 1.4 collective-permute-done.44
  182.8 1.5 collective-permute-start.45
  185.3 1.9 collective-permute-start.48
  187.3 4.7 %collective-permute-done.45 = bf16[128,1024]{1,0:T(8,128)(2,1)S(1)} collective-permute-done((bf16[128,1024]{1,0:T(8,128)(2,1)S(1)}, bf16[128,1024]{1,0:T(8,128)(2,1)S(1)}, u32[]{:S(2)}, u32[]{:S(2)}) %collective-permute-start.45) | collective-permute-done | bytes 262176 | tf_op jit(solution)/shard_map/ppermute | solution.py:61
  191.9 6.3 %collective-permute-done.47 = bf16[128,1024]{1,0:T(8,128)(2,1)S(1)} collective-permute-done((bf16[128,1024]{1,0:T(8,128)(2,1)S(1)}, bf16[128,1024]{1,0:T(8,128)(2,1)S(1)}, u32[]{:S(2)}, u32[]{:S(2)}) %collective-permute-start.47) | collective-permute-done | bytes 262176 | tf_op jit(solution)/shard_map/ppermute | solution.py:61
  (101 shorter events, 33.8 us)
Async XLA Ops:
  0.0 12.0 %collective-permute-start = (bf16[128,1024]{1,0:T(8,128)(2,1)}, bf16[128,1024]{1,0:T(8,128)(2,1)S(1)}, u32[]{:S(2)}, u32[]{:S(2)}) collective-permute-start(bf16[128,1024]{1,0:T(8,128)(2,1)} %param.4), channel_id=1, source_target_pairs={{0,16},{16,0},{32,48},{48,32},{64,80},{80,64},{96,112},{112,96},{1... | collective-permute-start | bytes 786440 | tf_op jit(solution)/shard_map/ppermute | solution.py:57
  1.4 12.1 %collective-permute-start.8 = (bf16[128,1024]{1,0:T(8,128)(2,1)}, bf16[128,1024]{1,0:T(8,128)(2,1)S(1)}, u32[]{:S(2)}, u32[]{:S(2)}) collective-permute-start(bf16[128,1024]{1,0:T(8,128)(2,1)} %param.4), channel_id=1, source_target_pairs={{0,32},{16,48},{32,64},{48,80},{64,96},{80,112},{96,0},{112,16},{1... | collective-permute-start | bytes 786440 | tf_op jit(solution)/shard_map/ppermute | solution.py:61
  3.1 11.0 %collective-permute-start.7 = (bf16[128,1024]{1,0:T(8,128)(2,1)}, bf16[128,1024]{1,0:T(8,128)(2,1)S(1)}, u32[]{:S(2)}, u32[]{:S(2)}) collective-permute-start(bf16[128,1024]{1,0:T(8,128)(2,1)} %param.4), channel_id=1, source_target_pairs={{0,96},{16,112},{32,0},{48,16},{64,32},{80,48},{96,64},{112,80},{1... | collective-permute-start | bytes 786440 | tf_op jit(solution)/shard_map/ppermute | solution.py:61
  8.3 26.5 %collective-permute-start.3 = (bf16[1024,896]{1,0:T(8,128)(2,1)S(1)}, bf16[1024,896]{1,0:T(8,128)(2,1)S(1)}, u32[]{:S(2)}, u32[]{:S(2)}) collective-permute-start(bf16[1024,896]{1,0:T(8,128)(2,1)S(1)} %get-tuple-element.53.refs_0_), channel_id=1, source_target_pairs={{0,16},{16,0},{32,48},{48,32},{64,80},{80,64},{96,112},{112,96},{1... | collective-permute-start | bytes 5505032 | tf_op jit(solution)/shard_map/ppermute | solution.py:57
  11.8 23.1 %collective-permute-start.5 = (bf16[1024,896]{1,0:T(8,128)(2,1)S(1)}, bf16[1024,896]{1,0:T(8,128)(2,1)S(1)}, u32[]{:S(2)}, u32[]{:S(2)}) collective-permute-start(bf16[1024,896]{1,0:T(8,128)(2,1)S(1)} %get-tuple-element.55.refs_0_), channel_id=1, source_target_pairs={{0,16},{16,0},{32,48},{48,32},{64,80},{80,64},{96,112},{112,96},{1... | collective-permute-start | bytes 5505032 | tf_op jit(solution)/shard_map/ppermute | solution.py:57
  12.0 9.0 %collective-permute-start.1 = (bf16[1,128,1024]{2,1,0:T(8,128)(2,1)S(1)}, bf16[1,128,1024]{2,1,0:T(8,128)(2,1)S(1)}, u32[]{:S(2)}, u32[]{:S(2)}) collective-permute-start(bf16[1,128,1024]{2,1,0:T(8,128)(2,1)S(1)} %bitcast.20), channel_id=1, source_target_pairs={{0,64},{16,80},{32,96},{48,112},{64,0},{80,16},{96,32},{112,48},{1... | collective-permute-start | bytes 786440 | tf_op jit(solution)/shard_map/ppermute | solution.py:61
  13.5 19.2 %collective-permute-start.4 = (bf16[1024,768]{1,0:T(8,128)(2,1)S(1)}, bf16[1024,768]{1,0:T(8,128)(2,1)S(1)}, u32[]{:S(2)}, u32[]{:S(2)}) collective-permute-start(bf16[1024,768]{1,0:T(8,128)(2,1)S(1)} %get-tuple-element.54), channel_id=1, source_target_pairs={{0,16},{16,0},{32,48},{48,32},{64,80},{80,64},{96,112},{112,96},{1... | collective-permute-start | bytes 4718600 | tf_op jit(solution)/shard_map/ppermute | solution.py:57
  14.2 20.6 %collective-permute-start.6 = (bf16[1024,768]{1,0:T(8,128)(2,1)S(1)}, bf16[1024,768]{1,0:T(8,128)(2,1)S(1)}, u32[]{:S(2)}, u32[]{:S(2)}) collective-permute-start(bf16[1024,768]{1,0:T(8,128)(2,1)S(1)} %get-tuple-element.56), channel_id=1, source_target_pairs={{0,16},{16,0},{32,48},{48,32},{64,80},{80,64},{96,112},{112,96},{1... | collective-permute-start | bytes 4718600 | tf_op jit(solution)/shard_map/ppermute | solution.py:57
  23.4 4.1 %collective-permute-start.9 = (bf16[2,128,1024]{2,1,0:T(8,128)(2,1)S(1)}, bf16[2,128,1024]{2,1,0:T(8,128)(2,1)S(1)}, u32[]{:S(2)}, u32[]{:S(2)}) collective-permute-start(bf16[2,128,1024]{2,1,0:T(8,128)(2,1)S(1)} %stack.1.refs_8_.refs_0_), channel_id=1, source_target_pairs={{0,16},{16,0},{32,48},{48,32},{64,80},{80,64},{96,112},{112,96},{1... | collective-permute-start | bytes 1572872 | tf_op jit(solution)/shard_map/ppermute | solution.py:57
  27.5 21.0 %collective-permute-start.12 = (bf16[2,2,128,1664]{3,2,1,0:T(8,128)(2,1)S(1)}, bf16[2,2,128,1664]{3,2,1,0:T(8,128)(2,1)S(1)}, u32[]{:S(2)}, u32[]{:S(2)}) collective-permute-start(bf16[2,2,128,1664]{3,2,1,0:T(8,128)(2,1)S(1)} %get-tuple-element.61.refs_6_), channel_id=1, source_target_pairs={{0,4},{1,5},{2,6},{3,7},{4,0},{5,1},{6,2},{7,3},{8,12},{9,13},{10,... | collective-permute-start | bytes 5111816 | tf_op jit(solution)/shard_map/ppermute | solution.py:53
  32.7 22.4 %collective-permute-start.11 = (bf16[2,2,128,1664]{3,2,1,0:T(8,128)(2,1)S(1)}, bf16[2,2,128,1664]{3,2,1,0:T(8,128)(2,1)S(1)}, u32[]{:S(2)}, u32[]{:S(2)}) collective-permute-start(bf16[2,2,128,1664]{3,2,1,0:T(8,128)(2,1)S(1)} %get-tuple-element.62.refs_8_), channel_id=1, source_target_pairs={{0,12},{1,13},{2,14},{3,15},{4,8},{5,9},{6,10},{7,11},{8,4},{9,5},... | collective-permute-start | bytes 5111816 | tf_op jit(solution)/shard_map/ppermute | solution.py:53
  42.3 31.0 %collective-permute-start.14 = (bf16[2,2,128,1664]{3,2,1,0:T(8,128)(2,1)S(1)}, bf16[2,2,128,1664]{3,2,1,0:T(8,128)(2,1)S(1)}, u32[]{:S(2)}, u32[]{:S(2)}) collective-permute-start(bf16[2,2,128,1664]{3,2,1,0:T(8,128)(2,1)S(1)} %get-tuple-element.67.refs_0_), channel_id=1, source_target_pairs={{0,12},{1,13},{2,14},{3,15},{4,8},{5,9},{6,10},{7,11},{8,4},{9,5},... | collective-permute-start | bytes 5111816 | tf_op jit(solution)/shard_map/ppermute | solution.py:53
  43.2 35.6 %collective-permute-start.10 = (bf16[2,2,128,1664]{3,2,1,0:T(8,128)(2,1)S(1)}, bf16[2,2,128,1664]{3,2,1,0:T(8,128)(2,1)S(1)}, u32[]{:S(2)}, u32[]{:S(2)}) collective-permute-start(bf16[2,2,128,1664]{3,2,1,0:T(8,128)(2,1)S(1)} %get-tuple-element.64.refs_6_), channel_id=1, source_target_pairs={{0,4},{1,5},{2,6},{3,7},{4,0},{5,1},{6,2},{7,3},{8,12},{9,13},{10,... | collective-permute-start | bytes 5111816 | tf_op jit(solution)/shard_map/ppermute | solution.py:53
  55.5 20.5 %collective-permute-start.13 = (bf16[2,2,64,1664]{3,2,1,0:T(8,128)(2,1)S(1)}, bf16[2,2,64,1664]{3,2,1,0:T(8,128)(2,1)S(1)}, u32[]{:S(2)}, u32[]{:S(2)}) collective-permute-start(bf16[2,2,64,1664]{3,2,1,0:T(8,128)(2,1)S(1)} %get-tuple-element.70.refs_0_), channel_id=1, source_target_pairs={{0,4},{1,5},{2,6},{3,7},{4,0},{5,1},{6,2},{7,3},{8,12},{9,13},{10,... | collective-permute-start | bytes 2555912 | tf_op jit(solution)/shard_map/ppermute | solution.py:53
  55.6 27.7 %collective-permute-start.17 = (bf16[2,2,64,1664]{3,2,1,0:T(8,128)(2,1)S(1)}, bf16[2,2,64,1664]{3,2,1,0:T(8,128)(2,1)S(1)}, u32[]{:S(2)}, u32[]{:S(2)}) collective-permute-start(bf16[2,2,64,1664]{3,2,1,0:T(8,128)(2,1)S(1)} %get-tuple-element.68.refs_0_), channel_id=1, source_target_pairs={{0,12},{1,13},{2,14},{3,15},{4,8},{5,9},{6,10},{7,11},{8,4},{9,5},... | collective-permute-start | bytes 2555912 | tf_op jit(solution)/shard_map/ppermute | solution.py:53
  73.8 15.8 %collective-permute-start.20 = (bf16[2,2,64,1664]{3,2,1,0:T(8,128)(2,1)S(1)}, bf16[2,2,64,1664]{3,2,1,0:T(8,128)(2,1)S(1)}, u32[]{:S(2)}, u32[]{:S(2)}) collective-permute-start(bf16[2,2,64,1664]{3,2,1,0:T(8,128)(2,1)S(1)} %get-tuple-element.72.refs_0_), channel_id=1, source_target_pairs={{0,4},{1,5},{2,6},{3,7},{4,0},{5,1},{6,2},{7,3},{8,12},{9,13},{10,... | collective-permute-start | bytes 2555912 | tf_op jit(solution)/shard_map/ppermute | solution.py:53
  76.2 13.2 %collective-permute-start.16 = (bf16[2,2,32,1664]{3,2,1,0:T(8,128)(2,1)S(1)}, bf16[2,2,32,1664]{3,2,1,0:T(8,128)(2,1)S(1)}, u32[]{:S(2)}, u32[]{:S(2)}) collective-permute-start(bf16[2,2,32,1664]{3,2,1,0:T(8,128)(2,1)S(1)} %get-tuple-element.73.refs_0_), channel_id=1, source_target_pairs={{0,3},{1,2},{2,1},{3,0},{4,7},{5,6},{6,5},{7,4},{8,11},{9,10},{10,... | collective-permute-start | bytes 1277960 | tf_op jit(solution)/shard_map/ppermute | solution.py:53
  79.1 17.1 %collective-permute-start.15 = (bf16[2,2,64,1664]{3,2,1,0:T(8,128)(2,1)S(1)}, bf16[2,2,64,1664]{3,2,1,0:T(8,128)(2,1)S(1)}, u32[]{:S(2)}, u32[]{:S(2)}) collective-permute-start(bf16[2,2,64,1664]{3,2,1,0:T(8,128)(2,1)S(1)} %get-tuple-element.75.refs_0_), channel_id=1, source_target_pairs={{0,12},{1,13},{2,14},{3,15},{4,8},{5,9},{6,10},{7,11},{8,4},{9,5},... | collective-permute-start | bytes 2555912 | tf_op jit(solution)/shard_map/ppermute | solution.py:53
  83.5 8.7 %collective-permute-start.19 = (bf16[2,2,32,1664]{3,2,1,0:T(8,128)(2,1)S(1)}, bf16[2,2,32,1664]{3,2,1,0:T(8,128)(2,1)S(1)}, u32[]{:S(2)}, u32[]{:S(2)}) collective-permute-start(bf16[2,2,32,1664]{3,2,1,0:T(8,128)(2,1)S(1)} %get-tuple-element.78.refs_0_), channel_id=1, source_target_pairs={{0,1},{1,0},{2,3},{3,2},{4,5},{5,4},{6,7},{7,6},{8,9},{9,8},{10,11... | collective-permute-start | bytes 1277960 | tf_op jit(solution)/shard_map/ppermute | solution.py:53
  89.5 5.1 %collective-permute-start.18 = (bf16[2,2,16,1664]{3,2,1,0:T(8,128)(2,1)S(1)}, bf16[2,2,16,1664]{3,2,1,0:T(8,128)(2,1)S(1)}, u32[]{:S(2)}, u32[]{:S(2)}) collective-permute-start(bf16[2,2,16,1664]{3,2,1,0:T(8,128)(2,1)S(1)} %get-tuple-element.80.refs_0_), channel_id=1, source_target_pairs={{0,1},{1,0},{2,3},{3,2},{4,5},{5,4},{6,7},{7,6},{8,9},{9,8},{10,11... | collective-permute-start | bytes 638984 | tf_op jit(solution)/shard_map/ppermute | solution.py:53
  89.8 11.8 %collective-permute-start.23 = (bf16[2,2,32,1664]{3,2,1,0:T(8,128)(2,1)S(1)}, bf16[2,2,32,1664]{3,2,1,0:T(8,128)(2,1)S(1)}, u32[]{:S(2)}, u32[]{:S(2)}) collective-permute-start(bf16[2,2,32,1664]{3,2,1,0:T(8,128)(2,1)S(1)} %get-tuple-element.83.refs_0_), channel_id=1, source_target_pairs={{0,3},{1,2},{2,1},{3,0},{4,7},{5,6},{6,5},{7,4},{8,11},{9,10},{10,... | collective-permute-start | bytes 1277960 | tf_op jit(solution)/shard_map/ppermute | solution.py:53
  92.3 16.6 %collective-permute-start.27 = (bf16[2,2,16,1664]{3,2,1,0:T(8,128)(2,1)S(1)}, bf16[2,2,16,1664]{3,2,1,0:T(8,128)(2,1)S(1)}, u32[]{:S(2)}, u32[]{:S(2)}) collective-permute-start(bf16[2,2,16,1664]{3,2,1,0:T(8,128)(2,1)S(1)} %get-tuple-element.84.refs_0_), channel_id=1, source_target_pairs={{0,3},{1,2},{2,1},{3,0},{4,7},{5,6},{6,5},{7,4},{8,11},{9,10},{10,... | collective-permute-start | bytes 638984 | tf_op jit(solution)/shard_map/ppermute | solution.py:53
  94.7 7.1 %collective-permute-start.22 = (bf16[2,16,1664]{2,1,0:T(8,128)(2,1)S(1)}, bf16[2,16,1664]{2,1,0:T(8,128)(2,1)S(1)}, u32[]{:S(2)}, u32[]{:S(2)}) collective-permute-start(bf16[2,16,1664]{2,1,0:T(8,128)(2,1)S(1)} %hidden.4.refs_0_.mine), channel_id=1, source_target_pairs={{0,1},{1,0},{2,3},{3,2},{4,5},{5,4},{6,7},{7,6},{8,9},{9,8},{10,11... | collective-permute-start | bytes 319496 | tf_op jit(solution)/shard_map/ppermute | solution.py:53
  96.4 7.3 %collective-permute-start.21 = (bf16[2,2,32,1664]{3,2,1,0:T(8,128)(2,1)S(1)}, bf16[2,2,32,1664]{3,2,1,0:T(8,128)(2,1)S(1)}, u32[]{:S(2)}, u32[]{:S(2)}) collective-permute-start(bf16[2,2,32,1664]{3,2,1,0:T(8,128)(2,1)S(1)} %get-tuple-element.86.refs_0_), channel_id=1, source_target_pairs={{0,1},{1,0},{2,3},{3,2},{4,5},{5,4},{6,7},{7,6},{8,9},{9,8},{10,11... | collective-permute-start | bytes 1277960 | tf_op jit(solution)/shard_map/ppermute | solution.py:53
  101.7 5.1 %collective-permute-start.25 = (bf16[2,2,16,1664]{3,2,1,0:T(8,128)(2,1)S(1)}, bf16[2,2,16,1664]{3,2,1,0:T(8,128)(2,1)S(1)}, u32[]{:S(2)}, u32[]{:S(2)}) collective-permute-start(bf16[2,2,16,1664]{3,2,1,0:T(8,128)(2,1)S(1)} %get-tuple-element.88.refs_0_), channel_id=1, source_target_pairs={{0,1},{1,0},{2,3},{3,2},{4,5},{5,4},{6,7},{7,6},{8,9},{9,8},{10,11... | collective-permute-start | bytes 638984 | tf_op jit(solution)/shard_map/ppermute | solution.py:53
  101.8 6.3 %collective-permute-start.28 = (bf16[2,32,1664]{2,1,0:T(8,128)(2,1)S(1)}, bf16[2,32,1664]{2,1,0:T(8,128)(2,1)S(1)}, u32[]{:S(2)}, u32[]{:S(2)}) collective-permute-start(bf16[2,32,1664]{2,1,0:T(8,128)(2,1)S(1)} %join.12.refs_0_.mine), channel_id=1, source_target_pairs={{0,3},{1,2},{2,1},{3,0},{4,7},{5,6},{6,5},{7,4},{8,11},{9,10},{10,... | collective-permute-start | bytes 638984 | tf_op jit(solution)/shard_map/ppermute | solution.py:53
  103.8 8.6 %collective-permute-start.24 = (bf16[2,2,16,1664]{3,2,1,0:T(8,128)(2,1)S(1)}, bf16[2,2,16,1664]{3,2,1,0:T(8,128)(2,1)S(1)}, u32[]{:S(2)}, u32[]{:S(2)}) collective-permute-start(bf16[2,2,16,1664]{3,2,1,0:T(8,128)(2,1)S(1)} %get-tuple-element.90.refs_0_), channel_id=1, source_target_pairs={{0,3},{1,2},{2,1},{3,0},{4,7},{5,6},{6,5},{7,4},{8,11},{9,10},{10,... | collective-permute-start | bytes 638984 | tf_op jit(solution)/shard_map/ppermute | solution.py:53
  106.8 4.1 %collective-permute-start.26 = (bf16[2,16,1664]{2,1,0:T(8,128)(2,1)S(1)}, bf16[2,16,1664]{2,1,0:T(8,128)(2,1)S(1)}, u32[]{:S(2)}, u32[]{:S(2)}) collective-permute-start(bf16[2,16,1664]{2,1,0:T(8,128)(2,1)S(1)} %hidden.5.refs_0_.mine), channel_id=1, source_target_pairs={{0,1},{1,0},{2,3},{3,2},{4,5},{5,4},{6,7},{7,6},{8,9},{9,8},{10,11... | collective-permute-start | bytes 319496 | tf_op jit(solution)/shard_map/ppermute | solution.py:53
  108.1 7.4 %collective-permute-start.31 = (bf16[2,64,1664]{2,1,0:T(8,128)(2,1)S(1)}, bf16[2,64,1664]{2,1,0:T(8,128)(2,1)S(1)}, u32[]{:S(2)}, u32[]{:S(2)}) collective-permute-start(bf16[2,64,1664]{2,1,0:T(8,128)(2,1)S(1)} %join.13.refs_0_.mine), channel_id=1, source_target_pairs={{0,4},{1,5},{2,6},{3,7},{4,0},{5,1},{6,2},{7,3},{8,12},{9,13},{10,... | collective-permute-start | bytes 1277960 | tf_op jit(solution)/shard_map/ppermute | solution.py:53
  109.0 6.5 %collective-permute-start.30 = (bf16[2,16,1664]{2,1,0:T(8,128)(2,1)S(1)}, bf16[2,16,1664]{2,1,0:T(8,128)(2,1)S(1)}, u32[]{:S(2)}, u32[]{:S(2)}) collective-permute-start(bf16[2,16,1664]{2,1,0:T(8,128)(2,1)S(1)} %hidden.6.refs_0_.mine), channel_id=1, source_target_pairs={{0,3},{1,2},{2,1},{3,0},{4,7},{5,6},{6,5},{7,4},{8,11},{9,10},{10,... | collective-permute-start | bytes 319496 | tf_op jit(solution)/shard_map/ppermute | solution.py:53
  110.9 7.4 %collective-permute-start.34 = (bf16[2,32,1664]{2,1,0:T(8,128)(2,1)S(1)}, bf16[2,32,1664]{2,1,0:T(8,128)(2,1)S(1)}, u32[]{:S(2)}, u32[]{:S(2)}) collective-permute-start(bf16[2,32,1664]{2,1,0:T(8,128)(2,1)S(1)} %join.14.refs_0_.mine), channel_id=1, source_target_pairs={{0,3},{1,2},{2,1},{3,0},{4,7},{5,6},{6,5},{7,4},{8,11},{9,10},{10,... | collective-permute-start | bytes 638984 | tf_op jit(solution)/shard_map/ppermute | solution.py:53
  112.5 5.8 %collective-permute-start.29 = (bf16[2,16,1664]{2,1,0:T(8,128)(2,1)S(1)}, bf16[2,16,1664]{2,1,0:T(8,128)(2,1)S(1)}, u32[]{:S(2)}, u32[]{:S(2)}) collective-permute-start(bf16[2,16,1664]{2,1,0:T(8,128)(2,1)S(1)} %hidden.7.refs_0_.mine), channel_id=1, source_target_pairs={{0,3},{1,2},{2,1},{3,0},{4,7},{5,6},{6,5},{7,4},{8,11},{9,10},{10,... | collective-permute-start | bytes 319496 | tf_op jit(solution)/shard_map/ppermute | solution.py:53
  115.6 7.4 %collective-permute-start.33 = (bf16[2,32,1664]{2,1,0:T(8,128)(2,1)S(1)}, bf16[2,32,1664]{2,1,0:T(8,128)(2,1)S(1)}, u32[]{:S(2)}, u32[]{:S(2)}) collective-permute-start(bf16[2,32,1664]{2,1,0:T(8,128)(2,1)S(1)} %join.16.refs_0_.mine), channel_id=1, source_target_pairs={{0,1},{1,0},{2,3},{3,2},{4,5},{5,4},{6,7},{7,6},{8,9},{9,8},{10,11... | collective-permute-start | bytes 638984 | tf_op jit(solution)/shard_map/ppermute | solution.py:53
  126.1 30.2 %collective-permute-start.40 = (bf16[1664,512]{1,0:T(8,128)(2,1)S(1)}, bf16[1664,512]{1,0:T(8,128)(2,1)S(1)}, u32[]{:S(2)}, u32[]{:S(2)}) collective-permute-start(bf16[1664,512]{1,0:T(8,128)(2,1)S(1)} %get-tuple-element.94), channel_id=1, source_target_pairs={{0,16},{16,0},{32,48},{48,32},{64,80},{80,64},{96,112},{112,96},{1... | collective-permute-start | bytes 5111816 | tf_op jit(solution)/shard_map/ppermute | solution.py:57
  133.1 24.7 %collective-permute-start.39 = (bf16[1664,512]{1,0:T(8,128)(2,1)S(1)}, bf16[1664,512]{1,0:T(8,128)(2,1)S(1)}, u32[]{:S(2)}, u32[]{:S(2)}) collective-permute-start(bf16[1664,512]{1,0:T(8,128)(2,1)S(1)} %get-tuple-element.93.refs_0_), channel_id=1, source_target_pairs={{0,16},{16,0},{32,48},{48,32},{64,80},{80,64},{96,112},{112,96},{1... | collective-permute-start | bytes 5111816 | tf_op jit(solution)/shard_map/ppermute | solution.py:57
  133.2 5.3 %collective-permute-start.32 = (bf16[2,32,1664]{2,1,0:T(8,128)(2,1)S(1)}, bf16[2,32,1664]{2,1,0:T(8,128)(2,1)S(1)}, u32[]{:S(2)}, u32[]{:S(2)}) collective-permute-start(bf16[2,32,1664]{2,1,0:T(8,128)(2,1)S(1)} %join.17.refs_0_.mine), channel_id=1, source_target_pairs={{0,1},{1,0},{2,3},{3,2},{4,5},{5,4},{6,7},{7,6},{8,9},{9,8},{10,11... | collective-permute-start | bytes 638984 | tf_op jit(solution)/shard_map/ppermute | solution.py:53
  133.2 9.6 %collective-permute-start.37 = (bf16[2,64,1664]{2,1,0:T(8,128)(2,1)S(1)}, bf16[2,64,1664]{2,1,0:T(8,128)(2,1)S(1)}, u32[]{:S(2)}, u32[]{:S(2)}) collective-permute-start(bf16[2,64,1664]{2,1,0:T(8,128)(2,1)S(1)} %join.18.refs_0_.mine), channel_id=1, source_target_pairs={{0,4},{1,5},{2,6},{3,7},{4,0},{5,1},{6,2},{7,3},{8,12},{9,13},{10,... | collective-permute-start | bytes 1277960 | tf_op jit(solution)/shard_map/ppermute | solution.py:53
  134.0 28.3 %collective-permute-start.43 = (bf16[2,128,1664]{2,1,0:T(8,128)(2,1)S(1)}, bf16[2,128,1664]{2,1,0:T(8,128)(2,1)S(1)}, u32[]{:S(2)}, u32[]{:S(2)}) collective-permute-start(bf16[2,128,1664]{2,1,0:T(8,128)(2,1)S(1)} %join.15.refs_0_), channel_id=1, source_target_pairs={{0,12},{1,13},{2,14},{3,15},{4,8},{5,9},{6,10},{7,11},{8,4},{9,5},... | collective-permute-start | bytes 2555912 | tf_op jit(solution)/shard_map/ppermute | solution.py:53
  138.5 13.1 %collective-permute-start.36 = (bf16[2,64,1664]{2,1,0:T(8,128)(2,1)S(1)}, bf16[2,64,1664]{2,1,0:T(8,128)(2,1)S(1)}, u32[]{:S(2)}, u32[]{:S(2)}) collective-permute-start(bf16[2,64,1664]{2,1,0:T(8,128)(2,1)S(1)} %join.19.refs_0_.mine), channel_id=1, source_target_pairs={{0,12},{1,13},{2,14},{3,15},{4,8},{5,9},{6,10},{7,11},{8,4},{9,5},... | collective-permute-start | bytes 1277960 | tf_op jit(solution)/shard_map/ppermute | solution.py:53
  142.8 13.4 %collective-permute-start.35 = (bf16[2,64,1664]{2,1,0:T(8,128)(2,1)S(1)}, bf16[2,64,1664]{2,1,0:T(8,128)(2,1)S(1)}, u32[]{:S(2)}, u32[]{:S(2)}) collective-permute-start(bf16[2,64,1664]{2,1,0:T(8,128)(2,1)S(1)} %join.20.refs_0_.mine), channel_id=1, source_target_pairs={{0,12},{1,13},{2,14},{3,15},{4,8},{5,9},{6,10},{7,11},{8,4},{9,5},... | collective-permute-start | bytes 1277960 | tf_op jit(solution)/shard_map/ppermute | solution.py:53
  151.6 13.7 %collective-permute-start.42 = (bf16[2,128,1664]{2,1,0:T(8,128)(2,1)S(1)}, bf16[2,128,1664]{2,1,0:T(8,128)(2,1)S(1)}, u32[]{:S(2)}, u32[]{:S(2)}) collective-permute-start(bf16[2,128,1664]{2,1,0:T(8,128)(2,1)S(1)} %join.21.refs_0_), channel_id=1, source_target_pairs={{0,12},{1,13},{2,14},{3,15},{4,8},{5,9},{6,10},{7,11},{8,4},{9,5},... | collective-permute-start | bytes 2555912 | tf_op jit(solution)/shard_map/ppermute | solution.py:53
  156.2 11.8 %collective-permute-start.41 = (bf16[2,128,1664]{2,1,0:T(8,128)(2,1)S(1)}, bf16[2,128,1664]{2,1,0:T(8,128)(2,1)S(1)}, u32[]{:S(2)}, u32[]{:S(2)}) collective-permute-start(bf16[2,128,1664]{2,1,0:T(8,128)(2,1)S(1)} %join.22.refs_0_), channel_id=1, source_target_pairs={{0,4},{1,5},{2,6},{3,7},{4,0},{5,1},{6,2},{7,3},{8,12},{9,13},{10,... | collective-permute-start | bytes 2555912 | tf_op jit(solution)/shard_map/ppermute | solution.py:53
  156.3 20.9 %collective-permute-start.38 = (bf16[2,128,1664]{2,1,0:T(8,128)(2,1)S(1)}, bf16[2,128,1664]{2,1,0:T(8,128)(2,1)S(1)}, u32[]{:S(2)}, u32[]{:S(2)}) collective-permute-start(bf16[2,128,1664]{2,1,0:T(8,128)(2,1)S(1)} %join.23.refs_0_.refs_3_), channel_id=1, source_target_pairs={{0,4},{1,5},{2,6},{3,7},{4,0},{5,1},{6,2},{7,3},{8,12},{9,13},{10,... | collective-permute-start | bytes 2555912 | tf_op jit(solution)/shard_map/ppermute | solution.py:53
  178.5 4.0 %collective-permute-start.44 = (bf16[2,128,1024]{2,1,0:T(8,128)(2,1)S(1)}, bf16[2,128,1024]{2,1,0:T(8,128)(2,1)S(1)}, u32[]{:S(2)}, u32[]{:S(2)}) collective-permute-start(bf16[2,128,1024]{2,1,0:T(8,128)(2,1)S(1)} %get-tuple-element.99), channel_id=1, source_target_pairs={{0,16},{16,0},{32,48},{48,32},{64,80},{80,64},{96,112},{112,96},{1... | collective-permute-start | bytes 1572872 | tf_op jit(solution)/shard_map/ppermute | solution.py:57
  181.0 3.3 %collective-permute-start.46 = (bf16[2,128,1024]{2,1,0:T(8,128)(2,1)S(1)}, bf16[2,128,1024]{2,1,0:T(8,128)(2,1)S(1)}, u32[]{:S(2)}, u32[]{:S(2)}) collective-permute-start(bf16[2,128,1024]{2,1,0:T(8,128)(2,1)S(1)} %get-tuple-element.97.refs_4_), channel_id=1, source_target_pairs={{0,16},{16,0},{32,48},{48,32},{64,80},{80,64},{96,112},{112,96},{1... | collective-permute-start | bytes 1572872 | tf_op jit(solution)/shard_map/ppermute | solution.py:57
  182.8 9.1 %collective-permute-start.45 = (bf16[128,1024]{1,0:T(8,128)(2,1)S(1)}, bf16[128,1024]{1,0:T(8,128)(2,1)S(1)}, u32[]{:S(2)}, u32[]{:S(2)}) collective-permute-start(bf16[128,1024]{1,0:T(8,128)(2,1)S(1)} %fusion.4), channel_id=1, source_target_pairs={{0,64},{16,80},{32,96},{48,112},{64,0},{80,16},{96,32},{112,48},{1... | collective-permute-start | bytes 786440 | tf_op jit(solution)/shard_map/ppermute | solution.py:61
  184.5 13.7 %collective-permute-start.47 = (bf16[128,1024]{1,0:T(8,128)(2,1)S(1)}, bf16[128,1024]{1,0:T(8,128)(2,1)S(1)}, u32[]{:S(2)}, u32[]{:S(2)}) collective-permute-start(bf16[128,1024]{1,0:T(8,128)(2,1)S(1)} %get-tuple-element.101), channel_id=1, source_target_pairs={{0,32},{16,48},{32,64},{48,80},{64,96},{80,112},{96,0},{112,16},{1... | collective-permute-start | bytes 786440 | tf_op jit(solution)/shard_map/ppermute | solution.py:61
  185.3 12.9 %collective-permute-start.48 = (bf16[128,1024]{1,0:T(8,128)(2,1)S(1)}, bf16[128,1024]{1,0:T(8,128)(2,1)S(1)}, u32[]{:S(2)}, u32[]{:S(2)}) collective-permute-start(bf16[128,1024]{1,0:T(8,128)(2,1)S(1)} %get-tuple-element.102), channel_id=1, source_target_pairs={{0,96},{16,112},{32,0},{48,16},{64,32},{80,48},{96,64},{112,80},{1... | collective-permute-start | bytes 786440 | tf_op jit(solution)/shard_map/ppermute | solution.py:61
  (2 other events, 12.0 us)

commit v4 on v3

--- a/solution.py
+++ b/solution.py
@@ -11,8 +11,6 @@
 F32 = jnp.float32
 
 TIMES = {
-    "project": 5.0,
-    "cut": 3.0,
     "down": 2.5,
     "halves": 2.0,
     "hidden": 2.0,
@@ -77,7 +75,7 @@
     return 15 ^ own
 
 
-def kernel(body, name, args, shapes, after, scratch=(), limit=2, specs=None):
+def kernel(body, name, args, shapes, after, scratch=(), limit=2, specs=None, time=None):
     specs = specs or [VMEM] * len(args)
     return pl.pallas_call(
         body,
@@ -87,47 +85,68 @@
         scratch_shapes=list(scratch),
         compiler_params=pltpu.CompilerParams(vmem_limit_bytes=limit << 20),
         cost_estimate=pl.CostEstimate(
-            flops=int(TIMES[name] * 1.15e9), bytes_accessed=0, transcendentals=0
+            flops=int((time or TIMES[name]) * 1.15e9), bytes_accessed=0, transcendentals=0
         ),
         name=name,
     )(*args, *after)
 
 
-def cut_body(axis, pieces, source, *refs):
-    outs, sem = refs[-1 - 2 * len(pieces) : -1], refs[-1]
+def cut_body(axis, pieces, parts, count, *refs):
+    sources, outs, sem = refs[:count], refs[-1 - count * len(parts) * len(pieces) : -1], refs[-1]
     copies = []
-    for which in range(2):
-        core = core_index()
-        begin = (core if which else 1 - core) * HALF
-        at = 0
-        for i, size in enumerate(pieces):
-            if axis == 1:
-                place = source.at[:, pl.ds(pl.multiple_of(begin + at, 128), size)]
-            else:
-                place = source.at[pl.ds(pl.multiple_of(begin, 128), HALF), pl.ds(at, size)]
-            at += size
-            n = which * len(pieces) + i
-            copies.append(pltpu.make_async_copy(place, outs[n], sem.at[n]))
+    core = core_index()
+    for source in sources:
+        for part in parts:
+            begin = (core if part == "own" else 1 - core) * HALF
+            at = 0
+            for size in pieces:
+                if axis == 1:
+                    place = source.at[:, pl.ds(pl.multiple_of(begin + at, 128), size)]
+                else:
+                    place = source.at[pl.ds(pl.multiple_of(begin, 128), HALF), pl.ds(at, size)]
+                at += size
+                n = len(copies)
+                copies.append(pltpu.make_async_copy(place, outs[n], sem.at[n]))
     for copy in copies:
         copy.start()
     for copy in copies:
         copy.wait()
 
 
-def cut(axis, pieces, weight, after=()):
-    weight = pltpu.with_memory_space_constraint(weight, pltpu.HBM)
-    rows = weight.shape[0] if axis == 1 else HALF
-    shapes = [pltpu.VMEM((rows, size), BF) for size in pieces] * 2
+def cut(axis, pieces, parts, weights, after=()):
+    weights = [pltpu.with_memory_space_constraint(w, pltpu.HBM) for w in weights]
+    rows = weights[0].shape[0] if axis == 1 else HALF
+    shapes = [pltpu.VMEM((rows, size), BF) for size in pieces] * (len(parts) * len(weights))
     out = kernel(
-        functools.partial(cut_body, axis, pieces),
+        functools.partial(cut_body, axis, pieces, parts, len(weights)),
         "cut",
-        (weight,),
+        weights,
         shapes,
         after,
-        [pltpu.SemaphoreType.DMA((2 * len(pieces),))],
+        [pltpu.SemaphoreType.DMA((len(shapes),))],
+        specs=[pl.BlockSpec(memory_space=pltpu.HBM)] * len(weights),
+        time=1.5 * len(weights) * len(parts),
+    )
+    return [out[i : i + len(pieces)] for i in range(0, len(out), len(pieces))]
+
+
+def hold_body(source, *refs):
+    out, sem = refs[-2:]
+    copy = pltpu.make_async_copy(source, out, sem)
+    copy.start()
+    copy.wait()
+
+
+def hold(tokens, after):
+    return kernel(
+        hold_body,
+        "stack",
+        (pltpu.with_memory_space_constraint(tokens, pltpu.HBM),),
+        [pltpu.VMEM(tokens.shape, BF)],
+        after,
+        [pltpu.SemaphoreType.DMA],
         specs=[pl.BlockSpec(memory_space=pltpu.HBM)],
-    )
-    return out[: len(pieces)], out[len(pieces) :]
+    )[0]
 
 
 def project_body(flow, sizes, *refs):
@@ -180,6 +199,7 @@
         after,
         [pltpu.VMEM((rows, 1024), BF)] * 2,
         8,
+        time=1.5,
     )
 
 
@@ -234,30 +254,48 @@
     return out if last else out[0]
 
 
-def halves_body(keep, came, *refs):
+def halves_body(before, keep, came, *refs):
     send, kept = refs[-2:]
     half = kept.shape[2]
+    at = 0
+    if before:
+        old_send, old_kept = refs[:2]
+        at = old_send.shape[1]
+        send[:, :at] = old_send[...]
+        kept[:, :at] = old_kept[...]
     for k in range(2):
-        for t in range(2):
+        for t in range(keep.shape[1]):
             total = keep[k, t].astype(F32) + came[k, t].astype(F32)
-            send[k, t] = total[:half].astype(BF)
-            kept[k, t] = total[half:].astype(BF)
-
-
-def halves(keep, came, after):
-    shape = jax.ShapeDtypeStruct((2, 2, keep.shape[2] // 2, HALF), BF)
-    return kernel(halves_body, "halves", (keep, came), [shape] * 2, after)
-
-
-def hidden_body(keep, came, *refs):
-    gate = keep[0].astype(F32) + came[0].astype(F32)
-    up = keep[1].astype(F32) + came[1].astype(F32)
-    refs[-1][...] = (gate / (1.0 + jnp.exp(-gate)) * up).astype(BF)
-
-
-def hidden(keep, came, after):
-    shape = jax.ShapeDtypeStruct(keep.shape[1:], BF)
-    return kernel(hidden_body, "hidden", (keep, came), [shape], after)[0]
+            send[k, at + t] = total[:half].astype(BF)
+            kept[k, at + t] = total[half:].astype(BF)
+
+
+def halves(keep, came, done=(), after=()):
+    spans = keep.shape[1] + (done[0].shape[1] if done else 0)
+    shape = jax.ShapeDtypeStruct((2, spans, keep.shape[2] // 2, HALF), BF)
+    body = functools.partial(halves_body, bool(done))
+    return kernel(body, "halves", (keep, came, *done), [shape] * 2, after)
+
+
+def add_body(keep, came, *refs):
+    refs[-1][...] = (keep[...].astype(F32) + came[...].astype(F32)).astype(BF)
+
+
+def add(keep, came, after):
+    return kernel(add_body, "halves", (keep, came), [jax.ShapeDtypeStruct(keep.shape, BF)], after)[0]
+
+
+def hidden_body(mine, theirs, *refs):
+    half = mine.shape[2] // 2
+    for at, other in ((0, half), (half, 0)):
+        gate = mine[0, :, at : at + half].astype(F32) + theirs[0, :, other : other + half].astype(F32)
+        up = mine[1, :, at : at + half].astype(F32) + theirs[1, :, other : other + half].astype(F32)
+        refs[-1][:, at : at + half] = (gate / (1.0 + jnp.exp(-gate)) * up).astype(BF)
+
+
+def hidden(mine, theirs, after):
+    shape = jax.ShapeDtypeStruct(mine.shape[1:], BF)
+    return kernel(hidden_body, "hidden", (mine, theirs), [shape], after)[0]
 
 
 def join_body(theirs, mine, *refs):
@@ -294,32 +332,44 @@
         return out
 
 
-TURNS = "guj0123013120130123123103210230w230221301302"
+TURNS = "oguj012301w230123012301230123012301230213"
 
 
 def local(tokens, gate_weight, up_weight, down_weight):
     line = Line()
     after, before = shift(tokens, -1), shift(tokens, 1)
-    near, beside = tokens[None], swap(tokens)[None]
-    far = shift(beside, 2)
-    pair_a = [(near, beside), (swap(far), far)]
-    weights = {"g": (1, WIDE, gate_weight), "u": (1, WIDE, up_weight), "w": (0, DOWN, down_weight)}
+    beside, far = swap(tokens), shift(tokens, 2)
+    near = line(hold, tokens)
+    pair_a = [(near[None], beside[None]), (far[None], swap(far)[None])]
+    sides = []
     own, other = {}, {}
-    sides = []
     finished = {}
 
     def unit(u):
         flow = u % 2
         held = own if u < 2 else other
-        send, keep = line(project, flow, pair_a if flow == 0 else sides, held["g"], held["u"])
-        for step in range(3):
-            came = exchange(send, flow, step)
+        groups = [sides] if flow else [pair_a]
+        parts = []
+        for group in groups:
+            send, keep = line(project, flow, group, held["g"], held["u"])
+            parts.append((keep, exchange(send, flow, 0)))
             yield
-            send, keep = line(halves, keep, came)
-        came = exchange(send, flow, 3)
-        yield
-        rows = line(hidden, keep, came)
-        for step in (3, 2, 1):
+        done = ()
+        for i, part in enumerate(parts):
+            if i:
+                yield
+            done = line(halves, *part, done)
+        send, keep = done
+        came = exchange(send, flow, 1)
+        yield
+        send, keep = line(halves, keep, came)
+        came = exchange(send, flow, 2)
+        yield
+        rows = line(add, keep, came)
+        came = exchange(rows, flow, 3)
+        yield
+        rows = line(hidden, rows, came)
+        for step in (2, 1):
             theirs = exchange(rows, flow, step)
             yield
             rows = line(join, theirs, rows)
@@ -332,9 +382,15 @@
 
     units = [unit(u) for u in range(4)]
     for turn in TURNS:
-        if turn in weights:
-            given, own[turn] = line(cut, *weights[turn])
+        if turn == "o":
+            own["g"], own["u"] = line(cut, 1, WIDE, ("own",), (gate_weight, up_weight))
+        elif turn in "gu":
+            weight = gate_weight if turn == "g" else up_weight
+            (given,) = line(cut, 1, WIDE, ("other",), (weight,))
             other[turn] = [swap(piece) for piece in given]
+        elif turn == "w":
+            own["w"], given = line(cut, 0, DOWN, ("own", "other"), (down_weight,))
+            other["w"] = [swap(piece) for piece in given]
         elif turn == "j":
             both = line(stack, after, before)
             sides.append((both, swap(both)))

time: 199 us -> 185 us (0.930)
  waiting for transfers between devices: 100 us -> 88.6 us
  starting transfers between devices: 59.6 us -> 55.3 us
  Pallas kernels: 37.3 us -> 39.6 us
    ppermute x32 -> x28, waiting for transfers between devices: 80.1 us -> 69.4 us  [exchange(): return lax.ppermute(a, ('group', 'mp'), pairs)]
    ppermute x11, starting transfers between devices: 14.2 us -> 9.7 us  [swap(): return lax.ppermute(a, 'group', SWAP)]
    pallas_call x44 -> x42, Pallas kernels: 37.3 us -> 39.6 us  [kernel(): pl.pallas_call(body, in_specs=specs + [ANY] * len(after), out_specs=[VMEM...]
    ppermute x6, starting transfers between devices: 9.57 us -> 11.6 us  [shift(): lax.ppermute(a, 'group', [(g, (g + 2 * chips) % 8) for g in range(8)])]
    ppermute x32 -> x28, starting transfers between devices: 35.9 us -> 34 us  [exchange(): return lax.ppermute(a, ('group', 'mp'), pairs)]
  transfers between devices with their start and end apart: 49 -> 45, of which waited for: 26 -> 24; matrix products, arithmetic and copies ran while one was open for 0% -> 0% of each run, Pallas kernels for 16% -> 21%
where the time goes in v4:
time: 185 us
  waiting for transfers between devices  88.6 us (48%)
  starting transfers between devices  55.3 us (30%)
  Pallas kernels  39.6 us (21%)
    ppermute x28, waiting for transfers between devices, exchange(): return lax.ppermute(a, ('group', 'mp'), pairs)  69.4 us
    pallas_call x42, Pallas kernels, kernel(): pl.pallas_call(body, in_specs=specs + [ANY] * len(after), out_specs=[VMEM...  39.6 us
    ppermute x28, starting transfers between devices, exchange(): return lax.ppermute(a, ('group', 'mp'), pairs)  34 us
    ppermute x6, waiting for transfers between devices, shift(): lax.ppermute(a, 'group', [(g, (g + 2 * chips) % 8) for g in range(8)])  16.6 us
    ppermute x6, starting transfers between devices, shift(): lax.ppermute(a, 'group', [(g, (g + 2 * chips) % 8) for g in range(8)])  11.6 us
    ppermute x11, starting transfers between devices, swap(): return lax.ppermute(a, 'group', SWAP)  9.7 us
  transfers between devices with their start and end apart: 45, of which 24 were waited for; matrix products, arithmetic and copies ran while one was open for 0% of the time, Pallas kernels for 21%

profile of v4, /device:TPU:1, one launch (start us, length us, event | category | flops | bytes accessed | tf_op | source)
XLA Modules:
  0.0 185.2 jit_solution(7954956049066513752)
XLA Ops:
  0.0 4.4 %collective-permute-start.1 = (bf16[128,1024]{1,0:T(8,128)(2,1)}, bf16[128,1024]{1,0:T(8,128)(2,1)S(1)}, u32[]{:S(2)}, u32[]{:S(2)}) collective-permute-start(bf16[128,1024]{1,0:T(8,128)(2,1)} %source.1), channel_id=1, source_target_pairs={{0,64},{16,80},{32,96},{48,112},{64,0},{80,16},{96,32},{112,48},{1... | collective-permute-start | bytes 786440 | tf_op jit(solution)/shard_map/ppermute | solution.py:59
  7.1 3.1 %cut.4 = (bf16[1024,896]{1,0:T(8,128)(2,1)S(1)}, bf16[1024,768]{1,0:T(8,128)(2,1)S(1)}, bf16[1024,896]{1,0:T(8,128)(2,1)S(1)}, bf16[1024,768]{1,0:T(8,128)(2,1)S(1)}) custom-call(bf16[1024,3328]{1,0:T(8,128)(2,1)} %refs_0_.5, bf16[1024,3328]{1,0:T(8,128)(2,1)} %refs_0_.6, bf16[128,1024]{1,0:T(8,128)(2,1)S(1)} %stack.2.refs_2_), custom_call_target="tpu_custom_call" | custom-call | flops 3449999872 | tf_op jit(solution)/shard_map/cut/pallas_call | solution.py:80
  10.2 2.0 %cut.5 = (bf16[1024,896]{1,0:T(8,128)(2,1)S(1)}, bf16[1024,768]{1,0:T(8,128)(2,1)S(1)}) custom-call(bf16[1024,3328]{1,0:T(8,128)(2,1)} %refs_0_.5, bf16[1024,896]{1,0:T(8,128)(2,1)S(1)} %get-tuple-element.45.refs_1_.refs_4_.refs_2_), custom_call_target="tpu_custom_call" | custom-call | flops 1724999936 | tf_op jit(solution)/shard_map/cut/pallas_call | solution.py:80
  12.8 2.0 %cut.6 = (bf16[1024,896]{1,0:T(8,128)(2,1)S(1)}, bf16[1024,768]{1,0:T(8,128)(2,1)S(1)}) custom-call(bf16[1024,3328]{1,0:T(8,128)(2,1)} %refs_0_.6, bf16[1024,896]{1,0:T(8,128)(2,1)S(1)} %get-tuple-element.46.refs_1_), custom_call_target="tpu_custom_call" | custom-call | flops 1724999936 | tf_op jit(solution)/shard_map/cut/pallas_call | solution.py:80
  15.2 1.9 %collective-permute-start.7 = (bf16[128,1024]{1,0:T(8,128)(2,1)S(1)}, bf16[128,1024]{1,0:T(8,128)(2,1)S(1)}, u32[]{:S(2)}, u32[]{:S(2)}) collective-permute-start(bf16[128,1024]{1,0:T(8,128)(2,1)S(1)} %copy-done), channel_id=1, source_target_pairs={{0,96},{16,112},{32,0},{48,16},{64,32},{80,48},{96,64},{112,80},{1... | collective-permute-start | bytes 786440 | tf_op jit(solution)/shard_map/ppermute | solution.py:59
  17.6 5.2 %collective-permute-done.7.first = bf16[128,1024]{1,0:T(8,128)(2,1)S(1)} collective-permute-done((bf16[128,1024]{1,0:T(8,128)(2,1)S(1)}, bf16[128,1024]{1,0:T(8,128)(2,1)S(1)}, u32[]{:S(2)}, u32[]{:S(2)}) %collective-permute-start.7) | collective-permute-done | bytes 262176 | tf_op jit(solution)/shard_map/ppermute | solution.py:59
  25.4 3.7 %project.4 = (bf16[2,2,128,1664]{3,2,1,0:T(8,128)(2,1)S(1)}, bf16[2,2,128,1664]{3,2,1,0:T(8,128)(2,1)S(1)}) custom-call(bf16[1,128,1024]{2,1,0:T(8,128)(2,1)S(1)} %bitcast.20, bf16[1,128,1024]{2,1,0:T(8,128)(2,1)S(1)} %bitcast.24, bf16[1,128,1024]{2,1,0:T(8,128)(2,1)S(1)} %bitcast.22, bf16[1,128,1024]{2,1,0:T(8,128)(2,1)S(1)} %bitcast.26, ...), custom_call_target="tpu_custom_call" | custom-call | flops 1724999936 | tf_op jit(solution)/shard_map/project/pallas_call | solution.py:80
  29.2 1.4 collective-permute-start.12
  30.6 3.7 %project.5 = (bf16[2,2,128,1664]{3,2,1,0:T(8,128)(2,1)S(1)}, bf16[2,2,128,1664]{3,2,1,0:T(8,128)(2,1)S(1)}) custom-call(bf16[2,128,1024]{2,1,0:T(8,128)(2,1)S(1)} %stack.3.refs_8_.refs_0_, bf16[2,128,1024]{2,1,0:T(8,128)(2,1)S(1)} %collective-permute-done.9.refs_1_, bf16[1024,896]{1,0:T(8,128)(2,1)S(1)} %get-tuple-element.45.refs_1_.refs_4_.refs_2_, ...), custom_call_target="tpu_custom_call" | custom-call | flops 1724999936 | tf_op jit(solution)/shard_map/project/pallas_call | solution.py:80
  34.3 2.0 %collective-permute-start.11 = (bf16[2,2,128,1664]{3,2,1,0:T(8,128)(2,1)S(1)}, bf16[2,2,128,1664]{3,2,1,0:T(8,128)(2,1)S(1)}, u32[]{:S(2)}, u32[]{:S(2)}) collective-permute-start(bf16[2,2,128,1664]{3,2,1,0:T(8,128)(2,1)S(1)} %get-tuple-element.54.refs_8_), channel_id=1, source_target_pairs={{0,12},{1,13},{2,14},{3,15},{4,8},{5,9},{6,10},{7,11},{8,4},{9,5},... | collective-permute-start | bytes 5111816 | tf_op jit(solution)/shard_map/ppermute | solution.py:51
  36.3 3.7 %project.6 = (bf16[2,2,128,1664]{3,2,1,0:T(8,128)(2,1)S(1)}, bf16[2,2,128,1664]{3,2,1,0:T(8,128)(2,1)S(1)}) custom-call(bf16[1,128,1024]{2,1,0:T(8,128)(2,1)S(1)} %bitcast.21, bf16[1,128,1024]{2,1,0:T(8,128)(2,1)S(1)} %bitcast.25, bf16[1,128,1024]{2,1,0:T(8,128)(2,1)S(1)} %bitcast.23, bf16[1,128,1024]{2,1,0:T(8,128)(2,1)S(1)} %bitcast.27, ...), custom_call_target="tpu_custom_call" | custom-call | flops 1724999936 | tf_op jit(solution)/shard_map/project/pallas_call | solution.py:80
  40.7 3.7 %project.7 = (bf16[2,2,128,1664]{3,2,1,0:T(8,128)(2,1)S(1)}, bf16[2,2,128,1664]{3,2,1,0:T(8,128)(2,1)S(1)}) custom-call(bf16[2,128,1024]{2,1,0:T(8,128)(2,1)S(1)} %stack.3.refs_8_.refs_0_, bf16[2,128,1024]{2,1,0:T(8,128)(2,1)S(1)} %collective-permute-done.9.refs_1_, bf16[1024,896]{1,0:T(8,128)(2,1)S(1)} %collective-permute-done.3.refs_4_.refs_2_, ...), custom_call_target="tpu_custom_call" | custom-call | flops 1724999936 | tf_op jit(solution)/shard_map/project/pallas_call | solution.py:80
  45.2 5.1 %collective-permute-done.12.came = bf16[2,2,128,1664]{3,2,1,0:T(8,128)(2,1)S(1)} collective-permute-done((bf16[2,2,128,1664]{3,2,1,0:T(8,128)(2,1)S(1)}, bf16[2,2,128,1664]{3,2,1,0:T(8,128)(2,1)S(1)}, u32[]{:S(2)}, u32[]{:S(2)}) %collective-permute-start.12) | collective-permute-done | bytes 1703968 | tf_op jit(solution)/shard_map/ppermute | solution.py:51
  50.6 2.8 %collective-permute-start.15 = (bf16[2,2,64,1664]{3,2,1,0:T(8,128)(2,1)S(1)}, bf16[2,2,64,1664]{3,2,1,0:T(8,128)(2,1)S(1)}, u32[]{:S(2)}, u32[]{:S(2)}) collective-permute-start(bf16[2,2,64,1664]{3,2,1,0:T(8,128)(2,1)S(1)} %get-tuple-element.60.refs_0_), channel_id=1, source_target_pairs={{0,12},{1,13},{2,14},{3,15},{4,8},{5,9},{6,10},{7,11},{8,4},{9,5},... | collective-permute-start | bytes 2555912 | tf_op jit(solution)/shard_map/ppermute | solution.py:51
  53.4 3.1 %collective-permute-done.11.came = bf16[2,2,128,1664]{3,2,1,0:T(8,128)(2,1)S(1)} collective-permute-done((bf16[2,2,128,1664]{3,2,1,0:T(8,128)(2,1)S(1)}, bf16[2,2,128,1664]{3,2,1,0:T(8,128)(2,1)S(1)}, u32[]{:S(2)}, u32[]{:S(2)}) %collective-permute-start.11) | collective-permute-done | bytes 1703968 | tf_op jit(solution)/shard_map/ppermute | solution.py:51
  57.1 3.0 %cut.7 = (bf16[1664,512]{1,0:T(8,128)(2,1)S(1)}, bf16[1664,512]{1,0:T(8,128)(2,1)S(1)}, bf16[1664,512]{1,0:T(8,128)(2,1)S(1)}, bf16[1664,512]{1,0:T(8,128)(2,1)S(1)}) custom-call(bf16[3328,1024]{1,0:T(8,128)(2,1)} %refs_0_.7, bf16[2,2,64,1664]{3,2,1,0:T(8,128)(2,1)S(1)} %get-tuple-element.61.refs_1_), custom_call_target="tpu_custom_call" | custom-call | flops 3449999872 | tf_op jit(solution)/shard_map/cut/pallas_call | solution.py:80
  60.1 8.4 %collective-permute-done.10.came = bf16[2,2,128,1664]{3,2,1,0:T(8,128)(2,1)S(1)} collective-permute-done((bf16[2,2,128,1664]{3,2,1,0:T(8,128)(2,1)S(1)}, bf16[2,2,128,1664]{3,2,1,0:T(8,128)(2,1)S(1)}, u32[]{:S(2)}, u32[]{:S(2)}) %collective-permute-start.10) | collective-permute-done | bytes 1703968 | tf_op jit(solution)/shard_map/ppermute | solution.py:51
  68.9 2.8 %collective-permute-start.13 = (bf16[2,2,64,1664]{3,2,1,0:T(8,128)(2,1)S(1)}, bf16[2,2,64,1664]{3,2,1,0:T(8,128)(2,1)S(1)}, u32[]{:S(2)}, u32[]{:S(2)}) collective-permute-start(bf16[2,2,64,1664]{3,2,1,0:T(8,128)(2,1)S(1)} %get-tuple-element.64.refs_0_), channel_id=1, source_target_pairs={{0,12},{1,13},{2,14},{3,15},{4,8},{5,9},{6,10},{7,11},{8,4},{9,5},... | collective-permute-start | bytes 2555912 | tf_op jit(solution)/shard_map/ppermute | solution.py:51
  71.7 3.1 %collective-permute-done.16.came = bf16[2,2,128,1664]{3,2,1,0:T(8,128)(2,1)S(1)} collective-permute-done((bf16[2,2,128,1664]{3,2,1,0:T(8,128)(2,1)S(1)}, bf16[2,2,128,1664]{3,2,1,0:T(8,128)(2,1)S(1)}, u32[]{:S(2)}, u32[]{:S(2)}) %collective-permute-start.16) | collective-permute-done | bytes 1703968 | tf_op jit(solution)/shard_map/ppermute | solution.py:51
  76.6 7.4 %collective-permute-done.15.came = bf16[2,2,64,1664]{3,2,1,0:T(8,128)(2,1)S(1)} collective-permute-done((bf16[2,2,64,1664]{3,2,1,0:T(8,128)(2,1)S(1)}, bf16[2,2,64,1664]{3,2,1,0:T(8,128)(2,1)S(1)}, u32[]{:S(2)}, u32[]{:S(2)}) %collective-permute-start.15) | collective-permute-done | bytes 852000 | tf_op jit(solution)/shard_map/ppermute | solution.py:51
  85.7 7.4 %collective-permute-done.13.came = bf16[2,2,64,1664]{3,2,1,0:T(8,128)(2,1)S(1)} collective-permute-done((bf16[2,2,64,1664]{3,2,1,0:T(8,128)(2,1)S(1)}, bf16[2,2,64,1664]{3,2,1,0:T(8,128)(2,1)S(1)}, u32[]{:S(2)}, u32[]{:S(2)}) %collective-permute-start.13) | collective-permute-done | bytes 852000 | tf_op jit(solution)/shard_map/ppermute | solution.py:51
  93.1 2.5 %collective-permute-start.18 = (bf16[2,2,32,1664]{3,2,1,0:T(8,128)(2,1)S(1)}, bf16[2,2,32,1664]{3,2,1,0:T(8,128)(2,1)S(1)}, u32[]{:S(2)}, u32[]{:S(2)}) collective-permute-start(bf16[2,2,32,1664]{3,2,1,0:T(8,128)(2,1)S(1)} %get-tuple-element.70.refs_0_), channel_id=1, source_target_pairs={{0,3},{1,2},{2,1},{3,0},{4,7},{5,6},{6,5},{7,4},{8,11},{9,10},{10,... | collective-permute-start | bytes 1277960 | tf_op jit(solution)/shard_map/ppermute | solution.py:51
  96.8 4.8 %collective-permute-done.18.came = bf16[2,2,32,1664]{3,2,1,0:T(8,128)(2,1)S(1)} collective-permute-done((bf16[2,2,32,1664]{3,2,1,0:T(8,128)(2,1)S(1)}, bf16[2,2,32,1664]{3,2,1,0:T(8,128)(2,1)S(1)}, u32[]{:S(2)}, u32[]{:S(2)}) %collective-permute-start.18) | collective-permute-done | bytes 426016 | tf_op jit(solution)/shard_map/ppermute | solution.py:51
  101.6 2.5 %collective-permute-start.23 = (bf16[2,2,32,1664]{3,2,1,0:T(8,128)(2,1)S(1)}, bf16[2,2,32,1664]{3,2,1,0:T(8,128)(2,1)S(1)}, u32[]{:S(2)}, u32[]{:S(2)}) collective-permute-start(bf16[2,2,32,1664]{3,2,1,0:T(8,128)(2,1)S(1)} %halves.20.refs_0_.mine), channel_id=1, source_target_pairs={{0,3},{1,2},{2,1},{3,0},{4,7},{5,6},{6,5},{7,4},{8,11},{9,10},{10,... | collective-permute-start | bytes 1277960 | tf_op jit(solution)/shard_map/ppermute | solution.py:51
  104.4 1.8 collective-permute-done.24.came
  106.1 2.5 %collective-permute-start.21 = (bf16[2,2,32,1664]{3,2,1,0:T(8,128)(2,1)S(1)}, bf16[2,2,32,1664]{3,2,1,0:T(8,128)(2,1)S(1)}, u32[]{:S(2)}, u32[]{:S(2)}) collective-permute-start(bf16[2,2,32,1664]{3,2,1,0:T(8,128)(2,1)S(1)} %halves.22.refs_0_.mine), channel_id=1, source_target_pairs={{0,3},{1,2},{2,1},{3,0},{4,7},{5,6},{6,5},{7,4},{8,11},{9,10},{10,... | collective-permute-start | bytes 1277960 | tf_op jit(solution)/shard_map/ppermute | solution.py:51
  108.7 2.0 %collective-permute-done.23.theirs = bf16[2,2,32,1664]{3,2,1,0:T(8,128)(2,1)S(1)} collective-permute-done((bf16[2,2,32,1664]{3,2,1,0:T(8,128)(2,1)S(1)}, bf16[2,2,32,1664]{3,2,1,0:T(8,128)(2,1)S(1)}, u32[]{:S(2)}, u32[]{:S(2)}) %collective-permute-start.23) | collective-permute-done | bytes 426016 | tf_op jit(solution)/shard_map/ppermute | solution.py:51
  112.7 2.6 %collective-permute-done.21.theirs = bf16[2,2,32,1664]{3,2,1,0:T(8,128)(2,1)S(1)} collective-permute-done((bf16[2,2,32,1664]{3,2,1,0:T(8,128)(2,1)S(1)}, bf16[2,2,32,1664]{3,2,1,0:T(8,128)(2,1)S(1)}, u32[]{:S(2)}, u32[]{:S(2)}) %collective-permute-start.21) | collective-permute-done | bytes 426016 | tf_op jit(solution)/shard_map/ppermute | solution.py:51
  115.3 2.5 %collective-permute-start.26 = (bf16[2,32,1664]{2,1,0:T(8,128)(2,1)S(1)}, bf16[2,32,1664]{2,1,0:T(8,128)(2,1)S(1)}, u32[]{:S(2)}, u32[]{:S(2)}) collective-permute-start(bf16[2,32,1664]{2,1,0:T(8,128)(2,1)S(1)} %hidden.5.refs_0_.mine), channel_id=1, source_target_pairs={{0,3},{1,2},{2,1},{3,0},{4,7},{5,6},{6,5},{7,4},{8,11},{9,10},{10,... | collective-permute-start | bytes 638984 | tf_op jit(solution)/shard_map/ppermute | solution.py:51
  118.2 2.0 %collective-permute-done.27.theirs = bf16[2,32,1664]{2,1,0:T(8,128)(2,1)S(1)} collective-permute-done((bf16[2,32,1664]{2,1,0:T(8,128)(2,1)S(1)}, bf16[2,32,1664]{2,1,0:T(8,128)(2,1)S(1)}, u32[]{:S(2)}, u32[]{:S(2)}) %collective-permute-start.27) | collective-permute-done | bytes 213024 | tf_op jit(solution)/shard_map/ppermute | solution.py:51
  120.3 2.5 %collective-permute-start.32 = (bf16[2,32,1664]{2,1,0:T(8,128)(2,1)S(1)}, bf16[2,32,1664]{2,1,0:T(8,128)(2,1)S(1)}, u32[]{:S(2)}, u32[]{:S(2)}) collective-permute-start(bf16[2,32,1664]{2,1,0:T(8,128)(2,1)S(1)} %hidden.7.refs_0_.mine), channel_id=1, source_target_pairs={{0,3},{1,2},{2,1},{3,0},{4,7},{5,6},{6,5},{7,4},{8,11},{9,10},{10,... | collective-permute-start | bytes 638984 | tf_op jit(solution)/shard_map/ppermute | solution.py:51
  122.8 2.0 %collective-permute-start.31 = (bf16[2,64,1664]{2,1,0:T(8,128)(2,1)S(1)}, bf16[2,64,1664]{2,1,0:T(8,128)(2,1)S(1)}, u32[]{:S(2)}, u32[]{:S(2)}) collective-permute-start(bf16[2,64,1664]{2,1,0:T(8,128)(2,1)S(1)} %join.8.refs_0_.mine), channel_id=1, source_target_pairs={{0,12},{1,13},{2,14},{3,15},{4,8},{5,9},{6,10},{7,11},{8,4},{9,5},... | collective-permute-start | bytes 1277960 | tf_op jit(solution)/shard_map/ppermute | solution.py:51
  126.2 1.9 %collective-permute-start.29 = (bf16[2,64,1664]{2,1,0:T(8,128)(2,1)S(1)}, bf16[2,64,1664]{2,1,0:T(8,128)(2,1)S(1)}, u32[]{:S(2)}, u32[]{:S(2)}) collective-permute-start(bf16[2,64,1664]{2,1,0:T(8,128)(2,1)S(1)} %join.10.refs_0_.mine), channel_id=1, source_target_pairs={{0,12},{1,13},{2,14},{3,15},{4,8},{5,9},{6,10},{7,11},{8,4},{9,5},... | collective-permute-start | bytes 1277960 | tf_op jit(solution)/shard_map/ppermute | solution.py:51
  128.1 5.5 %collective-permute-done.31.theirs = bf16[2,64,1664]{2,1,0:T(8,128)(2,1)S(1)} collective-permute-done((bf16[2,64,1664]{2,1,0:T(8,128)(2,1)S(1)}, bf16[2,64,1664]{2,1,0:T(8,128)(2,1)S(1)}, u32[]{:S(2)}, u32[]{:S(2)}) %collective-permute-start.31) | collective-permute-done | bytes 426016 | tf_op jit(solution)/shard_map/ppermute | solution.py:51
  133.7 1.5 collective-permute-start.37
  135.3 2.9 %collective-permute-done.29.theirs = bf16[2,64,1664]{2,1,0:T(8,128)(2,1)S(1)} collective-permute-done((bf16[2,64,1664]{2,1,0:T(8,128)(2,1)S(1)}, bf16[2,64,1664]{2,1,0:T(8,128)(2,1)S(1)}, u32[]{:S(2)}, u32[]{:S(2)}) %collective-permute-start.29) | collective-permute-done | bytes 426016 | tf_op jit(solution)/shard_map/ppermute | solution.py:51
  138.2 1.9 %collective-permute-start.41 = (bf16[2,128,1664]{2,1,0:T(8,128)(2,1)S(1)}, bf16[2,128,1664]{2,1,0:T(8,128)(2,1)S(1)}, u32[]{:S(2)}, u32[]{:S(2)}) collective-permute-start(bf16[2,128,1664]{2,1,0:T(8,128)(2,1)S(1)} %join.13.refs_0_), channel_id=1, source_target_pairs={{0,12},{1,13},{2,14},{3,15},{4,8},{5,9},{6,10},{7,11},{8,4},{9,5},... | collective-permute-start | bytes 2555912 | tf_op jit(solution)/shard_map/ppermute | solution.py:51
  143.2 2.0 %collective-permute-start.40 = (bf16[2,128,1664]{2,1,0:T(8,128)(2,1)S(1)}, bf16[2,128,1664]{2,1,0:T(8,128)(2,1)S(1)}, u32[]{:S(2)}, u32[]{:S(2)}) collective-permute-start(bf16[2,128,1664]{2,1,0:T(8,128)(2,1)S(1)} %join.15.refs_3_.refs_0_), channel_id=1, source_target_pairs={{0,12},{1,13},{2,14},{3,15},{4,8},{5,9},{6,10},{7,11},{8,4},{9,5},... | collective-permute-start | bytes 2555912 | tf_op jit(solution)/shard_map/ppermute | solution.py:51
  147.4 2.6 %collective-permute-done.37.refs_0_ = bf16[2,128,1664]{2,1,0:T(8,128)(2,1)S(1)} collective-permute-done((bf16[2,128,1664]{2,1,0:T(8,128)(2,1)S(1)}, bf16[2,128,1664]{2,1,0:T(8,128)(2,1)S(1)}, u32[]{:S(2)}, u32[]{:S(2)}) %collective-permute-start.37) | collective-permute-done | bytes 852000 | tf_op jit(solution)/shard_map/ppermute | solution.py:51
  151.2 7.9 %collective-permute-done.33.refs_0_ = bf16[2,128,1664]{2,1,0:T(8,128)(2,1)S(1)} collective-permute-done((bf16[2,128,1664]{2,1,0:T(8,128)(2,1)S(1)}, bf16[2,128,1664]{2,1,0:T(8,128)(2,1)S(1)}, u32[]{:S(2)}, u32[]{:S(2)}) %collective-permute-start.33) | collective-permute-done | bytes 852000 | tf_op jit(solution)/shard_map/ppermute | solution.py:51
  159.1 1.4 down.13
  161.8 1.4 down.15
  163.2 3.3 %collective-permute-start.42 = (bf16[2,128,1024]{2,1,0:T(8,128)(2,1)S(1)}, bf16[2,128,1024]{2,1,0:T(8,128)(2,1)S(1)}, u32[]{:S(2)}, u32[]{:S(2)}) collective-permute-start(bf16[2,128,1024]{2,1,0:T(8,128)(2,1)S(1)} %get-tuple-element.84), channel_id=1, source_target_pairs={{0,16},{16,0},{32,48},{48,32},{64,80},{80,64},{96,112},{112,96},{1... | collective-permute-start | bytes 1572872 | tf_op jit(solution)/shard_map/ppermute | solution.py:55
  166.6 1.4 collective-permute-done.42
  168.3 3.2 %collective-permute-start.44 = (bf16[128,1024]{1,0:T(8,128)(2,1)S(1)}, bf16[128,1024]{1,0:T(8,128)(2,1)S(1)}, u32[]{:S(2)}, u32[]{:S(2)}) collective-permute-start(bf16[128,1024]{1,0:T(8,128)(2,1)S(1)} %get-tuple-element.86), channel_id=1, source_target_pairs={{0,96},{16,112},{32,0},{48,16},{64,32},{80,48},{96,64},{112,80},{1... | collective-permute-start | bytes 786440 | tf_op jit(solution)/shard_map/ppermute | solution.py:59
  173.0 4.9 %collective-permute-done.43 = bf16[128,1024]{1,0:T(8,128)(2,1)S(1)} collective-permute-done((bf16[128,1024]{1,0:T(8,128)(2,1)S(1)}, bf16[128,1024]{1,0:T(8,128)(2,1)S(1)}, u32[]{:S(2)}, u32[]{:S(2)}) %collective-permute-start.43) | collective-permute-done | bytes 262176 | tf_op jit(solution)/shard_map/ppermute | solution.py:59
  177.8 4.5 %collective-permute-done.44 = bf16[128,1024]{1,0:T(8,128)(2,1)S(1)} collective-permute-done((bf16[128,1024]{1,0:T(8,128)(2,1)S(1)}, bf16[128,1024]{1,0:T(8,128)(2,1)S(1)}, u32[]{:S(2)}, u32[]{:S(2)}) %collective-permute-start.44) | collective-permute-done | bytes 262176 | tf_op jit(solution)/shard_map/ppermute | solution.py:59
  182.3 2.0 %collective-permute-done.39 = bf16[128,1024]{1,0:T(8,128)(2,1)S(1)} collective-permute-done((bf16[128,1024]{1,0:T(8,128)(2,1)S(1)}, bf16[128,1024]{1,0:T(8,128)(2,1)S(1)}, u32[]{:S(2)}, u32[]{:S(2)}) %collective-permute-start.39) | collective-permute-done | bytes 262176 | tf_op jit(solution)/shard_map/ppermute | solution.py:59
  (91 shorter events, 28.6 us)
Async XLA Ops:
  0.0 14.8 %collective-permute-start.1 = (bf16[128,1024]{1,0:T(8,128)(2,1)}, bf16[128,1024]{1,0:T(8,128)(2,1)S(1)}, u32[]{:S(2)}, u32[]{:S(2)}) collective-permute-start(bf16[128,1024]{1,0:T(8,128)(2,1)} %source.1), channel_id=1, source_target_pairs={{0,64},{16,80},{32,96},{48,112},{64,0},{80,16},{96,32},{112,48},{1... | collective-permute-start | bytes 786440 | tf_op jit(solution)/shard_map/ppermute | solution.py:59
  4.4 10.7 %collective-permute-start = (bf16[128,1024]{1,0:T(8,128)(2,1)}, bf16[128,1024]{1,0:T(8,128)(2,1)S(1)}, u32[]{:S(2)}, u32[]{:S(2)}) collective-permute-start(bf16[128,1024]{1,0:T(8,128)(2,1)} %source.1), channel_id=1, source_target_pairs={{0,16},{16,0},{32,48},{48,32},{64,80},{80,64},{96,112},{112,96},{1... | collective-permute-start | bytes 786440 | tf_op jit(solution)/shard_map/ppermute | solution.py:55
  5.4 11.7 %collective-permute-start.8 = (bf16[128,1024]{1,0:T(8,128)(2,1)}, bf16[128,1024]{1,0:T(8,128)(2,1)S(1)}, u32[]{:S(2)}, u32[]{:S(2)}) collective-permute-start(bf16[128,1024]{1,0:T(8,128)(2,1)} %source.1), channel_id=1, source_target_pairs={{0,32},{16,48},{32,64},{48,80},{64,96},{80,112},{96,0},{112,16},{1... | collective-permute-start | bytes 786440 | tf_op jit(solution)/shard_map/ppermute | solution.py:59
  12.2 22.1 %collective-permute-start.4 = (bf16[1024,768]{1,0:T(8,128)(2,1)S(1)}, bf16[1024,768]{1,0:T(8,128)(2,1)S(1)}, u32[]{:S(2)}, u32[]{:S(2)}) collective-permute-start(bf16[1024,768]{1,0:T(8,128)(2,1)S(1)} %get-tuple-element.47), channel_id=1, source_target_pairs={{0,16},{16,0},{32,48},{48,32},{64,80},{80,64},{96,112},{112,96},{1... | collective-permute-start | bytes 4718600 | tf_op jit(solution)/shard_map/ppermute | solution.py:55
  12.6 2.6 %copy-start = (bf16[128,1024]{1,0:T(8,128)(2,1)S(1)}, bf16[128,1024]{1,0:T(8,128)(2,1)}, u32[]{:S(2)}) copy-start(bf16[128,1024]{1,0:T(8,128)(2,1)} %source.1) | copy-start | bytes 786436
  12.6 23.7 %collective-permute-start.3 = (bf16[1024,896]{1,0:T(8,128)(2,1)S(1)}, bf16[1024,896]{1,0:T(8,128)(2,1)S(1)}, u32[]{:S(2)}, u32[]{:S(2)}) collective-permute-start(bf16[1024,896]{1,0:T(8,128)(2,1)S(1)} %get-tuple-element.46.refs_1_), channel_id=1, source_target_pairs={{0,16},{16,0},{32,48},{48,32},{64,80},{80,64},{96,112},{112,96},{1... | collective-permute-start | bytes 5505032 | tf_op jit(solution)/shard_map/ppermute | solution.py:55
  14.8 21.5 %collective-permute-start.5 = (bf16[1024,896]{1,0:T(8,128)(2,1)S(1)}, bf16[1024,896]{1,0:T(8,128)(2,1)S(1)}, u32[]{:S(2)}, u32[]{:S(2)}) collective-permute-start(bf16[1024,896]{1,0:T(8,128)(2,1)S(1)} %get-tuple-element.48.refs_0_), channel_id=1, source_target_pairs={{0,16},{16,0},{32,48},{48,32},{64,80},{80,64},{96,112},{112,96},{1... | collective-permute-start | bytes 5505032 | tf_op jit(solution)/shard_map/ppermute | solution.py:55
  15.2 7.7 %collective-permute-start.7 = (bf16[128,1024]{1,0:T(8,128)(2,1)S(1)}, bf16[128,1024]{1,0:T(8,128)(2,1)S(1)}, u32[]{:S(2)}, u32[]{:S(2)}) collective-permute-start(bf16[128,1024]{1,0:T(8,128)(2,1)S(1)} %copy-done), channel_id=1, source_target_pairs={{0,96},{16,112},{32,0},{48,16},{64,32},{80,48},{96,64},{112,80},{1... | collective-permute-start | bytes 786440 | tf_op jit(solution)/shard_map/ppermute | solution.py:59
  17.1 19.2 %collective-permute-start.6 = (bf16[1024,768]{1,0:T(8,128)(2,1)S(1)}, bf16[1024,768]{1,0:T(8,128)(2,1)S(1)}, u32[]{:S(2)}, u32[]{:S(2)}) collective-permute-start(bf16[1024,768]{1,0:T(8,128)(2,1)S(1)} %get-tuple-element.49), channel_id=1, source_target_pairs={{0,16},{16,0},{32,48},{48,32},{64,80},{80,64},{96,112},{112,96},{1... | collective-permute-start | bytes 4718600 | tf_op jit(solution)/shard_map/ppermute | solution.py:55
  22.9 2.2 %collective-permute-start.2 = (bf16[128,1024]{1,0:T(8,128)(2,1)S(1)}, bf16[128,1024]{1,0:T(8,128)(2,1)S(1)}, u32[]{:S(2)}, u32[]{:S(2)}) collective-permute-start(bf16[128,1024]{1,0:T(8,128)(2,1)S(1)} %collective-permute-done.1), channel_id=1, source_target_pairs={{0,16},{16,0},{32,48},{48,32},{64,80},{80,64},{96,112},{112,96},{1... | collective-permute-start | bytes 786440 | tf_op jit(solution)/shard_map/ppermute | solution.py:55
  25.1 4.1 %collective-permute-start.9 = (bf16[2,128,1024]{2,1,0:T(8,128)(2,1)S(1)}, bf16[2,128,1024]{2,1,0:T(8,128)(2,1)S(1)}, u32[]{:S(2)}, u32[]{:S(2)}) collective-permute-start(bf16[2,128,1024]{2,1,0:T(8,128)(2,1)S(1)} %stack.3.refs_8_.refs_0_), channel_id=1, source_target_pairs={{0,16},{16,0},{32,48},{48,32},{64,80},{80,64},{96,112},{112,96},{1... | collective-permute-start | bytes 1572872 | tf_op jit(solution)/shard_map/ppermute | solution.py:55
  29.2 21.0 %collective-permute-start.12 = (bf16[2,2,128,1664]{3,2,1,0:T(8,128)(2,1)S(1)}, bf16[2,2,128,1664]{3,2,1,0:T(8,128)(2,1)S(1)}, u32[]{:S(2)}, u32[]{:S(2)}) collective-permute-start(bf16[2,2,128,1664]{3,2,1,0:T(8,128)(2,1)S(1)} %get-tuple-element.53.refs_6_), channel_id=1, source_target_pairs={{0,4},{1,5},{2,6},{3,7},{4,0},{5,1},{6,2},{7,3},{8,12},{9,13},{10,... | collective-permute-start | bytes 5111816 | tf_op jit(solution)/shard_map/ppermute | solution.py:51
  34.3 22.3 %collective-permute-start.11 = (bf16[2,2,128,1664]{3,2,1,0:T(8,128)(2,1)S(1)}, bf16[2,2,128,1664]{3,2,1,0:T(8,128)(2,1)S(1)}, u32[]{:S(2)}, u32[]{:S(2)}) collective-permute-start(bf16[2,2,128,1664]{3,2,1,0:T(8,128)(2,1)S(1)} %get-tuple-element.54.refs_8_), channel_id=1, source_target_pairs={{0,12},{1,13},{2,14},{3,15},{4,8},{5,9},{6,10},{7,11},{8,4},{9,5},... | collective-permute-start | bytes 5111816 | tf_op jit(solution)/shard_map/ppermute | solution.py:51
  40.0 28.4 %collective-permute-start.10 = (bf16[2,2,128,1664]{3,2,1,0:T(8,128)(2,1)S(1)}, bf16[2,2,128,1664]{3,2,1,0:T(8,128)(2,1)S(1)}, u32[]{:S(2)}, u32[]{:S(2)}) collective-permute-start(bf16[2,2,128,1664]{3,2,1,0:T(8,128)(2,1)S(1)} %get-tuple-element.56.refs_6_), channel_id=1, source_target_pairs={{0,4},{1,5},{2,6},{3,7},{4,0},{5,1},{6,2},{7,3},{8,12},{9,13},{10,... | collective-permute-start | bytes 5111816 | tf_op jit(solution)/shard_map/ppermute | solution.py:51
  44.4 30.4 %collective-permute-start.16 = (bf16[2,2,128,1664]{3,2,1,0:T(8,128)(2,1)S(1)}, bf16[2,2,128,1664]{3,2,1,0:T(8,128)(2,1)S(1)}, u32[]{:S(2)}, u32[]{:S(2)}) collective-permute-start(bf16[2,2,128,1664]{3,2,1,0:T(8,128)(2,1)S(1)} %get-tuple-element.59.refs_0_), channel_id=1, source_target_pairs={{0,12},{1,13},{2,14},{3,15},{4,8},{5,9},{6,10},{7,11},{8,4},{9,5},... | collective-permute-start | bytes 5111816 | tf_op jit(solution)/shard_map/ppermute | solution.py:51
  50.6 33.3 %collective-permute-start.15 = (bf16[2,2,64,1664]{3,2,1,0:T(8,128)(2,1)S(1)}, bf16[2,2,64,1664]{3,2,1,0:T(8,128)(2,1)S(1)}, u32[]{:S(2)}, u32[]{:S(2)}) collective-permute-start(bf16[2,2,64,1664]{3,2,1,0:T(8,128)(2,1)S(1)} %get-tuple-element.60.refs_0_), channel_id=1, source_target_pairs={{0,12},{1,13},{2,14},{3,15},{4,8},{5,9},{6,10},{7,11},{8,4},{9,5},... | collective-permute-start | bytes 2555912 | tf_op jit(solution)/shard_map/ppermute | solution.py:51
  57.0 28.4 %collective-permute-start.14 = (bf16[2,2,64,1664]{3,2,1,0:T(8,128)(2,1)S(1)}, bf16[2,2,64,1664]{3,2,1,0:T(8,128)(2,1)S(1)}, u32[]{:S(2)}, u32[]{:S(2)}) collective-permute-start(bf16[2,2,64,1664]{3,2,1,0:T(8,128)(2,1)S(1)} %get-tuple-element.61.refs_1_), channel_id=1, source_target_pairs={{0,4},{1,5},{2,6},{3,7},{4,0},{5,1},{6,2},{7,3},{8,12},{9,13},{10,... | collective-permute-start | bytes 2555912 | tf_op jit(solution)/shard_map/ppermute | solution.py:51
  68.9 24.2 %collective-permute-start.13 = (bf16[2,2,64,1664]{3,2,1,0:T(8,128)(2,1)S(1)}, bf16[2,2,64,1664]{3,2,1,0:T(8,128)(2,1)S(1)}, u32[]{:S(2)}, u32[]{:S(2)}) collective-permute-start(bf16[2,2,64,1664]{3,2,1,0:T(8,128)(2,1)S(1)} %get-tuple-element.64.refs_0_), channel_id=1, source_target_pairs={{0,12},{1,13},{2,14},{3,15},{4,8},{5,9},{6,10},{7,11},{8,4},{9,5},... | collective-permute-start | bytes 2555912 | tf_op jit(solution)/shard_map/ppermute | solution.py:51
  75.2 20.5 %collective-permute-start.20 = (bf16[2,2,64,1664]{3,2,1,0:T(8,128)(2,1)S(1)}, bf16[2,2,64,1664]{3,2,1,0:T(8,128)(2,1)S(1)}, u32[]{:S(2)}, u32[]{:S(2)}) collective-permute-start(bf16[2,2,64,1664]{3,2,1,0:T(8,128)(2,1)S(1)} %get-tuple-element.68.refs_0_), channel_id=1, source_target_pairs={{0,4},{1,5},{2,6},{3,7},{4,0},{5,1},{6,2},{7,3},{8,12},{9,13},{10,... | collective-permute-start | bytes 2555912 | tf_op jit(solution)/shard_map/ppermute | solution.py:51
  75.3 67.9 %collective-permute-start.34 = (bf16[1664,512]{1,0:T(8,128)(2,1)S(1)}, bf16[1664,512]{1,0:T(8,128)(2,1)S(1)}, u32[]{:S(2)}, u32[]{:S(2)}) collective-permute-start(bf16[1664,512]{1,0:T(8,128)(2,1)S(1)} %get-tuple-element.78), channel_id=1, source_target_pairs={{0,16},{16,0},{32,48},{48,32},{64,80},{80,64},{96,112},{112,96},{1... | collective-permute-start | bytes 5111816 | tf_op jit(solution)/shard_map/ppermute | solution.py:55
  84.0 61.2 %collective-permute-start.35 = (bf16[1664,512]{1,0:T(8,128)(2,1)S(1)}, bf16[1664,512]{1,0:T(8,128)(2,1)S(1)}, u32[]{:S(2)}, u32[]{:S(2)}) collective-permute-start(bf16[1664,512]{1,0:T(8,128)(2,1)S(1)} %get-tuple-element.79), channel_id=1, source_target_pairs={{0,16},{16,0},{32,48},{48,32},{64,80},{80,64},{96,112},{112,96},{1... | collective-permute-start | bytes 5111816 | tf_op jit(solution)/shard_map/ppermute | solution.py:55
  85.3 10.7 %collective-permute-start.19 = (bf16[2,2,32,1664]{3,2,1,0:T(8,128)(2,1)S(1)}, bf16[2,2,32,1664]{3,2,1,0:T(8,128)(2,1)S(1)}, u32[]{:S(2)}, u32[]{:S(2)}) collective-permute-start(bf16[2,2,32,1664]{3,2,1,0:T(8,128)(2,1)S(1)} %get-tuple-element.69.refs_0_), channel_id=1, source_target_pairs={{0,1},{1,0},{2,3},{3,2},{4,5},{5,4},{6,7},{7,6},{8,9},{9,8},{10,11... | collective-permute-start | bytes 1277960 | tf_op jit(solution)/shard_map/ppermute | solution.py:51
  93.1 8.5 %collective-permute-start.18 = (bf16[2,2,32,1664]{3,2,1,0:T(8,128)(2,1)S(1)}, bf16[2,2,32,1664]{3,2,1,0:T(8,128)(2,1)S(1)}, u32[]{:S(2)}, u32[]{:S(2)}) collective-permute-start(bf16[2,2,32,1664]{3,2,1,0:T(8,128)(2,1)S(1)} %get-tuple-element.70.refs_0_), channel_id=1, source_target_pairs={{0,3},{1,2},{2,1},{3,0},{4,7},{5,6},{6,5},{7,4},{8,11},{9,10},{10,... | collective-permute-start | bytes 1277960 | tf_op jit(solution)/shard_map/ppermute | solution.py:51
  95.8 8.4 %collective-permute-start.17 = (bf16[2,2,32,1664]{3,2,1,0:T(8,128)(2,1)S(1)}, bf16[2,2,32,1664]{3,2,1,0:T(8,128)(2,1)S(1)}, u32[]{:S(2)}, u32[]{:S(2)}) collective-permute-start(bf16[2,2,32,1664]{3,2,1,0:T(8,128)(2,1)S(1)} %get-tuple-element.72.refs_0_), channel_id=1, source_target_pairs={{0,1},{1,0},{2,3},{3,2},{4,5},{5,4},{6,7},{7,6},{8,9},{9,8},{10,11... | collective-permute-start | bytes 1277960 | tf_op jit(solution)/shard_map/ppermute | solution.py:51
  96.1 10.1 %collective-permute-start.24 = (bf16[2,2,32,1664]{3,2,1,0:T(8,128)(2,1)S(1)}, bf16[2,2,32,1664]{3,2,1,0:T(8,128)(2,1)S(1)}, u32[]{:S(2)}, u32[]{:S(2)}) collective-permute-start(bf16[2,2,32,1664]{3,2,1,0:T(8,128)(2,1)S(1)} %get-tuple-element.76.refs_0_), channel_id=1, source_target_pairs={{0,3},{1,2},{2,1},{3,0},{4,7},{5,6},{6,5},{7,4},{8,11},{9,10},{10,... | collective-permute-start | bytes 1277960 | tf_op jit(solution)/shard_map/ppermute | solution.py:51
  101.6 9.1 %collective-permute-start.23 = (bf16[2,2,32,1664]{3,2,1,0:T(8,128)(2,1)S(1)}, bf16[2,2,32,1664]{3,2,1,0:T(8,128)(2,1)S(1)}, u32[]{:S(2)}, u32[]{:S(2)}) collective-permute-start(bf16[2,2,32,1664]{3,2,1,0:T(8,128)(2,1)S(1)} %halves.20.refs_0_.mine), channel_id=1, source_target_pairs={{0,3},{1,2},{2,1},{3,0},{4,7},{5,6},{6,5},{7,4},{8,11},{9,10},{10,... | collective-permute-start | bytes 1277960 | tf_op jit(solution)/shard_map/ppermute | solution.py:51
  104.2 7.4 %collective-permute-start.22 = (bf16[2,2,32,1664]{3,2,1,0:T(8,128)(2,1)S(1)}, bf16[2,2,32,1664]{3,2,1,0:T(8,128)(2,1)S(1)}, u32[]{:S(2)}, u32[]{:S(2)}) collective-permute-start(bf16[2,2,32,1664]{3,2,1,0:T(8,128)(2,1)S(1)} %halves.21.refs_0_.mine), channel_id=1, source_target_pairs={{0,1},{1,0},{2,3},{3,2},{4,5},{5,4},{6,7},{7,6},{8,9},{9,8},{10,11... | collective-permute-start | bytes 1277960 | tf_op jit(solution)/shard_map/ppermute | solution.py:51
  106.1 9.1 %collective-permute-start.21 = (bf16[2,2,32,1664]{3,2,1,0:T(8,128)(2,1)S(1)}, bf16[2,2,32,1664]{3,2,1,0:T(8,128)(2,1)S(1)}, u32[]{:S(2)}, u32[]{:S(2)}) collective-permute-start(bf16[2,2,32,1664]{3,2,1,0:T(8,128)(2,1)S(1)} %halves.22.refs_0_.mine), channel_id=1, source_target_pairs={{0,3},{1,2},{2,1},{3,0},{4,7},{5,6},{6,5},{7,4},{8,11},{9,10},{10,... | collective-permute-start | bytes 1277960 | tf_op jit(solution)/shard_map/ppermute | solution.py:51
  110.7 7.3 %collective-permute-start.28 = (bf16[2,2,32,1664]{3,2,1,0:T(8,128)(2,1)S(1)}, bf16[2,2,32,1664]{3,2,1,0:T(8,128)(2,1)S(1)}, u32[]{:S(2)}, u32[]{:S(2)}) collective-permute-start(bf16[2,2,32,1664]{3,2,1,0:T(8,128)(2,1)S(1)} %halves.23.refs_0_.mine), channel_id=1, source_target_pairs={{0,1},{1,0},{2,3},{3,2},{4,5},{5,4},{6,7},{7,6},{8,9},{9,8},{10,11... | collective-permute-start | bytes 1277960 | tf_op jit(solution)/shard_map/ppermute | solution.py:51
  111.5 8.8 %collective-permute-start.27 = (bf16[2,32,1664]{2,1,0:T(8,128)(2,1)S(1)}, bf16[2,32,1664]{2,1,0:T(8,128)(2,1)S(1)}, u32[]{:S(2)}, u32[]{:S(2)}) collective-permute-start(bf16[2,32,1664]{2,1,0:T(8,128)(2,1)S(1)} %hidden.4.refs_0_.mine), channel_id=1, source_target_pairs={{0,1},{1,0},{2,3},{3,2},{4,5},{5,4},{6,7},{7,6},{8,9},{9,8},{10,11... | collective-permute-start | bytes 638984 | tf_op jit(solution)/shard_map/ppermute | solution.py:51
  115.3 7.5 %collective-permute-start.26 = (bf16[2,32,1664]{2,1,0:T(8,128)(2,1)S(1)}, bf16[2,32,1664]{2,1,0:T(8,128)(2,1)S(1)}, u32[]{:S(2)}, u32[]{:S(2)}) collective-permute-start(bf16[2,32,1664]{2,1,0:T(8,128)(2,1)S(1)} %hidden.5.refs_0_.mine), channel_id=1, source_target_pairs={{0,3},{1,2},{2,1},{3,0},{4,7},{5,6},{6,5},{7,4},{8,11},{9,10},{10,... | collective-permute-start | bytes 638984 | tf_op jit(solution)/shard_map/ppermute | solution.py:51
  118.0 6.8 %collective-permute-start.25 = (bf16[2,32,1664]{2,1,0:T(8,128)(2,1)S(1)}, bf16[2,32,1664]{2,1,0:T(8,128)(2,1)S(1)}, u32[]{:S(2)}, u32[]{:S(2)}) collective-permute-start(bf16[2,32,1664]{2,1,0:T(8,128)(2,1)S(1)} %hidden.6.refs_0_.mine), channel_id=1, source_target_pairs={{0,1},{1,0},{2,3},{3,2},{4,5},{5,4},{6,7},{7,6},{8,9},{9,8},{10,11... | collective-permute-start | bytes 638984 | tf_op jit(solution)/shard_map/ppermute | solution.py:51
  120.3 5.9 %collective-permute-start.32 = (bf16[2,32,1664]{2,1,0:T(8,128)(2,1)S(1)}, bf16[2,32,1664]{2,1,0:T(8,128)(2,1)S(1)}, u32[]{:S(2)}, u32[]{:S(2)}) collective-permute-start(bf16[2,32,1664]{2,1,0:T(8,128)(2,1)S(1)} %hidden.7.refs_0_.mine), channel_id=1, source_target_pairs={{0,3},{1,2},{2,1},{3,0},{4,7},{5,6},{6,5},{7,4},{8,11},{9,10},{10,... | collective-permute-start | bytes 638984 | tf_op jit(solution)/shard_map/ppermute | solution.py:51
  122.8 10.8 %collective-permute-start.31 = (bf16[2,64,1664]{2,1,0:T(8,128)(2,1)S(1)}, bf16[2,64,1664]{2,1,0:T(8,128)(2,1)S(1)}, u32[]{:S(2)}, u32[]{:S(2)}) collective-permute-start(bf16[2,64,1664]{2,1,0:T(8,128)(2,1)S(1)} %join.8.refs_0_.mine), channel_id=1, source_target_pairs={{0,12},{1,13},{2,14},{3,15},{4,8},{5,9},{6,10},{7,11},{8,4},{9,5},... | collective-permute-start | bytes 1277960 | tf_op jit(solution)/shard_map/ppermute | solution.py:51
  124.8 8.9 %collective-permute-start.30 = (bf16[2,64,1664]{2,1,0:T(8,128)(2,1)S(1)}, bf16[2,64,1664]{2,1,0:T(8,128)(2,1)S(1)}, u32[]{:S(2)}, u32[]{:S(2)}) collective-permute-start(bf16[2,64,1664]{2,1,0:T(8,128)(2,1)S(1)} %join.9.refs_0_.mine), channel_id=1, source_target_pairs={{0,4},{1,5},{2,6},{3,7},{4,0},{5,1},{6,2},{7,3},{8,12},{9,13},{10,... | collective-permute-start | bytes 1277960 | tf_op jit(solution)/shard_map/ppermute | solution.py:51
  126.2 12.0 %collective-permute-start.29 = (bf16[2,64,1664]{2,1,0:T(8,128)(2,1)S(1)}, bf16[2,64,1664]{2,1,0:T(8,128)(2,1)S(1)}, u32[]{:S(2)}, u32[]{:S(2)}) collective-permute-start(bf16[2,64,1664]{2,1,0:T(8,128)(2,1)S(1)} %join.10.refs_0_.mine), channel_id=1, source_target_pairs={{0,12},{1,13},{2,14},{3,15},{4,8},{5,9},{6,10},{7,11},{8,4},{9,5},... | collective-permute-start | bytes 1277960 | tf_op jit(solution)/shard_map/ppermute | solution.py:51
  133.6 7.3 %collective-permute-start.36 = (bf16[2,64,1664]{2,1,0:T(8,128)(2,1)S(1)}, bf16[2,64,1664]{2,1,0:T(8,128)(2,1)S(1)}, u32[]{:S(2)}, u32[]{:S(2)}) collective-permute-start(bf16[2,64,1664]{2,1,0:T(8,128)(2,1)S(1)} %join.11.refs_0_.mine), channel_id=1, source_target_pairs={{0,4},{1,5},{2,6},{3,7},{4,0},{5,1},{6,2},{7,3},{8,12},{9,13},{10,... | collective-permute-start | bytes 1277960 | tf_op jit(solution)/shard_map/ppermute | solution.py:51
  133.7 16.3 %collective-permute-start.37 = (bf16[2,128,1664]{2,1,0:T(8,128)(2,1)S(1)}, bf16[2,128,1664]{2,1,0:T(8,128)(2,1)S(1)}, u32[]{:S(2)}, u32[]{:S(2)}) collective-permute-start(bf16[2,128,1664]{2,1,0:T(8,128)(2,1)S(1)} %join.12.refs_0_), channel_id=1, source_target_pairs={{0,4},{1,5},{2,6},{3,7},{4,0},{5,1},{6,2},{7,3},{8,12},{9,13},{10,... | collective-permute-start | bytes 2555912 | tf_op jit(solution)/shard_map/ppermute | solution.py:51
  138.2 22.4 %collective-permute-start.41 = (bf16[2,128,1664]{2,1,0:T(8,128)(2,1)S(1)}, bf16[2,128,1664]{2,1,0:T(8,128)(2,1)S(1)}, u32[]{:S(2)}, u32[]{:S(2)}) collective-permute-start(bf16[2,128,1664]{2,1,0:T(8,128)(2,1)S(1)} %join.13.refs_0_), channel_id=1, source_target_pairs={{0,12},{1,13},{2,14},{3,15},{4,8},{5,9},{6,10},{7,11},{8,4},{9,5},... | collective-permute-start | bytes 2555912 | tf_op jit(solution)/shard_map/ppermute | solution.py:51
  140.9 18.3 %collective-permute-start.33 = (bf16[2,128,1664]{2,1,0:T(8,128)(2,1)S(1)}, bf16[2,128,1664]{2,1,0:T(8,128)(2,1)S(1)}, u32[]{:S(2)}, u32[]{:S(2)}) collective-permute-start(bf16[2,128,1664]{2,1,0:T(8,128)(2,1)S(1)} %join.14.refs_0_), channel_id=1, source_target_pairs={{0,4},{1,5},{2,6},{3,7},{4,0},{5,1},{6,2},{7,3},{8,12},{9,13},{10,... | collective-permute-start | bytes 2555912 | tf_op jit(solution)/shard_map/ppermute | solution.py:51
  143.2 18.6 %collective-permute-start.40 = (bf16[2,128,1664]{2,1,0:T(8,128)(2,1)S(1)}, bf16[2,128,1664]{2,1,0:T(8,128)(2,1)S(1)}, u32[]{:S(2)}, u32[]{:S(2)}) collective-permute-start(bf16[2,128,1664]{2,1,0:T(8,128)(2,1)S(1)} %join.15.refs_3_.refs_0_), channel_id=1, source_target_pairs={{0,12},{1,13},{2,14},{3,15},{4,8},{5,9},{6,10},{7,11},{8,4},{9,5},... | collective-permute-start | bytes 2555912 | tf_op jit(solution)/shard_map/ppermute | solution.py:51
  163.2 4.9 %collective-permute-start.42 = (bf16[2,128,1024]{2,1,0:T(8,128)(2,1)S(1)}, bf16[2,128,1024]{2,1,0:T(8,128)(2,1)S(1)}, u32[]{:S(2)}, u32[]{:S(2)}) collective-permute-start(bf16[2,128,1024]{2,1,0:T(8,128)(2,1)S(1)} %get-tuple-element.84), channel_id=1, source_target_pairs={{0,16},{16,0},{32,48},{48,32},{64,80},{80,64},{96,112},{112,96},{1... | collective-permute-start | bytes 1572872 | tf_op jit(solution)/shard_map/ppermute | solution.py:55
  166.5 5.0 %collective-permute-start.38 = (bf16[2,128,1024]{2,1,0:T(8,128)(2,1)S(1)}, bf16[2,128,1024]{2,1,0:T(8,128)(2,1)S(1)}, u32[]{:S(2)}, u32[]{:S(2)}) collective-permute-start(bf16[2,128,1024]{2,1,0:T(8,128)(2,1)S(1)} %get-tuple-element.82.refs_4_), channel_id=1, source_target_pairs={{0,16},{16,0},{32,48},{48,32},{64,80},{80,64},{96,112},{112,96},{1... | collective-permute-start | bytes 1572872 | tf_op jit(solution)/shard_map/ppermute | solution.py:55
  168.3 9.6 %collective-permute-start.43 = (bf16[128,1024]{1,0:T(8,128)(2,1)S(1)}, bf16[128,1024]{1,0:T(8,128)(2,1)S(1)}, u32[]{:S(2)}, u32[]{:S(2)}) collective-permute-start(bf16[128,1024]{1,0:T(8,128)(2,1)S(1)} %get-tuple-element.85), channel_id=1, source_target_pairs={{0,32},{16,48},{32,64},{48,80},{64,96},{80,112},{96,0},{112,16},{1... | collective-permute-start | bytes 786440 | tf_op jit(solution)/shard_map/ppermute | solution.py:59
  168.3 14.0 %collective-permute-start.44 = (bf16[128,1024]{1,0:T(8,128)(2,1)S(1)}, bf16[128,1024]{1,0:T(8,128)(2,1)S(1)}, u32[]{:S(2)}, u32[]{:S(2)}) collective-permute-start(bf16[128,1024]{1,0:T(8,128)(2,1)S(1)} %get-tuple-element.86), channel_id=1, source_target_pairs={{0,96},{16,112},{32,0},{48,16},{64,32},{80,48},{96,64},{112,80},{1... | collective-permute-start | bytes 786440 | tf_op jit(solution)/shard_map/ppermute | solution.py:59
  171.8 12.5 %collective-permute-start.39 = (bf16[128,1024]{1,0:T(8,128)(2,1)S(1)}, bf16[128,1024]{1,0:T(8,128)(2,1)S(1)}, u32[]{:S(2)}, u32[]{:S(2)}) collective-permute-start(bf16[128,1024]{1,0:T(8,128)(2,1)S(1)} %fusion.4), channel_id=1, source_target_pairs={{0,64},{16,80},{32,96},{48,112},{64,0},{80,16},{96,32},{112,48},{1... | collective-permute-start | bytes 786440 | tf_op jit(solution)/shard_map/ppermute | solution.py:59

commit v5 on v4

--- a/solution.py
+++ b/solution.py
@@ -11,11 +11,11 @@
 F32 = jnp.float32
 
 TIMES = {
-    "down": 2.5,
+    "down": 0.4,
     "halves": 2.0,
     "hidden": 2.0,
     "join": 2.0,
-    "stack": 1.0,
+    "stack": 0.1,
 }
 
 PAIR = {"e": (1, 0, 3, 2), "o": (3, 2, 1, 0)}
@@ -125,7 +125,7 @@
         after,
         [pltpu.SemaphoreType.DMA((len(shapes),))],
         specs=[pl.BlockSpec(memory_space=pltpu.HBM)] * len(weights),
-        time=1.5 * len(weights) * len(parts),
+        time=5.0 * len(weights) * len(parts),
     )
     return [out[i : i + len(pieces)] for i in range(0, len(out), len(pieces))]
 
@@ -199,59 +199,54 @@
         after,
         [pltpu.VMEM((rows, 1024), BF)] * 2,
         8,
-        time=1.5,
+        time=1.0,
     )
 
 
-def down_body(flow, first, last, *refs):
-    rows, pieces, refs = refs[0], refs[1:3], refs[3:]
-    outs = refs[-1:]
+def down_body(flow, kind, t, count, *refs):
+    rows, pieces, refs = refs[:count], refs[count : count + 2], refs[count + 2 :]
     mask = mask_of(flow)
-    left = jnp.concatenate((rows[0], rows[1]), axis=0)
+    blocks = [block[i] for block in rows for i in range(block.shape[0])]
+    left = jnp.concatenate(blocks, axis=0) if len(blocks) > 1 else blocks[0]
     for j in range(4):
         columns = pl.ds(j * 256, 256)
         weight = pieces[j // 2][:, j % 2 * 256 : (j % 2 + 1) * 256]
         res = jnp.dot(left, weight, preferred_element_type=F32)
-        if first:
-            outs[0][:, columns] = res
+        if kind == "half":
+            refs[-1][:, columns] = res
             continue
-        for t in range(2):
+        for i in range(len(blocks)):
+            base = (t + i) * 128
             for r in range(16):
-                place = r ^ mask
+                spot = pl.ds(pl.multiple_of((r ^ mask) * 16, 16), 16)
                 if r < 8:
-                    value = res[t * 128 + r * 16 : t * 128 + (r + 1) * 16]
+                    value = res[i * 128 + r * 16 : i * 128 + (r + 1) * 16]
                 else:
-                    value = refs[0][pl.ds(t * 128 + (r - 8) * 16, 16), columns]
-                spot = pl.ds(pl.multiple_of(place * 16, 16), 16)
-                outs[0][t, spot, columns] = value
-    if last:
+                    value = refs[0][pl.ds(base + (r - 8) * 16, 16), columns]
+                refs[-1][i, spot, columns] = value
+    if kind == "last":
         send, keep, total = refs[-3:]
-        keep[...] = total[:, :128] + refs[1][:, :128]
-        send[...] = (total[:, 128:] + refs[1][:, 128:]).astype(BF)
-
-
-def down(flow, rows, weights, half=None, before=None, after=()):
-    first, last = half is None, before is not None
-    if first:
+        keep[...] = total[0, :128] + refs[1][t, :128]
+        send[...] = (total[0, 128:] + refs[1][t, 128:]).astype(BF)
+
+
+def down(flow, kind, rows, weights, extra=(), t=0, after=()):
+    if kind == "half":
         shapes = [jax.ShapeDtypeStruct((256, 1024), F32)]
-    elif last:
-        shapes = [
-            jax.ShapeDtypeStruct((2, 128, 1024), BF),
-            jax.ShapeDtypeStruct((2, 128, 1024), F32),
-        ]
+    elif kind == "last":
+        shapes = [jax.ShapeDtypeStruct((128, 1024), BF), jax.ShapeDtypeStruct((128, 1024), F32)]
     else:
         shapes = [jax.ShapeDtypeStruct((2, 256, 1024), F32)]
-    extra = [a for a in (half, before) if a is not None]
     out = kernel(
-        functools.partial(down_body, flow, first, last),
+        functools.partial(down_body, flow, kind, t, len(rows)),
         "down",
-        (rows, *weights, *extra),
+        (*rows, *weights, *extra),
         shapes,
         after,
-        [pltpu.VMEM((2, 256, 1024), F32)] if last else (),
+        [pltpu.VMEM((1, 256, 1024), F32)] if kind == "last" else (),
         limit=4,
     )
-    return out if last else out[0]
+    return out if kind == "last" else out[0]
 
 
 def halves_body(before, keep, came, *refs):
@@ -298,15 +293,18 @@
     return kernel(hidden_body, "hidden", (mine, theirs), [shape], after)[0]
 
 
-def join_body(theirs, mine, *refs):
+def join_body(count, theirs, mine, *refs):
     rows = mine.shape[1]
-    refs[-1][:, :rows] = theirs[...]
-    refs[-1][:, rows:] = mine[...]
-
-
-def join(theirs, mine, after):
-    shape = jax.ShapeDtypeStruct((2, 2 * mine.shape[1], HALF), BF)
-    return kernel(join_body, "join", (theirs, mine), [shape], after)[0]
+    each = 2 // count
+    for i, out in enumerate(refs[-count:]):
+        out[:, :rows] = theirs[i * each : (i + 1) * each]
+        out[:, rows:] = mine[i * each : (i + 1) * each]
+
+
+def join(theirs, mine, count=1, after=()):
+    shape = jax.ShapeDtypeStruct((2 // count, 2 * mine.shape[1], HALF), BF)
+    body = functools.partial(join_body, count)
+    return kernel(body, "join", (theirs, mine), [shape] * count, after)
 
 
 def stack_body(first, second, *refs):
@@ -332,15 +330,17 @@
         return out
 
 
-TURNS = "oguj012301w230123012301230123012301230213"
+TURNS = "ogj1u02310w23012301230123012301012323012323"
 
 
 def local(tokens, gate_weight, up_weight, down_weight):
     line = Line()
     after, before = shift(tokens, -1), shift(tokens, 1)
     beside, far = swap(tokens), shift(tokens, 2)
+    line.last = (beside,)
     near = line(hold, tokens)
-    pair_a = [(near[None], beside[None]), (far[None], swap(far)[None])]
+    far_beside = swap(far)
+    pair_a = [(near[None], beside[None]), (far[None], far_beside[None])]
     sides = []
     own, other = {}, {}
     finished = {}
@@ -369,16 +369,26 @@
         came = exchange(rows, flow, 3)
         yield
         rows = line(hidden, rows, came)
-        for step in (2, 1):
-            theirs = exchange(rows, flow, step)
+        theirs = exchange(rows, flow, 2)
+        yield
+        (rows,) = line(join, theirs, rows)
+        theirs = exchange(rows, flow, 1)
+        yield
+        rows = line(join, theirs, rows, 1 if u < 2 else 2)
+        theirs = [exchange(part, flow, 0) for part in rows[::-1]]
+        yield
+        half = line(down, flow, "half", rows, held["w"])
+        yield
+        if u < 2:
+            finished[u] = line(down, flow, "all", theirs, held["w"], (half,))
             yield
-            rows = line(join, theirs, rows)
-        theirs = exchange(rows, flow, 0)
-        yield
-        half = line(down, flow, rows, held["w"])
-        yield
-        finished[u] = line(down, flow, theirs, held["w"], half, finished.get(u - 2))
-        yield
+            return
+        before = finished[u - 2]
+        for t in (1, 0):
+            part = line(down, flow, "last", [theirs[1 - t]], held["w"], (half, before), t)
+            send, keep = part
+            finished[u, t] = keep + swap(send).astype(F32)
+            yield
 
     units = [unit(u) for u in range(4)]
     for turn in TURNS:
@@ -397,14 +407,11 @@
         else:
             next(units[int(turn)])
 
-    (a_send, a_keep), (b_send, b_keep) = finished[2], finished[3]
-    a_total = a_keep + swap(a_send).astype(F32)
-    b_total = b_keep + swap(b_send).astype(F32)
-    from_opposite = shift(a_total[1].astype(BF), 2)
-    from_before = shift(b_total[0].astype(BF), 1)
-    from_after = shift(b_total[1].astype(BF), -1)
-    total = a_total[0] + from_opposite.astype(F32)
-    total = total + from_before.astype(F32) + from_after.astype(F32)
+    from_opposite = shift(finished[2, 1].astype(BF), 2)
+    from_after = shift(finished[3, 1].astype(BF), -1)
+    from_before = shift(finished[3, 0].astype(BF), 1)
+    total = finished[2, 0] + from_opposite.astype(F32)
+    total = total + from_after.astype(F32) + from_before.astype(F32)
     return total.astype(BF)
 
 

time: 185 us -> 182 us (0.984)
    ppermute x28 -> x30, starting transfers between devices: 34 us -> 27.2 us  [exchange(): return lax.ppermute(a, ('group', 'mp'), pairs)]
    ppermute x11 -> x13, starting transfers between devices: 9.7 us -> 15.8 us  [swap(): return lax.ppermute(a, 'group', SWAP)]
    ppermute x6, waiting for transfers between devices: 16.6 us -> 11.7 us  [shift(): lax.ppermute(a, 'group', [(g, (g + 2 * chips) % 8) for g in range(8)])]
    ppermute x28 -> x30, waiting for transfers between devices: 69.4 us -> 71.9 us  [exchange(): return lax.ppermute(a, ('group', 'mp'), pairs)]
    pallas_call x42 -> x44, Pallas kernels: 39.6 us -> 40 us  [kernel(): pl.pallas_call(body, in_specs=specs + [ANY] * len(after), out_specs=[VMEM...]
  transfers between devices with their start and end apart: 45 -> 49, of which waited for: 24 -> 23; matrix products, arithmetic and copies ran while one was open for 0% -> 0% of each run, Pallas kernels for 21% -> 22%
where the time goes in v5:
time: 182 us
  waiting for transfers between devices  86.8 us (48%)
  starting transfers between devices  53.9 us (30%)
  Pallas kernels  40 us (22%)
    ppermute x30, waiting for transfers between devices, exchange(): return lax.ppermute(a, ('group', 'mp'), pairs)  71.9 us
    pallas_call x44, Pallas kernels, kernel(): pl.pallas_call(body, in_specs=specs + [ANY] * len(after), out_specs=[VMEM...  40 us
    ppermute x30, starting transfers between devices, exchange(): return lax.ppermute(a, ('group', 'mp'), pairs)  27.2 us
    ppermute x13, starting transfers between devices, swap(): return lax.ppermute(a, 'group', SWAP)  15.8 us
    ppermute x6, waiting for transfers between devices, shift(): lax.ppermute(a, 'group', [(g, (g + 2 * chips) % 8) for g in range(8)])  11.7 us
    ppermute x6, starting transfers between devices, shift(): lax.ppermute(a, 'group', [(g, (g + 2 * chips) % 8) for g in range(8)])  10.9 us
  transfers between devices with their start and end apart: 49, of which 23 were waited for; matrix products, arithmetic and copies ran while one was open for 0% of the time, Pallas kernels for 22%

profile of v5, /device:TPU:1, one launch (start us, length us, event | category | flops | bytes accessed | tf_op | source)
XLA Modules:
  0.0 182.3 jit_solution(518063255628688047)
XLA Ops:
  0.0 1.4 collective-permute-start
  1.4 1.7 collective-permute-start.6
  3.1 2.1 %collective-permute-start.5 = (bf16[128,1024]{1,0:T(8,128)(2,1)}, bf16[128,1024]{1,0:T(8,128)(2,1)S(1)}, u32[]{:S(2)}, u32[]{:S(2)}) collective-permute-start(bf16[128,1024]{1,0:T(8,128)(2,1)} %source.1), channel_id=1, source_target_pairs={{0,96},{16,112},{32,0},{48,16},{64,32},{80,48},{96,64},{112,80},{1... | collective-permute-start | bytes 786440 | tf_op jit(solution)/shard_map/ppermute | solution.py:59
  6.3 3.1 %cut.4 = (bf16[1024,896]{1,0:T(8,128)(2,1)S(1)}, bf16[1024,768]{1,0:T(8,128)(2,1)S(1)}, bf16[1024,896]{1,0:T(8,128)(2,1)S(1)}, bf16[1024,768]{1,0:T(8,128)(2,1)S(1)}) custom-call(bf16[1024,3328]{1,0:T(8,128)(2,1)} %refs_0_.5, bf16[1024,3328]{1,0:T(8,128)(2,1)} %refs_0_.6, bf16[128,1024]{1,0:T(8,128)(2,1)S(1)} %stack.2.refs_2_), custom_call_target="tpu_custom_call" | custom-call | flops 11500000256 | tf_op jit(solution)/shard_map/cut/pallas_call | solution.py:80
  9.3 2.0 %cut.5 = (bf16[1024,896]{1,0:T(8,128)(2,1)S(1)}, bf16[1024,768]{1,0:T(8,128)(2,1)S(1)}) custom-call(bf16[1024,3328]{1,0:T(8,128)(2,1)} %refs_0_.5, bf16[1024,896]{1,0:T(8,128)(2,1)S(1)} %get-tuple-element.53.refs_1_.refs_2_.refs_4_), custom_call_target="tpu_custom_call" | custom-call | flops 5750000128 | tf_op jit(solution)/shard_map/cut/pallas_call | solution.py:80
  13.0 2.6 %collective-permute-start.1 = (bf16[128,1024]{1,0:T(8,128)(2,1)S(1)}, bf16[128,1024]{1,0:T(8,128)(2,1)S(1)}, u32[]{:S(2)}, u32[]{:S(2)}) collective-permute-start(bf16[128,1024]{1,0:T(8,128)(2,1)S(1)} %copy-done), channel_id=1, source_target_pairs={{0,64},{16,80},{32,96},{48,112},{64,0},{80,16},{96,32},{112,48},{1... | collective-permute-start | bytes 786440 | tf_op jit(solution)/shard_map/ppermute | solution.py:59
  16.3 3.7 %project.4 = (bf16[2,2,128,1664]{3,2,1,0:T(8,128)(2,1)S(1)}, bf16[2,2,128,1664]{3,2,1,0:T(8,128)(2,1)S(1)}) custom-call(bf16[2,128,1024]{2,1,0:T(8,128)(2,1)S(1)} %stack.3.refs_0_.refs_6_, bf16[2,128,1024]{2,1,0:T(8,128)(2,1)S(1)} %collective-permute-done.7.refs_1_, bf16[1024,896]{1,0:T(8,128)(2,1)S(1)} %get-tuple-element.53.refs_1_.refs_2_.refs_4_, ...), custom_call_target="tpu_custom_call" | custom-call | flops 1150000000 | tf_op jit(solution)/shard_map/project/pallas_call | solution.py:80
  20.0 2.0 %cut.6 = (bf16[1024,896]{1,0:T(8,128)(2,1)S(1)}, bf16[1024,768]{1,0:T(8,128)(2,1)S(1)}) custom-call(bf16[1024,3328]{1,0:T(8,128)(2,1)} %refs_0_.6, bf16[2,2,128,1664]{3,2,1,0:T(8,128)(2,1)S(1)} %get-tuple-element.59.refs_1_), custom_call_target="tpu_custom_call" | custom-call | flops 5750000128 | tf_op jit(solution)/shard_map/cut/pallas_call | solution.py:80
  23.2 3.1 %collective-permute-done.2 = bf16[128,1024]{1,0:T(8,128)(2,1)S(1)} collective-permute-done((bf16[128,1024]{1,0:T(8,128)(2,1)S(1)}, bf16[128,1024]{1,0:T(8,128)(2,1)S(1)}, u32[]{:S(2)}, u32[]{:S(2)}) %collective-permute-start.2) | collective-permute-done | bytes 262176 | tf_op jit(solution)/shard_map/ppermute | solution.py:55
  26.3 2.7 %collective-permute-start.12 = (bf16[2,2,128,1664]{3,2,1,0:T(8,128)(2,1)S(1)}, bf16[2,2,128,1664]{3,2,1,0:T(8,128)(2,1)S(1)}, u32[]{:S(2)}, u32[]{:S(2)}) collective-permute-start(bf16[2,2,128,1664]{3,2,1,0:T(8,128)(2,1)S(1)} %get-tuple-element.59.refs_1_), channel_id=1, source_target_pairs={{0,12},{1,13},{2,14},{3,15},{4,8},{5,9},{6,10},{7,11},{8,4},{9,5},... | collective-permute-start | bytes 5111816 | tf_op jit(solution)/shard_map/ppermute | solution.py:51
  29.0 3.7 %project.5 = (bf16[2,2,128,1664]{3,2,1,0:T(8,128)(2,1)S(1)}, bf16[2,2,128,1664]{3,2,1,0:T(8,128)(2,1)S(1)}) custom-call(bf16[1,128,1024]{2,1,0:T(8,128)(2,1)S(1)} %bitcast.6, bf16[1,128,1024]{2,1,0:T(8,128)(2,1)S(1)} %bitcast.4, bf16[1,128,1024]{2,1,0:T(8,128)(2,1)S(1)} %bitcast.8, bf16[1,128,1024]{2,1,0:T(8,128)(2,1)S(1)} %bitcast.10, ...), custom_call_target="tpu_custom_call" | custom-call | flops 1150000000 | tf_op jit(solution)/shard_map/project/pallas_call | solution.py:80
  32.9 3.7 %project.6 = (bf16[2,2,128,1664]{3,2,1,0:T(8,128)(2,1)S(1)}, bf16[2,2,128,1664]{3,2,1,0:T(8,128)(2,1)S(1)}) custom-call(bf16[1,128,1024]{2,1,0:T(8,128)(2,1)S(1)} %bitcast.7, bf16[1,128,1024]{2,1,0:T(8,128)(2,1)S(1)} %bitcast.5, bf16[1,128,1024]{2,1,0:T(8,128)(2,1)S(1)} %bitcast.9, bf16[1,128,1024]{2,1,0:T(8,128)(2,1)S(1)} %bitcast.11, ...), custom_call_target="tpu_custom_call" | custom-call | flops 1150000000 | tf_op jit(solution)/shard_map/project/pallas_call | solution.py:80
  36.6 1.7 collective-permute-start.10
  38.3 3.7 %project.7 = (bf16[2,2,128,1664]{3,2,1,0:T(8,128)(2,1)S(1)}, bf16[2,2,128,1664]{3,2,1,0:T(8,128)(2,1)S(1)}) custom-call(bf16[2,128,1024]{2,1,0:T(8,128)(2,1)S(1)} %stack.3.refs_0_.refs_6_, bf16[2,128,1024]{2,1,0:T(8,128)(2,1)S(1)} %collective-permute-done.7.refs_1_, bf16[1024,896]{1,0:T(8,128)(2,1)S(1)} %collective-permute-done.3.refs_4_.refs_2_, ...), custom_call_target="tpu_custom_call" | custom-call | flops 1150000000 | tf_op jit(solution)/shard_map/project/pallas_call | solution.py:80
  42.2 6.4 %collective-permute-done.12.came = bf16[2,2,128,1664]{3,2,1,0:T(8,128)(2,1)S(1)} collective-permute-done((bf16[2,2,128,1664]{3,2,1,0:T(8,128)(2,1)S(1)}, bf16[2,2,128,1664]{3,2,1,0:T(8,128)(2,1)S(1)}, u32[]{:S(2)}, u32[]{:S(2)}) %collective-permute-start.12) | collective-permute-done | bytes 1703968 | tf_op jit(solution)/shard_map/ppermute | solution.py:51
  49.0 4.8 %collective-permute-done.11.came = bf16[2,2,128,1664]{3,2,1,0:T(8,128)(2,1)S(1)} collective-permute-done((bf16[2,2,128,1664]{3,2,1,0:T(8,128)(2,1)S(1)}, bf16[2,2,128,1664]{3,2,1,0:T(8,128)(2,1)S(1)}, u32[]{:S(2)}, u32[]{:S(2)}) %collective-permute-start.11) | collective-permute-done | bytes 1703968 | tf_op jit(solution)/shard_map/ppermute | solution.py:51
  54.3 3.0 %cut.7 = (bf16[1664,512]{1,0:T(8,128)(2,1)S(1)}, bf16[1664,512]{1,0:T(8,128)(2,1)S(1)}, bf16[1664,512]{1,0:T(8,128)(2,1)S(1)}, bf16[1664,512]{1,0:T(8,128)(2,1)S(1)}) custom-call(bf16[3328,1024]{1,0:T(8,128)(2,1)} %refs_0_.7, bf16[2,2,64,1664]{3,2,1,0:T(8,128)(2,1)S(1)} %get-tuple-element.69.refs_1_), custom_call_target="tpu_custom_call" | custom-call | flops 11500000256 | tf_op jit(solution)/shard_map/cut/pallas_call | solution.py:80
  57.4 14.7 %collective-permute-done.10.came = bf16[2,2,128,1664]{3,2,1,0:T(8,128)(2,1)S(1)} collective-permute-done((bf16[2,2,128,1664]{3,2,1,0:T(8,128)(2,1)S(1)}, bf16[2,2,128,1664]{3,2,1,0:T(8,128)(2,1)S(1)}, u32[]{:S(2)}, u32[]{:S(2)}) %collective-permute-start.10) | collective-permute-done | bytes 1703968 | tf_op jit(solution)/shard_map/ppermute | solution.py:51
  73.1 1.7 collective-permute-start.34
  77.0 4.2 %collective-permute-done.14.came = bf16[2,2,64,1664]{3,2,1,0:T(8,128)(2,1)S(1)} collective-permute-done((bf16[2,2,64,1664]{3,2,1,0:T(8,128)(2,1)S(1)}, bf16[2,2,64,1664]{3,2,1,0:T(8,128)(2,1)S(1)}, u32[]{:S(2)}, u32[]{:S(2)}) %collective-permute-start.14) | collective-permute-done | bytes 852000 | tf_op jit(solution)/shard_map/ppermute | solution.py:51
  81.2 1.2 collective-permute-start.19
  82.6 3.0 %collective-permute-done.13.came = bf16[2,2,64,1664]{3,2,1,0:T(8,128)(2,1)S(1)} collective-permute-done((bf16[2,2,64,1664]{3,2,1,0:T(8,128)(2,1)S(1)}, bf16[2,2,64,1664]{3,2,1,0:T(8,128)(2,1)S(1)}, u32[]{:S(2)}, u32[]{:S(2)}) %collective-permute-start.13) | collective-permute-done | bytes 852000 | tf_op jit(solution)/shard_map/ppermute | solution.py:51
  85.6 2.5 %collective-permute-start.18 = (bf16[2,2,32,1664]{3,2,1,0:T(8,128)(2,1)S(1)}, bf16[2,2,32,1664]{3,2,1,0:T(8,128)(2,1)S(1)}, u32[]{:S(2)}, u32[]{:S(2)}) collective-permute-start(bf16[2,2,32,1664]{3,2,1,0:T(8,128)(2,1)S(1)} %get-tuple-element.78.refs_0_), channel_id=1, source_target_pairs={{0,3},{1,2},{2,1},{3,0},{4,7},{5,6},{6,5},{7,4},{8,11},{9,10},{10,... | collective-permute-start | bytes 1277960 | tf_op jit(solution)/shard_map/ppermute | solution.py:51
  88.3 6.6 %collective-permute-done.20.came = bf16[2,2,64,1664]{3,2,1,0:T(8,128)(2,1)S(1)} collective-permute-done((bf16[2,2,64,1664]{3,2,1,0:T(8,128)(2,1)S(1)}, bf16[2,2,64,1664]{3,2,1,0:T(8,128)(2,1)S(1)}, u32[]{:S(2)}, u32[]{:S(2)}) %collective-permute-start.20) | collective-permute-done | bytes 852000 | tf_op jit(solution)/shard_map/ppermute | solution.py:51
  96.0 1.9 %collective-permute-start.24 = (bf16[2,2,32,1664]{3,2,1,0:T(8,128)(2,1)S(1)}, bf16[2,2,32,1664]{3,2,1,0:T(8,128)(2,1)S(1)}, u32[]{:S(2)}, u32[]{:S(2)}) collective-permute-start(bf16[2,2,32,1664]{3,2,1,0:T(8,128)(2,1)S(1)} %get-tuple-element.84.refs_0_), channel_id=1, source_target_pairs={{0,3},{1,2},{2,1},{3,0},{4,7},{5,6},{6,5},{7,4},{8,11},{9,10},{10,... | collective-permute-start | bytes 1277960 | tf_op jit(solution)/shard_map/ppermute | solution.py:51
  99.1 3.1 %collective-permute-done.17.came = bf16[2,2,32,1664]{3,2,1,0:T(8,128)(2,1)S(1)} collective-permute-done((bf16[2,2,32,1664]{3,2,1,0:T(8,128)(2,1)S(1)}, bf16[2,2,32,1664]{3,2,1,0:T(8,128)(2,1)S(1)}, u32[]{:S(2)}, u32[]{:S(2)}) %collective-permute-start.17) | collective-permute-done | bytes 426016 | tf_op jit(solution)/shard_map/ppermute | solution.py:51
  103.2 1.4 collective-permute-done.24.came
  104.6 1.8 collective-permute-start.21
  106.5 2.6 %collective-permute-done.23.theirs = bf16[2,2,32,1664]{3,2,1,0:T(8,128)(2,1)S(1)} collective-permute-done((bf16[2,2,32,1664]{3,2,1,0:T(8,128)(2,1)S(1)}, bf16[2,2,32,1664]{3,2,1,0:T(8,128)(2,1)S(1)}, u32[]{:S(2)}, u32[]{:S(2)}) %collective-permute-start.23) | collective-permute-done | bytes 426016 | tf_op jit(solution)/shard_map/ppermute | solution.py:51
  109.4 1.5 collective-permute-start.27
  111.1 2.6 %collective-permute-done.21.theirs = bf16[2,2,32,1664]{3,2,1,0:T(8,128)(2,1)S(1)} collective-permute-done((bf16[2,2,32,1664]{3,2,1,0:T(8,128)(2,1)S(1)}, bf16[2,2,32,1664]{3,2,1,0:T(8,128)(2,1)S(1)}, u32[]{:S(2)}, u32[]{:S(2)}) %collective-permute-start.21) | collective-permute-done | bytes 426016 | tf_op jit(solution)/shard_map/ppermute | solution.py:51
  113.7 1.8 collective-permute-start.26
  116.6 2.1 %collective-permute-done.27.theirs = bf16[2,32,1664]{2,1,0:T(8,128)(2,1)S(1)} collective-permute-done((bf16[2,32,1664]{2,1,0:T(8,128)(2,1)S(1)}, bf16[2,32,1664]{2,1,0:T(8,128)(2,1)S(1)}, u32[]{:S(2)}, u32[]{:S(2)}) %collective-permute-start.27) | collective-permute-done | bytes 213024 | tf_op jit(solution)/shard_map/ppermute | solution.py:51
  118.7 1.8 collective-permute-start.32
  121.5 3.2 %collective-permute-done.32.theirs = bf16[2,32,1664]{2,1,0:T(8,128)(2,1)S(1)} collective-permute-done((bf16[2,32,1664]{2,1,0:T(8,128)(2,1)S(1)}, bf16[2,32,1664]{2,1,0:T(8,128)(2,1)S(1)}, u32[]{:S(2)}, u32[]{:S(2)}) %collective-permute-start.32) | collective-permute-done | bytes 213024 | tf_op jit(solution)/shard_map/ppermute | solution.py:51
  124.7 6.5 %collective-permute-done.31.theirs = bf16[2,64,1664]{2,1,0:T(8,128)(2,1)S(1)} collective-permute-done((bf16[2,64,1664]{2,1,0:T(8,128)(2,1)S(1)}, bf16[2,64,1664]{2,1,0:T(8,128)(2,1)S(1)}, u32[]{:S(2)}, u32[]{:S(2)}) %collective-permute-start.31) | collective-permute-done | bytes 426016 | tf_op jit(solution)/shard_map/ppermute | solution.py:51
  131.2 1.5 collective-permute-start.37
  132.8 2.9 %collective-permute-done.29.theirs = bf16[2,64,1664]{2,1,0:T(8,128)(2,1)S(1)} collective-permute-done((bf16[2,64,1664]{2,1,0:T(8,128)(2,1)S(1)}, bf16[2,64,1664]{2,1,0:T(8,128)(2,1)S(1)}, u32[]{:S(2)}, u32[]{:S(2)}) %collective-permute-start.29) | collective-permute-done | bytes 426016 | tf_op jit(solution)/shard_map/ppermute | solution.py:51
  135.7 2.3 %collective-permute-start.39 = (bf16[2,128,1664]{2,1,0:T(8,128)(2,1)S(1)}, bf16[2,128,1664]{2,1,0:T(8,128)(2,1)S(1)}, u32[]{:S(2)}, u32[]{:S(2)}) collective-permute-start(bf16[2,128,1664]{2,1,0:T(8,128)(2,1)S(1)} %join.13.refs_3_.refs_0_), channel_id=1, source_target_pairs={{0,12},{1,13},{2,14},{3,15},{4,8},{5,9},{6,10},{7,11},{8,4},{9,5},... | collective-permute-start | bytes 2555912 | tf_op jit(solution)/shard_map/ppermute | solution.py:51
  142.1 5.4 %collective-permute-done.37.refs_0_ = bf16[2,128,1664]{2,1,0:T(8,128)(2,1)S(1)} collective-permute-done((bf16[2,128,1664]{2,1,0:T(8,128)(2,1)S(1)}, bf16[2,128,1664]{2,1,0:T(8,128)(2,1)S(1)}, u32[]{:S(2)}, u32[]{:S(2)}) %collective-permute-start.37) | collective-permute-done | bytes 852000 | tf_op jit(solution)/shard_map/ppermute | solution.py:51
  147.5 1.3 collective-permute-start.46
  151.0 1.2 down.14.refs_4_
  154.2 4.0 %collective-permute-start.42 = (bf16[128,1024]{1,0:T(8,128)(2,1)S(1)}, bf16[128,1024]{1,0:T(8,128)(2,1)S(1)}, u32[]{:S(2)}, u32[]{:S(2)}) collective-permute-start(bf16[128,1024]{1,0:T(8,128)(2,1)S(1)} %get-tuple-element.93.refs_5_), channel_id=1, source_target_pairs={{0,16},{16,0},{32,48},{48,32},{64,80},{80,64},{96,112},{112,96},{1... | collective-permute-start | bytes 786440 | tf_op jit(solution)/shard_map/ppermute | solution.py:55
  160.7 4.7 %collective-permute-start.47 = (bf16[128,1024]{1,0:T(8,128)(2,1)S(1)}, bf16[128,1024]{1,0:T(8,128)(2,1)S(1)}, u32[]{:S(2)}, u32[]{:S(2)}) collective-permute-start(bf16[128,1024]{1,0:T(8,128)(2,1)S(1)} %get-tuple-element.100), channel_id=1, source_target_pairs={{0,16},{16,0},{32,48},{48,32},{64,80},{80,64},{96,112},{112,96},{1... | collective-permute-start | bytes 786440 | tf_op jit(solution)/shard_map/ppermute | solution.py:55
  165.9 1.6 collective-permute-start.43
  168.3 2.1 %collective-permute-start.45 = (bf16[128,1024]{1,0:T(8,128)(2,1)S(1)}, bf16[128,1024]{1,0:T(8,128)(2,1)S(1)}, u32[]{:S(2)}, u32[]{:S(2)}) collective-permute-start(bf16[128,1024]{1,0:T(8,128)(2,1)S(1)} %add_convert_fusion.2), channel_id=1, source_target_pairs={{0,96},{16,112},{32,0},{48,16},{64,32},{80,48},{96,64},{112,80},{1... | collective-permute-start | bytes 786440 | tf_op jit(solution)/shard_map/ppermute | solution.py:59
  170.4 5.0 %collective-permute-done.43 = bf16[128,1024]{1,0:T(8,128)(2,1)S(1)} collective-permute-done((bf16[128,1024]{1,0:T(8,128)(2,1)S(1)}, bf16[128,1024]{1,0:T(8,128)(2,1)S(1)}, u32[]{:S(2)}, u32[]{:S(2)}) %collective-permute-start.43) | collective-permute-done | bytes 262176 | tf_op jit(solution)/shard_map/ppermute | solution.py:59
  175.4 6.0 %collective-permute-done.48 = bf16[128,1024]{1,0:T(8,128)(2,1)S(1)} collective-permute-done((bf16[128,1024]{1,0:T(8,128)(2,1)S(1)}, bf16[128,1024]{1,0:T(8,128)(2,1)S(1)}, u32[]{:S(2)}, u32[]{:S(2)}) %collective-permute-start.48) | collective-permute-done | bytes 262176 | tf_op jit(solution)/shard_map/ppermute | solution.py:59
  (100 shorter events, 28.1 us)
Async XLA Ops:
  0.0 5.3 %collective-permute-start = (bf16[128,1024]{1,0:T(8,128)(2,1)}, bf16[128,1024]{1,0:T(8,128)(2,1)S(1)}, u32[]{:S(2)}, u32[]{:S(2)}) collective-permute-start(bf16[128,1024]{1,0:T(8,128)(2,1)} %source.1), channel_id=1, source_target_pairs={{0,16},{16,0},{32,48},{48,32},{64,80},{80,64},{96,112},{112,96},{1... | collective-permute-start | bytes 786440 | tf_op jit(solution)/shard_map/ppermute | solution.py:55
  1.4 10.7 %collective-permute-start.6 = (bf16[128,1024]{1,0:T(8,128)(2,1)}, bf16[128,1024]{1,0:T(8,128)(2,1)S(1)}, u32[]{:S(2)}, u32[]{:S(2)}) collective-permute-start(bf16[128,1024]{1,0:T(8,128)(2,1)} %source.1), channel_id=1, source_target_pairs={{0,32},{16,48},{32,64},{48,80},{64,96},{80,112},{96,0},{112,16},{1... | collective-permute-start | bytes 786440 | tf_op jit(solution)/shard_map/ppermute | solution.py:59
  3.1 9.0 %collective-permute-start.5 = (bf16[128,1024]{1,0:T(8,128)(2,1)}, bf16[128,1024]{1,0:T(8,128)(2,1)S(1)}, u32[]{:S(2)}, u32[]{:S(2)}) collective-permute-start(bf16[128,1024]{1,0:T(8,128)(2,1)} %source.1), channel_id=1, source_target_pairs={{0,96},{16,112},{32,0},{48,16},{64,32},{80,48},{96,64},{112,80},{1... | collective-permute-start | bytes 786440 | tf_op jit(solution)/shard_map/ppermute | solution.py:59
  12.2 4.1 %collective-permute-start.7 = (bf16[2,128,1024]{2,1,0:T(8,128)(2,1)S(1)}, bf16[2,128,1024]{2,1,0:T(8,128)(2,1)S(1)}, u32[]{:S(2)}, u32[]{:S(2)}) collective-permute-start(bf16[2,128,1024]{2,1,0:T(8,128)(2,1)S(1)} %stack.3.refs_0_.refs_6_), channel_id=1, source_target_pairs={{0,16},{16,0},{32,48},{48,32},{64,80},{80,64},{96,112},{112,96},{1... | collective-permute-start | bytes 1572872 | tf_op jit(solution)/shard_map/ppermute | solution.py:55
  12.9 19.9 %collective-permute-start.4 = (bf16[1024,768]{1,0:T(8,128)(2,1)S(1)}, bf16[1024,768]{1,0:T(8,128)(2,1)S(1)}, u32[]{:S(2)}, u32[]{:S(2)}) collective-permute-start(bf16[1024,768]{1,0:T(8,128)(2,1)S(1)} %get-tuple-element.55), channel_id=1, source_target_pairs={{0,16},{16,0},{32,48},{48,32},{64,80},{80,64},{96,112},{112,96},{1... | collective-permute-start | bytes 4718600 | tf_op jit(solution)/shard_map/ppermute | solution.py:55
  13.0 9.2 %collective-permute-start.1 = (bf16[128,1024]{1,0:T(8,128)(2,1)S(1)}, bf16[128,1024]{1,0:T(8,128)(2,1)S(1)}, u32[]{:S(2)}, u32[]{:S(2)}) collective-permute-start(bf16[128,1024]{1,0:T(8,128)(2,1)S(1)} %copy-done), channel_id=1, source_target_pairs={{0,64},{16,80},{32,96},{48,112},{64,0},{80,16},{96,32},{112,48},{1... | collective-permute-start | bytes 786440 | tf_op jit(solution)/shard_map/ppermute | solution.py:59
  15.6 17.3 %collective-permute-start.3 = (bf16[1024,896]{1,0:T(8,128)(2,1)S(1)}, bf16[1024,896]{1,0:T(8,128)(2,1)S(1)}, u32[]{:S(2)}, u32[]{:S(2)}) collective-permute-start(bf16[1024,896]{1,0:T(8,128)(2,1)S(1)} %get-tuple-element.54.refs_0_), channel_id=1, source_target_pairs={{0,16},{16,0},{32,48},{48,32},{64,80},{80,64},{96,112},{112,96},{1... | collective-permute-start | bytes 5505032 | tf_op jit(solution)/shard_map/ppermute | solution.py:55
  22.0 10.8 %collective-permute-start.8 = (bf16[1024,896]{1,0:T(8,128)(2,1)S(1)}, bf16[1024,896]{1,0:T(8,128)(2,1)S(1)}, u32[]{:S(2)}, u32[]{:S(2)}) collective-permute-start(bf16[1024,896]{1,0:T(8,128)(2,1)S(1)} %get-tuple-element.60.refs_8_), channel_id=1, source_target_pairs={{0,16},{16,0},{32,48},{48,32},{64,80},{80,64},{96,112},{112,96},{1... | collective-permute-start | bytes 5505032 | tf_op jit(solution)/shard_map/ppermute | solution.py:55
  22.1 4.1 %collective-permute-start.2 = (bf16[128,1024]{1,0:T(8,128)(2,1)S(1)}, bf16[128,1024]{1,0:T(8,128)(2,1)S(1)}, u32[]{:S(2)}, u32[]{:S(2)}) collective-permute-start(bf16[128,1024]{1,0:T(8,128)(2,1)S(1)} %collective-permute-done.1), channel_id=1, source_target_pairs={{0,16},{16,0},{32,48},{48,32},{64,80},{80,64},{96,112},{112,96},{1... | collective-permute-start | bytes 786440 | tf_op jit(solution)/shard_map/ppermute | solution.py:55
  23.2 9.7 %collective-permute-start.9 = (bf16[1024,768]{1,0:T(8,128)(2,1)S(1)}, bf16[1024,768]{1,0:T(8,128)(2,1)S(1)}, u32[]{:S(2)}, u32[]{:S(2)}) collective-permute-start(bf16[1024,768]{1,0:T(8,128)(2,1)S(1)} %get-tuple-element.61), channel_id=1, source_target_pairs={{0,16},{16,0},{32,48},{48,32},{64,80},{80,64},{96,112},{112,96},{1... | collective-permute-start | bytes 4718600 | tf_op jit(solution)/shard_map/ppermute | solution.py:55
  26.3 22.2 %collective-permute-start.12 = (bf16[2,2,128,1664]{3,2,1,0:T(8,128)(2,1)S(1)}, bf16[2,2,128,1664]{3,2,1,0:T(8,128)(2,1)S(1)}, u32[]{:S(2)}, u32[]{:S(2)}) collective-permute-start(bf16[2,2,128,1664]{3,2,1,0:T(8,128)(2,1)S(1)} %get-tuple-element.59.refs_1_), channel_id=1, source_target_pairs={{0,12},{1,13},{2,14},{3,15},{4,8},{5,9},{6,10},{7,11},{8,4},{9,5},... | collective-permute-start | bytes 5111816 | tf_op jit(solution)/shard_map/ppermute | solution.py:51
  32.8 21.0 %collective-permute-start.11 = (bf16[2,2,128,1664]{3,2,1,0:T(8,128)(2,1)S(1)}, bf16[2,2,128,1664]{3,2,1,0:T(8,128)(2,1)S(1)}, u32[]{:S(2)}, u32[]{:S(2)}) collective-permute-start(bf16[2,2,128,1664]{3,2,1,0:T(8,128)(2,1)S(1)} %get-tuple-element.62.refs_8_), channel_id=1, source_target_pairs={{0,4},{1,5},{2,6},{3,7},{4,0},{5,1},{6,2},{7,3},{8,12},{9,13},{10,... | collective-permute-start | bytes 5111816 | tf_op jit(solution)/shard_map/ppermute | solution.py:51
  36.6 35.4 %collective-permute-start.10 = (bf16[2,2,128,1664]{3,2,1,0:T(8,128)(2,1)S(1)}, bf16[2,2,128,1664]{3,2,1,0:T(8,128)(2,1)S(1)}, u32[]{:S(2)}, u32[]{:S(2)}) collective-permute-start(bf16[2,2,128,1664]{3,2,1,0:T(8,128)(2,1)S(1)} %get-tuple-element.64.refs_6_), channel_id=1, source_target_pairs={{0,4},{1,5},{2,6},{3,7},{4,0},{5,1},{6,2},{7,3},{8,12},{9,13},{10,... | collective-permute-start | bytes 5111816 | tf_op jit(solution)/shard_map/ppermute | solution.py:51
  42.1 30.5 %collective-permute-start.16 = (bf16[2,2,128,1664]{3,2,1,0:T(8,128)(2,1)S(1)}, bf16[2,2,128,1664]{3,2,1,0:T(8,128)(2,1)S(1)}, u32[]{:S(2)}, u32[]{:S(2)}) collective-permute-start(bf16[2,2,128,1664]{3,2,1,0:T(8,128)(2,1)S(1)} %get-tuple-element.67.refs_0_), channel_id=1, source_target_pairs={{0,12},{1,13},{2,14},{3,15},{4,8},{5,9},{6,10},{7,11},{8,4},{9,5},... | collective-permute-start | bytes 5111816 | tf_op jit(solution)/shard_map/ppermute | solution.py:51
  48.9 32.3 %collective-permute-start.14 = (bf16[2,2,64,1664]{3,2,1,0:T(8,128)(2,1)S(1)}, bf16[2,2,64,1664]{3,2,1,0:T(8,128)(2,1)S(1)}, u32[]{:S(2)}, u32[]{:S(2)}) collective-permute-start(bf16[2,2,64,1664]{3,2,1,0:T(8,128)(2,1)S(1)} %get-tuple-element.68.refs_0_), channel_id=1, source_target_pairs={{0,4},{1,5},{2,6},{3,7},{4,0},{5,1},{6,2},{7,3},{8,12},{9,13},{10,... | collective-permute-start | bytes 2555912 | tf_op jit(solution)/shard_map/ppermute | solution.py:51
  54.2 21.7 %collective-permute-start.15 = (bf16[2,2,64,1664]{3,2,1,0:T(8,128)(2,1)S(1)}, bf16[2,2,64,1664]{3,2,1,0:T(8,128)(2,1)S(1)}, u32[]{:S(2)}, u32[]{:S(2)}) collective-permute-start(bf16[2,2,64,1664]{3,2,1,0:T(8,128)(2,1)S(1)} %get-tuple-element.69.refs_1_), channel_id=1, source_target_pairs={{0,12},{1,13},{2,14},{3,15},{4,8},{5,9},{6,10},{7,11},{8,4},{9,5},... | collective-permute-start | bytes 2555912 | tf_op jit(solution)/shard_map/ppermute | solution.py:51
  72.5 13.1 %collective-permute-start.13 = (bf16[2,2,64,1664]{3,2,1,0:T(8,128)(2,1)S(1)}, bf16[2,2,64,1664]{3,2,1,0:T(8,128)(2,1)S(1)}, u32[]{:S(2)}, u32[]{:S(2)}) collective-permute-start(bf16[2,2,64,1664]{3,2,1,0:T(8,128)(2,1)S(1)} %get-tuple-element.72.refs_0_), channel_id=1, source_target_pairs={{0,12},{1,13},{2,14},{3,15},{4,8},{5,9},{6,10},{7,11},{8,4},{9,5},... | collective-permute-start | bytes 2555912 | tf_op jit(solution)/shard_map/ppermute | solution.py:51
  73.0 21.9 %collective-permute-start.20 = (bf16[2,2,64,1664]{3,2,1,0:T(8,128)(2,1)S(1)}, bf16[2,2,64,1664]{3,2,1,0:T(8,128)(2,1)S(1)}, u32[]{:S(2)}, u32[]{:S(2)}) collective-permute-start(bf16[2,2,64,1664]{3,2,1,0:T(8,128)(2,1)S(1)} %get-tuple-element.76.refs_0_), channel_id=1, source_target_pairs={{0,4},{1,5},{2,6},{3,7},{4,0},{5,1},{6,2},{7,3},{8,12},{9,13},{10,... | collective-permute-start | bytes 2555912 | tf_op jit(solution)/shard_map/ppermute | solution.py:51
  73.1 67.4 %collective-permute-start.34 = (bf16[1664,512]{1,0:T(8,128)(2,1)S(1)}, bf16[1664,512]{1,0:T(8,128)(2,1)S(1)}, u32[]{:S(2)}, u32[]{:S(2)}) collective-permute-start(bf16[1664,512]{1,0:T(8,128)(2,1)S(1)} %get-tuple-element.88), channel_id=1, source_target_pairs={{0,16},{16,0},{32,48},{48,32},{64,80},{80,64},{96,112},{112,96},{1... | collective-permute-start | bytes 5111816 | tf_op jit(solution)/shard_map/ppermute | solution.py:55
  75.9 65.0 %collective-permute-start.35 = (bf16[1664,512]{1,0:T(8,128)(2,1)S(1)}, bf16[1664,512]{1,0:T(8,128)(2,1)S(1)}, u32[]{:S(2)}, u32[]{:S(2)}) collective-permute-start(bf16[1664,512]{1,0:T(8,128)(2,1)S(1)} %get-tuple-element.89), channel_id=1, source_target_pairs={{0,16},{16,0},{32,48},{48,32},{64,80},{80,64},{96,112},{112,96},{1... | collective-permute-start | bytes 5111816 | tf_op jit(solution)/shard_map/ppermute | solution.py:55
  81.2 14.8 %collective-permute-start.19 = (bf16[2,2,32,1664]{3,2,1,0:T(8,128)(2,1)S(1)}, bf16[2,2,32,1664]{3,2,1,0:T(8,128)(2,1)S(1)}, u32[]{:S(2)}, u32[]{:S(2)}) collective-permute-start(bf16[2,2,32,1664]{3,2,1,0:T(8,128)(2,1)S(1)} %get-tuple-element.77.refs_0_), channel_id=1, source_target_pairs={{0,1},{1,0},{2,3},{3,2},{4,5},{5,4},{6,7},{7,6},{8,9},{9,8},{10,11... | collective-permute-start | bytes 1277960 | tf_op jit(solution)/shard_map/ppermute | solution.py:51
  85.6 12.4 %collective-permute-start.18 = (bf16[2,2,32,1664]{3,2,1,0:T(8,128)(2,1)S(1)}, bf16[2,2,32,1664]{3,2,1,0:T(8,128)(2,1)S(1)}, u32[]{:S(2)}, u32[]{:S(2)}) collective-permute-start(bf16[2,2,32,1664]{3,2,1,0:T(8,128)(2,1)S(1)} %get-tuple-element.78.refs_0_), channel_id=1, source_target_pairs={{0,3},{1,2},{2,1},{3,0},{4,7},{5,6},{6,5},{7,4},{8,11},{9,10},{10,... | collective-permute-start | bytes 1277960 | tf_op jit(solution)/shard_map/ppermute | solution.py:51
  94.9 7.3 %collective-permute-start.17 = (bf16[2,2,32,1664]{3,2,1,0:T(8,128)(2,1)S(1)}, bf16[2,2,32,1664]{3,2,1,0:T(8,128)(2,1)S(1)}, u32[]{:S(2)}, u32[]{:S(2)}) collective-permute-start(bf16[2,2,32,1664]{3,2,1,0:T(8,128)(2,1)S(1)} %get-tuple-element.80.refs_0_), channel_id=1, source_target_pairs={{0,1},{1,0},{2,3},{3,2},{4,5},{5,4},{6,7},{7,6},{8,9},{9,8},{10,11... | collective-permute-start | bytes 1277960 | tf_op jit(solution)/shard_map/ppermute | solution.py:51
  96.0 8.6 %collective-permute-start.24 = (bf16[2,2,32,1664]{3,2,1,0:T(8,128)(2,1)S(1)}, bf16[2,2,32,1664]{3,2,1,0:T(8,128)(2,1)S(1)}, u32[]{:S(2)}, u32[]{:S(2)}) collective-permute-start(bf16[2,2,32,1664]{3,2,1,0:T(8,128)(2,1)S(1)} %get-tuple-element.84.refs_0_), channel_id=1, source_target_pairs={{0,3},{1,2},{2,1},{3,0},{4,7},{5,6},{6,5},{7,4},{8,11},{9,10},{10,... | collective-permute-start | bytes 1277960 | tf_op jit(solution)/shard_map/ppermute | solution.py:51
  98.0 11.1 %collective-permute-start.23 = (bf16[2,2,32,1664]{3,2,1,0:T(8,128)(2,1)S(1)}, bf16[2,2,32,1664]{3,2,1,0:T(8,128)(2,1)S(1)}, u32[]{:S(2)}, u32[]{:S(2)}) collective-permute-start(bf16[2,2,32,1664]{3,2,1,0:T(8,128)(2,1)S(1)} %halves.20.refs_0_.mine), channel_id=1, source_target_pairs={{0,3},{1,2},{2,1},{3,0},{4,7},{5,6},{6,5},{7,4},{8,11},{9,10},{10,... | collective-permute-start | bytes 1277960 | tf_op jit(solution)/shard_map/ppermute | solution.py:51
  102.2 7.3 %collective-permute-start.22 = (bf16[2,2,32,1664]{3,2,1,0:T(8,128)(2,1)S(1)}, bf16[2,2,32,1664]{3,2,1,0:T(8,128)(2,1)S(1)}, u32[]{:S(2)}, u32[]{:S(2)}) collective-permute-start(bf16[2,2,32,1664]{3,2,1,0:T(8,128)(2,1)S(1)} %halves.21.refs_0_.mine), channel_id=1, source_target_pairs={{0,1},{1,0},{2,3},{3,2},{4,5},{5,4},{6,7},{7,6},{8,9},{9,8},{10,11... | collective-permute-start | bytes 1277960 | tf_op jit(solution)/shard_map/ppermute | solution.py:51
  104.6 9.1 %collective-permute-start.21 = (bf16[2,2,32,1664]{3,2,1,0:T(8,128)(2,1)S(1)}, bf16[2,2,32,1664]{3,2,1,0:T(8,128)(2,1)S(1)}, u32[]{:S(2)}, u32[]{:S(2)}) collective-permute-start(bf16[2,2,32,1664]{3,2,1,0:T(8,128)(2,1)S(1)} %halves.22.refs_0_.mine), channel_id=1, source_target_pairs={{0,3},{1,2},{2,1},{3,0},{4,7},{5,6},{6,5},{7,4},{8,11},{9,10},{10,... | collective-permute-start | bytes 1277960 | tf_op jit(solution)/shard_map/ppermute | solution.py:51
  109.1 7.3 %collective-permute-start.28 = (bf16[2,2,32,1664]{3,2,1,0:T(8,128)(2,1)S(1)}, bf16[2,2,32,1664]{3,2,1,0:T(8,128)(2,1)S(1)}, u32[]{:S(2)}, u32[]{:S(2)}) collective-permute-start(bf16[2,2,32,1664]{3,2,1,0:T(8,128)(2,1)S(1)} %halves.23.refs_0_.mine), channel_id=1, source_target_pairs={{0,1},{1,0},{2,3},{3,2},{4,5},{5,4},{6,7},{7,6},{8,9},{9,8},{10,11... | collective-permute-start | bytes 1277960 | tf_op jit(solution)/shard_map/ppermute | solution.py:51
  109.4 9.3 %collective-permute-start.27 = (bf16[2,32,1664]{2,1,0:T(8,128)(2,1)S(1)}, bf16[2,32,1664]{2,1,0:T(8,128)(2,1)S(1)}, u32[]{:S(2)}, u32[]{:S(2)}) collective-permute-start(bf16[2,32,1664]{2,1,0:T(8,128)(2,1)S(1)} %hidden.4.refs_0_.mine), channel_id=1, source_target_pairs={{0,1},{1,0},{2,3},{3,2},{4,5},{5,4},{6,7},{7,6},{8,9},{9,8},{10,11... | collective-permute-start | bytes 638984 | tf_op jit(solution)/shard_map/ppermute | solution.py:51
  113.7 6.8 %collective-permute-start.26 = (bf16[2,32,1664]{2,1,0:T(8,128)(2,1)S(1)}, bf16[2,32,1664]{2,1,0:T(8,128)(2,1)S(1)}, u32[]{:S(2)}, u32[]{:S(2)}) collective-permute-start(bf16[2,32,1664]{2,1,0:T(8,128)(2,1)S(1)} %hidden.5.refs_0_.mine), channel_id=1, source_target_pairs={{0,3},{1,2},{2,1},{3,0},{4,7},{5,6},{6,5},{7,4},{8,11},{9,10},{10,... | collective-permute-start | bytes 638984 | tf_op jit(solution)/shard_map/ppermute | solution.py:51
  116.4 5.0 %collective-permute-start.25 = (bf16[2,32,1664]{2,1,0:T(8,128)(2,1)S(1)}, bf16[2,32,1664]{2,1,0:T(8,128)(2,1)S(1)}, u32[]{:S(2)}, u32[]{:S(2)}) collective-permute-start(bf16[2,32,1664]{2,1,0:T(8,128)(2,1)S(1)} %hidden.6.refs_0_.mine), channel_id=1, source_target_pairs={{0,1},{1,0},{2,3},{3,2},{4,5},{5,4},{6,7},{7,6},{8,9},{9,8},{10,11... | collective-permute-start | bytes 638984 | tf_op jit(solution)/shard_map/ppermute | solution.py:51
  118.7 5.9 %collective-permute-start.32 = (bf16[2,32,1664]{2,1,0:T(8,128)(2,1)S(1)}, bf16[2,32,1664]{2,1,0:T(8,128)(2,1)S(1)}, u32[]{:S(2)}, u32[]{:S(2)}) collective-permute-start(bf16[2,32,1664]{2,1,0:T(8,128)(2,1)S(1)} %hidden.7.refs_0_.mine), channel_id=1, source_target_pairs={{0,3},{1,2},{2,1},{3,0},{4,7},{5,6},{6,5},{7,4},{8,11},{9,10},{10,... | collective-permute-start | bytes 638984 | tf_op jit(solution)/shard_map/ppermute | solution.py:51
  120.6 10.5 %collective-permute-start.31 = (bf16[2,64,1664]{2,1,0:T(8,128)(2,1)S(1)}, bf16[2,64,1664]{2,1,0:T(8,128)(2,1)S(1)}, u32[]{:S(2)}, u32[]{:S(2)}) collective-permute-start(bf16[2,64,1664]{2,1,0:T(8,128)(2,1)S(1)} %join.8.refs_0_.mine), channel_id=1, source_target_pairs={{0,12},{1,13},{2,14},{3,15},{4,8},{5,9},{6,10},{7,11},{8,4},{9,5},... | collective-permute-start | bytes 1277960 | tf_op jit(solution)/shard_map/ppermute | solution.py:51
  121.4 9.8 %collective-permute-start.30 = (bf16[2,64,1664]{2,1,0:T(8,128)(2,1)S(1)}, bf16[2,64,1664]{2,1,0:T(8,128)(2,1)S(1)}, u32[]{:S(2)}, u32[]{:S(2)}) collective-permute-start(bf16[2,64,1664]{2,1,0:T(8,128)(2,1)S(1)} %join.9.refs_0_.mine), channel_id=1, source_target_pairs={{0,4},{1,5},{2,6},{3,7},{4,0},{5,1},{6,2},{7,3},{8,12},{9,13},{10,... | collective-permute-start | bytes 1277960 | tf_op jit(solution)/shard_map/ppermute | solution.py:51
  124.6 11.1 %collective-permute-start.29 = (bf16[2,64,1664]{2,1,0:T(8,128)(2,1)S(1)}, bf16[2,64,1664]{2,1,0:T(8,128)(2,1)S(1)}, u32[]{:S(2)}, u32[]{:S(2)}) collective-permute-start(bf16[2,64,1664]{2,1,0:T(8,128)(2,1)S(1)} %join.10.refs_0_.mine), channel_id=1, source_target_pairs={{0,12},{1,13},{2,14},{3,15},{4,8},{5,9},{6,10},{7,11},{8,4},{9,5},... | collective-permute-start | bytes 1277960 | tf_op jit(solution)/shard_map/ppermute | solution.py:51
  131.1 9.2 %collective-permute-start.36 = (bf16[2,64,1664]{2,1,0:T(8,128)(2,1)S(1)}, bf16[2,64,1664]{2,1,0:T(8,128)(2,1)S(1)}, u32[]{:S(2)}, u32[]{:S(2)}) collective-permute-start(bf16[2,64,1664]{2,1,0:T(8,128)(2,1)S(1)} %join.11.refs_0_.mine), channel_id=1, source_target_pairs={{0,4},{1,5},{2,6},{3,7},{4,0},{5,1},{6,2},{7,3},{8,12},{9,13},{10,... | collective-permute-start | bytes 1277960 | tf_op jit(solution)/shard_map/ppermute | solution.py:51
  131.2 16.3 %collective-permute-start.37 = (bf16[2,128,1664]{2,1,0:T(8,128)(2,1)S(1)}, bf16[2,128,1664]{2,1,0:T(8,128)(2,1)S(1)}, u32[]{:S(2)}, u32[]{:S(2)}) collective-permute-start(bf16[2,128,1664]{2,1,0:T(8,128)(2,1)S(1)} %join.12.refs_0_), channel_id=1, source_target_pairs={{0,4},{1,5},{2,6},{3,7},{4,0},{5,1},{6,2},{7,3},{8,12},{9,13},{10,... | collective-permute-start | bytes 2555912 | tf_op jit(solution)/shard_map/ppermute | solution.py:51
  135.7 16.5 %collective-permute-start.39 = (bf16[2,128,1664]{2,1,0:T(8,128)(2,1)S(1)}, bf16[2,128,1664]{2,1,0:T(8,128)(2,1)S(1)}, u32[]{:S(2)}, u32[]{:S(2)}) collective-permute-start(bf16[2,128,1664]{2,1,0:T(8,128)(2,1)S(1)} %join.13.refs_3_.refs_0_), channel_id=1, source_target_pairs={{0,12},{1,13},{2,14},{3,15},{4,8},{5,9},{6,10},{7,11},{8,4},{9,5},... | collective-permute-start | bytes 2555912 | tf_op jit(solution)/shard_map/ppermute | solution.py:51
  140.3 13.1 %collective-permute-start.40 = (bf16[1,128,1664]{2,1,0:T(8,128)(2,1)S(1)}, bf16[1,128,1664]{2,1,0:T(8,128)(2,1)S(1)}, u32[]{:S(2)}, u32[]{:S(2)}) collective-permute-start(bf16[1,128,1664]{2,1,0:T(8,128)(2,1)S(1)} %get-tuple-element.90.refs_1_), channel_id=1, source_target_pairs={{0,4},{1,5},{2,6},{3,7},{4,0},{5,1},{6,2},{7,3},{8,12},{9,13},{10,... | collective-permute-start | bytes 1277960 | tf_op jit(solution)/shard_map/ppermute | solution.py:51
  140.5 17.8 %collective-permute-start.38 = (bf16[1,128,1664]{2,1,0:T(8,128)(2,1)S(1)}, bf16[1,128,1664]{2,1,0:T(8,128)(2,1)S(1)}, u32[]{:S(2)}, u32[]{:S(2)}) collective-permute-start(bf16[1,128,1664]{2,1,0:T(8,128)(2,1)S(1)} %get-tuple-element.92.refs_1_), channel_id=1, source_target_pairs={{0,12},{1,13},{2,14},{3,15},{4,8},{5,9},{6,10},{7,11},{8,4},{9,5},... | collective-permute-start | bytes 1277960 | tf_op jit(solution)/shard_map/ppermute | solution.py:51
  140.9 18.1 %collective-permute-start.33 = (bf16[1,128,1664]{2,1,0:T(8,128)(2,1)S(1)}, bf16[1,128,1664]{2,1,0:T(8,128)(2,1)S(1)}, u32[]{:S(2)}, u32[]{:S(2)}) collective-permute-start(bf16[1,128,1664]{2,1,0:T(8,128)(2,1)S(1)} %get-tuple-element.87.refs_0_), channel_id=1, source_target_pairs={{0,4},{1,5},{2,6},{3,7},{4,0},{5,1},{6,2},{7,3},{8,12},{9,13},{10,... | collective-permute-start | bytes 1277960 | tf_op jit(solution)/shard_map/ppermute | solution.py:51
  147.5 12.4 %collective-permute-start.46 = (bf16[1,128,1664]{2,1,0:T(8,128)(2,1)S(1)}, bf16[1,128,1664]{2,1,0:T(8,128)(2,1)S(1)}, u32[]{:S(2)}, u32[]{:S(2)}) collective-permute-start(bf16[1,128,1664]{2,1,0:T(8,128)(2,1)S(1)} %get-tuple-element.91.refs_4_.refs_0_), channel_id=1, source_target_pairs={{0,12},{1,13},{2,14},{3,15},{4,8},{5,9},{6,10},{7,11},{8,4},{9,5},... | collective-permute-start | bytes 1277960 | tf_op jit(solution)/shard_map/ppermute | solution.py:51
  154.2 11.6 %collective-permute-start.42 = (bf16[128,1024]{1,0:T(8,128)(2,1)S(1)}, bf16[128,1024]{1,0:T(8,128)(2,1)S(1)}, u32[]{:S(2)}, u32[]{:S(2)}) collective-permute-start(bf16[128,1024]{1,0:T(8,128)(2,1)S(1)} %get-tuple-element.93.refs_5_), channel_id=1, source_target_pairs={{0,16},{16,0},{32,48},{48,32},{64,80},{80,64},{96,112},{112,96},{1... | collective-permute-start | bytes 786440 | tf_op jit(solution)/shard_map/ppermute | solution.py:55
  160.7 6.8 %collective-permute-start.47 = (bf16[128,1024]{1,0:T(8,128)(2,1)S(1)}, bf16[128,1024]{1,0:T(8,128)(2,1)S(1)}, u32[]{:S(2)}, u32[]{:S(2)}) collective-permute-start(bf16[128,1024]{1,0:T(8,128)(2,1)S(1)} %get-tuple-element.100), channel_id=1, source_target_pairs={{0,16},{16,0},{32,48},{48,32},{64,80},{80,64},{96,112},{112,96},{1... | collective-permute-start | bytes 786440 | tf_op jit(solution)/shard_map/ppermute | solution.py:55
  165.3 5.1 %collective-permute-start.41 = (bf16[128,1024]{1,0:T(8,128)(2,1)S(1)}, bf16[128,1024]{1,0:T(8,128)(2,1)S(1)}, u32[]{:S(2)}, u32[]{:S(2)}) collective-permute-start(bf16[128,1024]{1,0:T(8,128)(2,1)S(1)} %get-tuple-element.96.refs_5_), channel_id=1, source_target_pairs={{0,16},{16,0},{32,48},{48,32},{64,80},{80,64},{96,112},{112,96},{1... | collective-permute-start | bytes 786440 | tf_op jit(solution)/shard_map/ppermute | solution.py:55
  165.9 9.5 %collective-permute-start.43 = (bf16[128,1024]{1,0:T(8,128)(2,1)S(1)}, bf16[128,1024]{1,0:T(8,128)(2,1)S(1)}, u32[]{:S(2)}, u32[]{:S(2)}) collective-permute-start(bf16[128,1024]{1,0:T(8,128)(2,1)S(1)} %add_convert_fusion.3), channel_id=1, source_target_pairs={{0,64},{16,80},{32,96},{48,112},{64,0},{80,16},{96,32},{112,48},{1... | collective-permute-start | bytes 786440 | tf_op jit(solution)/shard_map/ppermute | solution.py:59
  167.6 13.8 %collective-permute-start.48 = (bf16[128,1024]{1,0:T(8,128)(2,1)S(1)}, bf16[128,1024]{1,0:T(8,128)(2,1)S(1)}, u32[]{:S(2)}, u32[]{:S(2)}) collective-permute-start(bf16[128,1024]{1,0:T(8,128)(2,1)S(1)} %add_convert_fusion.1), channel_id=1, source_target_pairs={{0,32},{16,48},{32,64},{48,80},{64,96},{80,112},{96,0},{112,16},{1... | collective-permute-start | bytes 786440 | tf_op jit(solution)/shard_map/ppermute | solution.py:59
  168.3 13.1 %collective-permute-start.45 = (bf16[128,1024]{1,0:T(8,128)(2,1)S(1)}, bf16[128,1024]{1,0:T(8,128)(2,1)S(1)}, u32[]{:S(2)}, u32[]{:S(2)}) collective-permute-start(bf16[128,1024]{1,0:T(8,128)(2,1)S(1)} %add_convert_fusion.2), channel_id=1, source_target_pairs={{0,96},{16,112},{32,0},{48,16},{64,32},{80,48},{96,64},{112,80},{1... | collective-permute-start | bytes 786440 | tf_op jit(solution)/shard_map/ppermute | solution.py:59
  (2 other events, 4.4 us)

commit v6 on v5

--- a/solution.py
+++ b/solution.py
@@ -317,6 +317,11 @@
     return kernel(stack_body, "stack", (first, second), [shape], after)[0]
 
 
+def keep_rows(rows, after):
+    body = lambda source, *refs: refs[-1].__setitem__(..., source[...])
+    return kernel(body, "stack", (rows,), [jax.ShapeDtypeStruct(rows.shape, BF)], after)[0]
+
+
 class Line:
     def __init__(self):
         self.last = ()
@@ -330,7 +335,7 @@
         return out
 
 
-TURNS = "ogj1u02310w23012301230123012301012323012323"
+TURNS = "ogju1k03120w32103210321032103210103232103232"
 
 
 def local(tokens, gate_weight, up_weight, down_weight):
@@ -339,8 +344,7 @@
     beside, far = swap(tokens), shift(tokens, 2)
     line.last = (beside,)
     near = line(hold, tokens)
-    far_beside = swap(far)
-    pair_a = [(near[None], beside[None]), (far[None], far_beside[None])]
+    pair_a = [(near[None], beside[None])]
     sides = []
     own, other = {}, {}
     finished = {}
@@ -401,6 +405,9 @@
         elif turn == "w":
             own["w"], given = line(cut, 0, DOWN, ("own", "other"), (down_weight,))
             other["w"] = [swap(piece) for piece in given]
+        elif turn == "k":
+            held = line(keep_rows, far)
+            pair_a.append((held[None], swap(held)[None]))
         elif turn == "j":
             both = line(stack, after, before)
             sides.append((both, swap(both)))

time: 182 us -> 181 us (level)
  waiting for transfers between devices: 86.8 us -> 69.5 us
  starting transfers between devices: 53.9 us -> 69.7 us
    ppermute x30, starting transfers between devices: 27.2 us -> 44.7 us  [exchange(): return lax.ppermute(a, ('group', 'mp'), pairs)]
    ppermute x30, waiting for transfers between devices: 71.9 us -> 54.9 us  [exchange(): return lax.ppermute(a, ('group', 'mp'), pairs)]
    ppermute x13, waiting for transfers between devices: 3.13 us -> 0.2 us  [swap(): return lax.ppermute(a, 'group', SWAP)]
    ppermute x6, waiting for transfers between devices: 11.7 us -> 14.5 us  [shift(): lax.ppermute(a, 'group', [(g, (g + 2 * chips) % 8) for g in range(8)])]
    ppermute x6, starting transfers between devices: 10.9 us -> 8.59 us  [shift(): lax.ppermute(a, 'group', [(g, (g + 2 * chips) % 8) for g in range(8)])]
    pallas_call x44 -> x45, Pallas kernels: 40 us -> 40 us  [kernel(): pl.pallas_call(body, in_specs=specs + [ANY] * len(after), out_specs=[VMEM...]
  transfers between devices with their start and end apart: 49 -> 49, of which waited for: 23 -> 20; matrix products, arithmetic and copies ran while one was open for 0% -> 0% of each run, Pallas kernels for 22% -> 22%
where the time goes in v6:
time: 181 us
  starting transfers between devices  69.7 us (39%)
  waiting for transfers between devices  69.5 us (38%)
  Pallas kernels  40 us (22%)
    ppermute x30, waiting for transfers between devices, exchange(): return lax.ppermute(a, ('group', 'mp'), pairs)  54.9 us
    ppermute x30, starting transfers between devices, exchange(): return lax.ppermute(a, ('group', 'mp'), pairs)  44.7 us
    pallas_call x45, Pallas kernels, kernel(): pl.pallas_call(body, in_specs=specs + [ANY] * len(after), out_specs=[VMEM...  40 us
    ppermute x13, starting transfers between devices, swap(): return lax.ppermute(a, 'group', SWAP)  16.4 us
    ppermute x6, waiting for transfers between devices, shift(): lax.ppermute(a, 'group', [(g, (g + 2 * chips) % 8) for g in range(8)])  14.5 us
    ppermute x6, starting transfers between devices, shift(): lax.ppermute(a, 'group', [(g, (g + 2 * chips) % 8) for g in range(8)])  8.59 us
  transfers between devices with their start and end apart: 49, of which 20 were waited for; matrix products, arithmetic and copies ran while one was open for 0% of the time, Pallas kernels for 22%

profile of v6, /device:TPU:1, one launch (start us, length us, event | category | flops | bytes accessed | tf_op | source)
XLA Modules:
  0.0 180.8 jit_solution(4042425065642185102)
XLA Ops:
  0.0 1.4 collective-permute-start
  1.4 1.7 collective-permute-start.3
  3.1 2.1 %collective-permute-start.2 = (bf16[128,1024]{1,0:T(8,128)(2,1)}, bf16[128,1024]{1,0:T(8,128)(2,1)S(1)}, u32[]{:S(2)}, u32[]{:S(2)}) collective-permute-start(bf16[128,1024]{1,0:T(8,128)(2,1)} %source.1), channel_id=1, source_target_pairs={{0,96},{16,112},{32,0},{48,16},{64,32},{80,48},{96,64},{112,80},{1... | collective-permute-start | bytes 786440 | tf_op jit(solution)/shard_map/ppermute | solution.py:59
  6.3 3.1 %cut.4 = (bf16[1024,896]{1,0:T(8,128)(2,1)S(1)}, bf16[1024,768]{1,0:T(8,128)(2,1)S(1)}, bf16[1024,896]{1,0:T(8,128)(2,1)S(1)}, bf16[1024,768]{1,0:T(8,128)(2,1)S(1)}) custom-call(bf16[1024,3328]{1,0:T(8,128)(2,1)} %refs_0_.5, bf16[1024,3328]{1,0:T(8,128)(2,1)} %refs_0_.6, bf16[128,1024]{1,0:T(8,128)(2,1)S(1)} %stack.3.refs_2_), custom_call_target="tpu_custom_call" | custom-call | flops 11500000256 | tf_op jit(solution)/shard_map/cut/pallas_call | solution.py:80
  9.3 2.0 %cut.5 = (bf16[1024,896]{1,0:T(8,128)(2,1)S(1)}, bf16[1024,768]{1,0:T(8,128)(2,1)S(1)}) custom-call(bf16[1024,3328]{1,0:T(8,128)(2,1)} %refs_0_.5, bf16[1024,896]{1,0:T(8,128)(2,1)S(1)} %get-tuple-element.53.refs_1_.refs_2_.refs_4_), custom_call_target="tpu_custom_call" | custom-call | flops 5750000128 | tf_op jit(solution)/shard_map/cut/pallas_call | solution.py:80
  11.8 1.5 collective-permute-start.1
  13.9 2.0 %cut.6 = (bf16[1024,896]{1,0:T(8,128)(2,1)S(1)}, bf16[1024,768]{1,0:T(8,128)(2,1)S(1)}) custom-call(bf16[1024,3328]{1,0:T(8,128)(2,1)} %refs_0_.6, bf16[2,128,1024]{2,1,0:T(8,128)(2,1)S(1)} %stack.4.refs_1_.refs_0_), custom_call_target="tpu_custom_call" | custom-call | flops 5750000128 | tf_op jit(solution)/shard_map/cut/pallas_call | solution.py:80
  15.9 3.7 %project.4 = (bf16[2,2,128,1664]{3,2,1,0:T(8,128)(2,1)S(1)}, bf16[2,2,128,1664]{3,2,1,0:T(8,128)(2,1)S(1)}) custom-call(bf16[2,128,1024]{2,1,0:T(8,128)(2,1)S(1)} %stack.4.refs_1_.refs_0_, bf16[2,128,1024]{2,1,0:T(8,128)(2,1)S(1)} %collective-permute-done.4.refs_1_, bf16[1024,896]{1,0:T(8,128)(2,1)S(1)} %get-tuple-element.53.refs_1_.refs_2_.refs_4_, ...), custom_call_target="tpu_custom_call" | custom-call | flops 1150000000 | tf_op jit(solution)/shard_map/project/pallas_call | solution.py:80
  19.6 1.5 collective-permute-done.1.source
  22.7 2.7 %collective-permute-start.10 = (bf16[2,2,128,1664]{3,2,1,0:T(8,128)(2,1)S(1)}, bf16[2,2,128,1664]{3,2,1,0:T(8,128)(2,1)S(1)}, u32[]{:S(2)}, u32[]{:S(2)}) collective-permute-start(bf16[2,2,128,1664]{3,2,1,0:T(8,128)(2,1)S(1)} %get-tuple-element.59.refs_0_), channel_id=1, source_target_pairs={{0,12},{1,13},{2,14},{3,15},{4,8},{5,9},{6,10},{7,11},{8,4},{9,5},... | collective-permute-start | bytes 5111816 | tf_op jit(solution)/shard_map/ppermute | solution.py:51
  25.5 3.7 %project.5 = (bf16[2,2,128,1664]{3,2,1,0:T(8,128)(2,1)S(1)}, bf16[2,2,128,1664]{3,2,1,0:T(8,128)(2,1)S(1)}) custom-call(bf16[1,128,1024]{2,1,0:T(8,128)(2,1)S(1)} %bitcast.8, bf16[1,128,1024]{2,1,0:T(8,128)(2,1)S(1)} %bitcast.6, bf16[1,128,1024]{2,1,0:T(8,128)(2,1)S(1)} %bitcast.4, bf16[1,128,1024]{2,1,0:T(8,128)(2,1)S(1)} %bitcast.10, ...), custom_call_target="tpu_custom_call" | custom-call | flops 1150000000 | tf_op jit(solution)/shard_map/project/pallas_call | solution.py:80
  30.8 3.7 %project.6 = (bf16[2,2,128,1664]{3,2,1,0:T(8,128)(2,1)S(1)}, bf16[2,2,128,1664]{3,2,1,0:T(8,128)(2,1)S(1)}) custom-call(bf16[2,128,1024]{2,1,0:T(8,128)(2,1)S(1)} %stack.4.refs_1_.refs_0_, bf16[2,128,1024]{2,1,0:T(8,128)(2,1)S(1)} %collective-permute-done.4.refs_1_, bf16[1024,896]{1,0:T(8,128)(2,1)S(1)} %collective-permute-done.6.refs_2_.refs_4_, ...), custom_call_target="tpu_custom_call" | custom-call | flops 1150000000 | tf_op jit(solution)/shard_map/project/pallas_call | solution.py:80
  34.6 3.0 %collective-permute-start.12 = (bf16[2,2,128,1664]{3,2,1,0:T(8,128)(2,1)S(1)}, bf16[2,2,128,1664]{3,2,1,0:T(8,128)(2,1)S(1)}, u32[]{:S(2)}, u32[]{:S(2)}) collective-permute-start(bf16[2,2,128,1664]{3,2,1,0:T(8,128)(2,1)S(1)} %get-tuple-element.64.refs_0_), channel_id=1, source_target_pairs={{0,12},{1,13},{2,14},{3,15},{4,8},{5,9},{6,10},{7,11},{8,4},{9,5},... | collective-permute-start | bytes 5111816 | tf_op jit(solution)/shard_map/ppermute | solution.py:51
  37.6 7.3 %collective-permute-done.10.came = bf16[2,2,128,1664]{3,2,1,0:T(8,128)(2,1)S(1)} collective-permute-done((bf16[2,2,128,1664]{3,2,1,0:T(8,128)(2,1)S(1)}, bf16[2,2,128,1664]{3,2,1,0:T(8,128)(2,1)S(1)}, u32[]{:S(2)}, u32[]{:S(2)}) %collective-permute-start.10) | collective-permute-done | bytes 1703968 | tf_op jit(solution)/shard_map/ppermute | solution.py:51
  45.3 3.7 %project.7 = (bf16[2,2,128,1664]{3,2,1,0:T(8,128)(2,1)S(1)}, bf16[2,2,128,1664]{3,2,1,0:T(8,128)(2,1)S(1)}) custom-call(bf16[1,128,1024]{2,1,0:T(8,128)(2,1)S(1)} %bitcast.9, bf16[1,128,1024]{2,1,0:T(8,128)(2,1)S(1)} %bitcast.7, bf16[1,128,1024]{2,1,0:T(8,128)(2,1)S(1)} %bitcast.5, bf16[1,128,1024]{2,1,0:T(8,128)(2,1)S(1)} %bitcast.11, ...), custom_call_target="tpu_custom_call" | custom-call | flops 1150000000 | tf_op jit(solution)/shard_map/project/pallas_call | solution.py:80
  49.2 1.4 collective-permute-start.17
  51.0 2.8 %collective-permute-start.16 = (bf16[2,2,64,1664]{3,2,1,0:T(8,128)(2,1)S(1)}, bf16[2,2,64,1664]{3,2,1,0:T(8,128)(2,1)S(1)}, u32[]{:S(2)}, u32[]{:S(2)}) collective-permute-start(bf16[2,2,64,1664]{3,2,1,0:T(8,128)(2,1)S(1)} %get-tuple-element.70.refs_1_), channel_id=1, source_target_pairs={{0,12},{1,13},{2,14},{3,15},{4,8},{5,9},{6,10},{7,11},{8,4},{9,5},... | collective-permute-start | bytes 2555912 | tf_op jit(solution)/shard_map/ppermute | solution.py:51
  53.8 3.0 %cut.7 = (bf16[1664,512]{1,0:T(8,128)(2,1)S(1)}, bf16[1664,512]{1,0:T(8,128)(2,1)S(1)}, bf16[1664,512]{1,0:T(8,128)(2,1)S(1)}, bf16[1664,512]{1,0:T(8,128)(2,1)S(1)}) custom-call(bf16[3328,1024]{1,0:T(8,128)(2,1)} %refs_0_.7, bf16[2,2,64,1664]{3,2,1,0:T(8,128)(2,1)S(1)} %get-tuple-element.70.refs_1_), custom_call_target="tpu_custom_call" | custom-call | flops 11500000256 | tf_op jit(solution)/shard_map/cut/pallas_call | solution.py:80
  56.8 6.4 %collective-permute-done.12.came = bf16[2,2,128,1664]{3,2,1,0:T(8,128)(2,1)S(1)} collective-permute-done((bf16[2,2,128,1664]{3,2,1,0:T(8,128)(2,1)S(1)}, bf16[2,2,128,1664]{3,2,1,0:T(8,128)(2,1)S(1)}, u32[]{:S(2)}, u32[]{:S(2)}) %collective-permute-start.12) | collective-permute-done | bytes 1703968 | tf_op jit(solution)/shard_map/ppermute | solution.py:51
  63.7 6.4 %collective-permute-done.11.came = bf16[2,2,128,1664]{3,2,1,0:T(8,128)(2,1)S(1)} collective-permute-done((bf16[2,2,128,1664]{3,2,1,0:T(8,128)(2,1)S(1)}, bf16[2,2,128,1664]{3,2,1,0:T(8,128)(2,1)S(1)}, u32[]{:S(2)}, u32[]{:S(2)}) %collective-permute-start.11) | collective-permute-done | bytes 1703968 | tf_op jit(solution)/shard_map/ppermute | solution.py:51
  70.5 2.8 %collective-permute-start.14 = (bf16[2,2,64,1664]{3,2,1,0:T(8,128)(2,1)S(1)}, bf16[2,2,64,1664]{3,2,1,0:T(8,128)(2,1)S(1)}, u32[]{:S(2)}, u32[]{:S(2)}) collective-permute-start(bf16[2,2,64,1664]{3,2,1,0:T(8,128)(2,1)S(1)} %get-tuple-element.74.refs_0_), channel_id=1, source_target_pairs={{0,12},{1,13},{2,14},{3,15},{4,8},{5,9},{6,10},{7,11},{8,4},{9,5},... | collective-permute-start | bytes 2555912 | tf_op jit(solution)/shard_map/ppermute | solution.py:51
  73.3 1.8 %collective-permute-start.35 = (bf16[1664,512]{1,0:T(8,128)(2,1)S(1)}, bf16[1664,512]{1,0:T(8,128)(2,1)S(1)}, u32[]{:S(2)}, u32[]{:S(2)}) collective-permute-start(bf16[1664,512]{1,0:T(8,128)(2,1)S(1)} %get-tuple-element.89), channel_id=1, source_target_pairs={{0,16},{16,0},{32,48},{48,32},{64,80},{80,64},{96,112},{112,96},{1... | collective-permute-start | bytes 5111816 | tf_op jit(solution)/shard_map/ppermute | solution.py:55
  75.1 4.2 %collective-permute-done.17.came = bf16[2,2,64,1664]{3,2,1,0:T(8,128)(2,1)S(1)} collective-permute-done((bf16[2,2,64,1664]{3,2,1,0:T(8,128)(2,1)S(1)}, bf16[2,2,64,1664]{3,2,1,0:T(8,128)(2,1)S(1)}, u32[]{:S(2)}, u32[]{:S(2)}) %collective-permute-start.17) | collective-permute-done | bytes 852000 | tf_op jit(solution)/shard_map/ppermute | solution.py:51
  79.2 1.7 collective-permute-start.36
  81.2 2.6 %collective-permute-start.21 = (bf16[2,2,32,1664]{3,2,1,0:T(8,128)(2,1)S(1)}, bf16[2,2,32,1664]{3,2,1,0:T(8,128)(2,1)S(1)}, u32[]{:S(2)}, u32[]{:S(2)}) collective-permute-start(bf16[2,2,32,1664]{3,2,1,0:T(8,128)(2,1)S(1)} %get-tuple-element.78.refs_0_), channel_id=1, source_target_pairs={{0,3},{1,2},{2,1},{3,0},{4,7},{5,6},{6,5},{7,4},{8,11},{9,10},{10,... | collective-permute-start | bytes 1277960 | tf_op jit(solution)/shard_map/ppermute | solution.py:51
  83.9 4.4 %collective-permute-done.15.came = bf16[2,2,64,1664]{3,2,1,0:T(8,128)(2,1)S(1)} collective-permute-done((bf16[2,2,64,1664]{3,2,1,0:T(8,128)(2,1)S(1)}, bf16[2,2,64,1664]{3,2,1,0:T(8,128)(2,1)S(1)}, u32[]{:S(2)}, u32[]{:S(2)}) %collective-permute-start.15) | collective-permute-done | bytes 852000 | tf_op jit(solution)/shard_map/ppermute | solution.py:51
  89.5 1.9 %collective-permute-start.19 = (bf16[2,2,32,1664]{3,2,1,0:T(8,128)(2,1)S(1)}, bf16[2,2,32,1664]{3,2,1,0:T(8,128)(2,1)S(1)}, u32[]{:S(2)}, u32[]{:S(2)}) collective-permute-start(bf16[2,2,32,1664]{3,2,1,0:T(8,128)(2,1)S(1)} %get-tuple-element.80.refs_0_), channel_id=1, source_target_pairs={{0,3},{1,2},{2,1},{3,0},{4,7},{5,6},{6,5},{7,4},{8,11},{9,10},{10,... | collective-permute-start | bytes 1277960 | tf_op jit(solution)/shard_map/ppermute | solution.py:51
  92.4 3.2 %collective-permute-done.20.came = bf16[2,2,32,1664]{3,2,1,0:T(8,128)(2,1)S(1)} collective-permute-done((bf16[2,2,32,1664]{3,2,1,0:T(8,128)(2,1)S(1)}, bf16[2,2,32,1664]{3,2,1,0:T(8,128)(2,1)S(1)}, u32[]{:S(2)}, u32[]{:S(2)}) %collective-permute-start.20) | collective-permute-done | bytes 426016 | tf_op jit(solution)/shard_map/ppermute | solution.py:51
  96.7 1.4 collective-permute-done.19.came
  98.0 1.8 %collective-permute-start.24 = (bf16[2,2,32,1664]{3,2,1,0:T(8,128)(2,1)S(1)}, bf16[2,2,32,1664]{3,2,1,0:T(8,128)(2,1)S(1)}, u32[]{:S(2)}, u32[]{:S(2)}) collective-permute-start(bf16[2,2,32,1664]{3,2,1,0:T(8,128)(2,1)S(1)} %halves.21.refs_0_.mine), channel_id=1, source_target_pairs={{0,3},{1,2},{2,1},{3,0},{4,7},{5,6},{6,5},{7,4},{8,11},{9,10},{10,... | collective-permute-start | bytes 1277960 | tf_op jit(solution)/shard_map/ppermute | solution.py:51
  101.2 3.5 %collective-permute-done.25.theirs = bf16[2,2,32,1664]{3,2,1,0:T(8,128)(2,1)S(1)} collective-permute-done((bf16[2,2,32,1664]{3,2,1,0:T(8,128)(2,1)S(1)}, bf16[2,2,32,1664]{3,2,1,0:T(8,128)(2,1)S(1)}, u32[]{:S(2)}, u32[]{:S(2)}) %collective-permute-start.25) | collective-permute-done | bytes 426016 | tf_op jit(solution)/shard_map/ppermute | solution.py:51
  104.8 2.5 %collective-permute-start.22 = (bf16[2,2,32,1664]{3,2,1,0:T(8,128)(2,1)S(1)}, bf16[2,2,32,1664]{3,2,1,0:T(8,128)(2,1)S(1)}, u32[]{:S(2)}, u32[]{:S(2)}) collective-permute-start(bf16[2,2,32,1664]{3,2,1,0:T(8,128)(2,1)S(1)} %halves.23.refs_0_.mine), channel_id=1, source_target_pairs={{0,3},{1,2},{2,1},{3,0},{4,7},{5,6},{6,5},{7,4},{8,11},{9,10},{10,... | collective-permute-start | bytes 1277960 | tf_op jit(solution)/shard_map/ppermute | solution.py:51
  110.4 2.8 %collective-permute-done.22.theirs = bf16[2,2,32,1664]{3,2,1,0:T(8,128)(2,1)S(1)} collective-permute-done((bf16[2,2,32,1664]{3,2,1,0:T(8,128)(2,1)S(1)}, bf16[2,2,32,1664]{3,2,1,0:T(8,128)(2,1)S(1)}, u32[]{:S(2)}, u32[]{:S(2)}) %collective-permute-start.22) | collective-permute-done | bytes 426016 | tf_op jit(solution)/shard_map/ppermute | solution.py:51
  113.2 2.5 %collective-permute-start.27 = (bf16[2,32,1664]{2,1,0:T(8,128)(2,1)S(1)}, bf16[2,32,1664]{2,1,0:T(8,128)(2,1)S(1)}, u32[]{:S(2)}, u32[]{:S(2)}) collective-permute-start(bf16[2,32,1664]{2,1,0:T(8,128)(2,1)S(1)} %hidden.6.refs_0_.mine), channel_id=1, source_target_pairs={{0,3},{1,2},{2,1},{3,0},{4,7},{5,6},{6,5},{7,4},{8,11},{9,10},{10,... | collective-permute-start | bytes 638984 | tf_op jit(solution)/shard_map/ppermute | solution.py:51
  116.2 2.9 %collective-permute-done.27.theirs = bf16[2,32,1664]{2,1,0:T(8,128)(2,1)S(1)} collective-permute-done((bf16[2,32,1664]{2,1,0:T(8,128)(2,1)S(1)}, bf16[2,32,1664]{2,1,0:T(8,128)(2,1)S(1)}, u32[]{:S(2)}, u32[]{:S(2)}) %collective-permute-start.27) | collective-permute-done | bytes 213024 | tf_op jit(solution)/shard_map/ppermute | solution.py:51
  119.2 2.7 %collective-permute-start.32 = (bf16[2,64,1664]{2,1,0:T(8,128)(2,1)S(1)}, bf16[2,64,1664]{2,1,0:T(8,128)(2,1)S(1)}, u32[]{:S(2)}, u32[]{:S(2)}) collective-permute-start(bf16[2,64,1664]{2,1,0:T(8,128)(2,1)S(1)} %join.9.refs_0_.mine), channel_id=1, source_target_pairs={{0,12},{1,13},{2,14},{3,15},{4,8},{5,9},{6,10},{7,11},{8,4},{9,5},... | collective-permute-start | bytes 1277960 | tf_op jit(solution)/shard_map/ppermute | solution.py:51
  122.2 1.4 collective-permute-done.33.theirs
  123.7 3.7 %collective-permute-start.38 = (bf16[2,128,1664]{2,1,0:T(8,128)(2,1)S(1)}, bf16[2,128,1664]{2,1,0:T(8,128)(2,1)S(1)}, u32[]{:S(2)}, u32[]{:S(2)}) collective-permute-start(bf16[2,128,1664]{2,1,0:T(8,128)(2,1)S(1)} %join.12.refs_0_), channel_id=1, source_target_pairs={{0,12},{1,13},{2,14},{3,15},{4,8},{5,9},{6,10},{7,11},{8,4},{9,5},... | collective-permute-start | bytes 2555912 | tf_op jit(solution)/shard_map/ppermute | solution.py:51
  127.8 2.5 %collective-permute-done.31.theirs = bf16[2,64,1664]{2,1,0:T(8,128)(2,1)S(1)} collective-permute-done((bf16[2,64,1664]{2,1,0:T(8,128)(2,1)S(1)}, bf16[2,64,1664]{2,1,0:T(8,128)(2,1)S(1)}, u32[]{:S(2)}, u32[]{:S(2)}) %collective-permute-start.31) | collective-permute-done | bytes 426016 | tf_op jit(solution)/shard_map/ppermute | solution.py:51
  130.3 2.7 %collective-permute-start.30 = (bf16[2,64,1664]{2,1,0:T(8,128)(2,1)S(1)}, bf16[2,64,1664]{2,1,0:T(8,128)(2,1)S(1)}, u32[]{:S(2)}, u32[]{:S(2)}) collective-permute-start(bf16[2,64,1664]{2,1,0:T(8,128)(2,1)S(1)} %join.11.refs_0_.mine), channel_id=1, source_target_pairs={{0,12},{1,13},{2,14},{3,15},{4,8},{5,9},{6,10},{7,11},{8,4},{9,5},... | collective-permute-start | bytes 1277960 | tf_op jit(solution)/shard_map/ppermute | solution.py:51
  135.2 7.1 %collective-permute-done.30.theirs = bf16[2,64,1664]{2,1,0:T(8,128)(2,1)S(1)} collective-permute-done((bf16[2,64,1664]{2,1,0:T(8,128)(2,1)S(1)}, bf16[2,64,1664]{2,1,0:T(8,128)(2,1)S(1)}, u32[]{:S(2)}, u32[]{:S(2)}) %collective-permute-start.30) | collective-permute-done | bytes 426016 | tf_op jit(solution)/shard_map/ppermute | solution.py:51
  142.4 2.7 %collective-permute-start.41 = (bf16[1,128,1664]{2,1,0:T(8,128)(2,1)S(1)}, bf16[1,128,1664]{2,1,0:T(8,128)(2,1)S(1)}, u32[]{:S(2)}, u32[]{:S(2)}) collective-permute-start(bf16[1,128,1664]{2,1,0:T(8,128)(2,1)S(1)} %get-tuple-element.92.refs_1_), channel_id=1, source_target_pairs={{0,12},{1,13},{2,14},{3,15},{4,8},{5,9},{6,10},{7,11},{8,4},{9,5},... | collective-permute-start | bytes 1277960 | tf_op jit(solution)/shard_map/ppermute | solution.py:51
  145.3 1.4 collective-permute-start.34
  152.2 5.4 %collective-permute-start.45 = (bf16[128,1024]{1,0:T(8,128)(2,1)S(1)}, bf16[128,1024]{1,0:T(8,128)(2,1)S(1)}, u32[]{:S(2)}, u32[]{:S(2)}) collective-permute-start(bf16[128,1024]{1,0:T(8,128)(2,1)S(1)} %get-tuple-element.93.refs_5_), channel_id=1, source_target_pairs={{0,16},{16,0},{32,48},{48,32},{64,80},{80,64},{96,112},{112,96},{1... | collective-permute-start | bytes 786440 | tf_op jit(solution)/shard_map/ppermute | solution.py:55
  159.7 2.2 %collective-permute-start.47 = (bf16[128,1024]{1,0:T(8,128)(2,1)S(1)}, bf16[128,1024]{1,0:T(8,128)(2,1)S(1)}, u32[]{:S(2)}, u32[]{:S(2)}) collective-permute-start(bf16[128,1024]{1,0:T(8,128)(2,1)S(1)} %get-tuple-element.95.refs_5_), channel_id=1, source_target_pairs={{0,16},{16,0},{32,48},{48,32},{64,80},{80,64},{96,112},{112,96},{1... | collective-permute-start | bytes 786440 | tf_op jit(solution)/shard_map/ppermute | solution.py:55
  163.5 1.8 collective-permute-start.46
  166.9 4.6 %collective-permute-done.46 = bf16[128,1024]{1,0:T(8,128)(2,1)S(1)} collective-permute-done((bf16[128,1024]{1,0:T(8,128)(2,1)S(1)}, bf16[128,1024]{1,0:T(8,128)(2,1)S(1)}, u32[]{:S(2)}, u32[]{:S(2)}) %collective-permute-start.46) | collective-permute-done | bytes 262176 | tf_op jit(solution)/shard_map/ppermute | solution.py:59
  171.5 8.3 %collective-permute-done.48 = bf16[128,1024]{1,0:T(8,128)(2,1)S(1)} collective-permute-done((bf16[128,1024]{1,0:T(8,128)(2,1)S(1)}, bf16[128,1024]{1,0:T(8,128)(2,1)S(1)}, u32[]{:S(2)}, u32[]{:S(2)}) %collective-permute-start.48) | collective-permute-done | bytes 262176 | tf_op jit(solution)/shard_map/ppermute | solution.py:59
  (101 shorter events, 30.3 us)
Async XLA Ops:
  0.0 5.3 %collective-permute-start = (bf16[128,1024]{1,0:T(8,128)(2,1)}, bf16[128,1024]{1,0:T(8,128)(2,1)S(1)}, u32[]{:S(2)}, u32[]{:S(2)}) collective-permute-start(bf16[128,1024]{1,0:T(8,128)(2,1)} %source.1), channel_id=1, source_target_pairs={{0,16},{16,0},{32,48},{48,32},{64,80},{80,64},{96,112},{112,96},{1... | collective-permute-start | bytes 786440 | tf_op jit(solution)/shard_map/ppermute | solution.py:55
  1.4 11.9 %collective-permute-start.3 = (bf16[128,1024]{1,0:T(8,128)(2,1)}, bf16[128,1024]{1,0:T(8,128)(2,1)S(1)}, u32[]{:S(2)}, u32[]{:S(2)}) collective-permute-start(bf16[128,1024]{1,0:T(8,128)(2,1)} %source.1), channel_id=1, source_target_pairs={{0,32},{16,48},{32,64},{48,80},{64,96},{80,112},{96,0},{112,16},{1... | collective-permute-start | bytes 786440 | tf_op jit(solution)/shard_map/ppermute | solution.py:59
  3.1 10.2 %collective-permute-start.2 = (bf16[128,1024]{1,0:T(8,128)(2,1)}, bf16[128,1024]{1,0:T(8,128)(2,1)S(1)}, u32[]{:S(2)}, u32[]{:S(2)}) collective-permute-start(bf16[128,1024]{1,0:T(8,128)(2,1)} %source.1), channel_id=1, source_target_pairs={{0,96},{16,112},{32,0},{48,16},{64,32},{80,48},{96,64},{112,80},{1... | collective-permute-start | bytes 786440 | tf_op jit(solution)/shard_map/ppermute | solution.py:59
  11.4 17.9 %collective-permute-start.7 = (bf16[1024,768]{1,0:T(8,128)(2,1)S(1)}, bf16[1024,768]{1,0:T(8,128)(2,1)S(1)}, u32[]{:S(2)}, u32[]{:S(2)}) collective-permute-start(bf16[1024,768]{1,0:T(8,128)(2,1)S(1)} %get-tuple-element.60), channel_id=1, source_target_pairs={{0,16},{16,0},{32,48},{48,32},{64,80},{80,64},{96,112},{112,96},{1... | collective-permute-start | bytes 4718600 | tf_op jit(solution)/shard_map/ppermute | solution.py:55
  11.8 9.3 %collective-permute-start.1 = (bf16[128,1024]{1,0:T(8,128)(2,1)S(1)}, bf16[128,1024]{1,0:T(8,128)(2,1)S(1)}, u32[]{:S(2)}, u32[]{:S(2)}) collective-permute-start(bf16[128,1024]{1,0:T(8,128)(2,1)S(1)} %copy-done), channel_id=1, source_target_pairs={{0,64},{16,80},{32,96},{48,112},{64,0},{80,16},{96,32},{112,48},{1... | collective-permute-start | bytes 786440 | tf_op jit(solution)/shard_map/ppermute | solution.py:59
  21.1 4.3 %collective-permute-start.5 = (bf16[128,1024]{1,0:T(8,128)(2,1)S(1)}, bf16[128,1024]{1,0:T(8,128)(2,1)S(1)}, u32[]{:S(2)}, u32[]{:S(2)}) collective-permute-start(bf16[128,1024]{1,0:T(8,128)(2,1)S(1)} %stack.5.refs_8_), channel_id=1, source_target_pairs={{0,16},{16,0},{32,48},{48,32},{64,80},{80,64},{96,112},{112,96},{1... | collective-permute-start | bytes 786440 | tf_op jit(solution)/shard_map/ppermute | solution.py:55
  22.2 8.7 %collective-permute-start.6 = (bf16[1024,896]{1,0:T(8,128)(2,1)S(1)}, bf16[1024,896]{1,0:T(8,128)(2,1)S(1)}, u32[]{:S(2)}, u32[]{:S(2)}) collective-permute-start(bf16[1024,896]{1,0:T(8,128)(2,1)S(1)} %get-tuple-element.54.refs_0_), channel_id=1, source_target_pairs={{0,16},{16,0},{32,48},{48,32},{64,80},{80,64},{96,112},{112,96},{1... | collective-permute-start | bytes 5505032 | tf_op jit(solution)/shard_map/ppermute | solution.py:55
  22.3 8.6 %collective-permute-start.8 = (bf16[1024,896]{1,0:T(8,128)(2,1)S(1)}, bf16[1024,896]{1,0:T(8,128)(2,1)S(1)}, u32[]{:S(2)}, u32[]{:S(2)}) collective-permute-start(bf16[1024,896]{1,0:T(8,128)(2,1)S(1)} %get-tuple-element.58.refs_6_), channel_id=1, source_target_pairs={{0,16},{16,0},{32,48},{48,32},{64,80},{80,64},{96,112},{112,96},{1... | collective-permute-start | bytes 5505032 | tf_op jit(solution)/shard_map/ppermute | solution.py:55
  22.7 22.2 %collective-permute-start.10 = (bf16[2,2,128,1664]{3,2,1,0:T(8,128)(2,1)S(1)}, bf16[2,2,128,1664]{3,2,1,0:T(8,128)(2,1)S(1)}, u32[]{:S(2)}, u32[]{:S(2)}) collective-permute-start(bf16[2,2,128,1664]{3,2,1,0:T(8,128)(2,1)S(1)} %get-tuple-element.59.refs_0_), channel_id=1, source_target_pairs={{0,12},{1,13},{2,14},{3,15},{4,8},{5,9},{6,10},{7,11},{8,4},{9,5},... | collective-permute-start | bytes 5111816 | tf_op jit(solution)/shard_map/ppermute | solution.py:51
  25.4 5.4 %collective-permute-start.9 = (bf16[1024,768]{1,0:T(8,128)(2,1)S(1)}, bf16[1024,768]{1,0:T(8,128)(2,1)S(1)}, u32[]{:S(2)}, u32[]{:S(2)}) collective-permute-start(bf16[1024,768]{1,0:T(8,128)(2,1)S(1)} %get-tuple-element.61), channel_id=1, source_target_pairs={{0,16},{16,0},{32,48},{48,32},{64,80},{80,64},{96,112},{112,96},{1... | collective-permute-start | bytes 4718600 | tf_op jit(solution)/shard_map/ppermute | solution.py:55
  29.3 21.3 %collective-permute-start.13 = (bf16[2,2,128,1664]{3,2,1,0:T(8,128)(2,1)S(1)}, bf16[2,2,128,1664]{3,2,1,0:T(8,128)(2,1)S(1)}, u32[]{:S(2)}, u32[]{:S(2)}) collective-permute-start(bf16[2,2,128,1664]{3,2,1,0:T(8,128)(2,1)S(1)} %get-tuple-element.63.refs_6_), channel_id=1, source_target_pairs={{0,4},{1,5},{2,6},{3,7},{4,0},{5,1},{6,2},{7,3},{8,12},{9,13},{10,... | collective-permute-start | bytes 5111816 | tf_op jit(solution)/shard_map/ppermute | solution.py:51
  34.6 28.6 %collective-permute-start.12 = (bf16[2,2,128,1664]{3,2,1,0:T(8,128)(2,1)S(1)}, bf16[2,2,128,1664]{3,2,1,0:T(8,128)(2,1)S(1)}, u32[]{:S(2)}, u32[]{:S(2)}) collective-permute-start(bf16[2,2,128,1664]{3,2,1,0:T(8,128)(2,1)S(1)} %get-tuple-element.64.refs_0_), channel_id=1, source_target_pairs={{0,12},{1,13},{2,14},{3,15},{4,8},{5,9},{6,10},{7,11},{8,4},{9,5},... | collective-permute-start | bytes 5111816 | tf_op jit(solution)/shard_map/ppermute | solution.py:51
  49.1 21.0 %collective-permute-start.11 = (bf16[2,2,128,1664]{3,2,1,0:T(8,128)(2,1)S(1)}, bf16[2,2,128,1664]{3,2,1,0:T(8,128)(2,1)S(1)}, u32[]{:S(2)}, u32[]{:S(2)}) collective-permute-start(bf16[2,2,128,1664]{3,2,1,0:T(8,128)(2,1)S(1)} %get-tuple-element.67.refs_0_), channel_id=1, source_target_pairs={{0,4},{1,5},{2,6},{3,7},{4,0},{5,1},{6,2},{7,3},{8,12},{9,13},{10,... | collective-permute-start | bytes 5111816 | tf_op jit(solution)/shard_map/ppermute | solution.py:51
  49.2 30.1 %collective-permute-start.17 = (bf16[2,2,64,1664]{3,2,1,0:T(8,128)(2,1)S(1)}, bf16[2,2,64,1664]{3,2,1,0:T(8,128)(2,1)S(1)}, u32[]{:S(2)}, u32[]{:S(2)}) collective-permute-start(bf16[2,2,64,1664]{3,2,1,0:T(8,128)(2,1)S(1)} %get-tuple-element.65.refs_8_), channel_id=1, source_target_pairs={{0,4},{1,5},{2,6},{3,7},{4,0},{5,1},{6,2},{7,3},{8,12},{9,13},{10,... | collective-permute-start | bytes 2555912 | tf_op jit(solution)/shard_map/ppermute | solution.py:51
  51.0 30.2 %collective-permute-start.16 = (bf16[2,2,64,1664]{3,2,1,0:T(8,128)(2,1)S(1)}, bf16[2,2,64,1664]{3,2,1,0:T(8,128)(2,1)S(1)}, u32[]{:S(2)}, u32[]{:S(2)}) collective-permute-start(bf16[2,2,64,1664]{3,2,1,0:T(8,128)(2,1)S(1)} %get-tuple-element.70.refs_1_), channel_id=1, source_target_pairs={{0,12},{1,13},{2,14},{3,15},{4,8},{5,9},{6,10},{7,11},{8,4},{9,5},... | collective-permute-start | bytes 2555912 | tf_op jit(solution)/shard_map/ppermute | solution.py:51
  63.6 24.8 %collective-permute-start.15 = (bf16[2,2,64,1664]{3,2,1,0:T(8,128)(2,1)S(1)}, bf16[2,2,64,1664]{3,2,1,0:T(8,128)(2,1)S(1)}, u32[]{:S(2)}, u32[]{:S(2)}) collective-permute-start(bf16[2,2,64,1664]{3,2,1,0:T(8,128)(2,1)S(1)} %get-tuple-element.72.refs_0_), channel_id=1, source_target_pairs={{0,4},{1,5},{2,6},{3,7},{4,0},{5,1},{6,2},{7,3},{8,12},{9,13},{10,... | collective-permute-start | bytes 2555912 | tf_op jit(solution)/shard_map/ppermute | solution.py:51
  70.5 19.0 %collective-permute-start.14 = (bf16[2,2,64,1664]{3,2,1,0:T(8,128)(2,1)S(1)}, bf16[2,2,64,1664]{3,2,1,0:T(8,128)(2,1)S(1)}, u32[]{:S(2)}, u32[]{:S(2)}) collective-permute-start(bf16[2,2,64,1664]{3,2,1,0:T(8,128)(2,1)S(1)} %get-tuple-element.74.refs_0_), channel_id=1, source_target_pairs={{0,12},{1,13},{2,14},{3,15},{4,8},{5,9},{6,10},{7,11},{8,4},{9,5},... | collective-permute-start | bytes 2555912 | tf_op jit(solution)/shard_map/ppermute | solution.py:51
  73.3 71.8 %collective-permute-start.35 = (bf16[1664,512]{1,0:T(8,128)(2,1)S(1)}, bf16[1664,512]{1,0:T(8,128)(2,1)S(1)}, u32[]{:S(2)}, u32[]{:S(2)}) collective-permute-start(bf16[1664,512]{1,0:T(8,128)(2,1)S(1)} %get-tuple-element.89), channel_id=1, source_target_pairs={{0,16},{16,0},{32,48},{48,32},{64,80},{80,64},{96,112},{112,96},{1... | collective-permute-start | bytes 5111816 | tf_op jit(solution)/shard_map/ppermute | solution.py:55
  79.2 66.0 %collective-permute-start.36 = (bf16[1664,512]{1,0:T(8,128)(2,1)S(1)}, bf16[1664,512]{1,0:T(8,128)(2,1)S(1)}, u32[]{:S(2)}, u32[]{:S(2)}) collective-permute-start(bf16[1664,512]{1,0:T(8,128)(2,1)S(1)} %get-tuple-element.90), channel_id=1, source_target_pairs={{0,16},{16,0},{32,48},{48,32},{64,80},{80,64},{96,112},{112,96},{1... | collective-permute-start | bytes 5111816 | tf_op jit(solution)/shard_map/ppermute | solution.py:55
  81.2 10.4 %collective-permute-start.21 = (bf16[2,2,32,1664]{3,2,1,0:T(8,128)(2,1)S(1)}, bf16[2,2,32,1664]{3,2,1,0:T(8,128)(2,1)S(1)}, u32[]{:S(2)}, u32[]{:S(2)}) collective-permute-start(bf16[2,2,32,1664]{3,2,1,0:T(8,128)(2,1)S(1)} %get-tuple-element.78.refs_0_), channel_id=1, source_target_pairs={{0,3},{1,2},{2,1},{3,0},{4,7},{5,6},{6,5},{7,4},{8,11},{9,10},{10,... | collective-permute-start | bytes 1277960 | tf_op jit(solution)/shard_map/ppermute | solution.py:51
  88.4 7.3 %collective-permute-start.20 = (bf16[2,2,32,1664]{3,2,1,0:T(8,128)(2,1)S(1)}, bf16[2,2,32,1664]{3,2,1,0:T(8,128)(2,1)S(1)}, u32[]{:S(2)}, u32[]{:S(2)}) collective-permute-start(bf16[2,2,32,1664]{3,2,1,0:T(8,128)(2,1)S(1)} %get-tuple-element.79.refs_0_), channel_id=1, source_target_pairs={{0,1},{1,0},{2,3},{3,2},{4,5},{5,4},{6,7},{7,6},{8,9},{9,8},{10,11... | collective-permute-start | bytes 1277960 | tf_op jit(solution)/shard_map/ppermute | solution.py:51
  89.5 8.6 %collective-permute-start.19 = (bf16[2,2,32,1664]{3,2,1,0:T(8,128)(2,1)S(1)}, bf16[2,2,32,1664]{3,2,1,0:T(8,128)(2,1)S(1)}, u32[]{:S(2)}, u32[]{:S(2)}) collective-permute-start(bf16[2,2,32,1664]{3,2,1,0:T(8,128)(2,1)S(1)} %get-tuple-element.80.refs_0_), channel_id=1, source_target_pairs={{0,3},{1,2},{2,1},{3,0},{4,7},{5,6},{6,5},{7,4},{8,11},{9,10},{10,... | collective-permute-start | bytes 1277960 | tf_op jit(solution)/shard_map/ppermute | solution.py:51
  91.6 8.6 %collective-permute-start.18 = (bf16[2,2,32,1664]{3,2,1,0:T(8,128)(2,1)S(1)}, bf16[2,2,32,1664]{3,2,1,0:T(8,128)(2,1)S(1)}, u32[]{:S(2)}, u32[]{:S(2)}) collective-permute-start(bf16[2,2,32,1664]{3,2,1,0:T(8,128)(2,1)S(1)} %get-tuple-element.82.refs_0_), channel_id=1, source_target_pairs={{0,1},{1,0},{2,3},{3,2},{4,5},{5,4},{6,7},{7,6},{8,9},{9,8},{10,11... | collective-permute-start | bytes 1277960 | tf_op jit(solution)/shard_map/ppermute | solution.py:51
  95.6 9.1 %collective-permute-start.25 = (bf16[2,2,32,1664]{3,2,1,0:T(8,128)(2,1)S(1)}, bf16[2,2,32,1664]{3,2,1,0:T(8,128)(2,1)S(1)}, u32[]{:S(2)}, u32[]{:S(2)}) collective-permute-start(bf16[2,2,32,1664]{3,2,1,0:T(8,128)(2,1)S(1)} %halves.20.refs_0_.mine), channel_id=1, source_target_pairs={{0,1},{1,0},{2,3},{3,2},{4,5},{5,4},{6,7},{7,6},{8,9},{9,8},{10,11... | collective-permute-start | bytes 1277960 | tf_op jit(solution)/shard_map/ppermute | solution.py:51
  98.0 9.4 %collective-permute-start.24 = (bf16[2,2,32,1664]{3,2,1,0:T(8,128)(2,1)S(1)}, bf16[2,2,32,1664]{3,2,1,0:T(8,128)(2,1)S(1)}, u32[]{:S(2)}, u32[]{:S(2)}) collective-permute-start(bf16[2,2,32,1664]{3,2,1,0:T(8,128)(2,1)S(1)} %halves.21.refs_0_.mine), channel_id=1, source_target_pairs={{0,3},{1,2},{2,1},{3,0},{4,7},{5,6},{6,5},{7,4},{8,11},{9,10},{10,... | collective-permute-start | bytes 1277960 | tf_op jit(solution)/shard_map/ppermute | solution.py:51
  100.2 9.1 %collective-permute-start.23 = (bf16[2,2,32,1664]{3,2,1,0:T(8,128)(2,1)S(1)}, bf16[2,2,32,1664]{3,2,1,0:T(8,128)(2,1)S(1)}, u32[]{:S(2)}, u32[]{:S(2)}) collective-permute-start(bf16[2,2,32,1664]{3,2,1,0:T(8,128)(2,1)S(1)} %halves.22.refs_0_.mine), channel_id=1, source_target_pairs={{0,1},{1,0},{2,3},{3,2},{4,5},{5,4},{6,7},{7,6},{8,9},{9,8},{10,11... | collective-permute-start | bytes 1277960 | tf_op jit(solution)/shard_map/ppermute | solution.py:51
  104.8 8.5 %collective-permute-start.22 = (bf16[2,2,32,1664]{3,2,1,0:T(8,128)(2,1)S(1)}, bf16[2,2,32,1664]{3,2,1,0:T(8,128)(2,1)S(1)}, u32[]{:S(2)}, u32[]{:S(2)}) collective-permute-start(bf16[2,2,32,1664]{3,2,1,0:T(8,128)(2,1)S(1)} %halves.23.refs_0_.mine), channel_id=1, source_target_pairs={{0,3},{1,2},{2,1},{3,0},{4,7},{5,6},{6,5},{7,4},{8,11},{9,10},{10,... | collective-permute-start | bytes 1277960 | tf_op jit(solution)/shard_map/ppermute | solution.py:51
  107.4 8.5 %collective-permute-start.29 = (bf16[2,32,1664]{2,1,0:T(8,128)(2,1)S(1)}, bf16[2,32,1664]{2,1,0:T(8,128)(2,1)S(1)}, u32[]{:S(2)}, u32[]{:S(2)}) collective-permute-start(bf16[2,32,1664]{2,1,0:T(8,128)(2,1)S(1)} %hidden.4.refs_0_.mine), channel_id=1, source_target_pairs={{0,3},{1,2},{2,1},{3,0},{4,7},{5,6},{6,5},{7,4},{8,11},{9,10},{10,... | collective-permute-start | bytes 638984 | tf_op jit(solution)/shard_map/ppermute | solution.py:51
  109.3 6.7 %collective-permute-start.28 = (bf16[2,32,1664]{2,1,0:T(8,128)(2,1)S(1)}, bf16[2,32,1664]{2,1,0:T(8,128)(2,1)S(1)}, u32[]{:S(2)}, u32[]{:S(2)}) collective-permute-start(bf16[2,32,1664]{2,1,0:T(8,128)(2,1)S(1)} %hidden.5.refs_0_.mine), channel_id=1, source_target_pairs={{0,1},{1,0},{2,3},{3,2},{4,5},{5,4},{6,7},{7,6},{8,9},{9,8},{10,11... | collective-permute-start | bytes 638984 | tf_op jit(solution)/shard_map/ppermute | solution.py:51
  113.2 5.9 %collective-permute-start.27 = (bf16[2,32,1664]{2,1,0:T(8,128)(2,1)S(1)}, bf16[2,32,1664]{2,1,0:T(8,128)(2,1)S(1)}, u32[]{:S(2)}, u32[]{:S(2)}) collective-permute-start(bf16[2,32,1664]{2,1,0:T(8,128)(2,1)S(1)} %hidden.6.refs_0_.mine), channel_id=1, source_target_pairs={{0,3},{1,2},{2,1},{3,0},{4,7},{5,6},{6,5},{7,4},{8,11},{9,10},{10,... | collective-permute-start | bytes 638984 | tf_op jit(solution)/shard_map/ppermute | solution.py:51
  115.9 5.9 %collective-permute-start.26 = (bf16[2,32,1664]{2,1,0:T(8,128)(2,1)S(1)}, bf16[2,32,1664]{2,1,0:T(8,128)(2,1)S(1)}, u32[]{:S(2)}, u32[]{:S(2)}) collective-permute-start(bf16[2,32,1664]{2,1,0:T(8,128)(2,1)S(1)} %hidden.7.refs_0_.mine), channel_id=1, source_target_pairs={{0,1},{1,0},{2,3},{3,2},{4,5},{5,4},{6,7},{7,6},{8,9},{9,8},{10,11... | collective-permute-start | bytes 638984 | tf_op jit(solution)/shard_map/ppermute | solution.py:51
  116.1 7.5 %collective-permute-start.33 = (bf16[2,64,1664]{2,1,0:T(8,128)(2,1)S(1)}, bf16[2,64,1664]{2,1,0:T(8,128)(2,1)S(1)}, u32[]{:S(2)}, u32[]{:S(2)}) collective-permute-start(bf16[2,64,1664]{2,1,0:T(8,128)(2,1)S(1)} %join.8.refs_0_.mine), channel_id=1, source_target_pairs={{0,4},{1,5},{2,6},{3,7},{4,0},{5,1},{6,2},{7,3},{8,12},{9,13},{10,... | collective-permute-start | bytes 1277960 | tf_op jit(solution)/shard_map/ppermute | solution.py:51
  119.2 8.5 %collective-permute-start.32 = (bf16[2,64,1664]{2,1,0:T(8,128)(2,1)S(1)}, bf16[2,64,1664]{2,1,0:T(8,128)(2,1)S(1)}, u32[]{:S(2)}, u32[]{:S(2)}) collective-permute-start(bf16[2,64,1664]{2,1,0:T(8,128)(2,1)S(1)} %join.9.refs_0_.mine), channel_id=1, source_target_pairs={{0,12},{1,13},{2,14},{3,15},{4,8},{5,9},{6,10},{7,11},{8,4},{9,5},... | collective-permute-start | bytes 1277960 | tf_op jit(solution)/shard_map/ppermute | solution.py:51
  121.9 8.4 %collective-permute-start.31 = (bf16[2,64,1664]{2,1,0:T(8,128)(2,1)S(1)}, bf16[2,64,1664]{2,1,0:T(8,128)(2,1)S(1)}, u32[]{:S(2)}, u32[]{:S(2)}) collective-permute-start(bf16[2,64,1664]{2,1,0:T(8,128)(2,1)S(1)} %join.10.refs_0_.mine), channel_id=1, source_target_pairs={{0,4},{1,5},{2,6},{3,7},{4,0},{5,1},{6,2},{7,3},{8,12},{9,13},{10,... | collective-permute-start | bytes 1277960 | tf_op jit(solution)/shard_map/ppermute | solution.py:51
  123.7 21.6 %collective-permute-start.38 = (bf16[2,128,1664]{2,1,0:T(8,128)(2,1)S(1)}, bf16[2,128,1664]{2,1,0:T(8,128)(2,1)S(1)}, u32[]{:S(2)}, u32[]{:S(2)}) collective-permute-start(bf16[2,128,1664]{2,1,0:T(8,128)(2,1)S(1)} %join.12.refs_0_), channel_id=1, source_target_pairs={{0,12},{1,13},{2,14},{3,15},{4,8},{5,9},{6,10},{7,11},{8,4},{9,5},... | collective-permute-start | bytes 2555912 | tf_op jit(solution)/shard_map/ppermute | solution.py:51
  127.7 22.5 %collective-permute-start.37 = (bf16[2,128,1664]{2,1,0:T(8,128)(2,1)S(1)}, bf16[2,128,1664]{2,1,0:T(8,128)(2,1)S(1)}, u32[]{:S(2)}, u32[]{:S(2)}) collective-permute-start(bf16[2,128,1664]{2,1,0:T(8,128)(2,1)S(1)} %join.13.refs_3_.refs_0_), channel_id=1, source_target_pairs={{0,4},{1,5},{2,6},{3,7},{4,0},{5,1},{6,2},{7,3},{8,12},{9,13},{10,... | collective-permute-start | bytes 2555912 | tf_op jit(solution)/shard_map/ppermute | solution.py:51
  130.3 12.1 %collective-permute-start.30 = (bf16[2,64,1664]{2,1,0:T(8,128)(2,1)S(1)}, bf16[2,64,1664]{2,1,0:T(8,128)(2,1)S(1)}, u32[]{:S(2)}, u32[]{:S(2)}) collective-permute-start(bf16[2,64,1664]{2,1,0:T(8,128)(2,1)S(1)} %join.11.refs_0_.mine), channel_id=1, source_target_pairs={{0,12},{1,13},{2,14},{3,15},{4,8},{5,9},{6,10},{7,11},{8,4},{9,5},... | collective-permute-start | bytes 1277960 | tf_op jit(solution)/shard_map/ppermute | solution.py:51
  142.4 9.0 %collective-permute-start.41 = (bf16[1,128,1664]{2,1,0:T(8,128)(2,1)S(1)}, bf16[1,128,1664]{2,1,0:T(8,128)(2,1)S(1)}, u32[]{:S(2)}, u32[]{:S(2)}) collective-permute-start(bf16[1,128,1664]{2,1,0:T(8,128)(2,1)S(1)} %get-tuple-element.92.refs_1_), channel_id=1, source_target_pairs={{0,12},{1,13},{2,14},{3,15},{4,8},{5,9},{6,10},{7,11},{8,4},{9,5},... | collective-permute-start | bytes 1277960 | tf_op jit(solution)/shard_map/ppermute | solution.py:51
  145.1 12.5 %collective-permute-start.40 = (bf16[1,128,1664]{2,1,0:T(8,128)(2,1)S(1)}, bf16[1,128,1664]{2,1,0:T(8,128)(2,1)S(1)}, u32[]{:S(2)}, u32[]{:S(2)}) collective-permute-start(bf16[1,128,1664]{2,1,0:T(8,128)(2,1)S(1)} %get-tuple-element.91.refs_1_), channel_id=1, source_target_pairs={{0,4},{1,5},{2,6},{3,7},{4,0},{5,1},{6,2},{7,3},{8,12},{9,13},{10,... | collective-permute-start | bytes 1277960 | tf_op jit(solution)/shard_map/ppermute | solution.py:51
  145.2 13.7 %collective-permute-start.39 = (bf16[1,128,1664]{2,1,0:T(8,128)(2,1)S(1)}, bf16[1,128,1664]{2,1,0:T(8,128)(2,1)S(1)}, u32[]{:S(2)}, u32[]{:S(2)}) collective-permute-start(bf16[1,128,1664]{2,1,0:T(8,128)(2,1)S(1)} %get-tuple-element.87.refs_0_), channel_id=1, source_target_pairs={{0,12},{1,13},{2,14},{3,15},{4,8},{5,9},{6,10},{7,11},{8,4},{9,5},... | collective-permute-start | bytes 1277960 | tf_op jit(solution)/shard_map/ppermute | solution.py:51
  145.3 16.6 %collective-permute-start.34 = (bf16[1,128,1664]{2,1,0:T(8,128)(2,1)S(1)}, bf16[1,128,1664]{2,1,0:T(8,128)(2,1)S(1)}, u32[]{:S(2)}, u32[]{:S(2)}) collective-permute-start(bf16[1,128,1664]{2,1,0:T(8,128)(2,1)S(1)} %get-tuple-element.88.refs_4_.refs_0_), channel_id=1, source_target_pairs={{0,4},{1,5},{2,6},{3,7},{4,0},{5,1},{6,2},{7,3},{8,12},{9,13},{10,... | collective-permute-start | bytes 1277960 | tf_op jit(solution)/shard_map/ppermute | solution.py:51
  152.2 11.3 %collective-permute-start.45 = (bf16[128,1024]{1,0:T(8,128)(2,1)S(1)}, bf16[128,1024]{1,0:T(8,128)(2,1)S(1)}, u32[]{:S(2)}, u32[]{:S(2)}) collective-permute-start(bf16[128,1024]{1,0:T(8,128)(2,1)S(1)} %get-tuple-element.93.refs_5_), channel_id=1, source_target_pairs={{0,16},{16,0},{32,48},{48,32},{64,80},{80,64},{96,112},{112,96},{1... | collective-permute-start | bytes 786440 | tf_op jit(solution)/shard_map/ppermute | solution.py:55
  158.4 7.1 %collective-permute-start.43 = (bf16[128,1024]{1,0:T(8,128)(2,1)S(1)}, bf16[128,1024]{1,0:T(8,128)(2,1)S(1)}, u32[]{:S(2)}, u32[]{:S(2)}) collective-permute-start(bf16[128,1024]{1,0:T(8,128)(2,1)S(1)} %get-tuple-element.94.refs_5_), channel_id=1, source_target_pairs={{0,16},{16,0},{32,48},{48,32},{64,80},{80,64},{96,112},{112,96},{1... | collective-permute-start | bytes 786440 | tf_op jit(solution)/shard_map/ppermute | solution.py:55
  159.7 5.6 %collective-permute-start.47 = (bf16[128,1024]{1,0:T(8,128)(2,1)S(1)}, bf16[128,1024]{1,0:T(8,128)(2,1)S(1)}, u32[]{:S(2)}, u32[]{:S(2)}) collective-permute-start(bf16[128,1024]{1,0:T(8,128)(2,1)S(1)} %get-tuple-element.95.refs_5_), channel_id=1, source_target_pairs={{0,16},{16,0},{32,48},{48,32},{64,80},{80,64},{96,112},{112,96},{1... | collective-permute-start | bytes 786440 | tf_op jit(solution)/shard_map/ppermute | solution.py:55
  162.7 4.2 %collective-permute-start.42 = (bf16[128,1024]{1,0:T(8,128)(2,1)S(1)}, bf16[128,1024]{1,0:T(8,128)(2,1)S(1)}, u32[]{:S(2)}, u32[]{:S(2)}) collective-permute-start(bf16[128,1024]{1,0:T(8,128)(2,1)S(1)} %get-tuple-element.97), channel_id=1, source_target_pairs={{0,16},{16,0},{32,48},{48,32},{64,80},{80,64},{96,112},{112,96},{1... | collective-permute-start | bytes 786440 | tf_op jit(solution)/shard_map/ppermute | solution.py:55
  163.5 8.0 %collective-permute-start.46 = (bf16[128,1024]{1,0:T(8,128)(2,1)S(1)}, bf16[128,1024]{1,0:T(8,128)(2,1)S(1)}, u32[]{:S(2)}, u32[]{:S(2)}) collective-permute-start(bf16[128,1024]{1,0:T(8,128)(2,1)S(1)} %add_convert_fusion.2), channel_id=1, source_target_pairs={{0,96},{16,112},{32,0},{48,16},{64,32},{80,48},{96,64},{112,80},{1... | collective-permute-start | bytes 786440 | tf_op jit(solution)/shard_map/ppermute | solution.py:59
  165.4 14.5 %collective-permute-start.48 = (bf16[128,1024]{1,0:T(8,128)(2,1)S(1)}, bf16[128,1024]{1,0:T(8,128)(2,1)S(1)}, u32[]{:S(2)}, u32[]{:S(2)}) collective-permute-start(bf16[128,1024]{1,0:T(8,128)(2,1)S(1)} %add_convert_fusion.1), channel_id=1, source_target_pairs={{0,32},{16,48},{32,64},{48,80},{64,96},{80,112},{96,0},{112,16},{1... | collective-permute-start | bytes 786440 | tf_op jit(solution)/shard_map/ppermute | solution.py:59
  165.5 14.3 %collective-permute-start.44 = (bf16[128,1024]{1,0:T(8,128)(2,1)S(1)}, bf16[128,1024]{1,0:T(8,128)(2,1)S(1)}, u32[]{:S(2)}, u32[]{:S(2)}) collective-permute-start(bf16[128,1024]{1,0:T(8,128)(2,1)S(1)} %add_convert_fusion.3), channel_id=1, source_target_pairs={{0,64},{16,80},{32,96},{48,112},{64,0},{80,16},{96,32},{112,48},{1... | collective-permute-start | bytes 786440 | tf_op jit(solution)/shard_map/ppermute | solution.py:59
  (2 other events, 4.9 us)

commit v7 on v6

--- a/solution.py
+++ b/solution.py
@@ -335,7 +335,7 @@
         return out
 
 
-TURNS = "ogju1k03120w32103210321032103210103232103232"
+TURNS = "ogju1k03120w32103210321032103210321032103232"
 
 
 def local(tokens, gate_weight, up_weight, down_weight):

time: 181 us -> 176 us (0.972)
  waiting for transfers between devices: 69.5 us -> 66.5 us
    ppermute x30, waiting for transfers between devices: 54.9 us -> 51.8 us  [exchange(): return lax.ppermute(a, ('group', 'mp'), pairs)]
  transfers between devices with their start and end apart: 49 -> 49, of which waited for: 20 -> 20; matrix products, arithmetic and copies ran while one was open for 0% -> 0% of each run, Pallas kernels for 22% -> 23%
where the time goes in v7:
time: 176 us
  starting transfers between devices  68.2 us (39%)
  waiting for transfers between devices  66.5 us (38%)
  Pallas kernels  40 us (23%)
    ppermute x30, waiting for transfers between devices, exchange(): return lax.ppermute(a, ('group', 'mp'), pairs)  51.8 us
    ppermute x30, starting transfers between devices, exchange(): return lax.ppermute(a, ('group', 'mp'), pairs)  43.3 us
    pallas_call x45, Pallas kernels, kernel(): pl.pallas_call(body, in_specs=specs + [ANY] * len(after), out_specs=[VMEM...  40 us
    ppermute x13, starting transfers between devices, swap(): return lax.ppermute(a, 'group', SWAP)  16.4 us
    ppermute x6, waiting for transfers between devices, shift(): lax.ppermute(a, 'group', [(g, (g + 2 * chips) % 8) for g in range(8)])  14.5 us
    ppermute x6, starting transfers between devices, shift(): lax.ppermute(a, 'group', [(g, (g + 2 * chips) % 8) for g in range(8)])  8.59 us
  transfers between devices with their start and end apart: 49, of which 20 were waited for; matrix products, arithmetic and copies ran while one was open for 0% of the time, Pallas kernels for 23%

profile of v7, /device:TPU:1, one launch (start us, length us, event | category | flops | bytes accessed | tf_op | source)
XLA Modules:
  0.0 176.2 jit_solution(2112364875113747380)
XLA Ops:
  0.0 1.4 collective-permute-start
  1.4 1.7 collective-permute-start.3
  3.1 2.1 %collective-permute-start.2 = (bf16[128,1024]{1,0:T(8,128)(2,1)}, bf16[128,1024]{1,0:T(8,128)(2,1)S(1)}, u32[]{:S(2)}, u32[]{:S(2)}) collective-permute-start(bf16[128,1024]{1,0:T(8,128)(2,1)} %source.1), channel_id=1, source_target_pairs={{0,96},{16,112},{32,0},{48,16},{64,32},{80,48},{96,64},{112,80},{1... | collective-permute-start | bytes 786440 | tf_op jit(solution)/shard_map/ppermute | solution.py:59
  6.3 3.1 %cut.4 = (bf16[1024,896]{1,0:T(8,128)(2,1)S(1)}, bf16[1024,768]{1,0:T(8,128)(2,1)S(1)}, bf16[1024,896]{1,0:T(8,128)(2,1)S(1)}, bf16[1024,768]{1,0:T(8,128)(2,1)S(1)}) custom-call(bf16[1024,3328]{1,0:T(8,128)(2,1)} %refs_0_.5, bf16[1024,3328]{1,0:T(8,128)(2,1)} %refs_0_.6, bf16[128,1024]{1,0:T(8,128)(2,1)S(1)} %stack.3.refs_2_), custom_call_target="tpu_custom_call" | custom-call | flops 11500000256 | tf_op jit(solution)/shard_map/cut/pallas_call | solution.py:80
  9.3 2.0 %cut.5 = (bf16[1024,896]{1,0:T(8,128)(2,1)S(1)}, bf16[1024,768]{1,0:T(8,128)(2,1)S(1)}) custom-call(bf16[1024,3328]{1,0:T(8,128)(2,1)} %refs_0_.5, bf16[1024,896]{1,0:T(8,128)(2,1)S(1)} %get-tuple-element.53.refs_1_.refs_2_.refs_4_), custom_call_target="tpu_custom_call" | custom-call | flops 5750000128 | tf_op jit(solution)/shard_map/cut/pallas_call | solution.py:80
  11.8 1.5 collective-permute-start.1
  13.9 2.0 %cut.6 = (bf16[1024,896]{1,0:T(8,128)(2,1)S(1)}, bf16[1024,768]{1,0:T(8,128)(2,1)S(1)}) custom-call(bf16[1024,3328]{1,0:T(8,128)(2,1)} %refs_0_.6, bf16[2,128,1024]{2,1,0:T(8,128)(2,1)S(1)} %stack.4.refs_1_.refs_0_), custom_call_target="tpu_custom_call" | custom-call | flops 5750000128 | tf_op jit(solution)/shard_map/cut/pallas_call | solution.py:80
  15.9 3.7 %project.4 = (bf16[2,2,128,1664]{3,2,1,0:T(8,128)(2,1)S(1)}, bf16[2,2,128,1664]{3,2,1,0:T(8,128)(2,1)S(1)}) custom-call(bf16[2,128,1024]{2,1,0:T(8,128)(2,1)S(1)} %stack.4.refs_1_.refs_0_, bf16[2,128,1024]{2,1,0:T(8,128)(2,1)S(1)} %collective-permute-done.4.refs_1_, bf16[1024,896]{1,0:T(8,128)(2,1)S(1)} %get-tuple-element.53.refs_1_.refs_2_.refs_4_, ...), custom_call_target="tpu_custom_call" | custom-call | flops 1150000000 | tf_op jit(solution)/shard_map/project/pallas_call | solution.py:80
  19.6 1.5 collective-permute-done.1.source
  22.7 2.7 %collective-permute-start.10 = (bf16[2,2,128,1664]{3,2,1,0:T(8,128)(2,1)S(1)}, bf16[2,2,128,1664]{3,2,1,0:T(8,128)(2,1)S(1)}, u32[]{:S(2)}, u32[]{:S(2)}) collective-permute-start(bf16[2,2,128,1664]{3,2,1,0:T(8,128)(2,1)S(1)} %get-tuple-element.59.refs_0_), channel_id=1, source_target_pairs={{0,12},{1,13},{2,14},{3,15},{4,8},{5,9},{6,10},{7,11},{8,4},{9,5},... | collective-permute-start | bytes 5111816 | tf_op jit(solution)/shard_map/ppermute | solution.py:51
  25.5 3.7 %project.5 = (bf16[2,2,128,1664]{3,2,1,0:T(8,128)(2,1)S(1)}, bf16[2,2,128,1664]{3,2,1,0:T(8,128)(2,1)S(1)}) custom-call(bf16[1,128,1024]{2,1,0:T(8,128)(2,1)S(1)} %bitcast.8, bf16[1,128,1024]{2,1,0:T(8,128)(2,1)S(1)} %bitcast.6, bf16[1,128,1024]{2,1,0:T(8,128)(2,1)S(1)} %bitcast.4, bf16[1,128,1024]{2,1,0:T(8,128)(2,1)S(1)} %bitcast.10, ...), custom_call_target="tpu_custom_call" | custom-call | flops 1150000000 | tf_op jit(solution)/shard_map/project/pallas_call | solution.py:80
  29.3 1.4 collective-permute-start.13
  30.8 3.7 %project.6 = (bf16[2,2,128,1664]{3,2,1,0:T(8,128)(2,1)S(1)}, bf16[2,2,128,1664]{3,2,1,0:T(8,128)(2,1)S(1)}) custom-call(bf16[2,128,1024]{2,1,0:T(8,128)(2,1)S(1)} %stack.4.refs_1_.refs_0_, bf16[2,128,1024]{2,1,0:T(8,128)(2,1)S(1)} %collective-permute-done.4.refs_1_, bf16[1024,896]{1,0:T(8,128)(2,1)S(1)} %collective-permute-done.6.refs_2_.refs_4_, ...), custom_call_target="tpu_custom_call" | custom-call | flops 1150000000 | tf_op jit(solution)/shard_map/project/pallas_call | solution.py:80
  34.6 3.0 %collective-permute-start.12 = (bf16[2,2,128,1664]{3,2,1,0:T(8,128)(2,1)S(1)}, bf16[2,2,128,1664]{3,2,1,0:T(8,128)(2,1)S(1)}, u32[]{:S(2)}, u32[]{:S(2)}) collective-permute-start(bf16[2,2,128,1664]{3,2,1,0:T(8,128)(2,1)S(1)} %get-tuple-element.64.refs_0_), channel_id=1, source_target_pairs={{0,12},{1,13},{2,14},{3,15},{4,8},{5,9},{6,10},{7,11},{8,4},{9,5},... | collective-permute-start | bytes 5111816 | tf_op jit(solution)/shard_map/ppermute | solution.py:51
  37.6 7.3 %collective-permute-done.10.came = bf16[2,2,128,1664]{3,2,1,0:T(8,128)(2,1)S(1)} collective-permute-done((bf16[2,2,128,1664]{3,2,1,0:T(8,128)(2,1)S(1)}, bf16[2,2,128,1664]{3,2,1,0:T(8,128)(2,1)S(1)}, u32[]{:S(2)}, u32[]{:S(2)}) %collective-permute-start.10) | collective-permute-done | bytes 1703968 | tf_op jit(solution)/shard_map/ppermute | solution.py:51
  45.3 3.7 %project.7 = (bf16[2,2,128,1664]{3,2,1,0:T(8,128)(2,1)S(1)}, bf16[2,2,128,1664]{3,2,1,0:T(8,128)(2,1)S(1)}) custom-call(bf16[1,128,1024]{2,1,0:T(8,128)(2,1)S(1)} %bitcast.9, bf16[1,128,1024]{2,1,0:T(8,128)(2,1)S(1)} %bitcast.7, bf16[1,128,1024]{2,1,0:T(8,128)(2,1)S(1)} %bitcast.5, bf16[1,128,1024]{2,1,0:T(8,128)(2,1)S(1)} %bitcast.11, ...), custom_call_target="tpu_custom_call" | custom-call | flops 1150000000 | tf_op jit(solution)/shard_map/project/pallas_call | solution.py:80
  49.2 1.4 collective-permute-start.17
  51.0 2.8 %collective-permute-start.16 = (bf16[2,2,64,1664]{3,2,1,0:T(8,128)(2,1)S(1)}, bf16[2,2,64,1664]{3,2,1,0:T(8,128)(2,1)S(1)}, u32[]{:S(2)}, u32[]{:S(2)}) collective-permute-start(bf16[2,2,64,1664]{3,2,1,0:T(8,128)(2,1)S(1)} %get-tuple-element.70.refs_1_), channel_id=1, source_target_pairs={{0,12},{1,13},{2,14},{3,15},{4,8},{5,9},{6,10},{7,11},{8,4},{9,5},... | collective-permute-start | bytes 2555912 | tf_op jit(solution)/shard_map/ppermute | solution.py:51
  53.8 3.0 %cut.7 = (bf16[1664,512]{1,0:T(8,128)(2,1)S(1)}, bf16[1664,512]{1,0:T(8,128)(2,1)S(1)}, bf16[1664,512]{1,0:T(8,128)(2,1)S(1)}, bf16[1664,512]{1,0:T(8,128)(2,1)S(1)}) custom-call(bf16[3328,1024]{1,0:T(8,128)(2,1)} %refs_0_.7, bf16[2,2,64,1664]{3,2,1,0:T(8,128)(2,1)S(1)} %get-tuple-element.70.refs_1_), custom_call_target="tpu_custom_call" | custom-call | flops 11500000256 | tf_op jit(solution)/shard_map/cut/pallas_call | solution.py:80
  56.8 6.4 %collective-permute-done.12.came = bf16[2,2,128,1664]{3,2,1,0:T(8,128)(2,1)S(1)} collective-permute-done((bf16[2,2,128,1664]{3,2,1,0:T(8,128)(2,1)S(1)}, bf16[2,2,128,1664]{3,2,1,0:T(8,128)(2,1)S(1)}, u32[]{:S(2)}, u32[]{:S(2)}) %collective-permute-start.12) | collective-permute-done | bytes 1703968 | tf_op jit(solution)/shard_map/ppermute | solution.py:51
  63.7 6.4 %collective-permute-done.11.came = bf16[2,2,128,1664]{3,2,1,0:T(8,128)(2,1)S(1)} collective-permute-done((bf16[2,2,128,1664]{3,2,1,0:T(8,128)(2,1)S(1)}, bf16[2,2,128,1664]{3,2,1,0:T(8,128)(2,1)S(1)}, u32[]{:S(2)}, u32[]{:S(2)}) %collective-permute-start.11) | collective-permute-done | bytes 1703968 | tf_op jit(solution)/shard_map/ppermute | solution.py:51
  70.5 2.8 %collective-permute-start.14 = (bf16[2,2,64,1664]{3,2,1,0:T(8,128)(2,1)S(1)}, bf16[2,2,64,1664]{3,2,1,0:T(8,128)(2,1)S(1)}, u32[]{:S(2)}, u32[]{:S(2)}) collective-permute-start(bf16[2,2,64,1664]{3,2,1,0:T(8,128)(2,1)S(1)} %get-tuple-element.74.refs_0_), channel_id=1, source_target_pairs={{0,12},{1,13},{2,14},{3,15},{4,8},{5,9},{6,10},{7,11},{8,4},{9,5},... | collective-permute-start | bytes 2555912 | tf_op jit(solution)/shard_map/ppermute | solution.py:51
  73.3 1.8 %collective-permute-start.35 = (bf16[1664,512]{1,0:T(8,128)(2,1)S(1)}, bf16[1664,512]{1,0:T(8,128)(2,1)S(1)}, u32[]{:S(2)}, u32[]{:S(2)}) collective-permute-start(bf16[1664,512]{1,0:T(8,128)(2,1)S(1)} %get-tuple-element.88), channel_id=1, source_target_pairs={{0,16},{16,0},{32,48},{48,32},{64,80},{80,64},{96,112},{112,96},{1... | collective-permute-start | bytes 5111816 | tf_op jit(solution)/shard_map/ppermute | solution.py:55
  75.1 4.2 %collective-permute-done.17.came = bf16[2,2,64,1664]{3,2,1,0:T(8,128)(2,1)S(1)} collective-permute-done((bf16[2,2,64,1664]{3,2,1,0:T(8,128)(2,1)S(1)}, bf16[2,2,64,1664]{3,2,1,0:T(8,128)(2,1)S(1)}, u32[]{:S(2)}, u32[]{:S(2)}) %collective-permute-start.17) | collective-permute-done | bytes 852000 | tf_op jit(solution)/shard_map/ppermute | solution.py:51
  79.2 1.7 collective-permute-start.36
  81.2 2.6 %collective-permute-start.21 = (bf16[2,2,32,1664]{3,2,1,0:T(8,128)(2,1)S(1)}, bf16[2,2,32,1664]{3,2,1,0:T(8,128)(2,1)S(1)}, u32[]{:S(2)}, u32[]{:S(2)}) collective-permute-start(bf16[2,2,32,1664]{3,2,1,0:T(8,128)(2,1)S(1)} %get-tuple-element.78.refs_0_), channel_id=1, source_target_pairs={{0,3},{1,2},{2,1},{3,0},{4,7},{5,6},{6,5},{7,4},{8,11},{9,10},{10,... | collective-permute-start | bytes 1277960 | tf_op jit(solution)/shard_map/ppermute | solution.py:51
  83.9 4.4 %collective-permute-done.15.came = bf16[2,2,64,1664]{3,2,1,0:T(8,128)(2,1)S(1)} collective-permute-done((bf16[2,2,64,1664]{3,2,1,0:T(8,128)(2,1)S(1)}, bf16[2,2,64,1664]{3,2,1,0:T(8,128)(2,1)S(1)}, u32[]{:S(2)}, u32[]{:S(2)}) %collective-permute-start.15) | collective-permute-done | bytes 852000 | tf_op jit(solution)/shard_map/ppermute | solution.py:51
  89.5 1.9 %collective-permute-start.19 = (bf16[2,2,32,1664]{3,2,1,0:T(8,128)(2,1)S(1)}, bf16[2,2,32,1664]{3,2,1,0:T(8,128)(2,1)S(1)}, u32[]{:S(2)}, u32[]{:S(2)}) collective-permute-start(bf16[2,2,32,1664]{3,2,1,0:T(8,128)(2,1)S(1)} %get-tuple-element.80.refs_0_), channel_id=1, source_target_pairs={{0,3},{1,2},{2,1},{3,0},{4,7},{5,6},{6,5},{7,4},{8,11},{9,10},{10,... | collective-permute-start | bytes 1277960 | tf_op jit(solution)/shard_map/ppermute | solution.py:51
  92.4 3.2 %collective-permute-done.20.came = bf16[2,2,32,1664]{3,2,1,0:T(8,128)(2,1)S(1)} collective-permute-done((bf16[2,2,32,1664]{3,2,1,0:T(8,128)(2,1)S(1)}, bf16[2,2,32,1664]{3,2,1,0:T(8,128)(2,1)S(1)}, u32[]{:S(2)}, u32[]{:S(2)}) %collective-permute-start.20) | collective-permute-done | bytes 426016 | tf_op jit(solution)/shard_map/ppermute | solution.py:51
  96.7 1.4 collective-permute-done.19.came
  98.0 1.8 %collective-permute-start.24 = (bf16[2,2,32,1664]{3,2,1,0:T(8,128)(2,1)S(1)}, bf16[2,2,32,1664]{3,2,1,0:T(8,128)(2,1)S(1)}, u32[]{:S(2)}, u32[]{:S(2)}) collective-permute-start(bf16[2,2,32,1664]{3,2,1,0:T(8,128)(2,1)S(1)} %halves.21.refs_0_.mine), channel_id=1, source_target_pairs={{0,3},{1,2},{2,1},{3,0},{4,7},{5,6},{6,5},{7,4},{8,11},{9,10},{10,... | collective-permute-start | bytes 1277960 | tf_op jit(solution)/shard_map/ppermute | solution.py:51
  101.2 3.5 %collective-permute-done.25.theirs = bf16[2,2,32,1664]{3,2,1,0:T(8,128)(2,1)S(1)} collective-permute-done((bf16[2,2,32,1664]{3,2,1,0:T(8,128)(2,1)S(1)}, bf16[2,2,32,1664]{3,2,1,0:T(8,128)(2,1)S(1)}, u32[]{:S(2)}, u32[]{:S(2)}) %collective-permute-start.25) | collective-permute-done | bytes 426016 | tf_op jit(solution)/shard_map/ppermute | solution.py:51
  104.8 2.5 %collective-permute-start.22 = (bf16[2,2,32,1664]{3,2,1,0:T(8,128)(2,1)S(1)}, bf16[2,2,32,1664]{3,2,1,0:T(8,128)(2,1)S(1)}, u32[]{:S(2)}, u32[]{:S(2)}) collective-permute-start(bf16[2,2,32,1664]{3,2,1,0:T(8,128)(2,1)S(1)} %halves.23.refs_0_.mine), channel_id=1, source_target_pairs={{0,3},{1,2},{2,1},{3,0},{4,7},{5,6},{6,5},{7,4},{8,11},{9,10},{10,... | collective-permute-start | bytes 1277960 | tf_op jit(solution)/shard_map/ppermute | solution.py:51
  110.4 2.8 %collective-permute-done.22.theirs = bf16[2,2,32,1664]{3,2,1,0:T(8,128)(2,1)S(1)} collective-permute-done((bf16[2,2,32,1664]{3,2,1,0:T(8,128)(2,1)S(1)}, bf16[2,2,32,1664]{3,2,1,0:T(8,128)(2,1)S(1)}, u32[]{:S(2)}, u32[]{:S(2)}) %collective-permute-start.22) | collective-permute-done | bytes 426016 | tf_op jit(solution)/shard_map/ppermute | solution.py:51
  113.2 2.5 %collective-permute-start.27 = (bf16[2,32,1664]{2,1,0:T(8,128)(2,1)S(1)}, bf16[2,32,1664]{2,1,0:T(8,128)(2,1)S(1)}, u32[]{:S(2)}, u32[]{:S(2)}) collective-permute-start(bf16[2,32,1664]{2,1,0:T(8,128)(2,1)S(1)} %hidden.6.refs_0_.mine), channel_id=1, source_target_pairs={{0,3},{1,2},{2,1},{3,0},{4,7},{5,6},{6,5},{7,4},{8,11},{9,10},{10,... | collective-permute-start | bytes 638984 | tf_op jit(solution)/shard_map/ppermute | solution.py:51
  116.2 2.9 %collective-permute-done.27.theirs = bf16[2,32,1664]{2,1,0:T(8,128)(2,1)S(1)} collective-permute-done((bf16[2,32,1664]{2,1,0:T(8,128)(2,1)S(1)}, bf16[2,32,1664]{2,1,0:T(8,128)(2,1)S(1)}, u32[]{:S(2)}, u32[]{:S(2)}) %collective-permute-start.27) | collective-permute-done | bytes 213024 | tf_op jit(solution)/shard_map/ppermute | solution.py:51
  119.2 2.7 %collective-permute-start.32 = (bf16[2,64,1664]{2,1,0:T(8,128)(2,1)S(1)}, bf16[2,64,1664]{2,1,0:T(8,128)(2,1)S(1)}, u32[]{:S(2)}, u32[]{:S(2)}) collective-permute-start(bf16[2,64,1664]{2,1,0:T(8,128)(2,1)S(1)} %join.9.refs_0_.mine), channel_id=1, source_target_pairs={{0,12},{1,13},{2,14},{3,15},{4,8},{5,9},{6,10},{7,11},{8,4},{9,5},... | collective-permute-start | bytes 1277960 | tf_op jit(solution)/shard_map/ppermute | solution.py:51
  122.2 1.4 collective-permute-done.33.theirs
  123.6 3.7 %collective-permute-start.30 = (bf16[2,64,1664]{2,1,0:T(8,128)(2,1)S(1)}, bf16[2,64,1664]{2,1,0:T(8,128)(2,1)S(1)}, u32[]{:S(2)}, u32[]{:S(2)}) collective-permute-start(bf16[2,64,1664]{2,1,0:T(8,128)(2,1)S(1)} %join.11.refs_0_.mine), channel_id=1, source_target_pairs={{0,12},{1,13},{2,14},{3,15},{4,8},{5,9},{6,10},{7,11},{8,4},{9,5},... | collective-permute-start | bytes 1277960 | tf_op jit(solution)/shard_map/ppermute | solution.py:51
  127.6 2.7 %collective-permute-start.38 = (bf16[2,128,1664]{2,1,0:T(8,128)(2,1)S(1)}, bf16[2,128,1664]{2,1,0:T(8,128)(2,1)S(1)}, u32[]{:S(2)}, u32[]{:S(2)}) collective-permute-start(bf16[2,128,1664]{2,1,0:T(8,128)(2,1)S(1)} %join.12.refs_0_), channel_id=1, source_target_pairs={{0,12},{1,13},{2,14},{3,15},{4,8},{5,9},{6,10},{7,11},{8,4},{9,5},... | collective-permute-start | bytes 2555912 | tf_op jit(solution)/shard_map/ppermute | solution.py:51
  130.6 2.5 %collective-permute-done.30.theirs = bf16[2,64,1664]{2,1,0:T(8,128)(2,1)S(1)} collective-permute-done((bf16[2,64,1664]{2,1,0:T(8,128)(2,1)S(1)}, bf16[2,64,1664]{2,1,0:T(8,128)(2,1)S(1)}, u32[]{:S(2)}, u32[]{:S(2)}) %collective-permute-start.30) | collective-permute-done | bytes 426016 | tf_op jit(solution)/shard_map/ppermute | solution.py:51
  133.1 2.7 %collective-permute-start.41 = (bf16[1,128,1664]{2,1,0:T(8,128)(2,1)S(1)}, bf16[1,128,1664]{2,1,0:T(8,128)(2,1)S(1)}, u32[]{:S(2)}, u32[]{:S(2)}) collective-permute-start(bf16[1,128,1664]{2,1,0:T(8,128)(2,1)S(1)} %get-tuple-element.91.refs_1_), channel_id=1, source_target_pairs={{0,12},{1,13},{2,14},{3,15},{4,8},{5,9},{6,10},{7,11},{8,4},{9,5},... | collective-permute-start | bytes 1277960 | tf_op jit(solution)/shard_map/ppermute | solution.py:51
  138.3 4.0 %collective-permute-done.38.refs_0_ = bf16[2,128,1664]{2,1,0:T(8,128)(2,1)S(1)} collective-permute-done((bf16[2,128,1664]{2,1,0:T(8,128)(2,1)S(1)}, bf16[2,128,1664]{2,1,0:T(8,128)(2,1)S(1)}, u32[]{:S(2)}, u32[]{:S(2)}) %collective-permute-start.38) | collective-permute-done | bytes 852000 | tf_op jit(solution)/shard_map/ppermute | solution.py:51
  147.7 5.5 %collective-permute-start.45 = (bf16[128,1024]{1,0:T(8,128)(2,1)S(1)}, bf16[128,1024]{1,0:T(8,128)(2,1)S(1)}, u32[]{:S(2)}, u32[]{:S(2)}) collective-permute-start(bf16[128,1024]{1,0:T(8,128)(2,1)S(1)} %get-tuple-element.93.refs_5_), channel_id=1, source_target_pairs={{0,16},{16,0},{32,48},{48,32},{64,80},{80,64},{96,112},{112,96},{1... | collective-permute-start | bytes 786440 | tf_op jit(solution)/shard_map/ppermute | solution.py:55
  155.2 2.1 %collective-permute-start.47 = (bf16[128,1024]{1,0:T(8,128)(2,1)S(1)}, bf16[128,1024]{1,0:T(8,128)(2,1)S(1)}, u32[]{:S(2)}, u32[]{:S(2)}) collective-permute-start(bf16[128,1024]{1,0:T(8,128)(2,1)S(1)} %get-tuple-element.95.refs_5_), channel_id=1, source_target_pairs={{0,16},{16,0},{32,48},{48,32},{64,80},{80,64},{96,112},{112,96},{1... | collective-permute-start | bytes 786440 | tf_op jit(solution)/shard_map/ppermute | solution.py:55
  159.0 1.8 %collective-permute-start.46 = (bf16[128,1024]{1,0:T(8,128)(2,1)S(1)}, bf16[128,1024]{1,0:T(8,128)(2,1)S(1)}, u32[]{:S(2)}, u32[]{:S(2)}) collective-permute-start(bf16[128,1024]{1,0:T(8,128)(2,1)S(1)} %add_convert_fusion.2), channel_id=1, source_target_pairs={{0,96},{16,112},{32,0},{48,16},{64,32},{80,48},{96,64},{112,80},{1... | collective-permute-start | bytes 786440 | tf_op jit(solution)/shard_map/ppermute | solution.py:59
  162.3 4.6 %collective-permute-done.46 = bf16[128,1024]{1,0:T(8,128)(2,1)S(1)} collective-permute-done((bf16[128,1024]{1,0:T(8,128)(2,1)S(1)}, bf16[128,1024]{1,0:T(8,128)(2,1)S(1)}, u32[]{:S(2)}, u32[]{:S(2)}) %collective-permute-start.46) | collective-permute-done | bytes 262176 | tf_op jit(solution)/shard_map/ppermute | solution.py:59
  167.0 8.3 %collective-permute-done.48 = bf16[128,1024]{1,0:T(8,128)(2,1)S(1)} collective-permute-done((bf16[128,1024]{1,0:T(8,128)(2,1)S(1)}, bf16[128,1024]{1,0:T(8,128)(2,1)S(1)}, u32[]{:S(2)}, u32[]{:S(2)}) %collective-permute-start.48) | collective-permute-done | bytes 262176 | tf_op jit(solution)/shard_map/ppermute | solution.py:59
  (101 shorter events, 29.0 us)
Async XLA Ops:
  0.0 5.3 %collective-permute-start = (bf16[128,1024]{1,0:T(8,128)(2,1)}, bf16[128,1024]{1,0:T(8,128)(2,1)S(1)}, u32[]{:S(2)}, u32[]{:S(2)}) collective-permute-start(bf16[128,1024]{1,0:T(8,128)(2,1)} %source.1), channel_id=1, source_target_pairs={{0,16},{16,0},{32,48},{48,32},{64,80},{80,64},{96,112},{112,96},{1... | collective-permute-start | bytes 786440 | tf_op jit(solution)/shard_map/ppermute | solution.py:55
  1.4 11.9 %collective-permute-start.3 = (bf16[128,1024]{1,0:T(8,128)(2,1)}, bf16[128,1024]{1,0:T(8,128)(2,1)S(1)}, u32[]{:S(2)}, u32[]{:S(2)}) collective-permute-start(bf16[128,1024]{1,0:T(8,128)(2,1)} %source.1), channel_id=1, source_target_pairs={{0,32},{16,48},{32,64},{48,80},{64,96},{80,112},{96,0},{112,16},{1... | collective-permute-start | bytes 786440 | tf_op jit(solution)/shard_map/ppermute | solution.py:59
  3.1 10.2 %collective-permute-start.2 = (bf16[128,1024]{1,0:T(8,128)(2,1)}, bf16[128,1024]{1,0:T(8,128)(2,1)S(1)}, u32[]{:S(2)}, u32[]{:S(2)}) collective-permute-start(bf16[128,1024]{1,0:T(8,128)(2,1)} %source.1), channel_id=1, source_target_pairs={{0,96},{16,112},{32,0},{48,16},{64,32},{80,48},{96,64},{112,80},{1... | collective-permute-start | bytes 786440 | tf_op jit(solution)/shard_map/ppermute | solution.py:59
  11.4 17.9 %collective-permute-start.7 = (bf16[1024,768]{1,0:T(8,128)(2,1)S(1)}, bf16[1024,768]{1,0:T(8,128)(2,1)S(1)}, u32[]{:S(2)}, u32[]{:S(2)}) collective-permute-start(bf16[1024,768]{1,0:T(8,128)(2,1)S(1)} %get-tuple-element.60), channel_id=1, source_target_pairs={{0,16},{16,0},{32,48},{48,32},{64,80},{80,64},{96,112},{112,96},{1... | collective-permute-start | bytes 4718600 | tf_op jit(solution)/shard_map/ppermute | solution.py:55
  11.8 9.3 %collective-permute-start.1 = (bf16[128,1024]{1,0:T(8,128)(2,1)S(1)}, bf16[128,1024]{1,0:T(8,128)(2,1)S(1)}, u32[]{:S(2)}, u32[]{:S(2)}) collective-permute-start(bf16[128,1024]{1,0:T(8,128)(2,1)S(1)} %copy-done), channel_id=1, source_target_pairs={{0,64},{16,80},{32,96},{48,112},{64,0},{80,16},{96,32},{112,48},{1... | collective-permute-start | bytes 786440 | tf_op jit(solution)/shard_map/ppermute | solution.py:59
  21.1 4.3 %collective-permute-start.5 = (bf16[128,1024]{1,0:T(8,128)(2,1)S(1)}, bf16[128,1024]{1,0:T(8,128)(2,1)S(1)}, u32[]{:S(2)}, u32[]{:S(2)}) collective-permute-start(bf16[128,1024]{1,0:T(8,128)(2,1)S(1)} %stack.5.refs_8_), channel_id=1, source_target_pairs={{0,16},{16,0},{32,48},{48,32},{64,80},{80,64},{96,112},{112,96},{1... | collective-permute-start | bytes 786440 | tf_op jit(solution)/shard_map/ppermute | solution.py:55
  22.2 8.7 %collective-permute-start.6 = (bf16[1024,896]{1,0:T(8,128)(2,1)S(1)}, bf16[1024,896]{1,0:T(8,128)(2,1)S(1)}, u32[]{:S(2)}, u32[]{:S(2)}) collective-permute-start(bf16[1024,896]{1,0:T(8,128)(2,1)S(1)} %get-tuple-element.54.refs_0_), channel_id=1, source_target_pairs={{0,16},{16,0},{32,48},{48,32},{64,80},{80,64},{96,112},{112,96},{1... | collective-permute-start | bytes 5505032 | tf_op jit(solution)/shard_map/ppermute | solution.py:55
  22.3 8.6 %collective-permute-start.8 = (bf16[1024,896]{1,0:T(8,128)(2,1)S(1)}, bf16[1024,896]{1,0:T(8,128)(2,1)S(1)}, u32[]{:S(2)}, u32[]{:S(2)}) collective-permute-start(bf16[1024,896]{1,0:T(8,128)(2,1)S(1)} %get-tuple-element.58.refs_6_), channel_id=1, source_target_pairs={{0,16},{16,0},{32,48},{48,32},{64,80},{80,64},{96,112},{112,96},{1... | collective-permute-start | bytes 5505032 | tf_op jit(solution)/shard_map/ppermute | solution.py:55
  22.7 22.2 %collective-permute-start.10 = (bf16[2,2,128,1664]{3,2,1,0:T(8,128)(2,1)S(1)}, bf16[2,2,128,1664]{3,2,1,0:T(8,128)(2,1)S(1)}, u32[]{:S(2)}, u32[]{:S(2)}) collective-permute-start(bf16[2,2,128,1664]{3,2,1,0:T(8,128)(2,1)S(1)} %get-tuple-element.59.refs_0_), channel_id=1, source_target_pairs={{0,12},{1,13},{2,14},{3,15},{4,8},{5,9},{6,10},{7,11},{8,4},{9,5},... | collective-permute-start | bytes 5111816 | tf_op jit(solution)/shard_map/ppermute | solution.py:51
  25.4 5.4 %collective-permute-start.9 = (bf16[1024,768]{1,0:T(8,128)(2,1)S(1)}, bf16[1024,768]{1,0:T(8,128)(2,1)S(1)}, u32[]{:S(2)}, u32[]{:S(2)}) collective-permute-start(bf16[1024,768]{1,0:T(8,128)(2,1)S(1)} %get-tuple-element.61), channel_id=1, source_target_pairs={{0,16},{16,0},{32,48},{48,32},{64,80},{80,64},{96,112},{112,96},{1... | collective-permute-start | bytes 4718600 | tf_op jit(solution)/shard_map/ppermute | solution.py:55
  29.3 21.3 %collective-permute-start.13 = (bf16[2,2,128,1664]{3,2,1,0:T(8,128)(2,1)S(1)}, bf16[2,2,128,1664]{3,2,1,0:T(8,128)(2,1)S(1)}, u32[]{:S(2)}, u32[]{:S(2)}) collective-permute-start(bf16[2,2,128,1664]{3,2,1,0:T(8,128)(2,1)S(1)} %get-tuple-element.63.refs_6_), channel_id=1, source_target_pairs={{0,4},{1,5},{2,6},{3,7},{4,0},{5,1},{6,2},{7,3},{8,12},{9,13},{10,... | collective-permute-start | bytes 5111816 | tf_op jit(solution)/shard_map/ppermute | solution.py:51
  34.6 28.6 %collective-permute-start.12 = (bf16[2,2,128,1664]{3,2,1,0:T(8,128)(2,1)S(1)}, bf16[2,2,128,1664]{3,2,1,0:T(8,128)(2,1)S(1)}, u32[]{:S(2)}, u32[]{:S(2)}) collective-permute-start(bf16[2,2,128,1664]{3,2,1,0:T(8,128)(2,1)S(1)} %get-tuple-element.64.refs_0_), channel_id=1, source_target_pairs={{0,12},{1,13},{2,14},{3,15},{4,8},{5,9},{6,10},{7,11},{8,4},{9,5},... | collective-permute-start | bytes 5111816 | tf_op jit(solution)/shard_map/ppermute | solution.py:51
  49.1 21.0 %collective-permute-start.11 = (bf16[2,2,128,1664]{3,2,1,0:T(8,128)(2,1)S(1)}, bf16[2,2,128,1664]{3,2,1,0:T(8,128)(2,1)S(1)}, u32[]{:S(2)}, u32[]{:S(2)}) collective-permute-start(bf16[2,2,128,1664]{3,2,1,0:T(8,128)(2,1)S(1)} %get-tuple-element.67.refs_0_), channel_id=1, source_target_pairs={{0,4},{1,5},{2,6},{3,7},{4,0},{5,1},{6,2},{7,3},{8,12},{9,13},{10,... | collective-permute-start | bytes 5111816 | tf_op jit(solution)/shard_map/ppermute | solution.py:51
  49.2 30.1 %collective-permute-start.17 = (bf16[2,2,64,1664]{3,2,1,0:T(8,128)(2,1)S(1)}, bf16[2,2,64,1664]{3,2,1,0:T(8,128)(2,1)S(1)}, u32[]{:S(2)}, u32[]{:S(2)}) collective-permute-start(bf16[2,2,64,1664]{3,2,1,0:T(8,128)(2,1)S(1)} %get-tuple-element.65.refs_8_), channel_id=1, source_target_pairs={{0,4},{1,5},{2,6},{3,7},{4,0},{5,1},{6,2},{7,3},{8,12},{9,13},{10,... | collective-permute-start | bytes 2555912 | tf_op jit(solution)/shard_map/ppermute | solution.py:51
  51.0 30.2 %collective-permute-start.16 = (bf16[2,2,64,1664]{3,2,1,0:T(8,128)(2,1)S(1)}, bf16[2,2,64,1664]{3,2,1,0:T(8,128)(2,1)S(1)}, u32[]{:S(2)}, u32[]{:S(2)}) collective-permute-start(bf16[2,2,64,1664]{3,2,1,0:T(8,128)(2,1)S(1)} %get-tuple-element.70.refs_1_), channel_id=1, source_target_pairs={{0,12},{1,13},{2,14},{3,15},{4,8},{5,9},{6,10},{7,11},{8,4},{9,5},... | collective-permute-start | bytes 2555912 | tf_op jit(solution)/shard_map/ppermute | solution.py:51
  63.6 24.8 %collective-permute-start.15 = (bf16[2,2,64,1664]{3,2,1,0:T(8,128)(2,1)S(1)}, bf16[2,2,64,1664]{3,2,1,0:T(8,128)(2,1)S(1)}, u32[]{:S(2)}, u32[]{:S(2)}) collective-permute-start(bf16[2,2,64,1664]{3,2,1,0:T(8,128)(2,1)S(1)} %get-tuple-element.72.refs_0_), channel_id=1, source_target_pairs={{0,4},{1,5},{2,6},{3,7},{4,0},{5,1},{6,2},{7,3},{8,12},{9,13},{10,... | collective-permute-start | bytes 2555912 | tf_op jit(solution)/shard_map/ppermute | solution.py:51
  70.5 19.0 %collective-permute-start.14 = (bf16[2,2,64,1664]{3,2,1,0:T(8,128)(2,1)S(1)}, bf16[2,2,64,1664]{3,2,1,0:T(8,128)(2,1)S(1)}, u32[]{:S(2)}, u32[]{:S(2)}) collective-permute-start(bf16[2,2,64,1664]{3,2,1,0:T(8,128)(2,1)S(1)} %get-tuple-element.74.refs_0_), channel_id=1, source_target_pairs={{0,12},{1,13},{2,14},{3,15},{4,8},{5,9},{6,10},{7,11},{8,4},{9,5},... | collective-permute-start | bytes 2555912 | tf_op jit(solution)/shard_map/ppermute | solution.py:51
  73.3 62.6 %collective-permute-start.35 = (bf16[1664,512]{1,0:T(8,128)(2,1)S(1)}, bf16[1664,512]{1,0:T(8,128)(2,1)S(1)}, u32[]{:S(2)}, u32[]{:S(2)}) collective-permute-start(bf16[1664,512]{1,0:T(8,128)(2,1)S(1)} %get-tuple-element.88), channel_id=1, source_target_pairs={{0,16},{16,0},{32,48},{48,32},{64,80},{80,64},{96,112},{112,96},{1... | collective-permute-start | bytes 5111816 | tf_op jit(solution)/shard_map/ppermute | solution.py:55
  79.2 57.8 %collective-permute-start.36 = (bf16[1664,512]{1,0:T(8,128)(2,1)S(1)}, bf16[1664,512]{1,0:T(8,128)(2,1)S(1)}, u32[]{:S(2)}, u32[]{:S(2)}) collective-permute-start(bf16[1664,512]{1,0:T(8,128)(2,1)S(1)} %get-tuple-element.89), channel_id=1, source_target_pairs={{0,16},{16,0},{32,48},{48,32},{64,80},{80,64},{96,112},{112,96},{1... | collective-permute-start | bytes 5111816 | tf_op jit(solution)/shard_map/ppermute | solution.py:55
  81.2 10.4 %collective-permute-start.21 = (bf16[2,2,32,1664]{3,2,1,0:T(8,128)(2,1)S(1)}, bf16[2,2,32,1664]{3,2,1,0:T(8,128)(2,1)S(1)}, u32[]{:S(2)}, u32[]{:S(2)}) collective-permute-start(bf16[2,2,32,1664]{3,2,1,0:T(8,128)(2,1)S(1)} %get-tuple-element.78.refs_0_), channel_id=1, source_target_pairs={{0,3},{1,2},{2,1},{3,0},{4,7},{5,6},{6,5},{7,4},{8,11},{9,10},{10,... | collective-permute-start | bytes 1277960 | tf_op jit(solution)/shard_map/ppermute | solution.py:51
  88.4 7.3 %collective-permute-start.20 = (bf16[2,2,32,1664]{3,2,1,0:T(8,128)(2,1)S(1)}, bf16[2,2,32,1664]{3,2,1,0:T(8,128)(2,1)S(1)}, u32[]{:S(2)}, u32[]{:S(2)}) collective-permute-start(bf16[2,2,32,1664]{3,2,1,0:T(8,128)(2,1)S(1)} %get-tuple-element.79.refs_0_), channel_id=1, source_target_pairs={{0,1},{1,0},{2,3},{3,2},{4,5},{5,4},{6,7},{7,6},{8,9},{9,8},{10,11... | collective-permute-start | bytes 1277960 | tf_op jit(solution)/shard_map/ppermute | solution.py:51
  89.5 8.6 %collective-permute-start.19 = (bf16[2,2,32,1664]{3,2,1,0:T(8,128)(2,1)S(1)}, bf16[2,2,32,1664]{3,2,1,0:T(8,128)(2,1)S(1)}, u32[]{:S(2)}, u32[]{:S(2)}) collective-permute-start(bf16[2,2,32,1664]{3,2,1,0:T(8,128)(2,1)S(1)} %get-tuple-element.80.refs_0_), channel_id=1, source_target_pairs={{0,3},{1,2},{2,1},{3,0},{4,7},{5,6},{6,5},{7,4},{8,11},{9,10},{10,... | collective-permute-start | bytes 1277960 | tf_op jit(solution)/shard_map/ppermute | solution.py:51
  91.6 8.6 %collective-permute-start.18 = (bf16[2,2,32,1664]{3,2,1,0:T(8,128)(2,1)S(1)}, bf16[2,2,32,1664]{3,2,1,0:T(8,128)(2,1)S(1)}, u32[]{:S(2)}, u32[]{:S(2)}) collective-permute-start(bf16[2,2,32,1664]{3,2,1,0:T(8,128)(2,1)S(1)} %get-tuple-element.82.refs_0_), channel_id=1, source_target_pairs={{0,1},{1,0},{2,3},{3,2},{4,5},{5,4},{6,7},{7,6},{8,9},{9,8},{10,11... | collective-permute-start | bytes 1277960 | tf_op jit(solution)/shard_map/ppermute | solution.py:51
  95.6 9.1 %collective-permute-start.25 = (bf16[2,2,32,1664]{3,2,1,0:T(8,128)(2,1)S(1)}, bf16[2,2,32,1664]{3,2,1,0:T(8,128)(2,1)S(1)}, u32[]{:S(2)}, u32[]{:S(2)}) collective-permute-start(bf16[2,2,32,1664]{3,2,1,0:T(8,128)(2,1)S(1)} %halves.20.refs_0_.mine), channel_id=1, source_target_pairs={{0,1},{1,0},{2,3},{3,2},{4,5},{5,4},{6,7},{7,6},{8,9},{9,8},{10,11... | collective-permute-start | bytes 1277960 | tf_op jit(solution)/shard_map/ppermute | solution.py:51
  98.0 9.4 %collective-permute-start.24 = (bf16[2,2,32,1664]{3,2,1,0:T(8,128)(2,1)S(1)}, bf16[2,2,32,1664]{3,2,1,0:T(8,128)(2,1)S(1)}, u32[]{:S(2)}, u32[]{:S(2)}) collective-permute-start(bf16[2,2,32,1664]{3,2,1,0:T(8,128)(2,1)S(1)} %halves.21.refs_0_.mine), channel_id=1, source_target_pairs={{0,3},{1,2},{2,1},{3,0},{4,7},{5,6},{6,5},{7,4},{8,11},{9,10},{10,... | collective-permute-start | bytes 1277960 | tf_op jit(solution)/shard_map/ppermute | solution.py:51
  100.2 9.1 %collective-permute-start.23 = (bf16[2,2,32,1664]{3,2,1,0:T(8,128)(2,1)S(1)}, bf16[2,2,32,1664]{3,2,1,0:T(8,128)(2,1)S(1)}, u32[]{:S(2)}, u32[]{:S(2)}) collective-permute-start(bf16[2,2,32,1664]{3,2,1,0:T(8,128)(2,1)S(1)} %halves.22.refs_0_.mine), channel_id=1, source_target_pairs={{0,1},{1,0},{2,3},{3,2},{4,5},{5,4},{6,7},{7,6},{8,9},{9,8},{10,11... | collective-permute-start | bytes 1277960 | tf_op jit(solution)/shard_map/ppermute | solution.py:51
  104.8 8.5 %collective-permute-start.22 = (bf16[2,2,32,1664]{3,2,1,0:T(8,128)(2,1)S(1)}, bf16[2,2,32,1664]{3,2,1,0:T(8,128)(2,1)S(1)}, u32[]{:S(2)}, u32[]{:S(2)}) collective-permute-start(bf16[2,2,32,1664]{3,2,1,0:T(8,128)(2,1)S(1)} %halves.23.refs_0_.mine), channel_id=1, source_target_pairs={{0,3},{1,2},{2,1},{3,0},{4,7},{5,6},{6,5},{7,4},{8,11},{9,10},{10,... | collective-permute-start | bytes 1277960 | tf_op jit(solution)/shard_map/ppermute | solution.py:51
  107.4 8.5 %collective-permute-start.29 = (bf16[2,32,1664]{2,1,0:T(8,128)(2,1)S(1)}, bf16[2,32,1664]{2,1,0:T(8,128)(2,1)S(1)}, u32[]{:S(2)}, u32[]{:S(2)}) collective-permute-start(bf16[2,32,1664]{2,1,0:T(8,128)(2,1)S(1)} %hidden.4.refs_0_.mine), channel_id=1, source_target_pairs={{0,3},{1,2},{2,1},{3,0},{4,7},{5,6},{6,5},{7,4},{8,11},{9,10},{10,... | collective-permute-start | bytes 638984 | tf_op jit(solution)/shard_map/ppermute | solution.py:51
  109.3 6.7 %collective-permute-start.28 = (bf16[2,32,1664]{2,1,0:T(8,128)(2,1)S(1)}, bf16[2,32,1664]{2,1,0:T(8,128)(2,1)S(1)}, u32[]{:S(2)}, u32[]{:S(2)}) collective-permute-start(bf16[2,32,1664]{2,1,0:T(8,128)(2,1)S(1)} %hidden.5.refs_0_.mine), channel_id=1, source_target_pairs={{0,1},{1,0},{2,3},{3,2},{4,5},{5,4},{6,7},{7,6},{8,9},{9,8},{10,11... | collective-permute-start | bytes 638984 | tf_op jit(solution)/shard_map/ppermute | solution.py:51
  113.2 5.9 %collective-permute-start.27 = (bf16[2,32,1664]{2,1,0:T(8,128)(2,1)S(1)}, bf16[2,32,1664]{2,1,0:T(8,128)(2,1)S(1)}, u32[]{:S(2)}, u32[]{:S(2)}) collective-permute-start(bf16[2,32,1664]{2,1,0:T(8,128)(2,1)S(1)} %hidden.6.refs_0_.mine), channel_id=1, source_target_pairs={{0,3},{1,2},{2,1},{3,0},{4,7},{5,6},{6,5},{7,4},{8,11},{9,10},{10,... | collective-permute-start | bytes 638984 | tf_op jit(solution)/shard_map/ppermute | solution.py:51
  115.9 5.9 %collective-permute-start.26 = (bf16[2,32,1664]{2,1,0:T(8,128)(2,1)S(1)}, bf16[2,32,1664]{2,1,0:T(8,128)(2,1)S(1)}, u32[]{:S(2)}, u32[]{:S(2)}) collective-permute-start(bf16[2,32,1664]{2,1,0:T(8,128)(2,1)S(1)} %hidden.7.refs_0_.mine), channel_id=1, source_target_pairs={{0,1},{1,0},{2,3},{3,2},{4,5},{5,4},{6,7},{7,6},{8,9},{9,8},{10,11... | collective-permute-start | bytes 638984 | tf_op jit(solution)/shard_map/ppermute | solution.py:51
  116.1 7.5 %collective-permute-start.33 = (bf16[2,64,1664]{2,1,0:T(8,128)(2,1)S(1)}, bf16[2,64,1664]{2,1,0:T(8,128)(2,1)S(1)}, u32[]{:S(2)}, u32[]{:S(2)}) collective-permute-start(bf16[2,64,1664]{2,1,0:T(8,128)(2,1)S(1)} %join.8.refs_0_.mine), channel_id=1, source_target_pairs={{0,4},{1,5},{2,6},{3,7},{4,0},{5,1},{6,2},{7,3},{8,12},{9,13},{10,... | collective-permute-start | bytes 1277960 | tf_op jit(solution)/shard_map/ppermute | solution.py:51
  119.2 8.5 %collective-permute-start.32 = (bf16[2,64,1664]{2,1,0:T(8,128)(2,1)S(1)}, bf16[2,64,1664]{2,1,0:T(8,128)(2,1)S(1)}, u32[]{:S(2)}, u32[]{:S(2)}) collective-permute-start(bf16[2,64,1664]{2,1,0:T(8,128)(2,1)S(1)} %join.9.refs_0_.mine), channel_id=1, source_target_pairs={{0,12},{1,13},{2,14},{3,15},{4,8},{5,9},{6,10},{7,11},{8,4},{9,5},... | collective-permute-start | bytes 1277960 | tf_op jit(solution)/shard_map/ppermute | solution.py:51
  121.9 8.6 %collective-permute-start.31 = (bf16[2,64,1664]{2,1,0:T(8,128)(2,1)S(1)}, bf16[2,64,1664]{2,1,0:T(8,128)(2,1)S(1)}, u32[]{:S(2)}, u32[]{:S(2)}) collective-permute-start(bf16[2,64,1664]{2,1,0:T(8,128)(2,1)S(1)} %join.10.refs_0_.mine), channel_id=1, source_target_pairs={{0,4},{1,5},{2,6},{3,7},{4,0},{5,1},{6,2},{7,3},{8,12},{9,13},{10,... | collective-permute-start | bytes 1277960 | tf_op jit(solution)/shard_map/ppermute | solution.py:51
  123.6 9.5 %collective-permute-start.30 = (bf16[2,64,1664]{2,1,0:T(8,128)(2,1)S(1)}, bf16[2,64,1664]{2,1,0:T(8,128)(2,1)S(1)}, u32[]{:S(2)}, u32[]{:S(2)}) collective-permute-start(bf16[2,64,1664]{2,1,0:T(8,128)(2,1)S(1)} %join.11.refs_0_.mine), channel_id=1, source_target_pairs={{0,12},{1,13},{2,14},{3,15},{4,8},{5,9},{6,10},{7,11},{8,4},{9,5},... | collective-permute-start | bytes 1277960 | tf_op jit(solution)/shard_map/ppermute | solution.py:51
  127.6 14.6 %collective-permute-start.38 = (bf16[2,128,1664]{2,1,0:T(8,128)(2,1)S(1)}, bf16[2,128,1664]{2,1,0:T(8,128)(2,1)S(1)}, u32[]{:S(2)}, u32[]{:S(2)}) collective-permute-start(bf16[2,128,1664]{2,1,0:T(8,128)(2,1)S(1)} %join.12.refs_0_), channel_id=1, source_target_pairs={{0,12},{1,13},{2,14},{3,15},{4,8},{5,9},{6,10},{7,11},{8,4},{9,5},... | collective-permute-start | bytes 2555912 | tf_op jit(solution)/shard_map/ppermute | solution.py:51
  130.4 15.2 %collective-permute-start.37 = (bf16[2,128,1664]{2,1,0:T(8,128)(2,1)S(1)}, bf16[2,128,1664]{2,1,0:T(8,128)(2,1)S(1)}, u32[]{:S(2)}, u32[]{:S(2)}) collective-permute-start(bf16[2,128,1664]{2,1,0:T(8,128)(2,1)S(1)} %join.13.refs_0_), channel_id=1, source_target_pairs={{0,4},{1,5},{2,6},{3,7},{4,0},{5,1},{6,2},{7,3},{8,12},{9,13},{10,... | collective-permute-start | bytes 2555912 | tf_op jit(solution)/shard_map/ppermute | solution.py:51
  133.1 13.8 %collective-permute-start.41 = (bf16[1,128,1664]{2,1,0:T(8,128)(2,1)S(1)}, bf16[1,128,1664]{2,1,0:T(8,128)(2,1)S(1)}, u32[]{:S(2)}, u32[]{:S(2)}) collective-permute-start(bf16[1,128,1664]{2,1,0:T(8,128)(2,1)S(1)} %get-tuple-element.91.refs_1_), channel_id=1, source_target_pairs={{0,12},{1,13},{2,14},{3,15},{4,8},{5,9},{6,10},{7,11},{8,4},{9,5},... | collective-permute-start | bytes 1277960 | tf_op jit(solution)/shard_map/ppermute | solution.py:51
  135.8 17.4 %collective-permute-start.40 = (bf16[1,128,1664]{2,1,0:T(8,128)(2,1)S(1)}, bf16[1,128,1664]{2,1,0:T(8,128)(2,1)S(1)}, u32[]{:S(2)}, u32[]{:S(2)}) collective-permute-start(bf16[1,128,1664]{2,1,0:T(8,128)(2,1)S(1)} %get-tuple-element.90.refs_1_), channel_id=1, source_target_pairs={{0,4},{1,5},{2,6},{3,7},{4,0},{5,1},{6,2},{7,3},{8,12},{9,13},{10,... | collective-permute-start | bytes 1277960 | tf_op jit(solution)/shard_map/ppermute | solution.py:51
  137.0 17.3 %collective-permute-start.39 = (bf16[1,128,1664]{2,1,0:T(8,128)(2,1)S(1)}, bf16[1,128,1664]{2,1,0:T(8,128)(2,1)S(1)}, u32[]{:S(2)}, u32[]{:S(2)}) collective-permute-start(bf16[1,128,1664]{2,1,0:T(8,128)(2,1)S(1)} %get-tuple-element.86.refs_0_), channel_id=1, source_target_pairs={{0,12},{1,13},{2,14},{3,15},{4,8},{5,9},{6,10},{7,11},{8,4},{9,5},... | collective-permute-start | bytes 1277960 | tf_op jit(solution)/shard_map/ppermute | solution.py:51
  142.2 15.0 %collective-permute-start.34 = (bf16[1,128,1664]{2,1,0:T(8,128)(2,1)S(1)}, bf16[1,128,1664]{2,1,0:T(8,128)(2,1)S(1)}, u32[]{:S(2)}, u32[]{:S(2)}) collective-permute-start(bf16[1,128,1664]{2,1,0:T(8,128)(2,1)S(1)} %get-tuple-element.87.refs_3_.refs_0_), channel_id=1, source_target_pairs={{0,4},{1,5},{2,6},{3,7},{4,0},{5,1},{6,2},{7,3},{8,12},{9,13},{10,... | collective-permute-start | bytes 1277960 | tf_op jit(solution)/shard_map/ppermute | solution.py:51
  147.7 11.2 %collective-permute-start.45 = (bf16[128,1024]{1,0:T(8,128)(2,1)S(1)}, bf16[128,1024]{1,0:T(8,128)(2,1)S(1)}, u32[]{:S(2)}, u32[]{:S(2)}) collective-permute-start(bf16[128,1024]{1,0:T(8,128)(2,1)S(1)} %get-tuple-element.93.refs_5_), channel_id=1, source_target_pairs={{0,16},{16,0},{32,48},{48,32},{64,80},{80,64},{96,112},{112,96},{1... | collective-permute-start | bytes 786440 | tf_op jit(solution)/shard_map/ppermute | solution.py:55
  154.0 6.9 %collective-permute-start.43 = (bf16[128,1024]{1,0:T(8,128)(2,1)S(1)}, bf16[128,1024]{1,0:T(8,128)(2,1)S(1)}, u32[]{:S(2)}, u32[]{:S(2)}) collective-permute-start(bf16[128,1024]{1,0:T(8,128)(2,1)S(1)} %get-tuple-element.94.refs_5_), channel_id=1, source_target_pairs={{0,16},{16,0},{32,48},{48,32},{64,80},{80,64},{96,112},{112,96},{1... | collective-permute-start | bytes 786440 | tf_op jit(solution)/shard_map/ppermute | solution.py:55
  155.2 5.6 %collective-permute-start.47 = (bf16[128,1024]{1,0:T(8,128)(2,1)S(1)}, bf16[128,1024]{1,0:T(8,128)(2,1)S(1)}, u32[]{:S(2)}, u32[]{:S(2)}) collective-permute-start(bf16[128,1024]{1,0:T(8,128)(2,1)S(1)} %get-tuple-element.95.refs_5_), channel_id=1, source_target_pairs={{0,16},{16,0},{32,48},{48,32},{64,80},{80,64},{96,112},{112,96},{1... | collective-permute-start | bytes 786440 | tf_op jit(solution)/shard_map/ppermute | solution.py:55
  158.0 4.3 %collective-permute-start.42 = (bf16[128,1024]{1,0:T(8,128)(2,1)S(1)}, bf16[128,1024]{1,0:T(8,128)(2,1)S(1)}, u32[]{:S(2)}, u32[]{:S(2)}) collective-permute-start(bf16[128,1024]{1,0:T(8,128)(2,1)S(1)} %get-tuple-element.97), channel_id=1, source_target_pairs={{0,16},{16,0},{32,48},{48,32},{64,80},{80,64},{96,112},{112,96},{1... | collective-permute-start | bytes 786440 | tf_op jit(solution)/shard_map/ppermute | solution.py:55
  159.0 8.0 %collective-permute-start.46 = (bf16[128,1024]{1,0:T(8,128)(2,1)S(1)}, bf16[128,1024]{1,0:T(8,128)(2,1)S(1)}, u32[]{:S(2)}, u32[]{:S(2)}) collective-permute-start(bf16[128,1024]{1,0:T(8,128)(2,1)S(1)} %add_convert_fusion.2), channel_id=1, source_target_pairs={{0,96},{16,112},{32,0},{48,16},{64,32},{80,48},{96,64},{112,80},{1... | collective-permute-start | bytes 786440 | tf_op jit(solution)/shard_map/ppermute | solution.py:59
  160.8 14.5 %collective-permute-start.48 = (bf16[128,1024]{1,0:T(8,128)(2,1)S(1)}, bf16[128,1024]{1,0:T(8,128)(2,1)S(1)}, u32[]{:S(2)}, u32[]{:S(2)}) collective-permute-start(bf16[128,1024]{1,0:T(8,128)(2,1)S(1)} %add_convert_fusion.1), channel_id=1, source_target_pairs={{0,32},{16,48},{32,64},{48,80},{64,96},{80,112},{96,0},{112,16},{1... | collective-permute-start | bytes 786440 | tf_op jit(solution)/shard_map/ppermute | solution.py:59
  161.0 14.3 %collective-permute-start.44 = (bf16[128,1024]{1,0:T(8,128)(2,1)S(1)}, bf16[128,1024]{1,0:T(8,128)(2,1)S(1)}, u32[]{:S(2)}, u32[]{:S(2)}) collective-permute-start(bf16[128,1024]{1,0:T(8,128)(2,1)S(1)} %add_convert_fusion.3), channel_id=1, source_target_pairs={{0,64},{16,80},{32,96},{48,112},{64,0},{80,16},{96,32},{112,48},{1... | collective-permute-start | bytes 786440 | tf_op jit(solution)/shard_map/ppermute | solution.py:59
  (2 other events, 4.9 us)
